TPU v7x, 32 devices: a whole 2x2x4 slice. The times are simulated.
32 devices in a mesh: groups: 2 (over y), ep: 4 (over z), tp: 4 (over x, core).
Axes of the slice: x: 2, y: 2, z: 4, core: 2. Of those that a mesh axis runs over, the one named last changes fastest.
Arguments:
- residual: bfloat16 [128, 3072], P(('groups', 'ep'), 'tp'), parts along dimension 0, may hold values from -6 to 6
- queries: bfloat16 [128, 3072], P(('groups', 'ep'), 'tp'), parts along dimension 0, may hold values from -150 to 150
- token_keys: bfloat16 [128, 1024], P(('groups', 'ep'), 'tp'), parts along dimension 0, may hold values from -5 to 5
- token_values: bfloat16 [128, 1024], P(('groups', 'ep'), 'tp'), parts along dimension 0, may hold values from -5 to 5
- stored_keys: bfloat16 [128, 128, 1024], P(('groups', 'ep'), None, 'tp'), parts along dimension 0, may hold values from -5 to 5
- stored_values: bfloat16 [128, 128, 1024], P(('groups', 'ep'), None, 'tp'), parts along dimension 0, may hold values from -5 to 5
- lengths: int32 [128], P(('groups', 'ep')), parts along dimension 0, may hold values from 2 to 128
- norm_gain_vector: float32 [3072], P('tp'), may hold values from 0.1 to 1.9
- router: bfloat16 [3072, 4], P('tp'), may hold values from -0.109375 to 0.109375
- expert_gate_weight: bfloat16 [3072, 32768], P(None, ('ep', 'tp')), may hold values from -0.109375 to 0.109375
- expert_up_weight: bfloat16 [3072, 32768], P(None, ('ep', 'tp')), may hold values from -0.109375 to 0.109375
- expert_down_weight: bfloat16 [32768, 3072], P(('ep', 'tp')), may hold values from -0.0625 to 0.0625
- adapter_down_map: bfloat16 [3072, 512], P('tp'), may hold values from -0.109375 to 0.109375
- adapter_up_map: bfloat16 [128, 32768], P(None, ('ep', 'tp')), may hold values from -0.75 to 0.75
- routes: int32 [128, 2], P(('groups', 'ep')), parts along dimension 0, may hold values from 0 to 3, all different within a row; in each aligned block of 16 rows (0 to 15, 16 to 31, ...) at most 10 rows name the same one
- tenants: int32 [128], P(('groups', 'ep')), parts along dimension 0, may hold values from 0 to 7
Outputs:
- layer_out: bfloat16 [128, 3072], P(('groups', 'ep'), 'tp'), parts along dimension 0
There are 2 independent parts, one for each index of `groups`. A program takes and returns all parts, laid end to end along the dimension named above; an argument that names none is the same for every part. Nothing has to cross between parts.
Inputs may be any that keep to these rules, and one draw needn't show every extreme that they name: `routes`: in the 16 rows of one index of ep no expert is named by more than 10 rows; the two experts of a row differ.
All inputs are finite; a program needn't handle non-finite values.
Results may differ from a plain program's by a relative error of at most 0.0061.
Values may be sent and summed in bfloat16 or wider, within the bound.
No kernel may reach another device: no remote copies, remote signals or barrier semaphores. Data moves between devices by JAX's collectives and lax.ppermute only.
A program may use at most 128 MiB of HBM per device.

v0:
```python
import jax
import jax.numpy as jnp
from jax import lax
from jax.sharding import PartitionSpec as P

HEADS = 24
KVH = 8
HD = 128
EXPERT_COUNT = 4
ADAPTER_RANK = 16
TENANT_COUNT = 8
CAP = 10


def per_device(
    residual,
    queries,
    token_keys,
    token_values,
    stored_keys,
    stored_values,
    lengths,
    norm_gain_vector,
    router,
    expert_gate_weight,
    expert_up_weight,
    expert_down_weight,
    adapter_down_map,
    adapter_up_map,
    routes,
    tenants,
):
    count_of_rows = residual.shape[0]
    expert_devices = lax.axis_size("ep")
    tensor_devices = lax.axis_size("tp")
    kv_local = token_keys.shape[1] // HD
    cache_length = stored_keys.shape[1]
    group_heads = HEADS // KVH
    score_scale = HD ** (-0.5)
    query_heads = queries.reshape(count_of_rows, kv_local, group_heads, HD)
    key_heads = stored_keys.reshape(count_of_rows, cache_length, kv_local, HD)
    value_heads = stored_values.reshape(count_of_rows, cache_length, kv_local, HD)
    fresh_keys = token_keys.reshape(count_of_rows, kv_local, HD)
    fresh_values = token_values.reshape(count_of_rows, kv_local, HD)
    cache_scores = (
        jnp.einsum("rgjd,rpgd->rgjp", query_heads, key_heads, preferred_element_type=jnp.float32)
        * score_scale
    )
    fresh_scores = (
        jnp.einsum("rgjd,rgd->rgj", query_heads, fresh_keys, preferred_element_type=jnp.float32)
        * score_scale
    )
    positions = lax.broadcasted_iota(jnp.int32, (count_of_rows, cache_length), 1)
    visible = positions < lengths[:, None]
    cache_scores = jnp.where(visible[:, None, None, :], cache_scores, -jnp.inf)
    largest = jnp.maximum(jnp.max(cache_scores, axis=3), fresh_scores)
    cache_exp = jnp.exp(cache_scores - largest[..., None])
    fresh_exp = jnp.exp(fresh_scores - largest)
    denominator = jnp.sum(cache_exp, axis=3) + fresh_exp
    cache_probs = (cache_exp / denominator[..., None]).astype(jnp.bfloat16)
    fresh_probs = (fresh_exp / denominator).astype(jnp.bfloat16)
    attended = jnp.einsum(
        "rgjp,rpgd->rgjd", cache_probs, value_heads, preferred_element_type=jnp.float32
    )
    attended = (
        attended
        + fresh_probs.astype(jnp.float32)[..., None]
        * fresh_values.astype(jnp.float32)[:, :, None, :]
    )
    attended = attended.reshape(count_of_rows, -1)
    state = (residual.astype(jnp.float32) + attended).astype(jnp.bfloat16)
    state_float = state.astype(jnp.float32)
    square_total = lax.psum(jnp.sum(state_float * state_float, axis=1), "tp")
    inverse_rms = lax.rsqrt(square_total / (state_float.shape[1] * tensor_devices) + 1e-05)
    normalized_slice = (state_float * inverse_rms[:, None] * norm_gain_vector[None, :]).astype(
        jnp.bfloat16
    )
    tenant_hot = (
        tenants[:, None] == lax.broadcasted_iota(jnp.int32, (count_of_rows, TENANT_COUNT), 1)
    ).astype(jnp.float32)
    expert_hot = (
        routes[:, :, None] == lax.broadcasted_iota(jnp.int32, (count_of_rows, 2, EXPERT_COUNT), 2)
    ).astype(jnp.float32)
    adapter_total = jnp.dot(
        normalized_slice, adapter_down_map, preferred_element_type=jnp.float32
    ).reshape(count_of_rows, TENANT_COUNT, EXPERT_COUNT, ADAPTER_RANK)
    lowrank_part = jnp.einsum(
        "rt,rke,rten->rkn", tenant_hot, expert_hot, adapter_total, precision=lax.Precision.HIGHEST
    )
    logit_part = jnp.dot(normalized_slice, router, preferred_element_type=jnp.float32)
    lowrank_sum, logits = lax.psum((lowrank_part, logit_part), "tp")
    chosen = jnp.take_along_axis(logits, routes, axis=1)
    first_weight = jax.nn.sigmoid(chosen[:, 0] - chosen[:, 1])
    route_weights = jnp.stack([first_weight, 1.0 - first_weight], axis=1)
    lowrank_round = lowrank_sum.astype(jnp.bfloat16)
    tenant_mask = tenant_hot.astype(jnp.bfloat16)
    adapter_rows = (tenant_mask[:, None, :, None] * lowrank_round[:, :, None, :]).reshape(
        count_of_rows * 2, TENANT_COUNT * ADAPTER_RANK
    )
    flat_routes = routes.reshape(-1)
    route_hot = (
        flat_routes[:, None]
        == lax.broadcasted_iota(jnp.int32, (count_of_rows * 2, EXPERT_COUNT), 1)
    ).astype(jnp.int32)
    before = jnp.cumsum(route_hot, axis=0) - route_hot
    slot_index = jnp.sum(before * route_hot, axis=1)
    target = flat_routes * CAP + slot_index
    selector = (
        lax.broadcasted_iota(jnp.int32, (EXPERT_COUNT * CAP, count_of_rows * 2), 0)
        == target[None, :]
    ).astype(jnp.bfloat16)
    payload = lax.all_gather(normalized_slice, "tp", axis=1, tiled=True)
    doubled = jnp.repeat(payload, 2, axis=0)
    per_expert = jnp.dot(selector, doubled, preferred_element_type=jnp.float32).astype(jnp.bfloat16)
    per_lowrank = jnp.dot(selector, adapter_rows, preferred_element_type=jnp.float32).astype(
        jnp.bfloat16
    )
    replicas = expert_devices // EXPERT_COUNT

    def spread(expert_block):
        width_cols = expert_block.shape[1]
        widened = jnp.broadcast_to(
            expert_block.reshape(EXPERT_COUNT, 1, CAP, width_cols),
            (EXPERT_COUNT, replicas, CAP, width_cols),
        )
        return widened.reshape(expert_devices, CAP, width_cols)

    send_rows = spread(per_expert)
    send_lowrank = spread(per_lowrank)
    rows_in = lax.all_to_all(send_rows, "ep", split_axis=0, concat_axis=0, tiled=True)
    lowrank_in = lax.all_to_all(send_lowrank, "ep", split_axis=0, concat_axis=0, tiled=True)
    sources = rows_in.shape[0]
    item_count = rows_in.shape[1]
    flat_rows = rows_in.reshape(sources * item_count, rows_in.shape[2])
    flattened_adapter = lowrank_in.reshape(sources * item_count, lowrank_in.shape[2])
    gate_value = jnp.dot(flat_rows, expert_gate_weight, preferred_element_type=jnp.float32)
    up_projected = jnp.dot(flat_rows, expert_up_weight, preferred_element_type=jnp.float32)
    up_projected = up_projected + jnp.dot(
        flattened_adapter, adapter_up_map, preferred_element_type=jnp.float32
    )
    activated = (jax.nn.silu(gate_value) * up_projected).astype(jnp.bfloat16)
    partial_out = jnp.dot(activated, expert_down_weight, preferred_element_type=jnp.float32)
    partial_out = partial_out.reshape(sources, item_count, partial_out.shape[1])
    returned = lax.all_to_all(partial_out, "ep", split_axis=0, concat_axis=0, tiled=True)
    column = lax.broadcasted_iota(jnp.int32, (expert_devices * CAP,), 0)
    column_expert = column // CAP // replicas
    column_slot = column % CAP
    slot_pairs = slot_index.reshape(count_of_rows, 2)
    matches = (column_expert[None, None, :] == routes[:, :, None]) & (
        column_slot[None, None, :] == slot_pairs[:, :, None]
    )
    mixing = jnp.sum(jnp.where(matches, route_weights[:, :, None], 0.0), axis=1)
    combined = jnp.dot(
        mixing,
        returned.reshape(expert_devices * CAP, returned.shape[2]),
        preferred_element_type=jnp.float32,
        precision=lax.Precision.HIGHEST,
    )
    own_share = lax.psum_scatter(combined, "tp", scatter_dimension=1, tiled=True)
    return (state_float + own_share).astype(jnp.bfloat16)


def solution(mesh):
    placed = (
        P(("groups", "ep"), "tp"),
        P(("groups", "ep"), "tp"),
        P(("groups", "ep"), "tp"),
        P(("groups", "ep"), "tp"),
        P(("groups", "ep"), None, "tp"),
        P(("groups", "ep"), None, "tp"),
        P(("groups", "ep")),
        P("tp"),
        P("tp", None),
        P(None, ("ep", "tp")),
        P(None, ("ep", "tp")),
        P(("ep", "tp"), None),
        P("tp", None),
        P(None, ("ep", "tp")),
        P(("groups", "ep"), None),
        P(("groups", "ep")),
    )
    return jax.shard_map(
        per_device, mesh=mesh, in_specs=placed, out_specs=P(("groups", "ep"), "tp"), check_vma=False
    )
```

profile of v0, /device:TPU:0, one launch (start us, length us, event | category | flops | bytes accessed | tf_op | source)
XLA Modules:
  0.0 140.3 jit_solution(17174005347903728681)
XLA Ops:
  6.5 0.8 iota_compare_fusion.5
  7.4 0.7 convert_convert_fusion
  8.1 0.8 copy.58
  8.8 0.1 eq.72
  9.1 0.2 select_reduce_fusion.1
  9.3 0.7 reshape.156
  10.0 0.7 reshape.139
  10.7 0.8 reshape.127
  11.4 0.1 fusion.41
  11.6 0.7 fusion.40
  12.4 0.2 fusion.16
  12.6 1.7 %convolution_add_fusion.1 = f32[16,2,3,128]{3,2,1,0:T(4,128)S(1)} fusion(f32[16,2,3,128]{3,2,1,0:T(4,128)S(1)} %get-tuple-element.16, f32[16,2,128]{2,1,0:T(2,128)S(1)} %reshape.139, f32[16,2,3]{2,1,0:T(2,128)S(1)} %get-tuple-element.12, f32[16,2,3]{2,1,0:T(2,128)S(1)} %get-tuple-element.11, f32[16,2,3]{2,1,0:T(2,128)S(1)} %multiply_maximum_fusion, ...), kind=kOutput, calls=%fused_computation.5 | convolution fusion | flops 3207168 | bytes 1164416 | tf_op jit(solution)/shard_map/rgjp,rpgd->rgjd/dot_general | solution.py:62
  14.3 0.9 fusion.17
  15.2 8.3 %psum.21 = f32[16]{0:T(128)S(1)} all-reduce(f32[16]{0:T(128)S(1)} %get-tuple-element.9), channel_id=1, replica_groups=mesh['groups'=2,'ep'=4,'tp'=4] {'tp'}, use_global_device_ids=true, to_apply=%region_5.6 | all-reduce | flops 16 | bytes 128 | tf_op jit(solution)/shard_map/psum | solution.py:73
  23.5 0.8 fusion.19
  24.3 0.8 fusion.42
  25.1 1.3 fusion.45
  26.5 0.2 reshape.135
  26.7 0.2 fusion.13
  27.0 0.3 fusion.24
  27.2 10.3 %all-reduce = (f32[16,4]{0,1:T(4,128)S(1)}, bf16[16,2,16]{2,1,0:T(2,128)(2,1)S(1)}) all-reduce(f32[16,4]{0,1:T(4,128)S(1)} %fusion.42, f32[16,2,16]{2,1,0:T(2,128)S(1)} %fusion.24), channel_id=1, replica_groups=mesh['groups'=2,'ep'=4,'tp'=4] {'tp'}, use_global_device_ids=true, to_apply=%region_6.7 | all-reduce | flops 576 | bytes 3584 | tf_op jit(solution)/shard_map/psum | solution.py:91
  37.6 0.1 mul.100
  37.7 0.1 convolution_convert_fusion.1
  37.8 0.6 reshape_reshape.7
  38.4 4.9 %all-to-all-start.1 = ((bf16[4,10,128]{2,1,0:T(8,128)(2,1)}), bf16[4,10,128]{2,1,0:T(8,128)(2,1)S(1)}, u32[]{:S(2)}, u32[]{:S(2)}) async-start(bf16[4,10,128]{2,1,0:T(8,128)(2,1)} %reshape_reshape.7), calls=%async_computation.1 | async-start | bytes 32768 | tf_op jit(solution)/shard_map/all_to_all | solution.py:131
  43.3 0.7 broadcast_add_fusion
  44.0 5.3 %all_gather.3 = bf16[16,3072]{1,0:T(8,128)(2,1)S(1)} all-gather(bf16[16,768]{1,0:T(8,128)(2,1)S(1)} %fusion.19), channel_id=1, replica_groups=mesh['groups'=2,'ep'=4,'tp'=4] {'tp'}, dimensions={1}, use_global_device_ids=true | all-gather | bytes 122880 | tf_op jit(solution)/shard_map/all_gather | solution.py:112
  49.3 0.1 broadcast_in_dim.31
  49.5 0.2 convolution_convert_fusion
  49.7 0.7 broadcast_compare_fusion
  50.5 0.1 copy.62
  50.7 0.8 reshape_reshape.6
  51.5 5.1 %all-to-all-start = ((bf16[4,10,3072]{2,1,0:T(8,128)(2,1)}), bf16[4,10,3072]{2,1,0:T(8,128)(2,1)S(1)}, u32[]{:S(2)}, u32[]{:S(2)}) async-start(bf16[4,10,3072]{2,1,0:T(8,128)(2,1)} %reshape_reshape.6), calls=%async_computation | async-start | bytes 786432 | tf_op jit(solution)/shard_map/all_to_all | solution.py:130
  56.7 0.1 copy.66
  56.8 0.1 reshape.140
  57.0 0.8 gather_fusion
  57.8 11.0 %all-to-all-done = bf16[4,10,3072]{2,1,0:T(8,128)(2,1)S(1)} async-done(((bf16[4,10,3072]{2,1,0:T(8,128)(2,1)}), bf16[4,10,3072]{2,1,0:T(8,128)(2,1)S(1)}, u32[]{:S(2)}, u32[]{:S(2)}) %all-to-all-start) | async-done | bytes 245792 | tf_op jit(solution)/shard_map/all_to_all | solution.py:130
  68.8 0.1 reshape.134
  68.9 6.8 %fusion.44 = f32[40,2048]{1,0:T(8,128)S(1)} fusion(bf16[40,3072]{1,0:T(8,128)(2,1)S(1)} %reshape.134, bf16[3072,2048]{1,0:T(8,128)(2,1)} %param.26), kind=kOutput, calls=%fused_computation.81 | convolution fusion | flops 503316480 | bytes 13156352 | tf_op jit(solution)/shard_map/dot_general | solution.py:137
  75.8 6.9 %fusion.43 = f32[40,2048]{1,0:T(8,128)S(1)} fusion(bf16[40,3072]{1,0:T(8,128)(2,1)S(1)} %reshape.134, bf16[3072,2048]{1,0:T(8,128)(2,1)} %param.25), kind=kOutput, calls=%fused_computation.80 | convolution fusion | flops 503316480 | bytes 13156352 | tf_op jit(solution)/shard_map/dot_general | solution.py:136
  82.7 5.9 %fusion.3 = f32[40,3072]{1,0:T(8,128)S(1)} fusion(bf16[2048,3072]{1,0:T(8,128)(2,1)} %param.27, f32[40,2048]{1,0:T(8,128)S(1)} %fusion.44, bf16[40,128]{1,0:T(8,128)(2,1)S(1)} %reshape.136, bf16[128,2048]{1,0:T(8,128)(2,1)S(1)} %copy-done.1, f32[40,2048]{1,0:T(8,128)S(1)} %fusion.43), kind=kOutput, calls=%fused_computation.8 | convolution fusion | flops 524861440 | bytes 14264320 | tf_op jit(solution)/shard_map/dot_general | solution.py:142
  88.6 1.0 reshape.137
  89.6 3.5 %all-to-all-start.2 = ((f32[4,10,3072]{2,1,0:T(8,128)}), f32[4,10,3072]{2,1,0:T(8,128)S(1)}, u32[]{:S(2)}, u32[]{:S(2)}) async-start(f32[4,10,3072]{2,1,0:T(8,128)} %reshape.137), calls=%async_computation.2 | async-start | bytes 1572864 | tf_op jit(solution)/shard_map/all_to_all | solution.py:144
  93.1 0.1 broadcast_subtract_fusion
  93.5 19.3 %all-to-all-done.2 = f32[4,10,3072]{2,1,0:T(8,128)S(1)} async-done(((f32[4,10,3072]{2,1,0:T(8,128)}), f32[4,10,3072]{2,1,0:T(8,128)S(1)}, u32[]{:S(2)}, u32[]{:S(2)}) %all-to-all-start.2) | async-done | bytes 491552 | tf_op jit(solution)/shard_map/all_to_all | solution.py:144
  112.9 1.0 fusion.46
  114.0 18.1 %reduce-scatter.2.cloned.1.call-done = f32[16,768]{1,0:T(8,128)} async-done(((f32[16,3072]{1,0:T(8,128)}), f32[16,768]{1,0:T(8,128)}) %reduce-scatter.2.cloned.1.call-update) | async-done | bytes 49168 | tf_op jit(solution)/shard_map/reduce_scatter | solution.py:159
  132.0 1.4 %fusion.20 = bf16[16,768]{1,0:T(8,128)(2,1)} fusion(f32[16,768]{1,0:T(8,128)} %reduce-scatter.2.cloned.1.call-done, bf16[16,768]{1,0:T(8,128)(2,1)S(1)} %get-tuple-element.10), kind=kLoop, calls=%fused_computation.31 | loop fusion | flops 36864 | bytes 98304 | tf_op jit(solution)/shard_map/convert_element_type | solution.py:160
  (32 shorter events, 1.3 us)
Async XLA Ops:
  6.5 5.1 %copy-start = (bf16[16,128,256]{2,1,0:T(8,128)(2,1)S(1)}, bf16[16,128,256]{2,1,0:T(8,128)(2,1)}, u32[]{:S(2)}) copy-start(bf16[16,128,256]{2,1,0:T(8,128)(2,1)} %param.20) | copy-start | bytes 3145732
  38.4 13.1 %all-to-all-start.1 = ((bf16[4,10,128]{2,1,0:T(8,128)(2,1)}), bf16[4,10,128]{2,1,0:T(8,128)(2,1)S(1)}, u32[]{:S(2)}, u32[]{:S(2)}) async-start(bf16[4,10,128]{2,1,0:T(8,128)(2,1)} %reshape_reshape.7), calls=%async_computation.1 | async-start | bytes 32768 | tf_op jit(solution)/shard_map/all_to_all | solution.py:131
  51.5 17.3 %all-to-all-start = ((bf16[4,10,3072]{2,1,0:T(8,128)(2,1)}), bf16[4,10,3072]{2,1,0:T(8,128)(2,1)S(1)}, u32[]{:S(2)}, u32[]{:S(2)}) async-start(bf16[4,10,3072]{2,1,0:T(8,128)(2,1)} %reshape_reshape.6), calls=%async_computation | async-start | bytes 786432 | tf_op jit(solution)/shard_map/all_to_all | solution.py:130
  75.7 6.9 %copy-start.1 = (bf16[128,2048]{1,0:T(8,128)(2,1)S(1)}, bf16[128,2048]{1,0:T(8,128)(2,1)}, u32[]{:S(2)}) copy-start(bf16[128,2048]{1,0:T(8,128)(2,1)} %param.29) | copy-start | bytes 1572868
  82.7 10.7 %copy-start.2 = (s32[16,2]{0,1:T(2,128)S(1)}, s32[16,2]{0,1:T(2,128)}, u32[]{:S(2)}) copy-start(s32[16,2]{0,1:T(2,128)} %param.30) | copy-start | bytes 388
  89.6 23.3 %all-to-all-start.2 = ((f32[4,10,3072]{2,1,0:T(8,128)}), f32[4,10,3072]{2,1,0:T(8,128)S(1)}, u32[]{:S(2)}, u32[]{:S(2)}) async-start(f32[4,10,3072]{2,1,0:T(8,128)} %reshape.137), calls=%async_computation.2 | async-start | bytes 1572864 | tf_op jit(solution)/shard_map/all_to_all | solution.py:144
  93.1 39.0 %reduce-scatter.2.cloned.1.call-start = ((), (), s32[]{:S(2)}) async-start(), calls=%async_computation.4 | async-start | bytes 245760 | tf_op jit(solution)/shard_map/reduce_scatter | solution.py:159
Sparse Core Ops, SparseCore 0:
  114.1 17.8 reduce-scatter.1
where the time goes:
time: 141 us; the launch traced here: 140 us
  waiting for transfers between devices  48.4 us (34%)
  matrix products  26.3 us (19%)
  blocking collectives  23.9 us (17%)
  between operations  13.6 us (10%)
  starting transfers between devices  13.5 us (10%)
  local copies, waits for them, and re-layouts  7.71 us (5%)
  other arithmetic  6.9 us (5%)
    all_to_all x1, waiting for transfers between devices, per_device(): lax.all_to_all(partial_out, 'ep', split_axis=0, concat_axis=0, tiled=True)  19.3 us
    reduce_scatter x1, waiting for transfers between devices, per_device(): lax.psum_scatter(combined, 'tp', scatter_dimension=1, tiled=True)  18.1 us
    all_to_all x1, waiting for transfers between devices, per_device(): lax.all_to_all(send_rows, 'ep', split_axis=0, concat_axis=0, tiled=True)  11 us
    psum x1, blocking collectives, per_device(): lowrank_sum, logits = lax.psum((lowrank_part, logit_part), 'tp')  10.3 us
    psum x1, blocking collectives, per_device(): square_total = lax.psum(jnp.sum(state_float * state_float, axis=1), 'tp')  8.34 us
    dot_general x1, matrix products, per_device(): jnp.dot(flat_rows, expert_gate_weight, preferred_element_type=jnp.float32)  6.9 us
    dot_general x1, matrix products, per_device(): jnp.dot(flat_rows, expert_up_weight, preferred_element_type=jnp.float32)  6.85 us
    dot_general x1, matrix products, per_device(): jnp.dot(activated, expert_down_weight, preferred_element_type=jnp.float32)  5.93 us
  transfers between devices with their start and end apart: 4, of which 3 were waited for; matrix products, arithmetic and copies ran while one was open for 3% of the time, Pallas kernels for 0%

commit v1 on v0

v1 whole, which is shorter than its diff:
```python
import functools

import jax
import jax.numpy as jnp
from jax import lax
from jax.experimental import pallas as pl
from jax.experimental.pallas import tpu as pltpu
from jax.sharding import PartitionSpec as P

HEADS = 24
KVH = 8
HD = 128
EXPERT_COUNT = 4
ADAPTER_RANK = 16
TENANT_COUNT = 8
LANES = 128
ADAPTER_LANES = EXPERT_COUNT * ADAPTER_RANK
DIFF_HI, DIFF_LO, SQ_HI, SQ_LO, FIRST, SECOND, TENANT = range(ADAPTER_LANES, ADAPTER_LANES + 7)
F32 = jnp.float32
BF16 = jnp.bfloat16
ANY_LANES = (((1,), (1,)), ((), ()))


def column(values, rows):
    index = lax.broadcasted_iota(jnp.int32, (rows, LANES), 0)
    out = jnp.zeros((rows, LANES), jnp.int32)
    for r in range(rows):
        out = jnp.where(index == r, values(r), out)
    return out


def attend_kernel(
    lengths,
    tenants,
    routes,
    residual,
    queries,
    token_keys,
    token_values,
    stored_keys,
    stored_values,
    gain,
    router,
    adapter_down,
    state_out,
    payload_out,
):
    rows, features = residual.shape
    kv_local = token_keys.shape[1] // HD
    cache = stored_keys.shape[1]
    group = HEADS // KVH
    scale = HD ** (-0.5)
    length_column = column(lambda r: lengths[r], rows)
    stacked_length = jnp.concatenate([length_column[:, :1]] * group, axis=0)
    stacked_row = lax.rem(
        lax.broadcasted_iota(jnp.int32, (group * rows, max(cache, HD)), 0), jnp.int32(rows)
    )
    visible = lax.broadcasted_iota(jnp.int32, (group * rows, cache), 1) < stacked_length
    squares = jnp.zeros((rows, 1), F32)
    for g in range(kv_local):
        key_lanes = slice(g * HD, (g + 1) * HD)
        query = jnp.concatenate(
            [queries[:, (g * group + j) * HD : (g * group + j + 1) * HD] for j in range(group)],
            axis=0,
        )
        scores = jnp.zeros((group * rows, cache), F32)
        for r in range(rows):
            every = lax.dot_general(
                query, stored_keys[r, :, key_lanes], ANY_LANES, preferred_element_type=F32
            )
            scores = jnp.where(stacked_row[:, :cache] == r, every, scores)
        scores = jnp.where(visible, scores * scale, -jnp.inf)
        fresh_key = jnp.concatenate([token_keys[:, key_lanes].astype(F32)] * group, axis=0)
        fresh = jnp.sum(query.astype(F32) * fresh_key, axis=1, keepdims=True) * scale
        largest = jnp.maximum(jnp.max(scores, axis=1, keepdims=True), fresh)
        cache_exp = jnp.exp(scores - largest)
        fresh_exp = jnp.exp(fresh - largest)
        denominator = jnp.sum(cache_exp, axis=1, keepdims=True) + fresh_exp
        probs = (cache_exp / denominator).astype(BF16)
        fresh_prob = (fresh_exp / denominator).astype(BF16).astype(F32)
        attended = jnp.zeros((group * rows, HD), F32)
        for r in range(rows):
            every = jnp.dot(probs, stored_values[r, :, key_lanes], preferred_element_type=F32)
            attended = jnp.where(stacked_row[:, :HD] == r, every, attended)
        fresh_value = jnp.concatenate([token_values[:, key_lanes].astype(F32)] * group, axis=0)
        attended = attended + fresh_prob * fresh_value
        for j in range(group):
            lanes = slice((g * group + j) * HD, (g * group + j + 1) * HD)
            state = (
                residual[:, lanes].astype(F32) + attended[j * rows : (j + 1) * rows]
            ).astype(BF16)
            state_out[:, lanes] = state
            state = state.astype(F32)
            squares = squares + jnp.sum(state * state, axis=1, keepdims=True)
            payload_out[:, lanes] = (state * gain[:, lanes]).astype(BF16)
    scaled = payload_out[:, :features]
    logits = lax.dot_general(scaled, router[...], ANY_LANES, preferred_element_type=F32)
    first = column(lambda r: routes[0, r], rows)
    second = column(lambda r: routes[1, r], rows)
    tenant = column(lambda r: tenants[r], rows)
    expert = lax.broadcasted_iota(jnp.int32, logits.shape, 1)
    chosen = jnp.where(expert == first[:, :EXPERT_COUNT], logits, 0.0) - jnp.where(
        expert == second[:, :EXPERT_COUNT], logits, 0.0
    )
    diff = jnp.sum(chosen, axis=1, keepdims=True)
    adapter = jnp.dot(scaled, adapter_down[...], preferred_element_type=F32)
    lane = lax.broadcasted_iota(jnp.int32, (rows, LANES), 1)
    tail = jnp.zeros((rows, LANES), F32)
    for start in range(0, adapter.shape[1], LANES):
        owner = (lane + start) // ADAPTER_LANES
        tail = tail + jnp.where(owner == tenant, adapter[:, start : start + LANES], 0.0)
    tail = tail + pltpu.roll(tail, ADAPTER_LANES, 1)
    diff_hi = diff.astype(BF16).astype(F32)
    squares_hi = squares.astype(BF16).astype(F32)
    for place, value in (
        (DIFF_HI, diff_hi),
        (DIFF_LO, diff - diff_hi),
        (SQ_HI, squares_hi),
        (SQ_LO, squares - squares_hi),
        (FIRST, first.astype(F32)),
        (SECOND, second.astype(F32)),
        (TENANT, tenant.astype(F32)),
    ):
        tail = jnp.where(lane == place, value, tail)
    payload_out[:, features:] = tail.astype(BF16)


def attend(args):
    rows, features = args[3].shape
    smem = pl.BlockSpec(memory_space=pltpu.SMEM)
    vmem = pl.BlockSpec(memory_space=pltpu.VMEM)
    return pl.pallas_call(
        attend_kernel,
        out_shape=(
            jax.ShapeDtypeStruct((rows, features), BF16),
            jax.ShapeDtypeStruct((rows, features + LANES), BF16),
        ),
        in_specs=[smem] * 3 + [vmem] * 9,
        out_specs=(vmem, vmem),
        compiler_params=pltpu.CompilerParams(vmem_limit_bytes=12 * 2**20),
        cost_estimate=pl.CostEstimate(
            flops=200_000_000, bytes_accessed=3_000_000, transcendentals=20_000
        ),
        name="attend",
    )(*args)


def expert_kernel(
    order, replicas, gathered, gate_weight, up_weight, down_weight, adapter_up, kept, sent, active
):
    tensor_devices, rows, width = gathered.shape
    features = width - LANES
    hidden = gate_weight.shape[1]
    mine = lax.axis_index("tp")
    expert = lax.axis_index("ep") // replicas
    tail = jnp.zeros((rows, LANES), F32)
    for i in range(tensor_devices):
        tail = tail + gathered[i, :, features:].astype(F32)
    place = lambda k: tail[:, k : k + 1]
    here = gathered[0, :, features:].astype(F32)
    inverse_rms = lax.rsqrt(
        (place(SQ_HI) + place(SQ_LO)) / (features * tensor_devices) + 1e-05
    )
    diff = (place(DIFF_HI) + place(DIFF_LO)) * inverse_rms
    expert_float = expert.astype(F32)
    is_first = here[:, FIRST : FIRST + 1] == expert_float
    is_second = here[:, SECOND : SECOND + 1] == expert_float
    weight = jnp.where(
        is_first, jax.nn.sigmoid(diff), jnp.where(is_second, jax.nn.sigmoid(-diff), 0.0)
    )
    lowrank = (tail * inverse_rms).astype(BF16)
    spread_shape = (LANES, TENANT_COUNT * ADAPTER_RANK)
    source = lax.broadcasted_iota(jnp.int32, spread_shape, 0)
    target = lax.broadcasted_iota(jnp.int32, spread_shape, 1)
    spread = jnp.where(
        source == expert * ADAPTER_RANK + lax.rem(target, jnp.int32(ADAPTER_RANK)), 1.0, 0.0
    ).astype(BF16)
    lane = lax.broadcasted_iota(jnp.int32, (rows, TENANT_COUNT * ADAPTER_RANK), 1)
    own_tenant = (lane // ADAPTER_RANK).astype(F32) == here[:, TENANT : TENANT + 1]
    adapter_rows = jnp.where(
        own_tenant, jnp.dot(lowrank, spread, preferred_element_type=F32), 0.0
    ).astype(BF16)
    tile = min(256, hidden)

    def hidden_tile(n, carry):
        lanes = pl.ds(pl.multiple_of(n * tile, tile), tile)
        gate = jnp.zeros((rows, tile), F32)
        up = jnp.zeros((rows, tile), F32)
        for i in range(tensor_devices):
            start = pl.multiple_of((mine ^ order[i]) * features, features)
            scaled = gathered[i, :, :features]
            gate = gate + jnp.dot(
                scaled, gate_weight[pl.ds(start, features), lanes], preferred_element_type=F32
            )
            up = up + jnp.dot(
                scaled, up_weight[pl.ds(start, features), lanes], preferred_element_type=F32
            )
        gate = gate * inverse_rms
        up = up * inverse_rms + jnp.dot(
            adapter_rows, adapter_up[:, lanes], preferred_element_type=F32
        )
        active[:, lanes] = (gate * jax.nn.sigmoid(gate) * up * weight).astype(BF16)
        return carry

    lax.fori_loop(0, hidden // tile, hidden_tile, 0)
    out_tile = 256 if features % 256 == 0 else LANES
    for i in range(tensor_devices):
        start = (mine ^ i) * features

        def out_tiles(n, carry):
            lanes = pl.ds(pl.multiple_of(start + n * out_tile, LANES), out_tile)
            result = jnp.dot(active[...], down_weight[:, lanes], preferred_element_type=F32)
            to = pl.ds(pl.multiple_of(n * out_tile, out_tile), out_tile)
            if i % 2 == 0:
                kept[i // 2, :, to] = result
            else:
                sent[i // 2, :, to] = result.astype(BF16)
            return carry

        lax.fori_loop(0, features // out_tile, out_tiles, 0)


def experts(gathered, order, replicas, gate_weight, up_weight, down_weight, adapter_up):
    tensor_devices, rows, width = gathered.shape
    features = width - LANES
    vmem = pl.BlockSpec(memory_space=pltpu.VMEM)
    placed = [
        pltpu.with_memory_space_constraint(w, pltpu.VMEM)
        for w in (gate_weight, up_weight, down_weight)
    ]
    return pl.pallas_call(
        functools.partial(expert_kernel, order, replicas),
        out_shape=(
            jax.ShapeDtypeStruct((tensor_devices // 2, rows, features), F32),
            jax.ShapeDtypeStruct((tensor_devices // 2, rows, features), BF16),
        ),
        in_specs=[vmem] * 5,
        out_specs=(vmem, vmem),
        scratch_shapes=[pltpu.VMEM((rows, gate_weight.shape[1]), BF16)],
        compiler_params=pltpu.CompilerParams(vmem_limit_bytes=16 * 2**20),
        cost_estimate=pl.CostEstimate(
            flops=2 * rows * 3 * gate_weight.size, bytes_accessed=4_000_000, transcendentals=0
        ),
        name="experts",
    )(gathered, *placed, adapter_up)


def swap(x, axis, distance):
    count = lax.axis_size(axis)
    return lax.ppermute(x, axis, [(i, i ^ distance) for i in range(count)])


def bits(count):
    return [1 << b for b in range(count.bit_length() - 1)]


def per_device(
    residual,
    queries,
    token_keys,
    token_values,
    stored_keys,
    stored_values,
    lengths,
    norm_gain_vector,
    router,
    expert_gate_weight,
    expert_up_weight,
    expert_down_weight,
    adapter_down_map,
    adapter_up_map,
    routes,
    tenants,
):
    rows, features = residual.shape
    expert_devices = lax.axis_size("ep")
    tensor_devices = lax.axis_size("tp")
    state, held = attend(
        (
            lengths,
            tenants,
            routes.T,
            residual,
            queries,
            token_keys,
            token_values,
            stored_keys,
            stored_values,
            norm_gain_vector.reshape(1, features),
            router.T,
            adapter_down_map,
        )
    )
    for distance in bits(expert_devices):
        held = jnp.concatenate([held, swap(held, "ep", distance)], axis=0)
    gathered, order = held[None], [0]
    for distance in reversed(bits(tensor_devices)):
        gathered = jnp.concatenate([gathered, swap(gathered, "tp", distance)], axis=0)
        order = order + [at ^ distance for at in order]
    kept, sent = experts(
        gathered,
        tuple(order),
        expert_devices // EXPERT_COUNT,
        expert_gate_weight,
        expert_up_weight,
        expert_down_weight,
        adapter_up_map,
    )
    for distance in bits(tensor_devices):
        if distance > 1:
            kept, sent = kept[0::2], kept[1::2].astype(BF16)
        kept = kept + swap(sent, "tp", distance).astype(F32)
    kept = kept.reshape(expert_devices, rows, features)
    for distance in bits(expert_devices):
        kept, sent = kept[0::2], kept[1::2].astype(BF16)
        kept = kept + swap(sent, "ep", distance).astype(F32)
    return (state.astype(F32) + kept[0]).astype(BF16)


def solution(mesh):
    placed = (
        P(("groups", "ep"), "tp"),
        P(("groups", "ep"), "tp"),
        P(("groups", "ep"), "tp"),
        P(("groups", "ep"), "tp"),
        P(("groups", "ep"), None, "tp"),
        P(("groups", "ep"), None, "tp"),
        P(("groups", "ep")),
        P("tp"),
        P("tp", None),
        P(None, ("ep", "tp")),
        P(None, ("ep", "tp")),
        P(("ep", "tp"), None),
        P("tp", None),
        P(None, ("ep", "tp")),
        P(("groups", "ep"), None),
        P(("groups", "ep")),
    )
    return jax.shard_map(
        per_device, mesh=mesh, in_specs=placed, out_specs=P(("groups", "ep"), "tp"), check_vma=False
    )
```

time: 141 us -> 70.5 us (0.50)
  waiting for transfers between devices: 48.4 us -> 17 us
  matrix products: 26.3 us -> 0 us
  blocking collectives: 23.9 us -> 0 us
  local copies, waits for them, and re-layouts: 7.71 us -> 24.6 us
  between operations: 13.6 us -> 0.1 us
  Pallas kernels: 0 us -> 12.4 us
  other arithmetic: 6.9 us -> 0.8 us
  starting transfers between devices: 13.5 us -> 15 us
    all_to_all x3 -> x0, waiting for transfers between devices: 30.3 us -> none  [the longest x1 19.3 us: per_device(): lax.all_to_all(partial_out, 'ep', split_axis=0, concat_axis=0, tiled=True)]
    dot_general x13 -> x0, matrix products: 26.3 us -> none  [the longest x1 6.9 us: per_device(): jnp.dot(flat_rows, expert_gate_weight, preferred_element_type=jnp.float32)]
    unnamed x7 -> x30, local copies, waits for them, and re-layouts: 0.79 us -> 23.9 us
    psum x2 -> x0, blocking collectives: 18.6 us -> none  [the longest x1 10.3 us: per_device(): lowrank_sum, logits = lax.psum((lowrank_part, logit_part), 'tp')]
    reduce_scatter x1 -> x0, waiting for transfers between devices: 18.1 us -> none  [per_device(): lax.psum_scatter(combined, 'tp', scatter_dimension=1, tiled=True)]
    ppermute x0 -> x8, waiting for transfers between devices: none -> 17 us  [swap(): return lax.ppermute(x, axis, [(i, i ^ distance) for i in range(count)])]
    ppermute x0 -> x8, starting transfers between devices: none -> 15 us  [swap(): return lax.ppermute(x, axis, [(i, i ^ distance) for i in range(count)])]
    all_to_all x3 -> x0, starting transfers between devices: 13.5 us -> none  [the longest x1 5.09 us: per_device(): lax.all_to_all(send_rows, 'ep', split_axis=0, concat_axis=0, tiled=True)]
  transfers between devices with their start and end apart: 4 -> 8, of which waited for: 3 -> 8; matrix products, arithmetic and copies ran while one was open for 3% -> 0% of each run, Pallas kernels for 0% -> 0%
where the time goes in v1:
time: 70.5 us; the launch traced here: 69.8 us
  local copies, waits for them, and re-layouts  24.6 us (35%)
  waiting for transfers between devices  17 us (24%)
  starting transfers between devices  15 us (21%)
  Pallas kernels  12.4 us (18%)
  other arithmetic  0.8 us (1%)
    unnamed x30, local copies, waits for them, and re-layouts  23.9 us
    ppermute x8, waiting for transfers between devices, swap(): return lax.ppermute(x, axis, [(i, i ^ distance) for i in range(count)])  17 us
    ppermute x8, starting transfers between devices, swap(): return lax.ppermute(x, axis, [(i, i ^ distance) for i in range(count)])  15 us
    pallas_call x1, Pallas kernels, experts(): pl.pallas_call(functools.partial(expert_kernel, order, replicas), out_sha...  9.86 us
    pallas_call x1, Pallas kernels, attend(): pl.pallas_call(attend_kernel, out_shape=(jax.ShapeDtypeStruct((rows, feat...  2.53 us
  transfers between devices with their start and end apart: 8, of which 8 were waited for; matrix products, arithmetic and copies ran while one was open for 0% of the time, Pallas kernels for 0%

profile of v1, /device:TPU:0, one launch (start us, length us, event | category | flops | bytes accessed | tf_op | source)
XLA Modules:
  0.0 69.8 jit_solution(10554931230342746098)
XLA Ops:
  0.0 0.7 reshape.6.gain
  0.7 0.0 copy-start.3
  0.7 1.2 %copy-done.3 = bf16[16,128,256]{2,1,0:T(8,128)(2,1)S(1)} copy-done((bf16[16,128,256]{2,1,0:T(8,128)(2,1)S(1)}, bf16[16,128,256]{2,1,0:T(8,128)(2,1)}, u32[]{:S(2)}) %copy-start.3) | copy-done | bytes 1048600
  1.9 0.0 copy-start.4
  1.9 1.2 %copy-done.4 = bf16[16,128,256]{2,1,0:T(8,128)(2,1)S(1)} copy-done((bf16[16,128,256]{2,1,0:T(8,128)(2,1)S(1)}, bf16[16,128,256]{2,1,0:T(8,128)(2,1)}, u32[]{:S(2)}) %copy-start.4) | copy-done | bytes 1048600
  3.1 0.0 copy-start.5
  3.1 1.1 %copy-done.5 = bf16[768,512]{1,0:T(8,128)(2,1)S(1)} copy-done((bf16[768,512]{1,0:T(8,128)(2,1)S(1)}, bf16[768,512]{1,0:T(8,128)(2,1)}, u32[]{:S(2)}) %copy-start.5) | copy-done | bytes 786456
  4.3 0.0 copy-start.7
  4.3 0.7 %copy-done.7 = bf16[16,768]{1,0:T(8,128)(2,1)S(1)} copy-done((bf16[16,768]{1,0:T(8,128)(2,1)S(1)}, bf16[16,768]{1,0:T(8,128)(2,1)}, u32[]{:S(2)}) %copy-start.7) | copy-done | bytes 24600
  5.0 0.0 copy-start.8
  5.0 0.7 %copy-done.8 = bf16[16,768]{1,0:T(8,128)(2,1)S(1)} copy-done((bf16[16,768]{1,0:T(8,128)(2,1)S(1)}, bf16[16,768]{1,0:T(8,128)(2,1)}, u32[]{:S(2)}) %copy-start.8) | copy-done | bytes 24600
  5.8 0.0 copy-start.9
  5.8 0.7 copy-done.9
  6.4 0.0 copy-start.10
  6.4 0.7 copy-done.10
  7.1 0.0 copy-start.11
  7.1 0.7 copy-done.11
  7.8 0.0 copy-start.12
  7.8 0.7 copy-done.12
  8.5 0.0 copy-start.13
  8.5 0.7 copy-done.13
  9.2 0.0 copy-start.14
  9.2 0.7 copy-done.14
  9.8 2.5 %attend.1 = (bf16[16,768]{1,0:T(8,128)(2,1)S(1)}, bf16[16,896]{1,0:T(8,128)(2,1)S(1)}) custom-call(s32[16]{0:T(128)S(1)} %copy-done.13, s32[16]{0:T(128)S(1)} %copy-done.14, s32[2,16]{1,0:T(2,128)S(1)} %bitcast.12, bf16[16,768]{1,0:T(8,128)(2,1)S(1)} %copy-done.7, bf16[16,768]{1,0:T(8,128)(2,1)S(1)} %copy-done.8, bf16[16,256]{1,0:T(8,128)(2,1)S(1)} %copy-done.9, ...), custom_call_target="tpu_custom_call" | custom-call | flops 200000000 | bytes 3000000 | tf_op jit(solution)/shard_map/attend/pallas_call | solution.py:132
  12.4 3.1 %collective-permute-start = (bf16[16,896]{1,0:T(8,128)(2,1)S(1)}, bf16[16,896]{1,0:T(8,128)(2,1)S(1)}, u32[]{:S(2)}, u32[]{:S(2)}) collective-permute-start(bf16[16,896]{1,0:T(8,128)(2,1)S(1)} %get-tuple-element.10), channel_id=1, source_target_pairs={{0,4},{4,0},{8,12},{12,8},{1,5},{5,1},{9,13},{13,9},{2,6},{6,2},{1... | collective-permute-start | bytes 86024 | tf_op jit(solution)/shard_map/ppermute | solution.py:250
  15.4 1.9 %collective-permute-done = bf16[16,896]{1,0:T(8,128)(2,1)S(1)} collective-permute-done((bf16[16,896]{1,0:T(8,128)(2,1)S(1)}, bf16[16,896]{1,0:T(8,128)(2,1)S(1)}, u32[]{:S(2)}, u32[]{:S(2)}) %collective-permute-start) | collective-permute-done | bytes 28704 | tf_op jit(solution)/shard_map/ppermute | solution.py:250
  17.3 3.0 %collective-permute-start.1 = (bf16[32,896]{1,0:T(8,128)(2,1)S(1)}, bf16[32,896]{1,0:T(8,128)(2,1)S(1)}, u32[]{:S(2)}, u32[]{:S(2)}) collective-permute-start(bf16[32,896]{1,0:T(8,128)(2,1)S(1)} %pad_maximum_fusion.2), channel_id=1, source_target_pairs={{0,8},{4,12},{8,0},{12,4},{1,9},{5,13},{9,1},{13,5},{2,10},{6,14},... | collective-permute-start | bytes 172040 | tf_op jit(solution)/shard_map/ppermute | solution.py:250
  20.3 2.2 %collective-permute-done.1 = bf16[32,896]{1,0:T(8,128)(2,1)S(1)} collective-permute-done((bf16[32,896]{1,0:T(8,128)(2,1)S(1)}, bf16[32,896]{1,0:T(8,128)(2,1)S(1)}, u32[]{:S(2)}, u32[]{:S(2)}) %collective-permute-start.1) | collective-permute-done | bytes 57376 | tf_op jit(solution)/shard_map/ppermute | solution.py:250
  22.5 1.9 %collective-permute-start.2 = (bf16[1,64,896]{2,1,0:T(8,128)(2,1)S(1)}, bf16[1,64,896]{2,1,0:T(8,128)(2,1)S(1)}, u32[]{:S(2)}, u32[]{:S(2)}) collective-permute-start(bf16[1,64,896]{2,1,0:T(8,128)(2,1)S(1)} %maximum_bitcast_fusion), channel_id=1, source_target_pairs={{0,2},{1,3},{2,0},{3,1},{4,6},{5,7},{6,4},{7,5},{8,10},{9,11},{10,... | collective-permute-start | bytes 344072 | tf_op jit(solution)/shard_map/ppermute | solution.py:250
  24.4 3.0 %collective-permute-done.2 = bf16[1,64,896]{2,1,0:T(8,128)(2,1)S(1)} collective-permute-done((bf16[1,64,896]{2,1,0:T(8,128)(2,1)S(1)}, bf16[1,64,896]{2,1,0:T(8,128)(2,1)S(1)}, u32[]{:S(2)}, u32[]{:S(2)}) %collective-permute-start.2) | collective-permute-done | bytes 114720 | tf_op jit(solution)/shard_map/ppermute | solution.py:250
  27.4 0.1 collective-permute-start.3
  27.4 1.5 %collective-permute-done.3 = bf16[2,64,896]{2,1,0:T(8,128)(2,1)S(1)} collective-permute-done((bf16[2,64,896]{2,1,0:T(8,128)(2,1)S(1)}, bf16[2,64,896]{2,1,0:T(8,128)(2,1)S(1)}, u32[]{:S(2)}, u32[]{:S(2)}) %collective-permute-start.3) | collective-permute-done | bytes 229408 | tf_op jit(solution)/shard_map/ppermute | solution.py:250
  28.9 0.1 pad_maximum_fusion.gathered
  29.0 0.0 copy-start
  29.0 4.6 %copy-done = bf16[3072,2048]{1,0:T(8,128)(2,1)S(1)} copy-done((bf16[3072,2048]{1,0:T(8,128)(2,1)S(1)}, bf16[3072,2048]{1,0:T(8,128)(2,1)}, u32[]{:S(2)}) %copy-start) | copy-done | bytes 12582936
  33.6 4.6 %copy-done.1 = bf16[3072,2048]{1,0:T(8,128)(2,1)S(1)} copy-done((bf16[3072,2048]{1,0:T(8,128)(2,1)S(1)}, bf16[3072,2048]{1,0:T(8,128)(2,1)}, u32[]{:S(2)}) %copy-start.1) | copy-done | bytes 12582936
  38.1 4.6 %copy-done.2 = bf16[2048,3072]{1,0:T(8,128)(2,1)S(1)} copy-done((bf16[2048,3072]{1,0:T(8,128)(2,1)S(1)}, bf16[2048,3072]{1,0:T(8,128)(2,1)}, u32[]{:S(2)}) %copy-start.2) | copy-done | bytes 12582936
  42.7 1.0 %copy-done.6 = bf16[128,2048]{1,0:T(8,128)(2,1)S(1)} copy-done((bf16[128,2048]{1,0:T(8,128)(2,1)S(1)}, bf16[128,2048]{1,0:T(8,128)(2,1)}, u32[]{:S(2)}) %copy-start.6) | copy-done | bytes 524312
  43.8 9.9 %experts.1 = (f32[2,64,768]{2,1,0:T(8,128)S(1)}, bf16[2,64,768]{2,1,0:T(8,128)(2,1)S(1)}) custom-call(bf16[4,64,896]{2,1,0:T(8,128)(2,1)S(1)} %pad_maximum_fusion.gathered, bf16[3072,2048]{1,0:T(8,128)(2,1)S(1)} %copy-done, bf16[3072,2048]{1,0:T(8,128)(2,1)S(1)} %copy-done.1, bf16[2048,3072]{1,0:T(8,128)(2,1)S(1)} %copy-done.2, bf16[128,2048]{1,0:T(8,128)(2,1)S(1)} %copy-done.6), custom_call_target="tpu_custom_call" | custom-call | flops 2415919104 | bytes 4000000 | tf_op jit(solution)/shard_map/experts/pallas_call | solution.py:231
  53.6 0.2 collective-permute-start.4
  53.8 1.3 %collective-permute-done.4 = bf16[2,64,768]{2,1,0:T(8,128)(2,1)S(1)} collective-permute-done((bf16[2,64,768]{2,1,0:T(8,128)(2,1)S(1)}, bf16[2,64,768]{2,1,0:T(8,128)(2,1)S(1)}, u32[]{:S(2)}, u32[]{:S(2)}) %collective-permute-start.4) | collective-permute-done | bytes 196640 | tf_op jit(solution)/shard_map/ppermute | solution.py:250
  55.2 1.9 %collective-permute-start.5 = (bf16[1,64,768]{2,1,0:T(8,128)(2,1)S(1)}, bf16[1,64,768]{2,1,0:T(8,128)(2,1)S(1)}, u32[]{:S(2)}, u32[]{:S(2)}) collective-permute-start(bf16[1,64,768]{2,1,0:T(8,128)(2,1)S(1)} %slice.46), channel_id=1, source_target_pairs={{0,2},{1,3},{2,0},{3,1},{4,6},{5,7},{6,4},{7,5},{8,10},{9,11},{10,... | collective-permute-start | bytes 294920 | tf_op jit(solution)/shard_map/ppermute | solution.py:250
  57.1 3.1 %collective-permute-done.5 = bf16[1,64,768]{2,1,0:T(8,128)(2,1)S(1)} collective-permute-done((bf16[1,64,768]{2,1,0:T(8,128)(2,1)S(1)}, bf16[1,64,768]{2,1,0:T(8,128)(2,1)S(1)}, u32[]{:S(2)}, u32[]{:S(2)}) %collective-permute-start.5) | collective-permute-done | bytes 98336 | tf_op jit(solution)/shard_map/ppermute | solution.py:250
  60.2 1.9 %collective-permute-start.6 = (bf16[2,16,768]{2,1,0:T(8,128)(2,1)S(1)}, bf16[2,16,768]{2,1,0:T(8,128)(2,1)S(1)}, u32[]{:S(2)}, u32[]{:S(2)}) collective-permute-start(bf16[2,16,768]{2,1,0:T(8,128)(2,1)S(1)} %slice.28), channel_id=1, source_target_pairs={{0,4},{4,0},{8,12},{12,8},{1,5},{5,1},{9,13},{13,9},{2,6},{6,2},{1... | collective-permute-start | bytes 147464 | tf_op jit(solution)/shard_map/ppermute | solution.py:250
  62.1 2.3 %collective-permute-done.6 = bf16[2,16,768]{2,1,0:T(8,128)(2,1)S(1)} collective-permute-done((bf16[2,16,768]{2,1,0:T(8,128)(2,1)S(1)}, bf16[2,16,768]{2,1,0:T(8,128)(2,1)S(1)}, u32[]{:S(2)}, u32[]{:S(2)}) %collective-permute-start.6) | collective-permute-done | bytes 49184 | tf_op jit(solution)/shard_map/ppermute | solution.py:250
  64.4 3.0 %collective-permute-start.7 = (bf16[1,16,768]{2,1,0:T(8,128)(2,1)S(1)}, bf16[1,16,768]{2,1,0:T(8,128)(2,1)S(1)}, u32[]{:S(2)}, u32[]{:S(2)}) collective-permute-start(bf16[1,16,768]{2,1,0:T(8,128)(2,1)S(1)} %slice.47), channel_id=1, source_target_pairs={{0,8},{4,12},{8,0},{12,4},{1,9},{5,13},{9,1},{13,5},{2,10},{6,14},... | collective-permute-start | bytes 73736 | tf_op jit(solution)/shard_map/ppermute | solution.py:250
  67.4 1.8 %collective-permute-done.7 = bf16[1,16,768]{2,1,0:T(8,128)(2,1)S(1)} collective-permute-done((bf16[1,16,768]{2,1,0:T(8,128)(2,1)S(1)}, bf16[1,16,768]{2,1,0:T(8,128)(2,1)S(1)}, u32[]{:S(2)}, u32[]{:S(2)}) %collective-permute-start.7) | collective-permute-done | bytes 24608 | tf_op jit(solution)/shard_map/ppermute | solution.py:250
  69.2 0.6 fusion.2
  (13 shorter events, 0.2 us)
Async XLA Ops:
  0.7 1.2 %copy-start.3 = (bf16[16,128,256]{2,1,0:T(8,128)(2,1)S(1)}, bf16[16,128,256]{2,1,0:T(8,128)(2,1)}, u32[]{:S(2)}) copy-start(bf16[16,128,256]{2,1,0:T(8,128)(2,1)} %stored_keys.1) | copy-start | bytes 3145732
  1.9 1.2 %copy-start.4 = (bf16[16,128,256]{2,1,0:T(8,128)(2,1)S(1)}, bf16[16,128,256]{2,1,0:T(8,128)(2,1)}, u32[]{:S(2)}) copy-start(bf16[16,128,256]{2,1,0:T(8,128)(2,1)} %stored_values.1) | copy-start | bytes 3145732
  3.1 1.1 %copy-start.5 = (bf16[768,512]{1,0:T(8,128)(2,1)S(1)}, bf16[768,512]{1,0:T(8,128)(2,1)}, u32[]{:S(2)}) copy-start(bf16[768,512]{1,0:T(8,128)(2,1)} %adapter_down.1) | copy-start | bytes 2359300
  4.3 0.7 %copy-start.7 = (bf16[16,768]{1,0:T(8,128)(2,1)S(1)}, bf16[16,768]{1,0:T(8,128)(2,1)}, u32[]{:S(2)}) copy-start(bf16[16,768]{1,0:T(8,128)(2,1)} %residual.1) | copy-start | bytes 73732
  5.0 0.7 %copy-start.8 = (bf16[16,768]{1,0:T(8,128)(2,1)S(1)}, bf16[16,768]{1,0:T(8,128)(2,1)}, u32[]{:S(2)}) copy-start(bf16[16,768]{1,0:T(8,128)(2,1)} %queries.1) | copy-start | bytes 73732
  5.8 0.7 copy-start.9
  6.4 0.7 copy-start.10
  7.1 0.7 copy-start.11
  7.8 0.7 copy-start.12
  8.5 0.7 copy-start.13
  9.2 0.7 copy-start.14
  12.4 4.9 %collective-permute-start = (bf16[16,896]{1,0:T(8,128)(2,1)S(1)}, bf16[16,896]{1,0:T(8,128)(2,1)S(1)}, u32[]{:S(2)}, u32[]{:S(2)}) collective-permute-start(bf16[16,896]{1,0:T(8,128)(2,1)S(1)} %get-tuple-element.10), channel_id=1, source_target_pairs={{0,4},{4,0},{8,12},{12,8},{1,5},{5,1},{9,13},{13,9},{2,6},{6,2},{1... | collective-permute-start | bytes 86024 | tf_op jit(solution)/shard_map/ppermute | solution.py:250
  17.3 5.2 %collective-permute-start.1 = (bf16[32,896]{1,0:T(8,128)(2,1)S(1)}, bf16[32,896]{1,0:T(8,128)(2,1)S(1)}, u32[]{:S(2)}, u32[]{:S(2)}) collective-permute-start(bf16[32,896]{1,0:T(8,128)(2,1)S(1)} %pad_maximum_fusion.2), channel_id=1, source_target_pairs={{0,8},{4,12},{8,0},{12,4},{1,9},{5,13},{9,1},{13,5},{2,10},{6,14},... | collective-permute-start | bytes 172040 | tf_op jit(solution)/shard_map/ppermute | solution.py:250
  22.5 4.9 %collective-permute-start.2 = (bf16[1,64,896]{2,1,0:T(8,128)(2,1)S(1)}, bf16[1,64,896]{2,1,0:T(8,128)(2,1)S(1)}, u32[]{:S(2)}, u32[]{:S(2)}) collective-permute-start(bf16[1,64,896]{2,1,0:T(8,128)(2,1)S(1)} %maximum_bitcast_fusion), channel_id=1, source_target_pairs={{0,2},{1,3},{2,0},{3,1},{4,6},{5,7},{6,4},{7,5},{8,10},{9,11},{10,... | collective-permute-start | bytes 344072 | tf_op jit(solution)/shard_map/ppermute | solution.py:250
  27.4 1.6 %collective-permute-start.3 = (bf16[2,64,896]{2,1,0:T(8,128)(2,1)S(1)}, bf16[2,64,896]{2,1,0:T(8,128)(2,1)S(1)}, u32[]{:S(2)}, u32[]{:S(2)}) collective-permute-start(bf16[2,64,896]{2,1,0:T(8,128)(2,1)S(1)} %pad_maximum_fusion.1), channel_id=1, source_target_pairs={{0,1},{1,0},{2,3},{3,2},{4,5},{5,4},{6,7},{7,6},{8,9},{9,8},{10,11... | collective-permute-start | bytes 688136 | tf_op jit(solution)/shard_map/ppermute | solution.py:250
  29.0 4.6 %copy-start = (bf16[3072,2048]{1,0:T(8,128)(2,1)S(1)}, bf16[3072,2048]{1,0:T(8,128)(2,1)}, u32[]{:S(2)}) copy-start(bf16[3072,2048]{1,0:T(8,128)(2,1)} %gate_weight.1) | copy-start | bytes 37748740
  33.6 4.6 %copy-start.1 = (bf16[3072,2048]{1,0:T(8,128)(2,1)S(1)}, bf16[3072,2048]{1,0:T(8,128)(2,1)}, u32[]{:S(2)}) copy-start(bf16[3072,2048]{1,0:T(8,128)(2,1)} %up_weight.1) | copy-start | bytes 37748740
  38.1 4.6 %copy-start.2 = (bf16[2048,3072]{1,0:T(8,128)(2,1)S(1)}, bf16[2048,3072]{1,0:T(8,128)(2,1)}, u32[]{:S(2)}) copy-start(bf16[2048,3072]{1,0:T(8,128)(2,1)} %down_weight.1) | copy-start | bytes 37748740
  42.7 1.0 %copy-start.6 = (bf16[128,2048]{1,0:T(8,128)(2,1)S(1)}, bf16[128,2048]{1,0:T(8,128)(2,1)}, u32[]{:S(2)}) copy-start(bf16[128,2048]{1,0:T(8,128)(2,1)} %adapter_up.1) | copy-start | bytes 1572868
  53.6 1.5 %collective-permute-start.4 = (bf16[2,64,768]{2,1,0:T(8,128)(2,1)S(1)}, bf16[2,64,768]{2,1,0:T(8,128)(2,1)S(1)}, u32[]{:S(2)}, u32[]{:S(2)}) collective-permute-start(bf16[2,64,768]{2,1,0:T(8,128)(2,1)S(1)} %get-tuple-element.12), channel_id=1, source_target_pairs={{0,1},{1,0},{2,3},{3,2},{4,5},{5,4},{6,7},{7,6},{8,9},{9,8},{10,11... | collective-permute-start | bytes 589832 | tf_op jit(solution)/shard_map/ppermute | solution.py:250
  55.2 5.0 %collective-permute-start.5 = (bf16[1,64,768]{2,1,0:T(8,128)(2,1)S(1)}, bf16[1,64,768]{2,1,0:T(8,128)(2,1)S(1)}, u32[]{:S(2)}, u32[]{:S(2)}) collective-permute-start(bf16[1,64,768]{2,1,0:T(8,128)(2,1)S(1)} %slice.46), channel_id=1, source_target_pairs={{0,2},{1,3},{2,0},{3,1},{4,6},{5,7},{6,4},{7,5},{8,10},{9,11},{10,... | collective-permute-start | bytes 294920 | tf_op jit(solution)/shard_map/ppermute | solution.py:250
  60.2 4.2 %collective-permute-start.6 = (bf16[2,16,768]{2,1,0:T(8,128)(2,1)S(1)}, bf16[2,16,768]{2,1,0:T(8,128)(2,1)S(1)}, u32[]{:S(2)}, u32[]{:S(2)}) collective-permute-start(bf16[2,16,768]{2,1,0:T(8,128)(2,1)S(1)} %slice.28), channel_id=1, source_target_pairs={{0,4},{4,0},{8,12},{12,8},{1,5},{5,1},{9,13},{13,9},{2,6},{6,2},{1... | collective-permute-start | bytes 147464 | tf_op jit(solution)/shard_map/ppermute | solution.py:250
  64.4 4.8 %collective-permute-start.7 = (bf16[1,16,768]{2,1,0:T(8,128)(2,1)S(1)}, bf16[1,16,768]{2,1,0:T(8,128)(2,1)S(1)}, u32[]{:S(2)}, u32[]{:S(2)}) collective-permute-start(bf16[1,16,768]{2,1,0:T(8,128)(2,1)S(1)} %slice.47), channel_id=1, source_target_pairs={{0,8},{4,12},{8,0},{12,4},{1,9},{5,13},{9,1},{13,5},{2,10},{6,14},... | collective-permute-start | bytes 73736 | tf_op jit(solution)/shard_map/ppermute | solution.py:250

commit v2 on v1

--- a/solution.py
+++ b/solution.py
@@ -29,7 +29,19 @@
     return out
 
 
-def attend_kernel(
+def attend_kernel(*refs):
+    count = 12
+    sources, outs, buffers, arrived = refs[:count], refs[count:-count - 1], refs[-count - 1:-1], refs[-1]
+    copies = [
+        pltpu.make_async_copy(source, buffer, arrived.at[i])
+        for i, (source, buffer) in enumerate(zip(sources, buffers, strict=True))
+    ]
+    for i in (7, 4, 0, 5, 8, 6, 3, 9, 1, 2, 10, 11):
+        copies[i].start()
+    attend_body(*buffers, *outs, wait=lambda *which: [copies[i].wait() for i in which])
+
+
+def attend_body(
     lengths,
     tenants,
     routes,
@@ -44,12 +56,15 @@
     adapter_down,
     state_out,
     payload_out,
+    *,
+    wait,
 ):
     rows, features = residual.shape
     kv_local = token_keys.shape[1] // HD
     cache = stored_keys.shape[1]
     group = HEADS // KVH
     scale = HD ** (-0.5)
+    wait(0, 4, 7)
     length_column = column(lambda r: lengths[r], rows)
     stacked_length = jnp.concatenate([length_column[:, :1]] * group, axis=0)
     stacked_row = lax.rem(
@@ -70,6 +85,8 @@
             )
             scores = jnp.where(stacked_row[:, :cache] == r, every, scores)
         scores = jnp.where(visible, scores * scale, -jnp.inf)
+        if g == 0:
+            wait(5)
         fresh_key = jnp.concatenate([token_keys[:, key_lanes].astype(F32)] * group, axis=0)
         fresh = jnp.sum(query.astype(F32) * fresh_key, axis=1, keepdims=True) * scale
         largest = jnp.maximum(jnp.max(scores, axis=1, keepdims=True), fresh)
@@ -78,10 +95,14 @@
         denominator = jnp.sum(cache_exp, axis=1, keepdims=True) + fresh_exp
         probs = (cache_exp / denominator).astype(BF16)
         fresh_prob = (fresh_exp / denominator).astype(BF16).astype(F32)
+        if g == 0:
+            wait(8)
         attended = jnp.zeros((group * rows, HD), F32)
         for r in range(rows):
             every = jnp.dot(probs, stored_values[r, :, key_lanes], preferred_element_type=F32)
             attended = jnp.where(stacked_row[:, :HD] == r, every, attended)
+        if g == 0:
+            wait(3, 6, 9)
         fresh_value = jnp.concatenate([token_values[:, key_lanes].astype(F32)] * group, axis=0)
         attended = attended + fresh_prob * fresh_value
         for j in range(group):
@@ -92,7 +113,10 @@
             state_out[:, lanes] = state
             state = state.astype(F32)
             squares = squares + jnp.sum(state * state, axis=1, keepdims=True)
-            payload_out[:, lanes] = (state * gain[:, lanes]).astype(BF16)
+            payload_out[:, lanes] = (
+                state * gain[lanes.start // LANES : lanes.start // LANES + 1, :]
+            ).astype(BF16)
+    wait(1, 2, 10, 11)
     scaled = payload_out[:, :features]
     logits = lax.dot_general(scaled, router[...], ANY_LANES, preferred_element_type=F32)
     first = column(lambda r: routes[0, r], rows)
@@ -127,7 +151,6 @@
 
 def attend(args):
     rows, features = args[3].shape
-    smem = pl.BlockSpec(memory_space=pltpu.SMEM)
     vmem = pl.BlockSpec(memory_space=pltpu.VMEM)
     return pl.pallas_call(
         attend_kernel,
@@ -135,24 +158,68 @@
             jax.ShapeDtypeStruct((rows, features), BF16),
             jax.ShapeDtypeStruct((rows, features + LANES), BF16),
         ),
-        in_specs=[smem] * 3 + [vmem] * 9,
+        in_specs=[pl.BlockSpec(memory_space=pl.ANY)] * len(args),
         out_specs=(vmem, vmem),
+        scratch_shapes=[
+            (pltpu.SMEM if i < 3 else pltpu.VMEM)(arg.shape, arg.dtype)
+            for i, arg in enumerate(args)
+        ]
+        + [pltpu.SemaphoreType.DMA((len(args),))],
         compiler_params=pltpu.CompilerParams(vmem_limit_bytes=12 * 2**20),
         cost_estimate=pl.CostEstimate(
             flops=200_000_000, bytes_accessed=3_000_000, transcendentals=20_000
         ),
         name="attend",
-    )(*args)
+    )(*[pltpu.with_memory_space_constraint(arg, pltpu.HBM) for arg in args])
 
 
 def expert_kernel(
-    order, replicas, gathered, gate_weight, up_weight, down_weight, adapter_up, kept, sent, active
+    order,
+    replicas,
+    gathered,
+    gate_weight,
+    up_weight,
+    down_weight,
+    adapter_weight,
+    kept,
+    sent,
+    gate_part,
+    up_part,
+    down_part,
+    adapter_up,
+    gate_sum,
+    up_sum,
+    active,
+    arrived,
 ):
     tensor_devices, rows, width = gathered.shape
     features = width - LANES
-    hidden = gate_weight.shape[1]
     mine = lax.axis_index("tp")
     expert = lax.axis_index("ep") // replicas
+    copies = []
+    for i in range(tensor_devices):
+        depth = pl.ds(pl.multiple_of((mine ^ order[i]) * features, features), features)
+        copies.append((gate_weight.at[depth, :], gate_part.at[i]))
+        copies.append((up_weight.at[depth, :], up_part.at[i]))
+    targets = [i for i in range(tensor_devices) if i % 2] + list(range(0, tensor_devices, 2))
+    for i in targets:
+        lanes = pl.ds(pl.multiple_of((mine ^ i) * features, features), features)
+        copies.append((down_weight.at[:, lanes], down_part.at[i]))
+    copies = [
+        pltpu.make_async_copy(source, part, arrived.at[i])
+        for i, (source, part) in enumerate(copies)
+    ]
+    adapter_copy = pltpu.make_async_copy(adapter_weight, adapter_up, arrived.at[len(copies)])
+    ahead = 4
+    for copy in copies[:ahead]:
+        copy.start()
+    adapter_copy.start()
+
+    def wait(i):
+        copies[i].wait()
+        if i + ahead < len(copies):
+            copies[i + ahead].start()
+
     tail = jnp.zeros((rows, LANES), F32)
     for i in range(tensor_devices):
         tail = tail + gathered[i, :, features:].astype(F32)
@@ -180,69 +247,65 @@
     adapter_rows = jnp.where(
         own_tenant, jnp.dot(lowrank, spread, preferred_element_type=F32), 0.0
     ).astype(BF16)
-    tile = min(256, hidden)
-
-    def hidden_tile(n, carry):
-        lanes = pl.ds(pl.multiple_of(n * tile, tile), tile)
-        gate = jnp.zeros((rows, tile), F32)
-        up = jnp.zeros((rows, tile), F32)
-        for i in range(tensor_devices):
-            start = pl.multiple_of((mine ^ order[i]) * features, features)
-            scaled = gathered[i, :, :features]
-            gate = gate + jnp.dot(
-                scaled, gate_weight[pl.ds(start, features), lanes], preferred_element_type=F32
-            )
-            up = up + jnp.dot(
-                scaled, up_weight[pl.ds(start, features), lanes], preferred_element_type=F32
-            )
-        gate = gate * inverse_rms
-        up = up * inverse_rms + jnp.dot(
-            adapter_rows, adapter_up[:, lanes], preferred_element_type=F32
-        )
-        active[:, lanes] = (gate * jax.nn.sigmoid(gate) * up * weight).astype(BF16)
-        return carry
-
-    lax.fori_loop(0, hidden // tile, hidden_tile, 0)
-    out_tile = 256 if features % 256 == 0 else LANES
     for i in range(tensor_devices):
-        start = (mine ^ i) * features
-
-        def out_tiles(n, carry):
-            lanes = pl.ds(pl.multiple_of(start + n * out_tile, LANES), out_tile)
-            result = jnp.dot(active[...], down_weight[:, lanes], preferred_element_type=F32)
-            to = pl.ds(pl.multiple_of(n * out_tile, out_tile), out_tile)
-            if i % 2 == 0:
-                kept[i // 2, :, to] = result
-            else:
-                sent[i // 2, :, to] = result.astype(BF16)
-            return carry
-
-        lax.fori_loop(0, features // out_tile, out_tiles, 0)
+        scaled = gathered[i, :, :features]
+        for weight_part, total, which in ((gate_part, gate_sum, 0), (up_part, up_sum, 1)):
+            wait(2 * i + which)
+            product = jnp.dot(scaled, weight_part[i], preferred_element_type=F32)
+            total[...] = product if i == 0 else total[...] + product
+    adapter_copy.wait()
+    gate = gate_sum[...] * inverse_rms
+    up = up_sum[...] * inverse_rms + jnp.dot(
+        adapter_rows, adapter_up[...], preferred_element_type=F32
+    )
+    active[...] = (gate * jax.nn.sigmoid(gate) * up * weight).astype(BF16)
+    for place_of, i in enumerate(targets):
+        wait(2 * tensor_devices + place_of)
+        result = jnp.dot(active[...], down_part[i], preferred_element_type=F32)
+        if i % 2 == 0:
+            kept[i // 2] = result
+        else:
+            sent[i // 2] = result.astype(BF16)
 
 
 def experts(gathered, order, replicas, gate_weight, up_weight, down_weight, adapter_up):
     tensor_devices, rows, width = gathered.shape
     features = width - LANES
+    hidden = gate_weight.shape[1]
     vmem = pl.BlockSpec(memory_space=pltpu.VMEM)
-    placed = [
-        pltpu.with_memory_space_constraint(w, pltpu.VMEM)
-        for w in (gate_weight, up_weight, down_weight)
-    ]
+    hbm = pl.BlockSpec(memory_space=pl.ANY)
     return pl.pallas_call(
         functools.partial(expert_kernel, order, replicas),
         out_shape=(
             jax.ShapeDtypeStruct((tensor_devices // 2, rows, features), F32),
             jax.ShapeDtypeStruct((tensor_devices // 2, rows, features), BF16),
         ),
-        in_specs=[vmem] * 5,
+        in_specs=[vmem, hbm, hbm, hbm, hbm],
         out_specs=(vmem, vmem),
-        scratch_shapes=[pltpu.VMEM((rows, gate_weight.shape[1]), BF16)],
-        compiler_params=pltpu.CompilerParams(vmem_limit_bytes=16 * 2**20),
+        scratch_shapes=[
+            pltpu.VMEM((tensor_devices, features, hidden), BF16),
+            pltpu.VMEM((tensor_devices, features, hidden), BF16),
+            pltpu.VMEM((tensor_devices, hidden, features), BF16),
+            pltpu.VMEM(adapter_up.shape, BF16),
+            pltpu.VMEM((rows, hidden), F32),
+            pltpu.VMEM((rows, hidden), F32),
+            pltpu.VMEM((rows, hidden), BF16),
+            pltpu.SemaphoreType.DMA((3 * tensor_devices + 1,)),
+        ],
+        compiler_params=pltpu.CompilerParams(vmem_limit_bytes=48 * 2**20),
         cost_estimate=pl.CostEstimate(
-            flops=2 * rows * 3 * gate_weight.size, bytes_accessed=4_000_000, transcendentals=0
+            flops=2 * rows * 3 * gate_weight.size,
+            bytes_accessed=6 * gate_weight.size,
+            transcendentals=0,
         ),
         name="experts",
-    )(gathered, *placed, adapter_up)
+    )(
+        gathered,
+        *[
+            pltpu.with_memory_space_constraint(weight, pltpu.HBM)
+            for weight in (gate_weight, up_weight, down_weight, adapter_up)
+        ],
+    )
 
 
 def swap(x, axis, distance):
@@ -286,7 +349,7 @@
             token_values,
             stored_keys,
             stored_values,
-            norm_gain_vector.reshape(1, features),
+            norm_gain_vector.reshape(features // LANES, LANES),
             router.T,
             adapter_down_map,
         )

time: 70.5 us -> 49.7 us (0.70)
  local copies, waits for them, and re-layouts: 24.6 us -> 0.02 us
  Pallas kernels: 12.4 us -> 16.7 us
    unnamed x30 -> x0, local copies, waits for them, and re-layouts: 23.9 us -> none
    pallas_call x1, Pallas kernels: 9.86 us -> 13.1 us  [experts(): pl.pallas_call(functools.partial(expert_kernel, order, replicas), out_sha...]
    pallas_call x1, Pallas kernels: 2.53 us -> 3.57 us  [attend(): pl.pallas_call(attend_kernel, out_shape=(jax.ShapeDtypeStruct((rows, feat...]
where the time goes in v2:
time: 49.7 us; the launch traced here: 49.6 us
  waiting for transfers between devices  16.9 us (34%)
  Pallas kernels  16.7 us (34%)
  starting transfers between devices  15 us (30%)
  other arithmetic  0.81 us (2%)
    ppermute x8, waiting for transfers between devices, swap(): return lax.ppermute(x, axis, [(i, i ^ distance) for i in range(count)])  16.9 us
    ppermute x8, starting transfers between devices, swap(): return lax.ppermute(x, axis, [(i, i ^ distance) for i in range(count)])  15 us
    pallas_call x1, Pallas kernels, experts(): pl.pallas_call(functools.partial(expert_kernel, order, replicas), out_sha...  13.1 us
    pallas_call x1, Pallas kernels, attend(): pl.pallas_call(attend_kernel, out_shape=(jax.ShapeDtypeStruct((rows, feat...  3.57 us
  transfers between devices with their start and end apart: 8, of which 8 were waited for; matrix products, arithmetic and copies ran while one was open for 0% of the time, Pallas kernels for 0%

profile of v2, /device:TPU:0, one launch (start us, length us, event | category | flops | bytes accessed | tf_op | source)
XLA Modules:
  0.0 49.6 jit_solution(8041201526428703621)
XLA Ops:
  0.0 3.6 %attend.1 = (bf16[16,768]{1,0:T(8,128)(2,1)S(1)}, bf16[16,896]{1,0:T(8,128)(2,1)S(1)}) custom-call(s32[16]{0:T(128)} %refs_0_.1, s32[16]{0:T(128)} %refs_1_.1, s32[2,16]{1,0:T(2,128)} %bitcast.16, bf16[16,768]{1,0:T(8,128)(2,1)} %refs_3_.1, bf16[16,768]{1,0:T(8,128)(2,1)} %refs_4_.1, bf16[16,256]{1,0:T(8,128)(2,1)} %refs_5_.1, bf16[16,256]{1,0:T(8,128)(2,1)} %refs_6_.1, ...), custom_call_target="tpu_custom_call" | custom-call | flops 200000000 | bytes 3000000 | tf_op jit(solution)/shard_map/attend/pallas_call | solution.py:155
  3.6 3.1 %collective-permute-start = (bf16[16,896]{1,0:T(8,128)(2,1)S(1)}, bf16[16,896]{1,0:T(8,128)(2,1)S(1)}, u32[]{:S(2)}, u32[]{:S(2)}) collective-permute-start(bf16[16,896]{1,0:T(8,128)(2,1)S(1)} %get-tuple-element.10), channel_id=1, source_target_pairs={{0,4},{4,0},{8,12},{12,8},{1,5},{5,1},{9,13},{13,9},{2,6},{6,2},{1... | collective-permute-start | bytes 86024 | tf_op jit(solution)/shard_map/ppermute | solution.py:313
  6.7 1.9 %collective-permute-done = bf16[16,896]{1,0:T(8,128)(2,1)S(1)} collective-permute-done((bf16[16,896]{1,0:T(8,128)(2,1)S(1)}, bf16[16,896]{1,0:T(8,128)(2,1)S(1)}, u32[]{:S(2)}, u32[]{:S(2)}) %collective-permute-start) | collective-permute-done | bytes 28704 | tf_op jit(solution)/shard_map/ppermute | solution.py:313
  8.5 3.0 %collective-permute-start.1 = (bf16[32,896]{1,0:T(8,128)(2,1)S(1)}, bf16[32,896]{1,0:T(8,128)(2,1)S(1)}, u32[]{:S(2)}, u32[]{:S(2)}) collective-permute-start(bf16[32,896]{1,0:T(8,128)(2,1)S(1)} %pad_maximum_fusion.2), channel_id=1, source_target_pairs={{0,8},{4,12},{8,0},{12,4},{1,9},{5,13},{9,1},{13,5},{2,10},{6,14},... | collective-permute-start | bytes 172040 | tf_op jit(solution)/shard_map/ppermute | solution.py:313
  11.6 2.2 %collective-permute-done.1 = bf16[32,896]{1,0:T(8,128)(2,1)S(1)} collective-permute-done((bf16[32,896]{1,0:T(8,128)(2,1)S(1)}, bf16[32,896]{1,0:T(8,128)(2,1)S(1)}, u32[]{:S(2)}, u32[]{:S(2)}) %collective-permute-start.1) | collective-permute-done | bytes 57376 | tf_op jit(solution)/shard_map/ppermute | solution.py:313
  13.7 1.9 %collective-permute-start.2 = (bf16[1,64,896]{2,1,0:T(8,128)(2,1)S(1)}, bf16[1,64,896]{2,1,0:T(8,128)(2,1)S(1)}, u32[]{:S(2)}, u32[]{:S(2)}) collective-permute-start(bf16[1,64,896]{2,1,0:T(8,128)(2,1)S(1)} %maximum_bitcast_fusion), channel_id=1, source_target_pairs={{0,2},{1,3},{2,0},{3,1},{4,6},{5,7},{6,4},{7,5},{8,10},{9,11},{10,... | collective-permute-start | bytes 344072 | tf_op jit(solution)/shard_map/ppermute | solution.py:313
  15.6 3.0 %collective-permute-done.2 = bf16[1,64,896]{2,1,0:T(8,128)(2,1)S(1)} collective-permute-done((bf16[1,64,896]{2,1,0:T(8,128)(2,1)S(1)}, bf16[1,64,896]{2,1,0:T(8,128)(2,1)S(1)}, u32[]{:S(2)}, u32[]{:S(2)}) %collective-permute-start.2) | collective-permute-done | bytes 114720 | tf_op jit(solution)/shard_map/ppermute | solution.py:313
  18.6 0.1 collective-permute-start.3
  18.7 1.5 %collective-permute-done.3 = bf16[2,64,896]{2,1,0:T(8,128)(2,1)S(1)} collective-permute-done((bf16[2,64,896]{2,1,0:T(8,128)(2,1)S(1)}, bf16[2,64,896]{2,1,0:T(8,128)(2,1)S(1)}, u32[]{:S(2)}, u32[]{:S(2)}) %collective-permute-start.3) | collective-permute-done | bytes 229408 | tf_op jit(solution)/shard_map/ppermute | solution.py:313
  20.2 0.1 pad_maximum_fusion.gathered
  20.2 13.1 %experts.1 = (f32[2,64,768]{2,1,0:T(8,128)S(1)}, bf16[2,64,768]{2,1,0:T(8,128)(2,1)S(1)}) custom-call(bf16[4,64,896]{2,1,0:T(8,128)(2,1)S(1)} %pad_maximum_fusion.gathered, bf16[3072,2048]{1,0:T(8,128)(2,1)} %gate_weight.1, bf16[3072,2048]{1,0:T(8,128)(2,1)} %up_weight.1, bf16[2048,3072]{1,0:T(8,128)(2,1)} %down_weight.1, bf16[128,2048]{1,0:T(8,128)(2,1)} %adapter_weight.1), custom_call_target="tpu_custom_call" | custom-call | flops 2415919104 | bytes 37748736 | tf_op jit(solution)/shard_map/experts/pallas_call | solution.py:277
  33.4 0.2 collective-permute-start.4
  33.6 1.3 %collective-permute-done.4 = bf16[2,64,768]{2,1,0:T(8,128)(2,1)S(1)} collective-permute-done((bf16[2,64,768]{2,1,0:T(8,128)(2,1)S(1)}, bf16[2,64,768]{2,1,0:T(8,128)(2,1)S(1)}, u32[]{:S(2)}, u32[]{:S(2)}) %collective-permute-start.4) | collective-permute-done | bytes 196640 | tf_op jit(solution)/shard_map/ppermute | solution.py:313
  34.9 1.9 %collective-permute-start.5 = (bf16[1,64,768]{2,1,0:T(8,128)(2,1)S(1)}, bf16[1,64,768]{2,1,0:T(8,128)(2,1)S(1)}, u32[]{:S(2)}, u32[]{:S(2)}) collective-permute-start(bf16[1,64,768]{2,1,0:T(8,128)(2,1)S(1)} %slice.46), channel_id=1, source_target_pairs={{0,2},{1,3},{2,0},{3,1},{4,6},{5,7},{6,4},{7,5},{8,10},{9,11},{10,... | collective-permute-start | bytes 294920 | tf_op jit(solution)/shard_map/ppermute | solution.py:313
  36.8 3.1 %collective-permute-done.5 = bf16[1,64,768]{2,1,0:T(8,128)(2,1)S(1)} collective-permute-done((bf16[1,64,768]{2,1,0:T(8,128)(2,1)S(1)}, bf16[1,64,768]{2,1,0:T(8,128)(2,1)S(1)}, u32[]{:S(2)}, u32[]{:S(2)}) %collective-permute-start.5) | collective-permute-done | bytes 98336 | tf_op jit(solution)/shard_map/ppermute | solution.py:313
  40.0 1.9 %collective-permute-start.6 = (bf16[2,16,768]{2,1,0:T(8,128)(2,1)S(1)}, bf16[2,16,768]{2,1,0:T(8,128)(2,1)S(1)}, u32[]{:S(2)}, u32[]{:S(2)}) collective-permute-start(bf16[2,16,768]{2,1,0:T(8,128)(2,1)S(1)} %slice.28), channel_id=1, source_target_pairs={{0,4},{4,0},{8,12},{12,8},{1,5},{5,1},{9,13},{13,9},{2,6},{6,2},{1... | collective-permute-start | bytes 147464 | tf_op jit(solution)/shard_map/ppermute | solution.py:313
  41.9 2.3 %collective-permute-done.6 = bf16[2,16,768]{2,1,0:T(8,128)(2,1)S(1)} collective-permute-done((bf16[2,16,768]{2,1,0:T(8,128)(2,1)S(1)}, bf16[2,16,768]{2,1,0:T(8,128)(2,1)S(1)}, u32[]{:S(2)}, u32[]{:S(2)}) %collective-permute-start.6) | collective-permute-done | bytes 49184 | tf_op jit(solution)/shard_map/ppermute | solution.py:313
  44.2 3.0 %collective-permute-start.7 = (bf16[1,16,768]{2,1,0:T(8,128)(2,1)S(1)}, bf16[1,16,768]{2,1,0:T(8,128)(2,1)S(1)}, u32[]{:S(2)}, u32[]{:S(2)}) collective-permute-start(bf16[1,16,768]{2,1,0:T(8,128)(2,1)S(1)} %slice.47), channel_id=1, source_target_pairs={{0,8},{4,12},{8,0},{12,4},{1,9},{5,13},{9,1},{13,5},{2,10},{6,14},... | collective-permute-start | bytes 73736 | tf_op jit(solution)/shard_map/ppermute | solution.py:313
  47.1 1.8 %collective-permute-done.7 = bf16[1,16,768]{2,1,0:T(8,128)(2,1)S(1)} collective-permute-done((bf16[1,16,768]{2,1,0:T(8,128)(2,1)S(1)}, bf16[1,16,768]{2,1,0:T(8,128)(2,1)S(1)}, u32[]{:S(2)}, u32[]{:S(2)}) %collective-permute-start.7) | collective-permute-done | bytes 24608 | tf_op jit(solution)/shard_map/ppermute | solution.py:313
  49.0 0.6 %fusion.2 = bf16[16,768]{1,0:T(8,128)(2,1)} fusion(f32[2,16,768]{2,1,0:T(8,128)S(1)} %convert_add_fusion.1, bf16[1,16,768]{2,1,0:T(8,128)(2,1)S(1)} %collective-permute-done.7, bf16[16,768]{1,0:T(8,128)(2,1)S(1)} %get-tuple-element.9), kind=kLoop, calls=%fused_computation.12 | loop fusion | flops 61440 | bytes 122880 | tf_op jit(solution)/shard_map/convert_element_type | solution.py:380
  (10 shorter events, 0.2 us)
Async XLA Ops:
  3.6 4.9 %collective-permute-start = (bf16[16,896]{1,0:T(8,128)(2,1)S(1)}, bf16[16,896]{1,0:T(8,128)(2,1)S(1)}, u32[]{:S(2)}, u32[]{:S(2)}) collective-permute-start(bf16[16,896]{1,0:T(8,128)(2,1)S(1)} %get-tuple-element.10), channel_id=1, source_target_pairs={{0,4},{4,0},{8,12},{12,8},{1,5},{5,1},{9,13},{13,9},{2,6},{6,2},{1... | collective-permute-start | bytes 86024 | tf_op jit(solution)/shard_map/ppermute | solution.py:313
  8.5 5.2 %collective-permute-start.1 = (bf16[32,896]{1,0:T(8,128)(2,1)S(1)}, bf16[32,896]{1,0:T(8,128)(2,1)S(1)}, u32[]{:S(2)}, u32[]{:S(2)}) collective-permute-start(bf16[32,896]{1,0:T(8,128)(2,1)S(1)} %pad_maximum_fusion.2), channel_id=1, source_target_pairs={{0,8},{4,12},{8,0},{12,4},{1,9},{5,13},{9,1},{13,5},{2,10},{6,14},... | collective-permute-start | bytes 172040 | tf_op jit(solution)/shard_map/ppermute | solution.py:313
  13.7 4.9 %collective-permute-start.2 = (bf16[1,64,896]{2,1,0:T(8,128)(2,1)S(1)}, bf16[1,64,896]{2,1,0:T(8,128)(2,1)S(1)}, u32[]{:S(2)}, u32[]{:S(2)}) collective-permute-start(bf16[1,64,896]{2,1,0:T(8,128)(2,1)S(1)} %maximum_bitcast_fusion), channel_id=1, source_target_pairs={{0,2},{1,3},{2,0},{3,1},{4,6},{5,7},{6,4},{7,5},{8,10},{9,11},{10,... | collective-permute-start | bytes 344072 | tf_op jit(solution)/shard_map/ppermute | solution.py:313
  18.6 1.6 %collective-permute-start.3 = (bf16[2,64,896]{2,1,0:T(8,128)(2,1)S(1)}, bf16[2,64,896]{2,1,0:T(8,128)(2,1)S(1)}, u32[]{:S(2)}, u32[]{:S(2)}) collective-permute-start(bf16[2,64,896]{2,1,0:T(8,128)(2,1)S(1)} %pad_maximum_fusion.1), channel_id=1, source_target_pairs={{0,1},{1,0},{2,3},{3,2},{4,5},{5,4},{6,7},{7,6},{8,9},{9,8},{10,11... | collective-permute-start | bytes 688136 | tf_op jit(solution)/shard_map/ppermute | solution.py:313
  33.4 1.5 %collective-permute-start.4 = (bf16[2,64,768]{2,1,0:T(8,128)(2,1)S(1)}, bf16[2,64,768]{2,1,0:T(8,128)(2,1)S(1)}, u32[]{:S(2)}, u32[]{:S(2)}) collective-permute-start(bf16[2,64,768]{2,1,0:T(8,128)(2,1)S(1)} %get-tuple-element.12), channel_id=1, source_target_pairs={{0,1},{1,0},{2,3},{3,2},{4,5},{5,4},{6,7},{7,6},{8,9},{9,8},{10,11... | collective-permute-start | bytes 589832 | tf_op jit(solution)/shard_map/ppermute | solution.py:313
  34.9 5.0 %collective-permute-start.5 = (bf16[1,64,768]{2,1,0:T(8,128)(2,1)S(1)}, bf16[1,64,768]{2,1,0:T(8,128)(2,1)S(1)}, u32[]{:S(2)}, u32[]{:S(2)}) collective-permute-start(bf16[1,64,768]{2,1,0:T(8,128)(2,1)S(1)} %slice.46), channel_id=1, source_target_pairs={{0,2},{1,3},{2,0},{3,1},{4,6},{5,7},{6,4},{7,5},{8,10},{9,11},{10,... | collective-permute-start | bytes 294920 | tf_op jit(solution)/shard_map/ppermute | solution.py:313
  40.0 4.2 %collective-permute-start.6 = (bf16[2,16,768]{2,1,0:T(8,128)(2,1)S(1)}, bf16[2,16,768]{2,1,0:T(8,128)(2,1)S(1)}, u32[]{:S(2)}, u32[]{:S(2)}) collective-permute-start(bf16[2,16,768]{2,1,0:T(8,128)(2,1)S(1)} %slice.28), channel_id=1, source_target_pairs={{0,4},{4,0},{8,12},{12,8},{1,5},{5,1},{9,13},{13,9},{2,6},{6,2},{1... | collective-permute-start | bytes 147464 | tf_op jit(solution)/shard_map/ppermute | solution.py:313
  44.2 4.8 %collective-permute-start.7 = (bf16[1,16,768]{2,1,0:T(8,128)(2,1)S(1)}, bf16[1,16,768]{2,1,0:T(8,128)(2,1)S(1)}, u32[]{:S(2)}, u32[]{:S(2)}) collective-permute-start(bf16[1,16,768]{2,1,0:T(8,128)(2,1)S(1)} %slice.47), channel_id=1, source_target_pairs={{0,8},{4,12},{8,0},{12,4},{1,9},{5,13},{9,1},{13,5},{2,10},{6,14},... | collective-permute-start | bytes 73736 | tf_op jit(solution)/shard_map/ppermute | solution.py:313

commit v3 on v1

--- a/solution.py
+++ b/solution.py
@@ -21,6 +21,14 @@
 ANY_LANES = (((1,), (1,)), ((), ()))
 
 
+VMEM = pl.BlockSpec(memory_space=pltpu.VMEM)
+HBM = pl.BlockSpec(memory_space=pl.ANY)
+
+
+def in_hbm(*arrays):
+    return [pltpu.with_memory_space_constraint(array, pltpu.HBM) for array in arrays]
+
+
 def column(values, rows):
     index = lax.broadcasted_iota(jnp.int32, (rows, LANES), 0)
     out = jnp.zeros((rows, LANES), jnp.int32)
@@ -29,7 +37,36 @@
     return out
 
 
-def attend_kernel(
+def fetch(gate_weight, up_weight, distance, part, arrived):
+    features = part.shape[1]
+    start = pl.multiple_of((lax.axis_index("tp") ^ distance) * features, features)
+    copies = [
+        pltpu.make_async_copy(weight.at[pl.ds(start, features), :], part.at[i], arrived.at[i])
+        for i, weight in enumerate((gate_weight, up_weight))
+    ]
+    for copy in copies:
+        copy.start()
+    return copies
+
+
+def attend_kernel(*refs):
+    count = 12
+    sources, weights = refs[:count], refs[count : count + 2]
+    outs, own_weights = refs[count + 2 : count + 4], refs[count + 4]
+    buffers, arrived, weights_arrived = refs[count + 5 : -2], refs[-2], refs[-1]
+    copies = [
+        pltpu.make_async_copy(source, buffer, arrived.at[i])
+        for i, (source, buffer) in enumerate(zip(sources, buffers, strict=True))
+    ]
+    for i in (7, 4, 0, 5, 8, 6, 3, 9, 1, 2, 10, 11):
+        copies[i].start()
+    fetched = fetch(*weights, 0, own_weights, weights_arrived)
+    attend_body(*buffers, *outs, wait=lambda *which: [copies[i].wait() for i in which])
+    for copy in fetched:
+        copy.wait()
+
+
+def attend_body(
     lengths,
     tenants,
     routes,
@@ -44,12 +81,15 @@
     adapter_down,
     state_out,
     payload_out,
+    *,
+    wait,
 ):
     rows, features = residual.shape
     kv_local = token_keys.shape[1] // HD
     cache = stored_keys.shape[1]
     group = HEADS // KVH
     scale = HD ** (-0.5)
+    wait(0, 4, 7)
     length_column = column(lambda r: lengths[r], rows)
     stacked_length = jnp.concatenate([length_column[:, :1]] * group, axis=0)
     stacked_row = lax.rem(
@@ -70,6 +110,8 @@
             )
             scores = jnp.where(stacked_row[:, :cache] == r, every, scores)
         scores = jnp.where(visible, scores * scale, -jnp.inf)
+        if g == 0:
+            wait(5)
         fresh_key = jnp.concatenate([token_keys[:, key_lanes].astype(F32)] * group, axis=0)
         fresh = jnp.sum(query.astype(F32) * fresh_key, axis=1, keepdims=True) * scale
         largest = jnp.maximum(jnp.max(scores, axis=1, keepdims=True), fresh)
@@ -78,10 +120,14 @@
         denominator = jnp.sum(cache_exp, axis=1, keepdims=True) + fresh_exp
         probs = (cache_exp / denominator).astype(BF16)
         fresh_prob = (fresh_exp / denominator).astype(BF16).astype(F32)
+        if g == 0:
+            wait(8)
         attended = jnp.zeros((group * rows, HD), F32)
         for r in range(rows):
             every = jnp.dot(probs, stored_values[r, :, key_lanes], preferred_element_type=F32)
             attended = jnp.where(stacked_row[:, :HD] == r, every, attended)
+        if g == 0:
+            wait(3, 6, 9)
         fresh_value = jnp.concatenate([token_values[:, key_lanes].astype(F32)] * group, axis=0)
         attended = attended + fresh_prob * fresh_value
         for j in range(group):
@@ -92,7 +138,10 @@
             state_out[:, lanes] = state
             state = state.astype(F32)
             squares = squares + jnp.sum(state * state, axis=1, keepdims=True)
-            payload_out[:, lanes] = (state * gain[:, lanes]).astype(BF16)
+            payload_out[:, lanes] = (
+                state * gain[lanes.start // LANES : lanes.start // LANES + 1, :]
+            ).astype(BF16)
+    wait(1, 2, 10, 11)
     scaled = payload_out[:, :features]
     logits = lax.dot_general(scaled, router[...], ANY_LANES, preferred_element_type=F32)
     first = column(lambda r: routes[0, r], rows)
@@ -125,39 +174,109 @@
     payload_out[:, features:] = tail.astype(BF16)
 
 
-def attend(args):
+def attend(args, gate_weight, up_weight):
     rows, features = args[3].shape
-    smem = pl.BlockSpec(memory_space=pltpu.SMEM)
-    vmem = pl.BlockSpec(memory_space=pltpu.VMEM)
     return pl.pallas_call(
         attend_kernel,
         out_shape=(
             jax.ShapeDtypeStruct((rows, features), BF16),
             jax.ShapeDtypeStruct((rows, features + LANES), BF16),
-        ),
-        in_specs=[smem] * 3 + [vmem] * 9,
-        out_specs=(vmem, vmem),
+            jax.ShapeDtypeStruct((2, features, gate_weight.shape[1]), BF16),
+        ),
+        in_specs=[HBM] * (len(args) + 2),
+        out_specs=(VMEM, VMEM, VMEM),
+        scratch_shapes=[
+            (pltpu.SMEM if i < 3 else pltpu.VMEM)(arg.shape, arg.dtype)
+            for i, arg in enumerate(args)
+        ]
+        + [pltpu.SemaphoreType.DMA((len(args),)), pltpu.SemaphoreType.DMA((2,))],
         compiler_params=pltpu.CompilerParams(vmem_limit_bytes=12 * 2**20),
         cost_estimate=pl.CostEstimate(
-            flops=200_000_000, bytes_accessed=3_000_000, transcendentals=20_000
+            flops=200_000_000, bytes_accessed=10_000_000, transcendentals=20_000
         ),
         name="attend",
-    )(*args)
-
-
-def expert_kernel(
-    order, replicas, gathered, gate_weight, up_weight, down_weight, adapter_up, kept, sent, active
-):
-    tensor_devices, rows, width = gathered.shape
+    )(*in_hbm(*args, gate_weight, up_weight))
+
+
+def load_kernel(distance, gate_weight, up_weight, after, part, arrived):
+    for copy in fetch(gate_weight, up_weight, distance, part, arrived):
+        copy.wait()
+
+
+def load(gate_weight, up_weight, distance, features, after):
+    shape = (2, features, gate_weight.shape[1])
+    return pl.pallas_call(
+        functools.partial(load_kernel, distance),
+        out_shape=jax.ShapeDtypeStruct(shape, BF16),
+        in_specs=[HBM] * 3,
+        out_specs=VMEM,
+        scratch_shapes=[pltpu.SemaphoreType.DMA((2,))],
+        compiler_params=pltpu.CompilerParams(vmem_limit_bytes=2**20),
+        cost_estimate=pl.CostEstimate(
+            flops=0, bytes_accessed=4 * features * gate_weight.shape[1], transcendentals=0
+        ),
+        name="load",
+    )(*in_hbm(gate_weight, up_weight), after)
+
+
+def partial_kernel(distance, block, part, *refs):
+    features = part.shape[1]
+    fetched = []
+    if distance is not None:
+        gate_weight, up_weight, *refs = refs
+        *refs, next_part, arrived = refs
+        fetched = fetch(gate_weight, up_weight, distance, next_part, arrived)
+    sums, totals = refs[:-1], refs[-1]
+    scaled = block[:, :features]
+    for i in range(2):
+        product = jnp.dot(scaled, part[i], preferred_element_type=F32)
+        totals[i] = sums[0][i] + product if sums else product
+    for copy in fetched:
+        copy.wait()
+
+
+def partial(block, part, sums, gate_weight, up_weight, distance):
+    rows, width = block.shape
     features = width - LANES
-    hidden = gate_weight.shape[1]
-    mine = lax.axis_index("tp")
+    hidden = part.shape[2]
+    fetching = distance is not None
+    totals = jax.ShapeDtypeStruct((2, rows, hidden), F32)
+    given = (block, part) + (tuple(in_hbm(gate_weight, up_weight)) if fetching else ())
+    given = given + ((sums,) if sums is not None else ())
+    return pl.pallas_call(
+        functools.partial(partial_kernel, distance),
+        out_shape=(totals, jax.ShapeDtypeStruct(part.shape, BF16)) if fetching else (totals,),
+        in_specs=[VMEM, VMEM] + [HBM] * (2 * fetching) + [VMEM] * (sums is not None),
+        out_specs=(VMEM,) * (1 + fetching),
+        scratch_shapes=[pltpu.SemaphoreType.DMA((2,))] * fetching,
+        compiler_params=pltpu.CompilerParams(vmem_limit_bytes=8 * 2**20),
+        cost_estimate=pl.CostEstimate(
+            flops=4 * rows * features * hidden,
+            bytes_accessed=4 * features * hidden,
+            transcendentals=0,
+        ),
+        name="partial",
+    )(*given)
+
+
+def expert_kernel(replicas, targets, known, count, sums, *refs):
+    tensor_devices = known + count
+    blocks, parts = refs[:tensor_devices], refs[tensor_devices : tensor_devices + count]
+    down_weight, adapter_weight, out, active, down_part, adapter_up, arrived = refs[
+        tensor_devices + count :
+    ]
+    rows, width = blocks[0].shape
+    features = width - LANES
+    copies = [pltpu.make_async_copy(adapter_weight, adapter_up, arrived.at[len(targets)])]
+    copies += down_copies(down_weight, targets, down_part, arrived)
+    for copy in copies:
+        copy.start()
     expert = lax.axis_index("ep") // replicas
     tail = jnp.zeros((rows, LANES), F32)
-    for i in range(tensor_devices):
-        tail = tail + gathered[i, :, features:].astype(F32)
+    for block in blocks:
+        tail = tail + block[:, features:].astype(F32)
     place = lambda k: tail[:, k : k + 1]
-    here = gathered[0, :, features:].astype(F32)
+    here = blocks[0][:, features:].astype(F32)
     inverse_rms = lax.rsqrt(
         (place(SQ_HI) + place(SQ_LO)) / (features * tensor_devices) + 1e-05
     )
@@ -180,69 +299,129 @@
     adapter_rows = jnp.where(
         own_tenant, jnp.dot(lowrank, spread, preferred_element_type=F32), 0.0
     ).astype(BF16)
-    tile = min(256, hidden)
-
-    def hidden_tile(n, carry):
-        lanes = pl.ds(pl.multiple_of(n * tile, tile), tile)
-        gate = jnp.zeros((rows, tile), F32)
-        up = jnp.zeros((rows, tile), F32)
-        for i in range(tensor_devices):
-            start = pl.multiple_of((mine ^ order[i]) * features, features)
-            scaled = gathered[i, :, :features]
-            gate = gate + jnp.dot(
-                scaled, gate_weight[pl.ds(start, features), lanes], preferred_element_type=F32
-            )
-            up = up + jnp.dot(
-                scaled, up_weight[pl.ds(start, features), lanes], preferred_element_type=F32
-            )
+    copies[0].wait()
+    hidden = active.shape[1]
+    tile = min(512, hidden)
+    for start in range(0, hidden, tile):
+        lanes = slice(start, start + tile)
+        gate, up = sums[0, :, lanes], sums[1, :, lanes]
+        for block, part in zip(blocks[known:], parts, strict=True):
+            scaled = block[:, :features]
+            gate = gate + jnp.dot(scaled, part[0, :, lanes], preferred_element_type=F32)
+            up = up + jnp.dot(scaled, part[1, :, lanes], preferred_element_type=F32)
         gate = gate * inverse_rms
         up = up * inverse_rms + jnp.dot(
             adapter_rows, adapter_up[:, lanes], preferred_element_type=F32
         )
         active[:, lanes] = (gate * jax.nn.sigmoid(gate) * up * weight).astype(BF16)
-        return carry
-
-    lax.fori_loop(0, hidden // tile, hidden_tile, 0)
-    out_tile = 256 if features % 256 == 0 else LANES
-    for i in range(tensor_devices):
-        start = (mine ^ i) * features
-
-        def out_tiles(n, carry):
-            lanes = pl.ds(pl.multiple_of(start + n * out_tile, LANES), out_tile)
-            result = jnp.dot(active[...], down_weight[:, lanes], preferred_element_type=F32)
-            to = pl.ds(pl.multiple_of(n * out_tile, out_tile), out_tile)
-            if i % 2 == 0:
-                kept[i // 2, :, to] = result
-            else:
-                sent[i // 2, :, to] = result.astype(BF16)
-            return carry
-
-        lax.fori_loop(0, features // out_tile, out_tiles, 0)
-
-
-def experts(gathered, order, replicas, gate_weight, up_weight, down_weight, adapter_up):
-    tensor_devices, rows, width = gathered.shape
-    features = width - LANES
-    vmem = pl.BlockSpec(memory_space=pltpu.VMEM)
-    placed = [
-        pltpu.with_memory_space_constraint(w, pltpu.VMEM)
-        for w in (gate_weight, up_weight, down_weight)
+    down_products(active, copies[1:], down_part, out)
+
+
+def down_copies(down_weight, targets, down_part, arrived):
+    features = down_part.shape[2]
+    return [
+        pltpu.make_async_copy(
+            down_weight.at[
+                :, pl.ds(pl.multiple_of((lax.axis_index("tp") ^ k) * features, features), features)
+            ],
+            down_part.at[i],
+            arrived.at[i],
+        )
+        for i, k in enumerate(targets)
     ]
-    return pl.pallas_call(
-        functools.partial(expert_kernel, order, replicas),
+
+
+def down_products(active, copies, down_part, out):
+    for i, copy in enumerate(copies):
+        copy.wait()
+        out[i] = jnp.dot(active[...], down_part[i], preferred_element_type=F32).astype(out.dtype)
+
+
+def experts(replicas, targets, sums, known, blocks, parts, down_weight, adapter_up):
+    rows, width = blocks[0].shape
+    features, hidden = width - LANES, sums.shape[2]
+    return pl.pallas_call(
+        functools.partial(expert_kernel, replicas, targets, known, len(parts)),
         out_shape=(
-            jax.ShapeDtypeStruct((tensor_devices // 2, rows, features), F32),
-            jax.ShapeDtypeStruct((tensor_devices // 2, rows, features), BF16),
-        ),
-        in_specs=[vmem] * 5,
-        out_specs=(vmem, vmem),
-        scratch_shapes=[pltpu.VMEM((rows, gate_weight.shape[1]), BF16)],
+            jax.ShapeDtypeStruct((len(targets), rows, features), BF16),
+            jax.ShapeDtypeStruct((rows, hidden), BF16),
+        ),
+        in_specs=[VMEM] * (1 + len(blocks) + len(parts)) + [HBM] * 2,
+        out_specs=(VMEM, VMEM),
+        scratch_shapes=[
+            pltpu.VMEM((len(targets), hidden, features), BF16),
+            pltpu.VMEM(adapter_up.shape, BF16),
+            pltpu.SemaphoreType.DMA((len(targets) + 1,)),
+        ],
         compiler_params=pltpu.CompilerParams(vmem_limit_bytes=16 * 2**20),
         cost_estimate=pl.CostEstimate(
-            flops=2 * rows * 3 * gate_weight.size, bytes_accessed=4_000_000, transcendentals=0
+            flops=2 * rows * hidden * features * (2 * len(parts) + len(targets)),
+            bytes_accessed=2 * len(targets) * hidden * features,
+            transcendentals=0,
         ),
         name="experts",
-    )(gathered, *placed, adapter_up)
+    )(sums, *blocks, *parts, *in_hbm(down_weight, adapter_up))
+
+
+def down_kernel(targets, active, down_weight, after, out, down_part, arrived):
+    copies = down_copies(down_weight, targets, down_part, arrived)
+    for copy in copies:
+        copy.start()
+    down_products(active, copies, down_part, out)
+
+
+def down(targets, active, down_weight, features, after):
+    rows, hidden = active.shape
+    return pl.pallas_call(
+        functools.partial(down_kernel, targets),
+        out_shape=jax.ShapeDtypeStruct((len(targets), rows, features), F32),
+        in_specs=[VMEM, HBM, HBM],
+        out_specs=VMEM,
+        scratch_shapes=[
+            pltpu.VMEM((len(targets), hidden, features), BF16),
+            pltpu.SemaphoreType.DMA((len(targets),)),
+        ],
+        compiler_params=pltpu.CompilerParams(vmem_limit_bytes=16 * 2**20),
+        cost_estimate=pl.CostEstimate(
+            flops=2 * rows * hidden * features * len(targets),
+            bytes_accessed=2 * len(targets) * hidden * features,
+            transcendentals=0,
+        ),
+        name="down",
+    )(active, *in_hbm(down_weight), after)
+
+
+def join_kernel(first, second, after, out):
+    count = first.shape[0]
+    out[:count] = first[...]
+    out[count:] = second[...]
+
+
+def join(first, second, after):
+    return pl.pallas_call(
+        join_kernel,
+        out_shape=jax.ShapeDtypeStruct((2 * first.shape[0], *first.shape[1:]), first.dtype),
+        in_specs=[VMEM, VMEM, HBM],
+        out_specs=VMEM,
+        compiler_params=pltpu.CompilerParams(vmem_limit_bytes=4 * 2**20),
+        name="join",
+    )(first, second, after)
+
+
+def tie_kernel(array, after, out):
+    pass
+
+
+def tie(array, after):
+    return pl.pallas_call(
+        tie_kernel,
+        out_shape=jax.ShapeDtypeStruct(array.shape, array.dtype),
+        in_specs=[HBM, HBM],
+        out_specs=HBM,
+        input_output_aliases={0: 0},
+        compiler_params=pltpu.CompilerParams(vmem_limit_bytes=2**20),
+        name="tie",
+    )(array, after)
 
 
 def swap(x, axis, distance):
@@ -275,7 +454,8 @@
     rows, features = residual.shape
     expert_devices = lax.axis_size("ep")
     tensor_devices = lax.axis_size("tp")
-    state, held = attend(
+    weights = (expert_gate_weight, expert_up_weight)
+    state, held, part = attend(
         (
             lengths,
             tenants,
@@ -286,31 +466,59 @@
             token_values,
             stored_keys,
             stored_values,
-            norm_gain_vector.reshape(1, features),
+            norm_gain_vector.reshape(features // LANES, LANES),
             router.T,
             adapter_down_map,
-        )
-    )
+        ),
+        *weights,
+    )
+    order = [0]
+    for distance in reversed(bits(tensor_devices)):
+        order += [at ^ distance for at in order]
+    parts = [part]
     for distance in bits(expert_devices):
-        held = jnp.concatenate([held, swap(held, "ep", distance)], axis=0)
-    gathered, order = held[None], [0]
+        other = swap(held, "ep", distance)
+        if len(parts) < tensor_devices - 1:
+            parts.append(load(*weights, order[len(parts)], features, held))
+        held = join(held, other, parts[-1])
+    blocks, known, sums = [held], 0, None
     for distance in reversed(bits(tensor_devices)):
-        gathered = jnp.concatenate([gathered, swap(gathered, "tp", distance)], axis=0)
-        order = order + [at ^ distance for at in order]
-    kept, sent = experts(
-        gathered,
-        tuple(order),
+        others = [swap(block, "tp", distance) for block in blocks]
+        for block in blocks[known:]:
+            fetching = len(parts) < tensor_devices
+            sums, *more = partial(
+                block, parts[known], sums, *weights, order[len(parts)] if fetching else None
+            )
+            parts += more
+            known += 1
+        blocks = blocks + [tie(block, sums) if distance > 1 else block for block in others]
+    while len(parts) < tensor_devices:
+        parts.append(load(*weights, order[len(parts)], features, held))
+    steps = bits(tensor_devices)
+    groups = [tuple(k for k in range(tensor_devices) if k & -k == step) for step in steps] + [(0,)]
+    sent, active = experts(
         expert_devices // EXPERT_COUNT,
-        expert_gate_weight,
-        expert_up_weight,
+        groups[0],
+        sums,
+        known,
+        blocks,
+        parts[known:],
         expert_down_weight,
         adapter_up_map,
     )
-    for distance in bits(tensor_devices):
-        if distance > 1:
-            kept, sent = kept[0::2], kept[1::2].astype(BF16)
-        kept = kept + swap(sent, "tp", distance).astype(F32)
-    kept = kept.reshape(expert_devices, rows, features)
+    received = {k: [] for k in range(tensor_devices)}
+    for step, group, following in zip(steps, groups[:-1], groups[1:], strict=True):
+        arriving = swap(sent, "tp", step)
+        made = down(following, active, expert_down_weight, features, sent)
+        for i, k in enumerate(group):
+            received[k ^ step].append(arriving[i])
+        kept = [
+            sum((block.astype(F32) for block in received[k]), made[i])
+            for i, k in enumerate(following)
+        ]
+        if following != (0,):
+            sent = jnp.stack([block.astype(BF16) for block in kept])
+    kept = kept[0].reshape(expert_devices, rows, features)
     for distance in bits(expert_devices):
         kept, sent = kept[0::2], kept[1::2].astype(BF16)
         kept = kept + swap(sent, "ep", distance).astype(F32)

time: 70.5 us -> 46.1 us (0.65)
  local copies, waits for them, and re-layouts: 24.6 us -> 0.01 us
  Pallas kernels: 12.4 us -> 24.9 us
  waiting for transfers between devices: 17 us -> 8.45 us
  starting transfers between devices: 15 us -> 11.7 us
    unnamed x30 -> x0, local copies, waits for them, and re-layouts: 23.9 us -> none
    pallas_call x1 -> x10, Pallas kernels: 9.86 us -> 21 us  [the longest x2 5.72 us: load(): pl.pallas_call(functools.partial(load_kernel, distance), out_shape=jax.Sh...]
    ppermute x8 -> x9, waiting for transfers between devices: 17 us -> 8.45 us  [swap(): return lax.ppermute(x, axis, [(i, i ^ distance) for i in range(count)])]
    ppermute x8 -> x9, starting transfers between devices: 15 us -> 11.7 us  [swap(): return lax.ppermute(x, axis, [(i, i ^ distance) for i in range(count)])]
    pallas_call x1, Pallas kernels: 2.53 us -> 3.91 us  [attend(): pl.pallas_call(attend_kernel, out_shape=(jax.ShapeDtypeStruct((rows, feat...]
  transfers between devices with their start and end apart: 8 -> 9, of which waited for: 8 -> 4; matrix products, arithmetic and copies ran while one was open for 0% -> 0% of each run, Pallas kernels for 0% -> 35%
where the time goes in v3:
time: 46.1 us; the launch traced here: 45.9 us
  Pallas kernels  24.9 us (54%)
  starting transfers between devices  11.7 us (25%)
  waiting for transfers between devices  8.45 us (18%)
  other arithmetic  0.69 us (1%)
    ppermute x9, starting transfers between devices, swap(): return lax.ppermute(x, axis, [(i, i ^ distance) for i in range(count)])  11.7 us
    ppermute x9, waiting for transfers between devices, swap(): return lax.ppermute(x, axis, [(i, i ^ distance) for i in range(count)])  8.45 us
    pallas_call x2, Pallas kernels, load(): pl.pallas_call(functools.partial(load_kernel, distance), out_shape=jax.Sh...  5.72 us
    pallas_call x2, Pallas kernels, partial(): pl.pallas_call(functools.partial(partial_kernel, distance), out_shape=(to...  5.12 us
    pallas_call x2, Pallas kernels, down(): pl.pallas_call(functools.partial(down_kernel, targets), out_shape=jax.Sha...  5.11 us
    pallas_call x1, Pallas kernels, experts(): pl.pallas_call(functools.partial(expert_kernel, replicas, targets, known,...  5.05 us
    pallas_call x1, Pallas kernels, attend(): pl.pallas_call(attend_kernel, out_shape=(jax.ShapeDtypeStruct((rows, feat...  3.91 us
  transfers between devices with their start and end apart: 9, of which 4 were waited for; matrix products, arithmetic and copies ran while one was open for 0% of the time, Pallas kernels for 35%

profile of v3, /device:TPU:0, one launch (start us, length us, event | category | flops | bytes accessed | tf_op | source)
XLA Modules:
  0.0 45.9 jit_solution(1633780561652695884)
XLA Ops:
  0.0 3.9 %attend.1 = (bf16[16,768]{1,0:T(8,128)(2,1)S(1)}, bf16[16,896]{1,0:T(8,128)(2,1)S(1)}, bf16[2,768,2048]{2,1,0:T(8,128)(2,1)S(1)}) custom-call(s32[16]{0:T(128)} %refs_0_.2, s32[16]{0:T(128)} %refs_1_.2, s32[2,16]{1,0:T(2,128)} %bitcast.14, bf16[16,768]{1,0:T(8,128)(2,1)} %refs_3_.1, bf16[16,768]{1,0:T(8,128)(2,1)} %refs_4_.1, bf16[16,256]{1,0:T(8,128)(2,1)} %refs_5_.1, ...), custom_call_target="tpu_custom_call" | custom-call | flops 200000000 | bytes 10000000 | tf_op jit(solution)/shard_map/attend/pallas_call | solution.py:179
  3.9 3.1 %collective-permute-start = (bf16[16,896]{1,0:T(8,128)(2,1)S(1)}, bf16[16,896]{1,0:T(8,128)(2,1)S(1)}, u32[]{:S(2)}, u32[]{:S(2)}) collective-permute-start(bf16[16,896]{1,0:T(8,128)(2,1)S(1)} %get-tuple-element.13.after.first), channel_id=1, source_target_pairs={{0,4},{4,0},{8,12},{12,8},{1,5},{5,1},{9,13},{13,9},{2,6},{6,2},{1... | collective-permute-start | bytes 86024 | tf_op jit(solution)/shard_map/ppermute | solution.py:429
  7.0 2.9 %load.2.after.part = bf16[2,768,2048]{2,1,0:T(8,128)(2,1)S(1)} custom-call(bf16[3072,2048]{1,0:T(8,128)(2,1)} %refs_0_.3, bf16[3072,2048]{1,0:T(8,128)(2,1)} %refs_1_.3, bf16[16,896]{1,0:T(8,128)(2,1)S(1)} %get-tuple-element.13.after.first), custom_call_target="tpu_custom_call" | custom-call | bytes 6291456 | tf_op jit(solution)/shard_map/load/pallas_call | solution.py:208
  9.9 0.0 collective-permute-done.second
  9.9 2.7 %collective-permute-start.1 = (bf16[32,896]{1,0:T(8,128)(2,1)S(1)}, bf16[32,896]{1,0:T(8,128)(2,1)S(1)}, u32[]{:S(2)}, u32[]{:S(2)}) collective-permute-start(bf16[32,896]{1,0:T(8,128)(2,1)S(1)} %join.2.after.first), channel_id=1, source_target_pairs={{0,8},{4,12},{8,0},{12,4},{1,9},{5,13},{9,1},{13,5},{2,10},{6,14},... | collective-permute-start | bytes 172040 | tf_op jit(solution)/shard_map/ppermute | solution.py:429
  12.6 2.9 %load.3.after.refs_4_ = bf16[2,768,2048]{2,1,0:T(8,128)(2,1)S(1)} custom-call(bf16[3072,2048]{1,0:T(8,128)(2,1)} %refs_0_.3, bf16[3072,2048]{1,0:T(8,128)(2,1)} %refs_1_.3, bf16[32,896]{1,0:T(8,128)(2,1)S(1)} %join.2.after.first), custom_call_target="tpu_custom_call" | custom-call | bytes 6291456 | tf_op jit(solution)/shard_map/load/pallas_call | solution.py:208
  15.4 0.2 collective-permute-done.1.second
  15.7 1.6 %collective-permute-start.2 = (bf16[64,896]{1,0:T(8,128)(2,1)S(1)}, bf16[64,896]{1,0:T(8,128)(2,1)S(1)}, u32[]{:S(2)}, u32[]{:S(2)}) collective-permute-start(bf16[64,896]{1,0:T(8,128)(2,1)S(1)} %join.3.block.refs_0_), channel_id=1, source_target_pairs={{0,2},{1,3},{2,0},{3,1},{4,6},{5,7},{6,4},{7,5},{8,10},{9,11},{10,... | collective-permute-start | bytes 344072 | tf_op jit(solution)/shard_map/ppermute | solution.py:429
  17.2 0.0 collective-permute-start.3
  17.2 3.9 %partial.2 = (f32[2,64,2048]{2,1,0:T(8,128)S(1)}, bf16[2,768,2048]{2,1,0:T(8,128)(2,1)S(1)}) custom-call(bf16[64,896]{1,0:T(8,128)(2,1)S(1)} %join.3.block.refs_0_, bf16[2,768,2048]{2,1,0:T(8,128)(2,1)S(1)} %get-tuple-element.14.part, bf16[3072,2048]{1,0:T(8,128)(2,1)} %refs_0_.3, bf16[3072,2048]{1,0:T(8,128)(2,1)} %refs_1_.3), custom_call_target="tpu_custom_call" | custom-call | flops 402653184 | bytes 6291456 | tf_op jit(solution)/shard_map/partial/pallas_call | solution.py:246
  21.2 0.0 collective-permute-done.2.array
  21.2 0.6 %collective-permute-start.4 = (bf16[64,896]{1,0:T(8,128)(2,1)S(1)}, bf16[64,896]{1,0:T(8,128)(2,1)S(1)}, u32[]{:S(2)}, u32[]{:S(2)}) collective-permute-start(bf16[64,896]{1,0:T(8,128)(2,1)S(1)} %tie.1.block.refs_1_), channel_id=1, source_target_pairs={{0,1},{1,0},{2,3},{3,2},{4,5},{5,4},{6,7},{7,6},{8,9},{9,8},{10,11... | collective-permute-start | bytes 344072 | tf_op jit(solution)/shard_map/ppermute | solution.py:429
  21.8 1.2 %partial.3.sums = f32[2,64,2048]{2,1,0:T(8,128)S(1)} custom-call(bf16[64,896]{1,0:T(8,128)(2,1)S(1)} %tie.1.block.refs_1_, bf16[2,768,2048]{2,1,0:T(8,128)(2,1)S(1)} %load.2.after.part, f32[2,64,2048]{2,1,0:T(8,128)S(1)} %get-tuple-element.15.after.refs_0_), custom_call_target="tpu_custom_call" | custom-call | flops 402653184 | bytes 6291456 | tf_op jit(solution)/shard_map/partial/pallas_call | solution.py:246
  23.0 0.0 collective-permute-done.3.refs_2_
  23.0 0.0 collective-permute-done.4.refs_3_
  23.0 5.0 %experts.1 = (bf16[2,64,768]{2,1,0:T(8,128)(2,1)S(1)}, bf16[64,2048]{1,0:T(8,128)(2,1)S(1)}) custom-call(f32[2,64,2048]{2,1,0:T(8,128)S(1)} %partial.3.sums, bf16[64,896]{1,0:T(8,128)(2,1)S(1)} %join.3.block.refs_0_, bf16[64,896]{1,0:T(8,128)(2,1)S(1)} %tie.1.block.refs_1_, bf16[64,896]{1,0:T(8,128)(2,1)S(1)} %collective-permute-done.3.refs_2_, ...), custom_call_target="tpu_custom_call" | custom-call | flops 1207959552 | bytes 6291456 | tf_op jit(solution)/shard_map/experts/pallas_call | solution.py:343
  28.0 0.2 collective-permute-start.5
  28.2 2.6 %down.2 = f32[1,64,768]{2,1,0:T(8,128)S(1)} custom-call(bf16[64,2048]{1,0:T(8,128)(2,1)S(1)} %get-tuple-element.17.active, bf16[2048,3072]{1,0:T(8,128)(2,1)} %down_weight.3, bf16[2,64,768]{2,1,0:T(8,128)(2,1)S(1)} %get-tuple-element.18.after), custom_call_target="tpu_custom_call" | custom-call | flops 201326592 | bytes 3145728 | tf_op jit(solution)/shard_map/down/pallas_call | solution.py:375
  30.8 0.0 collective-permute-done.5
  30.8 0.8 %collective-permute-start.6 = (bf16[1,64,768]{2,1,0:T(8,128)(2,1)S(1)}, bf16[1,64,768]{2,1,0:T(8,128)(2,1)S(1)}, u32[]{:S(2)}, u32[]{:S(2)}) collective-permute-start(bf16[1,64,768]{2,1,0:T(8,128)(2,1)S(1)} %add_convert_fusion.after), channel_id=1, source_target_pairs={{0,2},{1,3},{2,0},{3,1},{4,6},{5,7},{6,4},{7,5},{8,10},{9,11},{10,... | collective-permute-start | bytes 294920 | tf_op jit(solution)/shard_map/ppermute | solution.py:429
  31.6 2.6 %down.3 = f32[1,64,768]{2,1,0:T(8,128)S(1)} custom-call(bf16[64,2048]{1,0:T(8,128)(2,1)S(1)} %get-tuple-element.17.active, bf16[2048,3072]{1,0:T(8,128)(2,1)} %down_weight.3, bf16[1,64,768]{2,1,0:T(8,128)(2,1)S(1)} %add_convert_fusion.after), custom_call_target="tpu_custom_call" | custom-call | flops 201326592 | bytes 3145728 | tf_op jit(solution)/shard_map/down/pallas_call | solution.py:375
  34.1 1.9 %collective-permute-done.6 = bf16[1,64,768]{2,1,0:T(8,128)(2,1)S(1)} collective-permute-done((bf16[1,64,768]{2,1,0:T(8,128)(2,1)S(1)}, bf16[1,64,768]{2,1,0:T(8,128)(2,1)S(1)}, u32[]{:S(2)}, u32[]{:S(2)}) %collective-permute-start.6) | collective-permute-done | bytes 98336 | tf_op jit(solution)/shard_map/ppermute | solution.py:429
  36.1 0.8 %collective-permute-start.7 = (bf16[2,16,768]{2,1,0:T(8,128)(2,1)S(1)}, bf16[2,16,768]{2,1,0:T(8,128)(2,1)S(1)}, u32[]{:S(2)}, u32[]{:S(2)}) collective-permute-start(bf16[2,16,768]{2,1,0:T(8,128)(2,1)S(1)} %slice.25), channel_id=1, source_target_pairs={{0,4},{4,0},{8,12},{12,8},{1,5},{5,1},{9,13},{13,9},{2,6},{6,2},{1... | collective-permute-start | bytes 147464 | tf_op jit(solution)/shard_map/ppermute | solution.py:429
  36.8 3.4 %collective-permute-done.7 = bf16[2,16,768]{2,1,0:T(8,128)(2,1)S(1)} collective-permute-done((bf16[2,16,768]{2,1,0:T(8,128)(2,1)S(1)}, bf16[2,16,768]{2,1,0:T(8,128)(2,1)S(1)}, u32[]{:S(2)}, u32[]{:S(2)}) %collective-permute-start.7) | collective-permute-done | bytes 49184 | tf_op jit(solution)/shard_map/ppermute | solution.py:429
  40.2 2.1 %collective-permute-start.8 = (bf16[1,16,768]{2,1,0:T(8,128)(2,1)S(1)}, bf16[1,16,768]{2,1,0:T(8,128)(2,1)S(1)}, u32[]{:S(2)}, u32[]{:S(2)}) collective-permute-start(bf16[1,16,768]{2,1,0:T(8,128)(2,1)S(1)} %slice.43), channel_id=1, source_target_pairs={{0,8},{4,12},{8,0},{12,4},{1,9},{5,13},{9,1},{13,5},{2,10},{6,14},... | collective-permute-start | bytes 73736 | tf_op jit(solution)/shard_map/ppermute | solution.py:429
  42.4 2.9 %collective-permute-done.8 = bf16[1,16,768]{2,1,0:T(8,128)(2,1)S(1)} collective-permute-done((bf16[1,16,768]{2,1,0:T(8,128)(2,1)S(1)}, bf16[1,16,768]{2,1,0:T(8,128)(2,1)S(1)}, u32[]{:S(2)}, u32[]{:S(2)}) %collective-permute-start.8) | collective-permute-done | bytes 24608 | tf_op jit(solution)/shard_map/ppermute | solution.py:429
  45.3 0.6 %fusion.2 = bf16[16,768]{1,0:T(8,128)(2,1)} fusion(f32[2,16,768]{2,1,0:T(8,128)S(1)} %convert_add_fusion.1, bf16[1,16,768]{2,1,0:T(8,128)(2,1)S(1)} %collective-permute-done.8, bf16[16,768]{1,0:T(8,128)(2,1)S(1)} %get-tuple-element.12), kind=kLoop, calls=%fused_computation.7 | loop fusion | flops 61440 | bytes 122880 | tf_op jit(solution)/shard_map/convert_element_type | solution.py:525
  (9 shorter events, 0.1 us)
Async XLA Ops:
  3.9 6.0 %collective-permute-start = (bf16[16,896]{1,0:T(8,128)(2,1)S(1)}, bf16[16,896]{1,0:T(8,128)(2,1)S(1)}, u32[]{:S(2)}, u32[]{:S(2)}) collective-permute-start(bf16[16,896]{1,0:T(8,128)(2,1)S(1)} %get-tuple-element.13.after.first), channel_id=1, source_target_pairs={{0,4},{4,0},{8,12},{12,8},{1,5},{5,1},{9,13},{13,9},{2,6},{6,2},{1... | collective-permute-start | bytes 86024 | tf_op jit(solution)/shard_map/ppermute | solution.py:429
  9.9 5.8 %collective-permute-start.1 = (bf16[32,896]{1,0:T(8,128)(2,1)S(1)}, bf16[32,896]{1,0:T(8,128)(2,1)S(1)}, u32[]{:S(2)}, u32[]{:S(2)}) collective-permute-start(bf16[32,896]{1,0:T(8,128)(2,1)S(1)} %join.2.after.first), channel_id=1, source_target_pairs={{0,8},{4,12},{8,0},{12,4},{1,9},{5,13},{9,1},{13,5},{2,10},{6,14},... | collective-permute-start | bytes 172040 | tf_op jit(solution)/shard_map/ppermute | solution.py:429
  15.7 5.5 %collective-permute-start.2 = (bf16[64,896]{1,0:T(8,128)(2,1)S(1)}, bf16[64,896]{1,0:T(8,128)(2,1)S(1)}, u32[]{:S(2)}, u32[]{:S(2)}) collective-permute-start(bf16[64,896]{1,0:T(8,128)(2,1)S(1)} %join.3.block.refs_0_), channel_id=1, source_target_pairs={{0,2},{1,3},{2,0},{3,1},{4,6},{5,7},{6,4},{7,5},{8,10},{9,11},{10,... | collective-permute-start | bytes 344072 | tf_op jit(solution)/shard_map/ppermute | solution.py:429
  17.2 5.7 %collective-permute-start.3 = (bf16[64,896]{1,0:T(8,128)(2,1)S(1)}, bf16[64,896]{1,0:T(8,128)(2,1)S(1)}, u32[]{:S(2)}, u32[]{:S(2)}) collective-permute-start(bf16[64,896]{1,0:T(8,128)(2,1)S(1)} %join.3.block.refs_0_), channel_id=1, source_target_pairs={{0,1},{1,0},{2,3},{3,2},{4,5},{5,4},{6,7},{7,6},{8,9},{9,8},{10,11... | collective-permute-start | bytes 344072 | tf_op jit(solution)/shard_map/ppermute | solution.py:429
  21.2 1.8 %collective-permute-start.4 = (bf16[64,896]{1,0:T(8,128)(2,1)S(1)}, bf16[64,896]{1,0:T(8,128)(2,1)S(1)}, u32[]{:S(2)}, u32[]{:S(2)}) collective-permute-start(bf16[64,896]{1,0:T(8,128)(2,1)S(1)} %tie.1.block.refs_1_), channel_id=1, source_target_pairs={{0,1},{1,0},{2,3},{3,2},{4,5},{5,4},{6,7},{7,6},{8,9},{9,8},{10,11... | collective-permute-start | bytes 344072 | tf_op jit(solution)/shard_map/ppermute | solution.py:429
  28.0 2.7 %collective-permute-start.5 = (bf16[2,64,768]{2,1,0:T(8,128)(2,1)S(1)}, bf16[2,64,768]{2,1,0:T(8,128)(2,1)S(1)}, u32[]{:S(2)}, u32[]{:S(2)}) collective-permute-start(bf16[2,64,768]{2,1,0:T(8,128)(2,1)S(1)} %get-tuple-element.18.after), channel_id=1, source_target_pairs={{0,1},{1,0},{2,3},{3,2},{4,5},{5,4},{6,7},{7,6},{8,9},{9,8},{10,11... | collective-permute-start | bytes 589832 | tf_op jit(solution)/shard_map/ppermute | solution.py:429
  30.8 5.2 %collective-permute-start.6 = (bf16[1,64,768]{2,1,0:T(8,128)(2,1)S(1)}, bf16[1,64,768]{2,1,0:T(8,128)(2,1)S(1)}, u32[]{:S(2)}, u32[]{:S(2)}) collective-permute-start(bf16[1,64,768]{2,1,0:T(8,128)(2,1)S(1)} %add_convert_fusion.after), channel_id=1, source_target_pairs={{0,2},{1,3},{2,0},{3,1},{4,6},{5,7},{6,4},{7,5},{8,10},{9,11},{10,... | collective-permute-start | bytes 294920 | tf_op jit(solution)/shard_map/ppermute | solution.py:429
  36.1 4.2 %collective-permute-start.7 = (bf16[2,16,768]{2,1,0:T(8,128)(2,1)S(1)}, bf16[2,16,768]{2,1,0:T(8,128)(2,1)S(1)}, u32[]{:S(2)}, u32[]{:S(2)}) collective-permute-start(bf16[2,16,768]{2,1,0:T(8,128)(2,1)S(1)} %slice.25), channel_id=1, source_target_pairs={{0,4},{4,0},{8,12},{12,8},{1,5},{5,1},{9,13},{13,9},{2,6},{6,2},{1... | collective-permute-start | bytes 147464 | tf_op jit(solution)/shard_map/ppermute | solution.py:429
  40.2 5.1 %collective-permute-start.8 = (bf16[1,16,768]{2,1,0:T(8,128)(2,1)S(1)}, bf16[1,16,768]{2,1,0:T(8,128)(2,1)S(1)}, u32[]{:S(2)}, u32[]{:S(2)}) collective-permute-start(bf16[1,16,768]{2,1,0:T(8,128)(2,1)S(1)} %slice.43), channel_id=1, source_target_pairs={{0,8},{4,12},{8,0},{12,4},{1,9},{5,13},{9,1},{13,5},{2,10},{6,14},... | collective-permute-start | bytes 73736 | tf_op jit(solution)/shard_map/ppermute | solution.py:429

commit v4 on v3

v4 whole, which is shorter than its diff:
```python
import functools

import jax
import jax.numpy as jnp
from jax import lax
from jax.experimental import pallas as pl
from jax.experimental.pallas import tpu as pltpu
from jax.sharding import PartitionSpec as P

HEADS = 24
KVH = 8
HD = 128
EXPERT_COUNT = 4
ADAPTER_RANK = 16
TENANT_COUNT = 8
LANES = 128
ADAPTER_LANES = EXPERT_COUNT * ADAPTER_RANK
DIFF_HI, DIFF_LO, SQ_HI, SQ_LO, FIRST, SECOND, TENANT = range(ADAPTER_LANES, ADAPTER_LANES + 7)
F32 = jnp.float32
BF16 = jnp.bfloat16
ANY_LANES = (((1,), (1,)), ((), ()))


VMEM = pl.BlockSpec(memory_space=pltpu.VMEM)
HBM = pl.BlockSpec(memory_space=pl.ANY)


def in_hbm(*arrays):
    return [pltpu.with_memory_space_constraint(array, pltpu.HBM) for array in arrays]


def column(values, rows):
    index = lax.broadcasted_iota(jnp.int32, (rows, LANES), 0)
    out = jnp.zeros((rows, LANES), jnp.int32)
    for r in range(rows):
        out = jnp.where(index == r, values(r), out)
    return out


def fetch(weights, items, parts, arrived):
    copies = []
    for i, ((distance, which), part) in enumerate(zip(items, parts, strict=True)):
        features = part.shape[0]
        start = pl.multiple_of((lax.axis_index("tp") ^ distance) * features, features)
        copies.append(
            pltpu.make_async_copy(
                weights[which].at[pl.ds(start, features), :], part, arrived.at[i]
            )
        )
        copies[-1].start()
    return copies


def attend_kernel(*refs):
    count = 12
    sources, weights = refs[:count], refs[count : count + 2]
    outs, parts = refs[count + 2 : count + 4], refs[count + 4 : count + 6]
    buffers, arrived, weights_arrived = refs[count + 6 : -2], refs[-2], refs[-1]
    copies = [
        pltpu.make_async_copy(source, buffer, arrived.at[i])
        for i, (source, buffer) in enumerate(zip(sources, buffers, strict=True))
    ]
    for i in (7, 4, 0, 5, 8, 6, 3, 9, 1, 2, 10, 11):
        copies[i].start()
    fetched = fetch(weights, ((0, 0), (0, 1)), parts, weights_arrived)
    attend_body(*buffers, *outs, wait=lambda *which: [copies[i].wait() for i in which])
    for copy in fetched:
        copy.wait()


def attend_body(
    lengths,
    tenants,
    routes,
    residual,
    queries,
    token_keys,
    token_values,
    stored_keys,
    stored_values,
    gain,
    router,
    adapter_down,
    state_out,
    payload_out,
    *,
    wait,
):
    rows, features = residual.shape
    kv_local = token_keys.shape[1] // HD
    cache = stored_keys.shape[1]
    group = HEADS // KVH
    scale = HD ** (-0.5)
    wait(0, 4, 7)
    heads = kv_local * group
    together = 2 if rows % 2 == 0 else 1
    length_column = column(lambda r: lengths[r], rows)
    stacked_length = jnp.concatenate([length_column[:, :1]] * heads, axis=0)
    stacked_row = lax.rem(
        lax.broadcasted_iota(jnp.int32, (heads * rows, cache), 0), jnp.int32(rows)
    )
    visible = lax.broadcasted_iota(jnp.int32, (heads * rows, cache), 1) < stacked_length

    def stacked(get):
        return jnp.concatenate([get(g, j) for g in range(kv_local) for j in range(group)], axis=0)

    def head_lanes(g, j=None):
        h = g if j is None else g * group + j
        return slice(h * HD, (h + 1) * HD)

    query = stacked(lambda g, j: queries[:, head_lanes(g, j)])
    wide = jnp.concatenate([query] * kv_local, axis=1)
    lane_head = lax.broadcasted_iota(jnp.int32, wide.shape, 1) // HD
    row_head = lax.broadcasted_iota(jnp.int32, wide.shape, 0) // (group * rows)
    wide = jnp.where(lane_head == row_head, wide.astype(F32), 0.0).astype(BF16)
    scores = jnp.zeros((heads * rows, cache), F32)
    for r in range(0, rows, together):
        keys = stored_keys[r : r + together].reshape(together * cache, kv_local * HD)
        every = lax.dot_general(wide, keys, ANY_LANES, preferred_element_type=F32)
        for i in range(together):
            scores = jnp.where(
                stacked_row == r + i, every[:, i * cache : (i + 1) * cache], scores
            )
    scores = jnp.where(visible, scores * scale, -jnp.inf)
    wait(5)
    fresh_key = stacked(lambda g, j: token_keys[:, head_lanes(g)].astype(F32))
    fresh = jnp.sum(query.astype(F32) * fresh_key, axis=1, keepdims=True) * scale
    largest = jnp.maximum(jnp.max(scores, axis=1, keepdims=True), fresh)
    cache_exp = jnp.exp(scores - largest)
    fresh_exp = jnp.exp(fresh - largest)
    denominator = jnp.sum(cache_exp, axis=1, keepdims=True) + fresh_exp
    probs = cache_exp / denominator
    fresh_prob = (fresh_exp / denominator).astype(BF16).astype(F32)
    wait(8)
    every = jnp.zeros((heads * rows, kv_local * HD), F32)
    for r in range(0, rows, together):
        values = stored_values[r : r + together].reshape(together * cache, kv_local * HD)
        own = [jnp.where(stacked_row == r + i, probs, 0.0).astype(BF16) for i in range(together)]
        every = every + jnp.dot(
            jnp.concatenate(own, axis=1), values, preferred_element_type=F32
        )
    wait(3, 6, 9)
    squares = jnp.zeros((rows, 1), F32)
    for g in range(kv_local):
        fresh_value = token_values[:, head_lanes(g)].astype(F32)
        for j in range(group):
            lanes = head_lanes(g, j)
            place = slice((g * group + j) * rows, (g * group + j + 1) * rows)
            attended = every[place, head_lanes(g)] + fresh_prob[place] * fresh_value
            state = (residual[:, lanes].astype(F32) + attended).astype(BF16)
            state_out[:, lanes] = state
            state = state.astype(F32)
            squares = squares + jnp.sum(state * state, axis=1, keepdims=True)
            payload_out[:, lanes] = (
                state * gain[lanes.start // LANES : lanes.start // LANES + 1, :]
            ).astype(BF16)
    wait(1, 2, 10, 11)
    scaled = payload_out[:, :features]
    logits = lax.dot_general(scaled, router[...], ANY_LANES, preferred_element_type=F32)
    first = column(lambda r: routes[0, r], rows)
    second = column(lambda r: routes[1, r], rows)
    tenant = column(lambda r: tenants[r], rows)
    expert = lax.broadcasted_iota(jnp.int32, logits.shape, 1)
    chosen = jnp.where(expert == first[:, :EXPERT_COUNT], logits, 0.0) - jnp.where(
        expert == second[:, :EXPERT_COUNT], logits, 0.0
    )
    diff = jnp.sum(chosen, axis=1, keepdims=True)
    adapter = jnp.dot(scaled, adapter_down[...], preferred_element_type=F32)
    lane = lax.broadcasted_iota(jnp.int32, (rows, LANES), 1)
    tail = jnp.zeros((rows, LANES), F32)
    for start in range(0, adapter.shape[1], LANES):
        owner = (lane + start) // ADAPTER_LANES
        tail = tail + jnp.where(owner == tenant, adapter[:, start : start + LANES], 0.0)
    tail = tail + pltpu.roll(tail, ADAPTER_LANES, 1)
    diff_hi = diff.astype(BF16).astype(F32)
    squares_hi = squares.astype(BF16).astype(F32)
    for place, value in (
        (DIFF_HI, diff_hi),
        (DIFF_LO, diff - diff_hi),
        (SQ_HI, squares_hi),
        (SQ_LO, squares - squares_hi),
        (FIRST, first.astype(F32)),
        (SECOND, second.astype(F32)),
        (TENANT, tenant.astype(F32)),
    ):
        tail = jnp.where(lane == place, value, tail)
    payload_out[:, features:] = tail.astype(BF16)


def attend(args, gate_weight, up_weight):
    rows, features = args[3].shape
    return pl.pallas_call(
        attend_kernel,
        out_shape=(
            jax.ShapeDtypeStruct((rows, features), BF16),
            jax.ShapeDtypeStruct((rows, features + LANES), BF16),
            *[jax.ShapeDtypeStruct((features, gate_weight.shape[1]), BF16)] * 2,
        ),
        in_specs=[HBM] * (len(args) + 2),
        out_specs=(VMEM,) * 4,
        scratch_shapes=[
            (pltpu.SMEM if i < 3 else pltpu.VMEM)(arg.shape, arg.dtype)
            for i, arg in enumerate(args)
        ]
        + [pltpu.SemaphoreType.DMA((len(args),)), pltpu.SemaphoreType.DMA((2,))],
        compiler_params=pltpu.CompilerParams(vmem_limit_bytes=12 * 2**20),
        cost_estimate=pl.CostEstimate(
            flops=200_000_000, bytes_accessed=10_000_000, transcendentals=20_000
        ),
        name="attend",
    )(*in_hbm(*args, gate_weight, up_weight))


def load_kernel(item, gate_weight, up_weight, after, part, arrived):
    for copy in fetch((gate_weight, up_weight), (item,), (part,), arrived):
        copy.wait()


def load(weights, item, features, after):
    hidden = weights[0].shape[1]
    return pl.pallas_call(
        functools.partial(load_kernel, item),
        out_shape=jax.ShapeDtypeStruct((features, hidden), BF16),
        in_specs=[HBM] * 3,
        out_specs=VMEM,
        scratch_shapes=[pltpu.SemaphoreType.DMA((1,))],
        compiler_params=pltpu.CompilerParams(vmem_limit_bytes=2**20),
        cost_estimate=pl.CostEstimate(
            flops=0, bytes_accessed=2 * features * hidden, transcendentals=0
        ),
        name="load",
    )(*in_hbm(*weights), after)


def partial_kernel(items, first, block, gate_part, up_part, *refs):
    features = gate_part.shape[0]
    sums, refs = (None, refs) if first else (refs[0], refs[1:])
    weights, totals = refs[:2], refs[2]
    fetched = fetch(weights, items, refs[3 : 3 + len(items)], refs[-1])

    def tile(n, carry):
        for i, part in enumerate((gate_part, up_part)):
            width = part.shape[1] // 2
            lanes = pl.ds(pl.multiple_of(n * width, LANES if width % LANES == 0 else width), width)
            product = jnp.dot(
                block[:, :features], part[:, lanes], preferred_element_type=F32
            )
            totals[i, :, lanes] = product if first else sums[i, :, lanes] + product
        return carry

    if gate_part.shape[1] % (2 * LANES) == 0:
        lax.fori_loop(0, 2, tile, 0)
    else:
        for i, part in enumerate((gate_part, up_part)):
            product = jnp.dot(block[:, :features], part[...], preferred_element_type=F32)
            totals[i] = product if first else sums[i] + product
    for copy in fetched:
        copy.wait()


def partial(block, parts, sums, weights, items):
    rows, width = block.shape
    features = width - LANES
    hidden = weights[0].shape[1]
    first = sums is None
    return pl.pallas_call(
        functools.partial(partial_kernel, items, first),
        out_shape=(
            jax.ShapeDtypeStruct((2, rows, hidden), F32),
            *[jax.ShapeDtypeStruct((features, hidden), BF16)] * len(items),
        ),
        in_specs=[VMEM] * (3 if first else 4) + [HBM] * 2,
        out_specs=(VMEM,) * (1 + len(items)),
        scratch_shapes=[pltpu.SemaphoreType.DMA((max(1, len(items)),))],
        compiler_params=pltpu.CompilerParams(vmem_limit_bytes=8 * 2**20),
        cost_estimate=pl.CostEstimate(
            flops=4 * rows * features * hidden,
            bytes_accessed=2 * len(items) * features * hidden,
            transcendentals=0,
        ),
        name="partial",
    )(block, *parts, *(() if first else (sums,)), *in_hbm(*weights))


def expert_kernel(replicas, targets, known, tensor_devices, items, sums, *refs):
    blocks, refs = refs[:tensor_devices], refs[tensor_devices:]
    present = 2 * (tensor_devices - known) - len(items)
    parts, refs = list(refs[:present]), refs[present:]
    weights, down_weight, adapter_weight, out, active, totals = refs[:2], *refs[2:7]
    late, refs = refs[7 : 7 + len(items)], refs[7 + len(items) :]
    down_part, adapter_up, late_arrived, arrived = refs
    rows, width = blocks[0].shape
    features = width - LANES
    hidden = active.shape[1]
    fetched = fetch(weights, items, late, late_arrived)
    adapter_copy = pltpu.make_async_copy(adapter_weight, adapter_up, arrived.at[len(targets)])
    adapter_copy.start()
    parts += late
    pairs = [
        (block, parts[2 * i], parts[2 * i + 1]) for i, block in enumerate(blocks[known:])
    ]
    early = present // 2
    tile = hidden // 2 if hidden % (2 * LANES) == 0 else hidden

    def products(n, which, some, total):
        lanes = pl.ds(pl.multiple_of(n * tile, tile), tile)
        total = total[which, :, lanes]
        for pair in some:
            total = total + jnp.dot(
                pair[0][:, :features], pair[1 + which][:, lanes], preferred_element_type=F32
            )
        return lanes, total

    def first_pass(n, carry):
        for which in range(2):
            lanes, total = products(n, which, pairs[:early], sums)
            totals[which, :, lanes] = total
        return carry

    lax.fori_loop(0, hidden // tile, first_pass, 0)
    expert = lax.axis_index("ep") // replicas
    tail = jnp.zeros((rows, LANES), F32)
    for block in blocks:
        tail = tail + block[:, features:].astype(F32)
    place = lambda k: tail[:, k : k + 1]
    here = blocks[0][:, features:].astype(F32)
    inverse_rms = lax.rsqrt(
        (place(SQ_HI) + place(SQ_LO)) / (features * tensor_devices) + 1e-05
    )
    diff = (place(DIFF_HI) + place(DIFF_LO)) * inverse_rms
    expert_float = expert.astype(F32)
    is_first = here[:, FIRST : FIRST + 1] == expert_float
    is_second = here[:, SECOND : SECOND + 1] == expert_float
    weight = jnp.where(
        is_first, jax.nn.sigmoid(diff), jnp.where(is_second, jax.nn.sigmoid(-diff), 0.0)
    )
    lowrank = (tail * inverse_rms).astype(BF16)
    spread_shape = (LANES, TENANT_COUNT * ADAPTER_RANK)
    source = lax.broadcasted_iota(jnp.int32, spread_shape, 0)
    target = lax.broadcasted_iota(jnp.int32, spread_shape, 1)
    spread = jnp.where(
        source == expert * ADAPTER_RANK + lax.rem(target, jnp.int32(ADAPTER_RANK)), 1.0, 0.0
    ).astype(BF16)
    lane = lax.broadcasted_iota(jnp.int32, (rows, TENANT_COUNT * ADAPTER_RANK), 1)
    own_tenant = (lane // ADAPTER_RANK).astype(F32) == here[:, TENANT : TENANT + 1]
    adapter_rows = jnp.where(
        own_tenant, jnp.dot(lowrank, spread, preferred_element_type=F32), 0.0
    ).astype(BF16)
    adapter_copy.wait()
    copies = down_copies(down_weight, targets, down_part, arrived)
    for i, copy in enumerate(fetched):
        copy.wait()
        if i < len(copies):
            copies[i].start()
    for copy in copies[len(fetched) :]:
        copy.start()

    def second_pass(n, carry):
        lanes, gate = products(n, 0, pairs[early:], totals)
        _, up = products(n, 1, pairs[early:], totals)
        gate = gate * inverse_rms
        up = up * inverse_rms + jnp.dot(
            adapter_rows, adapter_up[:, lanes], preferred_element_type=F32
        )
        active[:, lanes] = (gate * jax.nn.sigmoid(gate) * up * weight).astype(BF16)
        return carry

    lax.fori_loop(0, hidden // tile, second_pass, 0)
    down_products(active, copies, down_part, out)


def experts(replicas, targets, sums, known, blocks, parts, weights, items, down_weight, adapter_up):
    rows, width = blocks[0].shape
    features, hidden = width - LANES, sums.shape[2]
    missing = len(blocks) - known
    return pl.pallas_call(
        functools.partial(expert_kernel, replicas, targets, known, len(blocks), items),
        out_shape=(
            jax.ShapeDtypeStruct((len(targets), rows, features), BF16),
            jax.ShapeDtypeStruct((rows, hidden), BF16),
        ),
        in_specs=[VMEM] * (1 + len(blocks) + len(parts)) + [HBM] * 4,
        out_specs=(VMEM, VMEM),
        scratch_shapes=[
            pltpu.VMEM(sums.shape, F32),
            *[pltpu.VMEM((features, hidden), BF16)] * len(items),
            pltpu.VMEM((len(targets), hidden, features), BF16),
            pltpu.VMEM(adapter_up.shape, BF16),
            pltpu.SemaphoreType.DMA((max(1, len(items)),)),
            pltpu.SemaphoreType.DMA((len(targets) + 1,)),
        ],
        compiler_params=pltpu.CompilerParams(vmem_limit_bytes=20 * 2**20),
        cost_estimate=pl.CostEstimate(
            flops=2 * rows * hidden * features * (2 * missing + len(targets)),
            bytes_accessed=2 * (len(items) + len(targets)) * hidden * features,
            transcendentals=0,
        ),
        name="experts",
    )(sums, *blocks, *parts, *in_hbm(*weights, down_weight, adapter_up))


def down_copies(down_weight, targets, down_part, arrived):
    features = down_part.shape[2]
    return [
        pltpu.make_async_copy(
            down_weight.at[
                :, pl.ds(pl.multiple_of((lax.axis_index("tp") ^ k) * features, features), features)
            ],
            down_part.at[i],
            arrived.at[i],
        )
        for i, k in enumerate(targets)
    ]


def down_products(active, copies, down_part, out):
    for i, copy in enumerate(copies):
        copy.wait()
        out[i] = jnp.dot(active[...], down_part[i], preferred_element_type=F32).astype(out.dtype)


def down_kernel(targets, active, down_weight, after, out, down_part, arrived):
    copies = down_copies(down_weight, targets, down_part, arrived)
    for copy in copies:
        copy.start()
    down_products(active, copies, down_part, out)


def down(targets, active, down_weight, features, after):
    rows, hidden = active.shape
    return pl.pallas_call(
        functools.partial(down_kernel, targets),
        out_shape=jax.ShapeDtypeStruct((len(targets), rows, features), F32),
        in_specs=[VMEM, HBM, HBM],
        out_specs=VMEM,
        scratch_shapes=[
            pltpu.VMEM((len(targets), hidden, features), BF16),
            pltpu.SemaphoreType.DMA((len(targets),)),
        ],
        compiler_params=pltpu.CompilerParams(vmem_limit_bytes=16 * 2**20),
        cost_estimate=pl.CostEstimate(
            flops=2 * rows * hidden * features * len(targets),
            bytes_accessed=2 * len(targets) * hidden * features,
            transcendentals=0,
        ),
        name="down",
    )(active, *in_hbm(down_weight), after)


def join_kernel(first, second, after, out):
    count = first.shape[0]
    out[:count] = first[...]
    out[count:] = second[...]


def join(first, second, after):
    return pl.pallas_call(
        join_kernel,
        out_shape=jax.ShapeDtypeStruct((2 * first.shape[0], *first.shape[1:]), first.dtype),
        in_specs=[VMEM, VMEM, HBM],
        out_specs=VMEM,
        compiler_params=pltpu.CompilerParams(vmem_limit_bytes=4 * 2**20),
        name="join",
    )(first, second, after)


def tie_kernel(array, after, out):
    pass


def tie(array, after):
    return pl.pallas_call(
        tie_kernel,
        out_shape=jax.ShapeDtypeStruct(array.shape, array.dtype),
        in_specs=[HBM, HBM],
        out_specs=HBM,
        input_output_aliases={0: 0},
        compiler_params=pltpu.CompilerParams(vmem_limit_bytes=2**20),
        name="tie",
    )(array, after)


def swap(x, axis, distance):
    count = lax.axis_size(axis)
    return lax.ppermute(x, axis, [(i, i ^ distance) for i in range(count)])


def bits(count):
    return [1 << b for b in range(count.bit_length() - 1)]


def per_device(
    residual,
    queries,
    token_keys,
    token_values,
    stored_keys,
    stored_values,
    lengths,
    norm_gain_vector,
    router,
    expert_gate_weight,
    expert_up_weight,
    expert_down_weight,
    adapter_down_map,
    adapter_up_map,
    routes,
    tenants,
):
    rows, features = residual.shape
    expert_devices = lax.axis_size("ep")
    tensor_devices = lax.axis_size("tp")
    weights = (expert_gate_weight, expert_up_weight)
    state, held, *parts = attend(
        (
            lengths,
            tenants,
            routes.T,
            residual,
            queries,
            token_keys,
            token_values,
            stored_keys,
            stored_values,
            norm_gain_vector.reshape(features // LANES, LANES),
            router.T,
            adapter_down_map,
        ),
        *weights,
    )
    order = [0]
    for distance in reversed(bits(tensor_devices)):
        order += [at ^ distance for at in order]
    items = [(at, which) for at in order[1:] for which in range(2)]
    for distance in bits(expert_devices):
        other = swap(held, "ep", distance)
        if items:
            parts.append(load(weights, items.pop(0), features, held))
        held = join(held, other, parts[-1])
    blocks, known, sums = [held], 0, None
    for distance in reversed(bits(tensor_devices)):
        others = [swap(block, "tp", distance) for block in blocks]
        for block in blocks[known:]:
            some = tuple(items[:2]) if distance > 1 else ()
            items = items[len(some) :]
            sums, *more = partial(
                block, parts[2 * known : 2 * known + 2], sums, weights, some
            )
            parts += more
            known += 1
        blocks = blocks + [tie(block, sums) if distance > 1 else block for block in others]
    half = tensor_devices // 2
    sent, active = experts(
        expert_devices // EXPERT_COUNT,
        tuple(range(half, tensor_devices)),
        sums,
        known,
        blocks,
        parts[2 * known :],
        weights,
        tuple(items),
        expert_down_weight,
        adapter_up_map,
    )
    kept = None
    while half:
        other = swap(sent, "tp", half)
        if kept is None:
            kept = down(tuple(range(half)), active, expert_down_weight, features, sent)
        kept = kept + other.astype(F32)
        half //= 2
        if half:
            kept, sent = kept[:half], kept[half:].astype(BF16)
    kept = kept[0].reshape(expert_devices, rows, features)
    for distance in bits(expert_devices):
        kept, sent = kept[0::2], kept[1::2].astype(BF16)
        kept = kept + swap(sent, "ep", distance).astype(F32)
    return (state.astype(F32) + kept[0]).astype(BF16)


def solution(mesh):
    placed = (
        P(("groups", "ep"), "tp"),
        P(("groups", "ep"), "tp"),
        P(("groups", "ep"), "tp"),
        P(("groups", "ep"), "tp"),
        P(("groups", "ep"), None, "tp"),
        P(("groups", "ep"), None, "tp"),
        P(("groups", "ep")),
        P("tp"),
        P("tp", None),
        P(None, ("ep", "tp")),
        P(None, ("ep", "tp")),
        P(("ep", "tp"), None),
        P("tp", None),
        P(None, ("ep", "tp")),
        P(("groups", "ep"), None),
        P(("groups", "ep")),
    )
    return jax.shard_map(
        per_device, mesh=mesh, in_specs=placed, out_specs=P(("groups", "ep"), "tp"), check_vma=False
    )
```

time: 46.1 us -> 45.1 us (0.978)
  Pallas kernels: 24.9 us -> 21.6 us
  starting transfers between devices: 11.7 us -> 14.7 us
  waiting for transfers between devices: 8.45 us -> 7.73 us
    ppermute x9, starting transfers between devices: 11.7 us -> 14.7 us  [swap(): return lax.ppermute(x, axis, [(i, i ^ distance) for i in range(count)])]
    pallas_call x4, Pallas kernels: 10.8 us -> 7.99 us  [the longest x2 4.2 us: partial(): pl.pallas_call(functools.partial(partial_kernel, items, first), out_shape...]
    pallas_call x2 -> x1, Pallas kernels: 5.11 us -> 3.64 us  [down(): pl.pallas_call(functools.partial(down_kernel, targets), out_shape=jax.Sha...]
    pallas_call x1, Pallas kernels: 5.05 us -> 6.06 us  [experts(): pl.pallas_call(functools.partial(expert_kernel, replicas, targets, known,...]
    ppermute x9, waiting for transfers between devices: 8.45 us -> 7.73 us  [swap(): return lax.ppermute(x, axis, [(i, i ^ distance) for i in range(count)])]
  transfers between devices with their start and end apart: 9 -> 9, of which waited for: 4 -> 6; matrix products, arithmetic and copies ran while one was open for 0% -> 0% of each run, Pallas kernels for 35% -> 26%
where the time goes in v4:
time: 45.1 us; the launch traced here: 44.9 us
  Pallas kernels  21.6 us (48%)
  starting transfers between devices  14.7 us (33%)
  waiting for transfers between devices  7.73 us (17%)
  other arithmetic  0.7 us (2%)
    ppermute x9, starting transfers between devices, swap(): return lax.ppermute(x, axis, [(i, i ^ distance) for i in range(count)])  14.7 us
    ppermute x9, waiting for transfers between devices, swap(): return lax.ppermute(x, axis, [(i, i ^ distance) for i in range(count)])  7.73 us
    pallas_call x1, Pallas kernels, experts(): pl.pallas_call(functools.partial(expert_kernel, replicas, targets, known,...  6.06 us
    pallas_call x2, Pallas kernels, partial(): pl.pallas_call(functools.partial(partial_kernel, items, first), out_shape...  4.2 us
    pallas_call x1, Pallas kernels, attend(): pl.pallas_call(attend_kernel, out_shape=(jax.ShapeDtypeStruct((rows, feat...  3.91 us
    pallas_call x2, Pallas kernels, load(): pl.pallas_call(functools.partial(load_kernel, item), out_shape=jax.ShapeD...  3.79 us
    pallas_call x1, Pallas kernels, down(): pl.pallas_call(functools.partial(down_kernel, targets), out_shape=jax.Sha...  3.64 us
  transfers between devices with their start and end apart: 9, of which 6 were waited for; matrix products, arithmetic and copies ran while one was open for 0% of the time, Pallas kernels for 26%

profile of v4, /device:TPU:0, one launch (start us, length us, event | category | flops | bytes accessed | tf_op | source)
XLA Modules:
  0.0 44.9 jit_solution(10005947981882586407)
XLA Ops:
  0.0 3.9 %attend.1 = (bf16[16,768]{1,0:T(8,128)(2,1)S(1)}, bf16[16,896]{1,0:T(8,128)(2,1)S(1)}, bf16[768,2048]{1,0:T(8,128)(2,1)S(1)}, bf16[768,2048]{1,0:T(8,128)(2,1)S(1)}) custom-call(s32[16]{0:T(128)} %refs_0_.2, s32[16]{0:T(128)} %refs_1_.3, s32[2,16]{1,0:T(2,128)} %bitcast.14, bf16[16,768]{1,0:T(8,128)(2,1)} %refs_3_.1, bf16[16,768]{1,0:T(8,128)(2,1)} %refs_4_.1, ...), custom_call_target="tpu_custom_call" | custom-call | flops 200000000 | bytes 10000000 | tf_op jit(solution)/shard_map/attend/pallas_call | solution.py:192
  3.9 3.1 %collective-permute-start = (bf16[16,896]{1,0:T(8,128)(2,1)S(1)}, bf16[16,896]{1,0:T(8,128)(2,1)S(1)}, u32[]{:S(2)}, u32[]{:S(2)}) collective-permute-start(bf16[16,896]{1,0:T(8,128)(2,1)S(1)} %get-tuple-element.15.after.first), channel_id=1, source_target_pairs={{0,4},{4,0},{8,12},{12,8},{1,5},{5,1},{9,13},{13,9},{2,6},{6,2},{1... | collective-permute-start | bytes 86024 | tf_op jit(solution)/shard_map/ppermute | solution.py:485
  7.0 1.9 %load.2.after.gate_part = bf16[768,2048]{1,0:T(8,128)(2,1)S(1)} custom-call(bf16[3072,2048]{1,0:T(8,128)(2,1)} %refs_6_.3, bf16[3072,2048]{1,0:T(8,128)(2,1)} %refs_7_.3, bf16[16,896]{1,0:T(8,128)(2,1)S(1)} %get-tuple-element.15.after.first), custom_call_target="tpu_custom_call" | custom-call | bytes 3145728 | tf_op jit(solution)/shard_map/load/pallas_call | solution.py:221
  8.9 0.0 collective-permute-done.second
  8.9 3.0 %collective-permute-start.1 = (bf16[32,896]{1,0:T(8,128)(2,1)S(1)}, bf16[32,896]{1,0:T(8,128)(2,1)S(1)}, u32[]{:S(2)}, u32[]{:S(2)}) collective-permute-start(bf16[32,896]{1,0:T(8,128)(2,1)S(1)} %join.2.after.first), channel_id=1, source_target_pairs={{0,8},{4,12},{8,0},{12,4},{1,9},{5,13},{9,1},{13,5},{2,10},{6,14},... | collective-permute-start | bytes 172040 | tf_op jit(solution)/shard_map/ppermute | solution.py:485
  11.9 1.9 %load.3.after.up_part = bf16[768,2048]{1,0:T(8,128)(2,1)S(1)} custom-call(bf16[3072,2048]{1,0:T(8,128)(2,1)} %refs_6_.3, bf16[3072,2048]{1,0:T(8,128)(2,1)} %refs_7_.3, bf16[32,896]{1,0:T(8,128)(2,1)S(1)} %join.2.after.first), custom_call_target="tpu_custom_call" | custom-call | bytes 3145728 | tf_op jit(solution)/shard_map/load/pallas_call | solution.py:221
  13.8 0.3 collective-permute-done.1.second
  14.1 1.9 %collective-permute-start.2 = (bf16[64,896]{1,0:T(8,128)(2,1)S(1)}, bf16[64,896]{1,0:T(8,128)(2,1)S(1)}, u32[]{:S(2)}, u32[]{:S(2)}) collective-permute-start(bf16[64,896]{1,0:T(8,128)(2,1)S(1)} %join.3.block.refs_0_), channel_id=1, source_target_pairs={{0,2},{1,3},{2,0},{3,1},{4,6},{5,7},{6,4},{7,5},{8,10},{9,11},{10,... | collective-permute-start | bytes 344072 | tf_op jit(solution)/shard_map/ppermute | solution.py:485
  16.0 0.0 collective-permute-start.3
  16.0 2.9 %partial.2 = (f32[2,64,2048]{2,1,0:T(8,128)S(1)}, bf16[768,2048]{1,0:T(8,128)(2,1)S(1)}, bf16[768,2048]{1,0:T(8,128)(2,1)S(1)}) custom-call(bf16[64,896]{1,0:T(8,128)(2,1)S(1)} %join.3.block.refs_0_, bf16[768,2048]{1,0:T(8,128)(2,1)S(1)} %get-tuple-element.16.gate_part, bf16[768,2048]{1,0:T(8,128)(2,1)S(1)} %get-tuple-element.17.up_part, ...), custom_call_target="tpu_custom_call" | custom-call | flops 402653184 | bytes 6291456 | tf_op jit(solution)/shard_map/partial/pallas_call | solution.py:266
  18.8 0.1 collective-permute-done.2.array
  19.0 0.5 %collective-permute-start.4 = (bf16[64,896]{1,0:T(8,128)(2,1)S(1)}, bf16[64,896]{1,0:T(8,128)(2,1)S(1)}, u32[]{:S(2)}, u32[]{:S(2)}) collective-permute-start(bf16[64,896]{1,0:T(8,128)(2,1)S(1)} %tie.1.block.refs_1_), channel_id=1, source_target_pairs={{0,1},{1,0},{2,3},{3,2},{4,5},{5,4},{6,7},{7,6},{8,9},{9,8},{10,11... | collective-permute-start | bytes 344072 | tf_op jit(solution)/shard_map/ppermute | solution.py:485
  19.4 1.3 %partial.3.sums = f32[2,64,2048]{2,1,0:T(8,128)S(1)} custom-call(bf16[64,896]{1,0:T(8,128)(2,1)S(1)} %tie.1.block.refs_1_, bf16[768,2048]{1,0:T(8,128)(2,1)S(1)} %load.2.after.gate_part, bf16[768,2048]{1,0:T(8,128)(2,1)S(1)} %load.3.after.up_part, f32[2,64,2048]{2,1,0:T(8,128)S(1)} %get-tuple-element.18.after.refs_0_, bf16[3072,2048]{1,0:T(8,128)(2,1)} %refs_6_.3, ...), custom_call_target="tpu_custom_call" | custom-call | flops 402653184 | tf_op jit(solution)/shard_map/partial/pallas_call | solution.py:266
  20.8 0.0 collective-permute-done.3.refs_2_
  20.8 0.0 collective-permute-done.4.refs_3_
  20.8 6.1 %experts.1 = (bf16[2,64,768]{2,1,0:T(8,128)(2,1)S(1)}, bf16[64,2048]{1,0:T(8,128)(2,1)S(1)}) custom-call(f32[2,64,2048]{2,1,0:T(8,128)S(1)} %partial.3.sums, bf16[64,896]{1,0:T(8,128)(2,1)S(1)} %join.3.block.refs_0_, bf16[64,896]{1,0:T(8,128)(2,1)S(1)} %tie.1.block.refs_1_, bf16[64,896]{1,0:T(8,128)(2,1)S(1)} %collective-permute-done.3.refs_2_, ...), custom_call_target="tpu_custom_call" | custom-call | flops 1207959552 | bytes 12582912 | tf_op jit(solution)/shard_map/experts/pallas_call | solution.py:376
  26.9 1.4 %collective-permute-start.5 = (bf16[2,64,768]{2,1,0:T(8,128)(2,1)S(1)}, bf16[2,64,768]{2,1,0:T(8,128)(2,1)S(1)}, u32[]{:S(2)}, u32[]{:S(2)}) collective-permute-start(bf16[2,64,768]{2,1,0:T(8,128)(2,1)S(1)} %get-tuple-element.22.after), channel_id=1, source_target_pairs={{0,2},{1,3},{2,0},{3,1},{4,6},{5,7},{6,4},{7,5},{8,10},{9,11},{10,... | collective-permute-start | bytes 589832 | tf_op jit(solution)/shard_map/ppermute | solution.py:485
  28.2 3.6 %down.1 = f32[2,64,768]{2,1,0:T(8,128)S(1)} custom-call(bf16[64,2048]{1,0:T(8,128)(2,1)S(1)} %get-tuple-element.21.active, bf16[2048,3072]{1,0:T(8,128)(2,1)} %down_weight.1, bf16[2,64,768]{2,1,0:T(8,128)(2,1)S(1)} %get-tuple-element.22.after), custom_call_target="tpu_custom_call" | custom-call | flops 402653184 | bytes 6291456 | tf_op jit(solution)/shard_map/down/pallas_call | solution.py:431
  31.9 1.9 %collective-permute-done.5 = bf16[2,64,768]{2,1,0:T(8,128)(2,1)S(1)} collective-permute-done((bf16[2,64,768]{2,1,0:T(8,128)(2,1)S(1)}, bf16[2,64,768]{2,1,0:T(8,128)(2,1)S(1)}, u32[]{:S(2)}, u32[]{:S(2)}) %collective-permute-start.5) | collective-permute-done | bytes 196640 | tf_op jit(solution)/shard_map/ppermute | solution.py:485
  33.9 0.1 collective-permute-start.6
  34.0 1.3 %collective-permute-done.6 = bf16[1,64,768]{2,1,0:T(8,128)(2,1)S(1)} collective-permute-done((bf16[1,64,768]{2,1,0:T(8,128)(2,1)S(1)}, bf16[1,64,768]{2,1,0:T(8,128)(2,1)S(1)}, u32[]{:S(2)}, u32[]{:S(2)}) %collective-permute-start.6) | collective-permute-done | bytes 98336 | tf_op jit(solution)/shard_map/ppermute | solution.py:485
  35.3 1.9 %collective-permute-start.7 = (bf16[2,16,768]{2,1,0:T(8,128)(2,1)S(1)}, bf16[2,16,768]{2,1,0:T(8,128)(2,1)S(1)}, u32[]{:S(2)}, u32[]{:S(2)}) collective-permute-start(bf16[2,16,768]{2,1,0:T(8,128)(2,1)S(1)} %slice.26), channel_id=1, source_target_pairs={{0,4},{4,0},{8,12},{12,8},{1,5},{5,1},{9,13},{13,9},{2,6},{6,2},{1... | collective-permute-start | bytes 147464 | tf_op jit(solution)/shard_map/ppermute | solution.py:485
  37.2 2.3 %collective-permute-done.7 = bf16[2,16,768]{2,1,0:T(8,128)(2,1)S(1)} collective-permute-done((bf16[2,16,768]{2,1,0:T(8,128)(2,1)S(1)}, bf16[2,16,768]{2,1,0:T(8,128)(2,1)S(1)}, u32[]{:S(2)}, u32[]{:S(2)}) %collective-permute-start.7) | collective-permute-done | bytes 49184 | tf_op jit(solution)/shard_map/ppermute | solution.py:485
  39.5 3.0 %collective-permute-start.8 = (bf16[1,16,768]{2,1,0:T(8,128)(2,1)S(1)}, bf16[1,16,768]{2,1,0:T(8,128)(2,1)S(1)}, u32[]{:S(2)}, u32[]{:S(2)}) collective-permute-start(bf16[1,16,768]{2,1,0:T(8,128)(2,1)S(1)} %slice.45), channel_id=1, source_target_pairs={{0,8},{4,12},{8,0},{12,4},{1,9},{5,13},{9,1},{13,5},{2,10},{6,14},... | collective-permute-start | bytes 73736 | tf_op jit(solution)/shard_map/ppermute | solution.py:485
  42.4 1.8 %collective-permute-done.8 = bf16[1,16,768]{2,1,0:T(8,128)(2,1)S(1)} collective-permute-done((bf16[1,16,768]{2,1,0:T(8,128)(2,1)S(1)}, bf16[1,16,768]{2,1,0:T(8,128)(2,1)S(1)}, u32[]{:S(2)}, u32[]{:S(2)}) %collective-permute-start.8) | collective-permute-done | bytes 24608 | tf_op jit(solution)/shard_map/ppermute | solution.py:485
  44.3 0.6 %fusion.2 = bf16[16,768]{1,0:T(8,128)(2,1)} fusion(f32[2,16,768]{2,1,0:T(8,128)S(1)} %convert_add_fusion.1, bf16[1,16,768]{2,1,0:T(8,128)(2,1)S(1)} %collective-permute-done.8, bf16[16,768]{1,0:T(8,128)(2,1)S(1)} %get-tuple-element.14), kind=kLoop, calls=%fused_computation.8 | loop fusion | flops 61440 | bytes 122880 | tf_op jit(solution)/shard_map/convert_element_type | solution.py:578
  (10 shorter events, 0.1 us)
Async XLA Ops:
  3.9 5.0 %collective-permute-start = (bf16[16,896]{1,0:T(8,128)(2,1)S(1)}, bf16[16,896]{1,0:T(8,128)(2,1)S(1)}, u32[]{:S(2)}, u32[]{:S(2)}) collective-permute-start(bf16[16,896]{1,0:T(8,128)(2,1)S(1)} %get-tuple-element.15.after.first), channel_id=1, source_target_pairs={{0,4},{4,0},{8,12},{12,8},{1,5},{5,1},{9,13},{13,9},{2,6},{6,2},{1... | collective-permute-start | bytes 86024 | tf_op jit(solution)/shard_map/ppermute | solution.py:485
  8.9 5.1 %collective-permute-start.1 = (bf16[32,896]{1,0:T(8,128)(2,1)S(1)}, bf16[32,896]{1,0:T(8,128)(2,1)S(1)}, u32[]{:S(2)}, u32[]{:S(2)}) collective-permute-start(bf16[32,896]{1,0:T(8,128)(2,1)S(1)} %join.2.after.first), channel_id=1, source_target_pairs={{0,8},{4,12},{8,0},{12,4},{1,9},{5,13},{9,1},{13,5},{2,10},{6,14},... | collective-permute-start | bytes 172040 | tf_op jit(solution)/shard_map/ppermute | solution.py:485
  14.1 4.9 %collective-permute-start.2 = (bf16[64,896]{1,0:T(8,128)(2,1)S(1)}, bf16[64,896]{1,0:T(8,128)(2,1)S(1)}, u32[]{:S(2)}, u32[]{:S(2)}) collective-permute-start(bf16[64,896]{1,0:T(8,128)(2,1)S(1)} %join.3.block.refs_0_), channel_id=1, source_target_pairs={{0,2},{1,3},{2,0},{3,1},{4,6},{5,7},{6,4},{7,5},{8,10},{9,11},{10,... | collective-permute-start | bytes 344072 | tf_op jit(solution)/shard_map/ppermute | solution.py:485
  16.0 4.8 %collective-permute-start.3 = (bf16[64,896]{1,0:T(8,128)(2,1)S(1)}, bf16[64,896]{1,0:T(8,128)(2,1)S(1)}, u32[]{:S(2)}, u32[]{:S(2)}) collective-permute-start(bf16[64,896]{1,0:T(8,128)(2,1)S(1)} %join.3.block.refs_0_), channel_id=1, source_target_pairs={{0,1},{1,0},{2,3},{3,2},{4,5},{5,4},{6,7},{7,6},{8,9},{9,8},{10,11... | collective-permute-start | bytes 344072 | tf_op jit(solution)/shard_map/ppermute | solution.py:485
  19.0 1.8 %collective-permute-start.4 = (bf16[64,896]{1,0:T(8,128)(2,1)S(1)}, bf16[64,896]{1,0:T(8,128)(2,1)S(1)}, u32[]{:S(2)}, u32[]{:S(2)}) collective-permute-start(bf16[64,896]{1,0:T(8,128)(2,1)S(1)} %tie.1.block.refs_1_), channel_id=1, source_target_pairs={{0,1},{1,0},{2,3},{3,2},{4,5},{5,4},{6,7},{7,6},{8,9},{9,8},{10,11... | collective-permute-start | bytes 344072 | tf_op jit(solution)/shard_map/ppermute | solution.py:485
  26.9 7.0 %collective-permute-start.5 = (bf16[2,64,768]{2,1,0:T(8,128)(2,1)S(1)}, bf16[2,64,768]{2,1,0:T(8,128)(2,1)S(1)}, u32[]{:S(2)}, u32[]{:S(2)}) collective-permute-start(bf16[2,64,768]{2,1,0:T(8,128)(2,1)S(1)} %get-tuple-element.22.after), channel_id=1, source_target_pairs={{0,2},{1,3},{2,0},{3,1},{4,6},{5,7},{6,4},{7,5},{8,10},{9,11},{10,... | collective-permute-start | bytes 589832 | tf_op jit(solution)/shard_map/ppermute | solution.py:485
  33.9 1.4 %collective-permute-start.6 = (bf16[1,64,768]{2,1,0:T(8,128)(2,1)S(1)}, bf16[1,64,768]{2,1,0:T(8,128)(2,1)S(1)}, u32[]{:S(2)}, u32[]{:S(2)}) collective-permute-start(bf16[1,64,768]{2,1,0:T(8,128)(2,1)S(1)} %slice.44), channel_id=1, source_target_pairs={{0,1},{1,0},{2,3},{3,2},{4,5},{5,4},{6,7},{7,6},{8,9},{9,8},{10,11... | collective-permute-start | bytes 294920 | tf_op jit(solution)/shard_map/ppermute | solution.py:485
  35.3 4.2 %collective-permute-start.7 = (bf16[2,16,768]{2,1,0:T(8,128)(2,1)S(1)}, bf16[2,16,768]{2,1,0:T(8,128)(2,1)S(1)}, u32[]{:S(2)}, u32[]{:S(2)}) collective-permute-start(bf16[2,16,768]{2,1,0:T(8,128)(2,1)S(1)} %slice.26), channel_id=1, source_target_pairs={{0,4},{4,0},{8,12},{12,8},{1,5},{5,1},{9,13},{13,9},{2,6},{6,2},{1... | collective-permute-start | bytes 147464 | tf_op jit(solution)/shard_map/ppermute | solution.py:485
  39.5 4.8 %collective-permute-start.8 = (bf16[1,16,768]{2,1,0:T(8,128)(2,1)S(1)}, bf16[1,16,768]{2,1,0:T(8,128)(2,1)S(1)}, u32[]{:S(2)}, u32[]{:S(2)}) collective-permute-start(bf16[1,16,768]{2,1,0:T(8,128)(2,1)S(1)} %slice.45), channel_id=1, source_target_pairs={{0,8},{4,12},{8,0},{12,4},{1,9},{5,13},{9,1},{13,5},{2,10},{6,14},... | collective-permute-start | bytes 73736 | tf_op jit(solution)/shard_map/ppermute | solution.py:485

commit v5 on v4

v5 whole, which is shorter than its diff:
```python
import functools

import jax
import jax.numpy as jnp
from jax import lax
from jax.experimental import pallas as pl
from jax.experimental.pallas import tpu as pltpu
from jax.sharding import PartitionSpec as P

HEADS = 24
KVH = 8
HD = 128
EXPERT_COUNT = 4
ADAPTER_RANK = 16
TENANT_COUNT = 8
LANES = 128
ADAPTER_LANES = EXPERT_COUNT * ADAPTER_RANK
DIFF_HI, DIFF_LO, SQ_HI, SQ_LO, FIRST, SECOND, TENANT = range(ADAPTER_LANES, ADAPTER_LANES + 7)
F32 = jnp.float32
BF16 = jnp.bfloat16
ANY_LANES = (((1,), (1,)), ((), ()))


VMEM = pl.BlockSpec(memory_space=pltpu.VMEM)
HBM = pl.BlockSpec(memory_space=pl.ANY)


def in_hbm(*arrays):
    return [pltpu.with_memory_space_constraint(array, pltpu.HBM) for array in arrays]


def column(values, rows):
    index = lax.broadcasted_iota(jnp.int32, (rows, LANES), 0)
    out = jnp.zeros((rows, LANES), jnp.int32)
    for r in range(rows):
        out = jnp.where(index == r, values(r), out)
    return out


def at_distance(distance, size):
    return pl.ds(pl.multiple_of((lax.axis_index("tp") ^ distance) * size, size), size)


def fetch(gate_weight, distance, part, arrived):
    copy = pltpu.make_async_copy(
        gate_weight.at[at_distance(distance, part.shape[0]), :], part, arrived
    )
    copy.start()
    return copy


def attend_kernel(*refs):
    count = 12
    sources, gate_weight, outs, part = refs[:count], refs[count], refs[count + 1 : count + 3], refs[count + 3]
    buffers, arrived, part_arrived = refs[count + 4 : -2], refs[-2], refs[-1]
    copies = [
        pltpu.make_async_copy(source, buffer, arrived.at[i])
        for i, (source, buffer) in enumerate(zip(sources, buffers, strict=True))
    ]
    for i in (7, 4, 0, 5, 8, 6, 3, 9, 1, 2, 10, 11):
        copies[i].start()
    fetched = fetch(gate_weight, 0, part, part_arrived)
    attend_body(*buffers, *outs, wait=lambda *which: [copies[i].wait() for i in which])
    fetched.wait()


def attend_body(
    lengths,
    tenants,
    routes,
    residual,
    queries,
    token_keys,
    token_values,
    stored_keys,
    stored_values,
    gain,
    router,
    adapter_down,
    state_out,
    payload_out,
    *,
    wait,
):
    rows, features = residual.shape
    kv_local = token_keys.shape[1] // HD
    cache = stored_keys.shape[1]
    group = HEADS // KVH
    scale = HD ** (-0.5)
    wait(0, 4, 7)
    heads = kv_local * group
    together = 2 if rows % 2 == 0 else 1
    length_column = column(lambda r: lengths[r], rows)
    stacked_length = jnp.concatenate([length_column[:, :1]] * heads, axis=0)
    stacked_row = lax.rem(
        lax.broadcasted_iota(jnp.int32, (heads * rows, cache), 0), jnp.int32(rows)
    )
    visible = lax.broadcasted_iota(jnp.int32, (heads * rows, cache), 1) < stacked_length

    def stacked(get):
        return jnp.concatenate([get(g, j) for g in range(kv_local) for j in range(group)], axis=0)

    def head_lanes(g, j=None):
        h = g if j is None else g * group + j
        return slice(h * HD, (h + 1) * HD)

    query = stacked(lambda g, j: queries[:, head_lanes(g, j)])
    wide = jnp.concatenate([query] * kv_local, axis=1)
    lane_head = lax.broadcasted_iota(jnp.int32, wide.shape, 1) // HD
    row_head = lax.broadcasted_iota(jnp.int32, wide.shape, 0) // (group * rows)
    wide = jnp.where(lane_head == row_head, wide.astype(F32), 0.0).astype(BF16)
    scores = jnp.zeros((heads * rows, cache), F32)
    for r in range(0, rows, together):
        keys = stored_keys[r : r + together].reshape(together * cache, kv_local * HD)
        every = lax.dot_general(wide, keys, ANY_LANES, preferred_element_type=F32)
        for i in range(together):
            scores = jnp.where(
                stacked_row == r + i, every[:, i * cache : (i + 1) * cache], scores
            )
    scores = jnp.where(visible, scores * scale, -jnp.inf)
    wait(5)
    fresh_key = stacked(lambda g, j: token_keys[:, head_lanes(g)].astype(F32))
    fresh = jnp.sum(query.astype(F32) * fresh_key, axis=1, keepdims=True) * scale
    largest = jnp.maximum(jnp.max(scores, axis=1, keepdims=True), fresh)
    cache_exp = jnp.exp(scores - largest)
    fresh_exp = jnp.exp(fresh - largest)
    denominator = jnp.sum(cache_exp, axis=1, keepdims=True) + fresh_exp
    probs = cache_exp / denominator
    fresh_prob = (fresh_exp / denominator).astype(BF16).astype(F32)
    wait(8)
    every = jnp.zeros((heads * rows, kv_local * HD), F32)
    for r in range(0, rows, together):
        values = stored_values[r : r + together].reshape(together * cache, kv_local * HD)
        own = [jnp.where(stacked_row == r + i, probs, 0.0).astype(BF16) for i in range(together)]
        every = every + jnp.dot(
            jnp.concatenate(own, axis=1), values, preferred_element_type=F32
        )
    wait(3, 6, 9)
    squares = jnp.zeros((rows, 1), F32)
    for g in range(kv_local):
        fresh_value = token_values[:, head_lanes(g)].astype(F32)
        for j in range(group):
            lanes = head_lanes(g, j)
            place = slice((g * group + j) * rows, (g * group + j + 1) * rows)
            attended = every[place, head_lanes(g)] + fresh_prob[place] * fresh_value
            state = (residual[:, lanes].astype(F32) + attended).astype(BF16)
            state_out[:, lanes] = state
            state = state.astype(F32)
            squares = squares + jnp.sum(state * state, axis=1, keepdims=True)
            payload_out[:, lanes] = (
                state * gain[lanes.start // LANES : lanes.start // LANES + 1, :]
            ).astype(BF16)
    wait(1, 2, 10, 11)
    scaled = payload_out[:, :features]
    logits = lax.dot_general(scaled, router[...], ANY_LANES, preferred_element_type=F32)
    first = column(lambda r: routes[0, r], rows)
    second = column(lambda r: routes[1, r], rows)
    tenant = column(lambda r: tenants[r], rows)
    expert = lax.broadcasted_iota(jnp.int32, logits.shape, 1)
    chosen = jnp.where(expert == first[:, :EXPERT_COUNT], logits, 0.0) - jnp.where(
        expert == second[:, :EXPERT_COUNT], logits, 0.0
    )
    diff = jnp.sum(chosen, axis=1, keepdims=True)
    adapter = jnp.dot(scaled, adapter_down[...], preferred_element_type=F32)
    lane = lax.broadcasted_iota(jnp.int32, (rows, LANES), 1)
    tail = jnp.zeros((rows, LANES), F32)
    for start in range(0, adapter.shape[1], LANES):
        owner = (lane + start) // ADAPTER_LANES
        tail = tail + jnp.where(owner == tenant, adapter[:, start : start + LANES], 0.0)
    tail = tail + pltpu.roll(tail, ADAPTER_LANES, 1)
    diff_hi = diff.astype(BF16).astype(F32)
    squares_hi = squares.astype(BF16).astype(F32)
    for place, value in (
        (DIFF_HI, diff_hi),
        (DIFF_LO, diff - diff_hi),
        (SQ_HI, squares_hi),
        (SQ_LO, squares - squares_hi),
        (FIRST, first.astype(F32)),
        (SECOND, second.astype(F32)),
        (TENANT, tenant.astype(F32)),
    ):
        tail = jnp.where(lane == place, value, tail)
    payload_out[:, features:] = tail.astype(BF16)


def attend(args, gate_weight):
    rows, features = args[3].shape
    return pl.pallas_call(
        attend_kernel,
        out_shape=(
            jax.ShapeDtypeStruct((rows, features), BF16),
            jax.ShapeDtypeStruct((rows, features + LANES), BF16),
            jax.ShapeDtypeStruct((features, gate_weight.shape[1]), BF16),
        ),
        in_specs=[HBM] * (len(args) + 1),
        out_specs=(VMEM,) * 3,
        scratch_shapes=[
            (pltpu.SMEM if i < 3 else pltpu.VMEM)(arg.shape, arg.dtype)
            for i, arg in enumerate(args)
        ]
        + [pltpu.SemaphoreType.DMA((len(args),)), pltpu.SemaphoreType.DMA],
        compiler_params=pltpu.CompilerParams(vmem_limit_bytes=12 * 2**20),
        cost_estimate=pl.CostEstimate(
            flops=200_000_000, bytes_accessed=6_000_000, transcendentals=20_000
        ),
        name="attend",
    )(*in_hbm(*args, gate_weight))


def load_kernel(distance, gate_weight, after, part, arrived):
    fetch(gate_weight, distance, part, arrived).wait()


def load(gate_weight, distance, features, after):
    hidden = gate_weight.shape[1]
    return pl.pallas_call(
        functools.partial(load_kernel, distance),
        out_shape=jax.ShapeDtypeStruct((features, hidden), BF16),
        in_specs=[HBM] * 2,
        out_specs=VMEM,
        scratch_shapes=[pltpu.SemaphoreType.DMA],
        compiler_params=pltpu.CompilerParams(vmem_limit_bytes=2**20),
        cost_estimate=pl.CostEstimate(
            flops=0, bytes_accessed=2 * features * hidden, transcendentals=0
        ),
        name="load",
    )(*in_hbm(gate_weight), after)


def halves(hidden):
    return hidden // 2 if hidden % (2 * LANES) == 0 else hidden


def partial_kernel(distance, fetched, first, soon, block, gate_part, up_weight, *refs):
    features, hidden = gate_part.shape
    sums, refs = (None, refs) if first else (refs[0], refs[1:])
    gate_weight, totals = refs[0], refs[1 + soon]
    copy = None if fetched is None else fetch(gate_weight, fetched, refs[2 + soon], refs[-1])
    tile = halves(hidden)
    depth = at_distance(distance, features)

    def products(n, carry):
        lanes = pl.ds(pl.multiple_of(n * tile, tile), tile)
        for i, part in enumerate((gate_part[:, lanes], up_weight[depth, lanes])):
            product = jnp.dot(block[:, :features], part, preferred_element_type=F32)
            totals[i, :, lanes] = product if first else sums[i, :, lanes] + product
        return carry

    lax.fori_loop(0, hidden // tile, products, 0)
    if copy is not None:
        copy.wait()


def partial(block, distance, part, sums, gate_weight, up_weight, fetched, soon):
    rows, width = block.shape
    features = width - LANES
    hidden = gate_weight.shape[1]
    first = sums is None
    more = int(fetched is not None)
    return pl.pallas_call(
        functools.partial(partial_kernel, distance, fetched, first, len(soon)),
        out_shape=(
            jax.ShapeDtypeStruct((2, rows, hidden), F32),
            *[jax.ShapeDtypeStruct((features, hidden), BF16)] * more,
        ),
        in_specs=[VMEM] * (3 if first else 4) + [HBM] * (1 + len(soon)),
        out_specs=(VMEM,) * (1 + more),
        scratch_shapes=[pltpu.SemaphoreType.DMA],
        compiler_params=pltpu.CompilerParams(vmem_limit_bytes=6 * 2**20),
        cost_estimate=pl.CostEstimate(
            flops=4 * rows * features * hidden,
            bytes_accessed=2 * features * hidden,
            transcendentals=0,
        ),
        name="partial",
    )(block, part, up_weight, *(() if first else (sums,)), *in_hbm(gate_weight), *soon)


def expert_kernel(replicas, targets, order, known, sums, *refs):
    tensor_devices = len(order)
    blocks, parts = refs[:tensor_devices], refs[tensor_devices : 2 * tensor_devices - known]
    up_weight, down_weight, adapter_weight, out, active, adapter_up, arrived = refs[
        2 * tensor_devices - known :
    ]
    rows, width = blocks[0].shape
    features = width - LANES
    hidden = active.shape[1]
    adapter_copy = pltpu.make_async_copy(adapter_weight, adapter_up, arrived)
    adapter_copy.start()
    expert = lax.axis_index("ep") // replicas
    tail = jnp.zeros((rows, LANES), F32)
    for block in blocks:
        tail = tail + block[:, features:].astype(F32)
    place = lambda k: tail[:, k : k + 1]
    here = blocks[0][:, features:].astype(F32)
    inverse_rms = lax.rsqrt(
        (place(SQ_HI) + place(SQ_LO)) / (features * tensor_devices) + 1e-05
    )
    diff = (place(DIFF_HI) + place(DIFF_LO)) * inverse_rms
    expert_float = expert.astype(F32)
    is_first = here[:, FIRST : FIRST + 1] == expert_float
    is_second = here[:, SECOND : SECOND + 1] == expert_float
    weight = jnp.where(
        is_first, jax.nn.sigmoid(diff), jnp.where(is_second, jax.nn.sigmoid(-diff), 0.0)
    )
    lowrank = (tail * inverse_rms).astype(BF16)
    spread_shape = (LANES, TENANT_COUNT * ADAPTER_RANK)
    source = lax.broadcasted_iota(jnp.int32, spread_shape, 0)
    target = lax.broadcasted_iota(jnp.int32, spread_shape, 1)
    spread = jnp.where(
        source == expert * ADAPTER_RANK + lax.rem(target, jnp.int32(ADAPTER_RANK)), 1.0, 0.0
    ).astype(BF16)
    lane = lax.broadcasted_iota(jnp.int32, (rows, TENANT_COUNT * ADAPTER_RANK), 1)
    own_tenant = (lane // ADAPTER_RANK).astype(F32) == here[:, TENANT : TENANT + 1]
    adapter_rows = jnp.where(
        own_tenant, jnp.dot(lowrank, spread, preferred_element_type=F32), 0.0
    ).astype(BF16)
    adapter_copy.wait()
    tile = halves(hidden)

    def products(n, carry):
        lanes = pl.ds(pl.multiple_of(n * tile, tile), tile)
        gate, up = sums[0, :, lanes], sums[1, :, lanes]
        for block, part, distance in zip(blocks[known:], parts, order[known:], strict=True):
            scaled = block[:, :features]
            gate = gate + jnp.dot(scaled, part[:, lanes], preferred_element_type=F32)
            up = up + jnp.dot(
                scaled,
                up_weight[at_distance(distance, features), lanes],
                preferred_element_type=F32,
            )
        gate = gate * inverse_rms
        up = up * inverse_rms + jnp.dot(
            adapter_rows, adapter_up[:, lanes], preferred_element_type=F32
        )
        active[:, lanes] = (gate * jax.nn.sigmoid(gate) * up * weight).astype(BF16)
        return carry

    lax.fori_loop(0, hidden // tile, products, 0)
    down_products(targets, active, down_weight, out)


def down_products(targets, active, down_weight, out):
    for i, distance in enumerate(targets):
        lanes = at_distance(distance, out.shape[2])
        out[i] = jnp.dot(
            active[...], down_weight[:, lanes], preferred_element_type=F32
        ).astype(out.dtype)


def experts(replicas, targets, order, sums, known, blocks, parts, up_weight, down_weight, adapter_up):
    rows, width = blocks[0].shape
    features, hidden = width - LANES, sums.shape[2]
    return pl.pallas_call(
        functools.partial(expert_kernel, replicas, targets, order, known),
        out_shape=(
            jax.ShapeDtypeStruct((len(targets), rows, features), BF16),
            jax.ShapeDtypeStruct((rows, hidden), BF16),
        ),
        in_specs=[VMEM] * (3 + len(blocks) + len(parts)) + [HBM],
        out_specs=(VMEM, VMEM),
        scratch_shapes=[pltpu.VMEM(adapter_up.shape, BF16), pltpu.SemaphoreType.DMA],
        compiler_params=pltpu.CompilerParams(vmem_limit_bytes=8 * 2**20),
        cost_estimate=pl.CostEstimate(
            flops=2 * rows * hidden * features * (2 * len(parts) + len(targets)),
            bytes_accessed=0,
            transcendentals=0,
        ),
        name="experts",
    )(sums, *blocks, *parts, up_weight, down_weight, *in_hbm(adapter_up))


def down_kernel(targets, active, down_weight, after, out):
    down_products(targets, active, down_weight, out)


def down(targets, active, down_weight, features, after):
    rows, hidden = active.shape
    return pl.pallas_call(
        functools.partial(down_kernel, targets),
        out_shape=jax.ShapeDtypeStruct((len(targets), rows, features), F32),
        in_specs=[VMEM, VMEM, HBM],
        out_specs=VMEM,
        compiler_params=pltpu.CompilerParams(vmem_limit_bytes=4 * 2**20),
        cost_estimate=pl.CostEstimate(
            flops=2 * rows * hidden * features * len(targets),
            bytes_accessed=0,
            transcendentals=0,
        ),
        name="down",
    )(active, down_weight, after)


def join_kernel(first, second, *refs):
    out = refs[-1]
    count = first.shape[0]
    out[:count] = first[...]
    out[count:] = second[...]


def join(first, second, *after):
    return pl.pallas_call(
        join_kernel,
        out_shape=jax.ShapeDtypeStruct((2 * first.shape[0], *first.shape[1:]), first.dtype),
        in_specs=[VMEM, VMEM] + [HBM] * len(after),
        out_specs=VMEM,
        compiler_params=pltpu.CompilerParams(vmem_limit_bytes=4 * 2**20),
        name="join",
    )(first, second, *after)


def tie_kernel(array, after, out):
    pass


def tie(array, after):
    return pl.pallas_call(
        tie_kernel,
        out_shape=jax.ShapeDtypeStruct(array.shape, array.dtype),
        in_specs=[HBM, HBM],
        out_specs=HBM,
        input_output_aliases={0: 0},
        compiler_params=pltpu.CompilerParams(vmem_limit_bytes=2**20),
        name="tie",
    )(array, after)


def swap(x, axis, distance):
    count = lax.axis_size(axis)
    return lax.ppermute(x, axis, [(i, i ^ distance) for i in range(count)])


def bits(count):
    return [1 << b for b in range(count.bit_length() - 1)]


def per_device(
    residual,
    queries,
    token_keys,
    token_values,
    stored_keys,
    stored_values,
    lengths,
    norm_gain_vector,
    router,
    expert_gate_weight,
    expert_up_weight,
    expert_down_weight,
    adapter_down_map,
    adapter_up_map,
    routes,
    tenants,
):
    rows, features = residual.shape
    expert_devices = lax.axis_size("ep")
    tensor_devices = lax.axis_size("tp")
    state, held, *parts = attend(
        (
            lengths,
            tenants,
            routes.T,
            residual,
            queries,
            token_keys,
            token_values,
            stored_keys,
            stored_values,
            norm_gain_vector.reshape(features // LANES, LANES),
            router.T,
            adapter_down_map,
        ),
        expert_gate_weight,
    )
    order = [0]
    for distance in reversed(bits(tensor_devices)):
        order += [at ^ distance for at in order]
    for distance in bits(expert_devices):
        other = swap(held, "ep", distance)
        if len(parts) < tensor_devices:
            parts.append(load(expert_gate_weight, order[len(parts)], features, held))
        last = 2 * distance == expert_devices
        held = join(held, other, parts[-1], *((expert_up_weight,) if last else ()))
    blocks, known, sums = [held], 0, None
    for distance in reversed(bits(tensor_devices)):
        others = [swap(block, "tp", distance) for block in blocks]
        for block in blocks[known:]:
            fetched = order[len(parts)] if len(parts) < tensor_devices else None
            sums, *more = partial(
                block,
                order[known],
                parts[known],
                sums,
                expert_gate_weight,
                expert_up_weight,
                fetched,
                () if known else (expert_down_weight,),
            )
            parts += more
            known += 1
        blocks = blocks + [tie(block, sums) if distance > 1 else block for block in others]
    steps = bits(tensor_devices)
    groups = [tuple(k for k in range(tensor_devices) if k & -k == step) for step in steps] + [(0,)]
    sent, active = experts(
        expert_devices // EXPERT_COUNT,
        groups[0],
        tuple(order),
        sums,
        known,
        blocks,
        parts[known:],
        expert_up_weight,
        expert_down_weight,
        adapter_up_map,
    )
    received = {k: [] for k in range(tensor_devices)}
    for step, group, following in zip(steps, groups[:-1], groups[1:], strict=True):
        arriving = swap(sent, "tp", step)
        made = down(following, active, expert_down_weight, features, sent)
        for i, k in enumerate(group):
            received[k ^ step].append(arriving[i])
        kept = [
            sum((block.astype(F32) for block in received[k]), made[i])
            for i, k in enumerate(following)
        ]
        if following != (0,):
            sent = jnp.stack([block.astype(BF16) for block in kept])
    kept = kept[0].reshape(expert_devices, rows, features)
    for distance in bits(expert_devices):
        kept, sent = kept[0::2], kept[1::2].astype(BF16)
        kept = kept + swap(sent, "ep", distance).astype(F32)
    return (state.astype(F32) + kept[0]).astype(BF16)


def solution(mesh):
    placed = (
        P(("groups", "ep"), "tp"),
        P(("groups", "ep"), "tp"),
        P(("groups", "ep"), "tp"),
        P(("groups", "ep"), "tp"),
        P(("groups", "ep"), None, "tp"),
        P(("groups", "ep"), None, "tp"),
        P(("groups", "ep")),
        P("tp"),
        P("tp", None),
        P(None, ("ep", "tp")),
        P(None, ("ep", "tp")),
        P(("ep", "tp"), None),
        P("tp", None),
        P(None, ("ep", "tp")),
        P(("groups", "ep"), None),
        P(("groups", "ep")),
    )
    return jax.shard_map(
        per_device, mesh=mesh, in_specs=placed, out_specs=P(("groups", "ep"), "tp"), check_vma=False
    )
```

time: 45.1 us -> 41.6 us (0.922)
  Pallas kernels: 21.6 us -> 16.5 us
  local copies, waits for them, and re-layouts: 0.02 us -> 1.69 us
  starting transfers between devices: 14.7 us -> 14 us
  waiting for transfers between devices: 7.73 us -> 8.37 us
    pallas_call x1 -> x2, Pallas kernels: 3.64 us -> 1.34 us  [down(): pl.pallas_call(functools.partial(down_kernel, targets), out_shape=jax.Sha...]
    pallas_call x5, Pallas kernels: 14 us -> 12.2 us  [the longest x1 4.83 us: experts(): pl.pallas_call(functools.partial(expert_kernel, replicas, targets, order,...]
    unnamed x0 -> x12, local copies, waits for them, and re-layouts: none -> 1.68 us
    pallas_call x1, Pallas kernels: 3.91 us -> 2.98 us  [attend(): pl.pallas_call(attend_kernel, out_shape=(jax.ShapeDtypeStruct((rows, feat...]
    ppermute x9, starting transfers between devices: 14.7 us -> 14 us  [swap(): return lax.ppermute(x, axis, [(i, i ^ distance) for i in range(count)])]
    ppermute x9, waiting for transfers between devices: 7.73 us -> 8.37 us  [swap(): return lax.ppermute(x, axis, [(i, i ^ distance) for i in range(count)])]
  transfers between devices with their start and end apart: 9 -> 9, of which waited for: 6 -> 5; matrix products, arithmetic and copies ran while one was open for 0% -> 0% of each run, Pallas kernels for 26% -> 21%
where the time goes in v5:
time: 41.6 us; the launch traced here: 41.5 us
  Pallas kernels  16.5 us (40%)
  starting transfers between devices  14 us (34%)
  waiting for transfers between devices  8.37 us (20%)
  local copies, waits for them, and re-layouts  1.69 us (4%)
  other arithmetic  0.69 us (2%)
    ppermute x9, starting transfers between devices, swap(): return lax.ppermute(x, axis, [(i, i ^ distance) for i in range(count)])  14 us
    ppermute x9, waiting for transfers between devices, swap(): return lax.ppermute(x, axis, [(i, i ^ distance) for i in range(count)])  8.37 us
    pallas_call x1, Pallas kernels, experts(): pl.pallas_call(functools.partial(expert_kernel, replicas, targets, order,...  4.83 us
    pallas_call x2, Pallas kernels, load(): pl.pallas_call(functools.partial(load_kernel, distance), out_shape=jax.Sh...  4.09 us
    pallas_call x2, Pallas kernels, partial(): pl.pallas_call(functools.partial(partial_kernel, distance, fetched, first...  3.24 us
    pallas_call x1, Pallas kernels, attend(): pl.pallas_call(attend_kernel, out_shape=(jax.ShapeDtypeStruct((rows, feat...  2.98 us
    unnamed x12, local copies, waits for them, and re-layouts  1.68 us
    pallas_call x2, Pallas kernels, down(): pl.pallas_call(functools.partial(down_kernel, targets), out_shape=jax.Sha...  1.34 us
  transfers between devices with their start and end apart: 9, of which 5 were waited for; matrix products, arithmetic and copies ran while one was open for 0% of the time, Pallas kernels for 21%

profile of v5, /device:TPU:0, one launch (start us, length us, event | category | flops | bytes accessed | tf_op | source)
XLA Modules:
  0.0 41.5 jit_solution(4475586023241564114)
XLA Ops:
  0.0 3.0 %attend.1 = (bf16[16,768]{1,0:T(8,128)(2,1)S(1)}, bf16[16,896]{1,0:T(8,128)(2,1)S(1)}, bf16[768,2048]{1,0:T(8,128)(2,1)S(1)}) custom-call(s32[16]{0:T(128)} %refs_0_.2, s32[16]{0:T(128)} %refs_1_.4, s32[2,16]{1,0:T(2,128)} %bitcast.18, bf16[16,768]{1,0:T(8,128)(2,1)} %refs_3_.1, bf16[16,768]{1,0:T(8,128)(2,1)} %refs_4_.1, bf16[16,256]{1,0:T(8,128)(2,1)} %refs_5_.1, ...), custom_call_target="tpu_custom_call" | custom-call | flops 200000000 | bytes 6000000 | tf_op jit(solution)/shard_map/attend/pallas_call | solution.py:188
  3.0 3.1 %collective-permute-start = (bf16[16,896]{1,0:T(8,128)(2,1)S(1)}, bf16[16,896]{1,0:T(8,128)(2,1)S(1)}, u32[]{:S(2)}, u32[]{:S(2)}) collective-permute-start(bf16[16,896]{1,0:T(8,128)(2,1)S(1)} %get-tuple-element.13.after.first), channel_id=1, source_target_pairs={{0,4},{4,0},{8,12},{12,8},{1,5},{5,1},{9,13},{13,9},{2,6},{6,2},{1... | collective-permute-start | bytes 86024 | tf_op jit(solution)/shard_map/ppermute | solution.py:430
  6.1 0.0 slice-start.3
  6.1 0.0 slice-start.4
  6.1 2.0 %load.2.refs_0_.gate_part = bf16[768,2048]{1,0:T(8,128)(2,1)S(1)} custom-call(bf16[3072,2048]{1,0:T(8,128)(2,1)} %refs_1_.7, bf16[16,896]{1,0:T(8,128)(2,1)S(1)} %get-tuple-element.13.after.first), custom_call_target="tpu_custom_call" | custom-call | bytes 3145728 | tf_op jit(solution)/shard_map/load/pallas_call | solution.py:216
  8.1 0.0 collective-permute-done.second
  8.2 0.0 slice-start.5
  8.2 2.9 %collective-permute-start.1 = (bf16[32,896]{1,0:T(8,128)(2,1)S(1)}, bf16[32,896]{1,0:T(8,128)(2,1)S(1)}, u32[]{:S(2)}, u32[]{:S(2)}) collective-permute-start(bf16[32,896]{1,0:T(8,128)(2,1)S(1)} %join.2.after.first), channel_id=1, source_target_pairs={{0,8},{4,12},{8,0},{12,4},{1,9},{5,13},{9,1},{13,5},{2,10},{6,14},... | collective-permute-start | bytes 172040 | tf_op jit(solution)/shard_map/ppermute | solution.py:430
  11.0 0.0 slice-start
  11.0 0.0 slice-start.1
  11.0 2.0 %load.3.refs_0_.refs_4_ = bf16[768,2048]{1,0:T(8,128)(2,1)S(1)} custom-call(bf16[3072,2048]{1,0:T(8,128)(2,1)} %refs_1_.7, bf16[32,896]{1,0:T(8,128)(2,1)S(1)} %join.2.after.first), custom_call_target="tpu_custom_call" | custom-call | bytes 3145728 | tf_op jit(solution)/shard_map/load/pallas_call | solution.py:216
  13.1 0.0 slice-start.2
  13.1 0.2 collective-permute-done.1.second
  13.3 0.0 slice-done.3
  13.3 0.0 slice-done.4
  13.3 0.0 slice-done.5
  13.4 1.8 %collective-permute-start.2 = (bf16[64,896]{1,0:T(8,128)(2,1)S(1)}, bf16[64,896]{1,0:T(8,128)(2,1)S(1)}, u32[]{:S(2)}, u32[]{:S(2)}) collective-permute-start(bf16[64,896]{1,0:T(8,128)(2,1)S(1)} %join.3.block.refs_0_), channel_id=1, source_target_pairs={{0,2},{1,3},{2,0},{3,1},{4,6},{5,7},{6,4},{7,5},{8,10},{9,11},{10,... | collective-permute-start | bytes 344072 | tf_op jit(solution)/shard_map/ppermute | solution.py:430
  15.1 0.0 collective-permute-start.3
  15.1 0.0 slice-done
  15.1 0.5 %slice-done.1 = s8[4194304]{0:T(1024)(128)(4,1)S(1)} async-done(((s8[12582912]{0:T(1024)(128)(4,1)}), s8[4194304]{0:T(1024)(128)(4,1)S(1)}, s32[]{:S(2)}) %slice-start.1) | async-done | bytes 4194328
  15.6 1.2 %slice-done.2 = s8[4194304]{0:T(1024)(128)(4,1)S(1)} async-done(((s8[12582912]{0:T(1024)(128)(4,1)}), s8[4194304]{0:T(1024)(128)(4,1)S(1)}, s32[]{:S(2)}) %slice-start.2) | async-done | bytes 4194328
  16.8 1.9 %partial.2 = (f32[2,64,2048]{2,1,0:T(8,128)S(1)}, bf16[768,2048]{1,0:T(8,128)(2,1)S(1)}) custom-call(bf16[64,896]{1,0:T(8,128)(2,1)S(1)} %join.3.block.refs_0_, bf16[768,2048]{1,0:T(8,128)(2,1)S(1)} %get-tuple-element.14.gate_part, bf16[3072,2048]{1,0:T(8,128)(2,1)S(1)} %bitcast.13, bf16[3072,2048]{1,0:T(8,128)(2,1)} %refs_1_.7, bf16[2048,3072]{1,0:T(8,128)(2,1)S(1)} %bitcast.11), custom_call_target="tpu_custom_call" | custom-call | flops 402653184 | bytes 3145728 | tf_op jit(solution)/shard_map/partial/pallas_call | solution.py:260
  18.7 0.0 collective-permute-done.2.array
  18.7 0.1 collective-permute-start.4
  18.8 1.3 %partial.3.sums = f32[2,64,2048]{2,1,0:T(8,128)S(1)} custom-call(bf16[64,896]{1,0:T(8,128)(2,1)S(1)} %tie.1.block.refs_1_, bf16[768,2048]{1,0:T(8,128)(2,1)S(1)} %load.2.refs_0_.gate_part, bf16[3072,2048]{1,0:T(8,128)(2,1)S(1)} %bitcast.13, f32[2,64,2048]{2,1,0:T(8,128)S(1)} %get-tuple-element.15.after.refs_0_, bf16[3072,2048]{1,0:T(8,128)(2,1)} %refs_1_.7), custom_call_target="tpu_custom_call" | custom-call | flops 402653184 | bytes 3145728 | tf_op jit(solution)/shard_map/partial/pallas_call | solution.py:260
  20.1 0.0 collective-permute-done.3.refs_2_
  20.2 0.0 collective-permute-done.4.refs_3_
  20.2 4.8 %experts.1 = (bf16[2,64,768]{2,1,0:T(8,128)(2,1)S(1)}, bf16[64,2048]{1,0:T(8,128)(2,1)S(1)}) custom-call(f32[2,64,2048]{2,1,0:T(8,128)S(1)} %partial.3.sums, bf16[64,896]{1,0:T(8,128)(2,1)S(1)} %join.3.block.refs_0_, bf16[64,896]{1,0:T(8,128)(2,1)S(1)} %tie.1.block.refs_1_, bf16[64,896]{1,0:T(8,128)(2,1)S(1)} %collective-permute-done.3.refs_2_, ...), custom_call_target="tpu_custom_call" | custom-call | flops 1207959552 | tf_op jit(solution)/shard_map/experts/pallas_call | solution.py:354
  25.0 0.6 %collective-permute-start.5 = (bf16[2,64,768]{2,1,0:T(8,128)(2,1)S(1)}, bf16[2,64,768]{2,1,0:T(8,128)(2,1)S(1)}, u32[]{:S(2)}, u32[]{:S(2)}) collective-permute-start(bf16[2,64,768]{2,1,0:T(8,128)(2,1)S(1)} %get-tuple-element.18.after), channel_id=1, source_target_pairs={{0,1},{1,0},{2,3},{3,2},{4,5},{5,4},{6,7},{7,6},{8,9},{9,8},{10,11... | collective-permute-start | bytes 589832 | tf_op jit(solution)/shard_map/ppermute | solution.py:430
  25.6 0.7 %down.2 = f32[1,64,768]{2,1,0:T(8,128)S(1)} custom-call(bf16[64,2048]{1,0:T(8,128)(2,1)S(1)} %get-tuple-element.17.active, bf16[2048,3072]{1,0:T(8,128)(2,1)S(1)} %bitcast.11, bf16[2,64,768]{2,1,0:T(8,128)(2,1)S(1)} %get-tuple-element.18.after), custom_call_target="tpu_custom_call" | custom-call | flops 201326592 | tf_op jit(solution)/shard_map/down/pallas_call | solution.py:379
  26.2 0.4 collective-permute-done.5
  26.7 1.6 %collective-permute-start.6 = (bf16[1,64,768]{2,1,0:T(8,128)(2,1)S(1)}, bf16[1,64,768]{2,1,0:T(8,128)(2,1)S(1)}, u32[]{:S(2)}, u32[]{:S(2)}) collective-permute-start(bf16[1,64,768]{2,1,0:T(8,128)(2,1)S(1)} %add_convert_fusion.after), channel_id=1, source_target_pairs={{0,2},{1,3},{2,0},{3,1},{4,6},{5,7},{6,4},{7,5},{8,10},{9,11},{10,... | collective-permute-start | bytes 294920 | tf_op jit(solution)/shard_map/ppermute | solution.py:430
  28.2 0.7 %down.3 = f32[1,64,768]{2,1,0:T(8,128)S(1)} custom-call(bf16[64,2048]{1,0:T(8,128)(2,1)S(1)} %get-tuple-element.17.active, bf16[2048,3072]{1,0:T(8,128)(2,1)S(1)} %bitcast.11, bf16[1,64,768]{2,1,0:T(8,128)(2,1)S(1)} %add_convert_fusion.after), custom_call_target="tpu_custom_call" | custom-call | flops 201326592 | tf_op jit(solution)/shard_map/down/pallas_call | solution.py:379
  28.9 2.9 %collective-permute-done.6 = bf16[1,64,768]{2,1,0:T(8,128)(2,1)S(1)} collective-permute-done((bf16[1,64,768]{2,1,0:T(8,128)(2,1)S(1)}, bf16[1,64,768]{2,1,0:T(8,128)(2,1)S(1)}, u32[]{:S(2)}, u32[]{:S(2)}) %collective-permute-start.6) | collective-permute-done | bytes 98336 | tf_op jit(solution)/shard_map/ppermute | solution.py:430
  31.9 1.7 %collective-permute-start.7 = (bf16[2,16,768]{2,1,0:T(8,128)(2,1)S(1)}, bf16[2,16,768]{2,1,0:T(8,128)(2,1)S(1)}, u32[]{:S(2)}, u32[]{:S(2)}) collective-permute-start(bf16[2,16,768]{2,1,0:T(8,128)(2,1)S(1)} %slice.25), channel_id=1, source_target_pairs={{0,4},{4,0},{8,12},{12,8},{1,5},{5,1},{9,13},{13,9},{2,6},{6,2},{1... | collective-permute-start | bytes 147464 | tf_op jit(solution)/shard_map/ppermute | solution.py:430
  33.6 2.4 %collective-permute-done.7 = bf16[2,16,768]{2,1,0:T(8,128)(2,1)S(1)} collective-permute-done((bf16[2,16,768]{2,1,0:T(8,128)(2,1)S(1)}, bf16[2,16,768]{2,1,0:T(8,128)(2,1)S(1)}, u32[]{:S(2)}, u32[]{:S(2)}) %collective-permute-start.7) | collective-permute-done | bytes 49184 | tf_op jit(solution)/shard_map/ppermute | solution.py:430
  36.0 2.3 %collective-permute-start.8 = (bf16[1,16,768]{2,1,0:T(8,128)(2,1)S(1)}, bf16[1,16,768]{2,1,0:T(8,128)(2,1)S(1)}, u32[]{:S(2)}, u32[]{:S(2)}) collective-permute-start(bf16[1,16,768]{2,1,0:T(8,128)(2,1)S(1)} %slice.43), channel_id=1, source_target_pairs={{0,8},{4,12},{8,0},{12,4},{1,9},{5,13},{9,1},{13,5},{2,10},{6,14},... | collective-permute-start | bytes 73736 | tf_op jit(solution)/shard_map/ppermute | solution.py:430
  38.4 2.4 %collective-permute-done.8 = bf16[1,16,768]{2,1,0:T(8,128)(2,1)S(1)} collective-permute-done((bf16[1,16,768]{2,1,0:T(8,128)(2,1)S(1)}, bf16[1,16,768]{2,1,0:T(8,128)(2,1)S(1)}, u32[]{:S(2)}, u32[]{:S(2)}) %collective-permute-start.8) | collective-permute-done | bytes 24608 | tf_op jit(solution)/shard_map/ppermute | solution.py:430
  40.8 0.6 %fusion.2 = bf16[16,768]{1,0:T(8,128)(2,1)} fusion(f32[2,16,768]{2,1,0:T(8,128)S(1)} %convert_add_fusion.1, bf16[1,16,768]{2,1,0:T(8,128)(2,1)S(1)} %collective-permute-done.8, bf16[16,768]{1,0:T(8,128)(2,1)S(1)} %get-tuple-element.12), kind=kLoop, calls=%fused_computation.7 | loop fusion | flops 61440 | bytes 122880 | tf_op jit(solution)/shard_map/convert_element_type | solution.py:532
  (11 shorter events, 0.1 us)
Async XLA Ops:
  3.0 5.2 %collective-permute-start = (bf16[16,896]{1,0:T(8,128)(2,1)S(1)}, bf16[16,896]{1,0:T(8,128)(2,1)S(1)}, u32[]{:S(2)}, u32[]{:S(2)}) collective-permute-start(bf16[16,896]{1,0:T(8,128)(2,1)S(1)} %get-tuple-element.13.after.first), channel_id=1, source_target_pairs={{0,4},{4,0},{8,12},{12,8},{1,5},{5,1},{9,13},{13,9},{2,6},{6,2},{1... | collective-permute-start | bytes 86024 | tf_op jit(solution)/shard_map/ppermute | solution.py:430
  6.1 7.2 %slice-start.3 = ((s8[12582912]{0:T(1024)(128)(4,1)}), s8[4194304]{0:T(1024)(128)(4,1)S(1)}, s32[]{:S(2)}) async-start(s8[12582912]{0:T(1024)(128)(4,1)} %bitcast.12), calls=%async_computation.3 | async-start | bytes 8388608
  6.1 7.2 %slice-start.4 = ((s8[12582912]{0:T(1024)(128)(4,1)}), s8[4194304]{0:T(1024)(128)(4,1)S(1)}, s32[]{:S(2)}) async-start(s8[12582912]{0:T(1024)(128)(4,1)} %bitcast.12), calls=%async_computation.4 | async-start | bytes 8388608
  8.2 5.2 %slice-start.5 = ((s8[12582912]{0:T(1024)(128)(4,1)}), s8[4194304]{0:T(1024)(128)(4,1)S(1)}, s32[]{:S(2)}) async-start(s8[12582912]{0:T(1024)(128)(4,1)} %bitcast.12), calls=%async_computation.5 | async-start | bytes 8388608
  8.2 5.1 %collective-permute-start.1 = (bf16[32,896]{1,0:T(8,128)(2,1)S(1)}, bf16[32,896]{1,0:T(8,128)(2,1)S(1)}, u32[]{:S(2)}, u32[]{:S(2)}) collective-permute-start(bf16[32,896]{1,0:T(8,128)(2,1)S(1)} %join.2.after.first), channel_id=1, source_target_pairs={{0,8},{4,12},{8,0},{12,4},{1,9},{5,13},{9,1},{13,5},{2,10},{6,14},... | collective-permute-start | bytes 172040 | tf_op jit(solution)/shard_map/ppermute | solution.py:430
  11.0 4.1 %slice-start = ((s8[12582912]{0:T(1024)(128)(4,1)}), s8[4194304]{0:T(1024)(128)(4,1)S(1)}, s32[]{:S(2)}) async-start(s8[12582912]{0:T(1024)(128)(4,1)} %bitcast.10), calls=%async_computation | async-start | bytes 8388608
  11.0 4.5 %slice-start.1 = ((s8[12582912]{0:T(1024)(128)(4,1)}), s8[4194304]{0:T(1024)(128)(4,1)S(1)}, s32[]{:S(2)}) async-start(s8[12582912]{0:T(1024)(128)(4,1)} %bitcast.10), calls=%async_computation.1 | async-start | bytes 8388608
  13.1 3.7 %slice-start.2 = ((s8[12582912]{0:T(1024)(128)(4,1)}), s8[4194304]{0:T(1024)(128)(4,1)S(1)}, s32[]{:S(2)}) async-start(s8[12582912]{0:T(1024)(128)(4,1)} %bitcast.10), calls=%async_computation.2 | async-start | bytes 8388608
  13.4 5.3 %collective-permute-start.2 = (bf16[64,896]{1,0:T(8,128)(2,1)S(1)}, bf16[64,896]{1,0:T(8,128)(2,1)S(1)}, u32[]{:S(2)}, u32[]{:S(2)}) collective-permute-start(bf16[64,896]{1,0:T(8,128)(2,1)S(1)} %join.3.block.refs_0_), channel_id=1, source_target_pairs={{0,2},{1,3},{2,0},{3,1},{4,6},{5,7},{6,4},{7,5},{8,10},{9,11},{10,... | collective-permute-start | bytes 344072 | tf_op jit(solution)/shard_map/ppermute | solution.py:430
  15.1 5.0 %collective-permute-start.3 = (bf16[64,896]{1,0:T(8,128)(2,1)S(1)}, bf16[64,896]{1,0:T(8,128)(2,1)S(1)}, u32[]{:S(2)}, u32[]{:S(2)}) collective-permute-start(bf16[64,896]{1,0:T(8,128)(2,1)S(1)} %join.3.block.refs_0_), channel_id=1, source_target_pairs={{0,1},{1,0},{2,3},{3,2},{4,5},{5,4},{6,7},{7,6},{8,9},{9,8},{10,11... | collective-permute-start | bytes 344072 | tf_op jit(solution)/shard_map/ppermute | solution.py:430
  18.7 1.4 %collective-permute-start.4 = (bf16[64,896]{1,0:T(8,128)(2,1)S(1)}, bf16[64,896]{1,0:T(8,128)(2,1)S(1)}, u32[]{:S(2)}, u32[]{:S(2)}) collective-permute-start(bf16[64,896]{1,0:T(8,128)(2,1)S(1)} %tie.1.block.refs_1_), channel_id=1, source_target_pairs={{0,1},{1,0},{2,3},{3,2},{4,5},{5,4},{6,7},{7,6},{8,9},{9,8},{10,11... | collective-permute-start | bytes 344072 | tf_op jit(solution)/shard_map/ppermute | solution.py:430
  25.0 1.6 %collective-permute-start.5 = (bf16[2,64,768]{2,1,0:T(8,128)(2,1)S(1)}, bf16[2,64,768]{2,1,0:T(8,128)(2,1)S(1)}, u32[]{:S(2)}, u32[]{:S(2)}) collective-permute-start(bf16[2,64,768]{2,1,0:T(8,128)(2,1)S(1)} %get-tuple-element.18.after), channel_id=1, source_target_pairs={{0,1},{1,0},{2,3},{3,2},{4,5},{5,4},{6,7},{7,6},{8,9},{9,8},{10,11... | collective-permute-start | bytes 589832 | tf_op jit(solution)/shard_map/ppermute | solution.py:430
  26.7 5.1 %collective-permute-start.6 = (bf16[1,64,768]{2,1,0:T(8,128)(2,1)S(1)}, bf16[1,64,768]{2,1,0:T(8,128)(2,1)S(1)}, u32[]{:S(2)}, u32[]{:S(2)}) collective-permute-start(bf16[1,64,768]{2,1,0:T(8,128)(2,1)S(1)} %add_convert_fusion.after), channel_id=1, source_target_pairs={{0,2},{1,3},{2,0},{3,1},{4,6},{5,7},{6,4},{7,5},{8,10},{9,11},{10,... | collective-permute-start | bytes 294920 | tf_op jit(solution)/shard_map/ppermute | solution.py:430
  31.9 4.2 %collective-permute-start.7 = (bf16[2,16,768]{2,1,0:T(8,128)(2,1)S(1)}, bf16[2,16,768]{2,1,0:T(8,128)(2,1)S(1)}, u32[]{:S(2)}, u32[]{:S(2)}) collective-permute-start(bf16[2,16,768]{2,1,0:T(8,128)(2,1)S(1)} %slice.25), channel_id=1, source_target_pairs={{0,4},{4,0},{8,12},{12,8},{1,5},{5,1},{9,13},{13,9},{2,6},{6,2},{1... | collective-permute-start | bytes 147464 | tf_op jit(solution)/shard_map/ppermute | solution.py:430
  36.0 4.8 %collective-permute-start.8 = (bf16[1,16,768]{2,1,0:T(8,128)(2,1)S(1)}, bf16[1,16,768]{2,1,0:T(8,128)(2,1)S(1)}, u32[]{:S(2)}, u32[]{:S(2)}) collective-permute-start(bf16[1,16,768]{2,1,0:T(8,128)(2,1)S(1)} %slice.43), channel_id=1, source_target_pairs={{0,8},{4,12},{8,0},{12,4},{1,9},{5,13},{9,1},{13,5},{2,10},{6,14},... | collective-permute-start | bytes 73736 | tf_op jit(solution)/shard_map/ppermute | solution.py:430

commit v6 on v5

--- a/solution.py
+++ b/solution.py
@@ -199,7 +199,7 @@
             for i, arg in enumerate(args)
         ]
         + [pltpu.SemaphoreType.DMA((len(args),)), pltpu.SemaphoreType.DMA],
-        compiler_params=pltpu.CompilerParams(vmem_limit_bytes=12 * 2**20),
+        compiler_params=pltpu.CompilerParams(vmem_limit_bytes=6 * 2**20),
         cost_estimate=pl.CostEstimate(
             flops=200_000_000, bytes_accessed=6_000_000, transcendentals=20_000
         ),
@@ -266,7 +266,7 @@
         in_specs=[VMEM] * (3 if first else 4) + [HBM] * (1 + len(soon)),
         out_specs=(VMEM,) * (1 + more),
         scratch_shapes=[pltpu.SemaphoreType.DMA],
-        compiler_params=pltpu.CompilerParams(vmem_limit_bytes=6 * 2**20),
+        compiler_params=pltpu.CompilerParams(vmem_limit_bytes=3 * 2**20),
         cost_estimate=pl.CostEstimate(
             flops=4 * rows * features * hidden,
             bytes_accessed=2 * features * hidden,
@@ -279,14 +279,10 @@
 def expert_kernel(replicas, targets, order, known, sums, *refs):
     tensor_devices = len(order)
     blocks, parts = refs[:tensor_devices], refs[tensor_devices : 2 * tensor_devices - known]
-    up_weight, down_weight, adapter_weight, out, active, adapter_up, arrived = refs[
-        2 * tensor_devices - known :
-    ]
+    up_weight, down_weight, adapter_up, out, active = refs[2 * tensor_devices - known :]
     rows, width = blocks[0].shape
     features = width - LANES
     hidden = active.shape[1]
-    adapter_copy = pltpu.make_async_copy(adapter_weight, adapter_up, arrived)
-    adapter_copy.start()
     expert = lax.axis_index("ep") // replicas
     tail = jnp.zeros((rows, LANES), F32)
     for block in blocks:
@@ -315,11 +311,9 @@
     adapter_rows = jnp.where(
         own_tenant, jnp.dot(lowrank, spread, preferred_element_type=F32), 0.0
     ).astype(BF16)
-    adapter_copy.wait()
     tile = halves(hidden)
-
-    def products(n, carry):
-        lanes = pl.ds(pl.multiple_of(n * tile, tile), tile)
+    for start in range(0, hidden, tile):
+        lanes = slice(start, start + tile)
         gate, up = sums[0, :, lanes], sums[1, :, lanes]
         for block, part, distance in zip(blocks[known:], parts, order[known:], strict=True):
             scaled = block[:, :features]
@@ -334,9 +328,6 @@
             adapter_rows, adapter_up[:, lanes], preferred_element_type=F32
         )
         active[:, lanes] = (gate * jax.nn.sigmoid(gate) * up * weight).astype(BF16)
-        return carry
-
-    lax.fori_loop(0, hidden // tile, products, 0)
     down_products(targets, active, down_weight, out)
 
 
@@ -357,17 +348,16 @@
             jax.ShapeDtypeStruct((len(targets), rows, features), BF16),
             jax.ShapeDtypeStruct((rows, hidden), BF16),
         ),
-        in_specs=[VMEM] * (3 + len(blocks) + len(parts)) + [HBM],
+        in_specs=[VMEM] * (4 + len(blocks) + len(parts)),
         out_specs=(VMEM, VMEM),
-        scratch_shapes=[pltpu.VMEM(adapter_up.shape, BF16), pltpu.SemaphoreType.DMA],
-        compiler_params=pltpu.CompilerParams(vmem_limit_bytes=8 * 2**20),
+        compiler_params=pltpu.CompilerParams(vmem_limit_bytes=4 * 2**20),
         cost_estimate=pl.CostEstimate(
             flops=2 * rows * hidden * features * (2 * len(parts) + len(targets)),
             bytes_accessed=0,
             transcendentals=0,
         ),
         name="experts",
-    )(sums, *blocks, *parts, up_weight, down_weight, *in_hbm(adapter_up))
+    )(sums, *blocks, *parts, up_weight, down_weight, adapter_up)
 
 
 def down_kernel(targets, active, down_weight, after, out):
@@ -404,7 +394,7 @@
         out_shape=jax.ShapeDtypeStruct((2 * first.shape[0], *first.shape[1:]), first.dtype),
         in_specs=[VMEM, VMEM] + [HBM] * len(after),
         out_specs=VMEM,
-        compiler_params=pltpu.CompilerParams(vmem_limit_bytes=4 * 2**20),
+        compiler_params=pltpu.CompilerParams(vmem_limit_bytes=1 * 2**20),
         name="join",
     )(first, second, *after)
 
@@ -494,7 +484,7 @@
                 expert_gate_weight,
                 expert_up_weight,
                 fetched,
-                () if known else (expert_down_weight,),
+                (adapter_up_map, expert_down_weight) if not known else (),
             )
             parts += more
             known += 1

time: 41.6 us -> 39.9 us (0.959)
  Pallas kernels: 16.5 us -> 14.8 us
    pallas_call x1, Pallas kernels: 4.83 us -> 3.14 us  [experts(): pl.pallas_call(functools.partial(expert_kernel, replicas, targets, order,...]
    unnamed x12 -> x14, local copies, waits for them, and re-layouts: 1.68 us -> 1.71 us
  transfers between devices with their start and end apart: 9 -> 9, of which waited for: 5 -> 5; matrix products, arithmetic and copies ran while one was open for 0% -> 0% of each run, Pallas kernels for 21% -> 22%
where the time goes in v6:
time: 39.9 us; the launch traced here: 39.7 us
  Pallas kernels  14.8 us (37%)
  starting transfers between devices  13.9 us (35%)
  waiting for transfers between devices  8.35 us (21%)
  local copies, waits for them, and re-layouts  1.72 us (4%)
  other arithmetic  0.7 us (2%)
    ppermute x9, starting transfers between devices, swap(): return lax.ppermute(x, axis, [(i, i ^ distance) for i in range(count)])  13.9 us
    ppermute x9, waiting for transfers between devices, swap(): return lax.ppermute(x, axis, [(i, i ^ distance) for i in range(count)])  8.35 us
    pallas_call x2, Pallas kernels, load(): pl.pallas_call(functools.partial(load_kernel, distance), out_shape=jax.Sh...  4.09 us
    pallas_call x2, Pallas kernels, partial(): pl.pallas_call(functools.partial(partial_kernel, distance, fetched, first...  3.24 us
    pallas_call x1, Pallas kernels, experts(): pl.pallas_call(functools.partial(expert_kernel, replicas, targets, order,...  3.14 us
    pallas_call x1, Pallas kernels, attend(): pl.pallas_call(attend_kernel, out_shape=(jax.ShapeDtypeStruct((rows, feat...  2.98 us
    unnamed x14, local copies, waits for them, and re-layouts  1.71 us
    pallas_call x2, Pallas kernels, down(): pl.pallas_call(functools.partial(down_kernel, targets), out_shape=jax.Sha...  1.34 us
  transfers between devices with their start and end apart: 9, of which 5 were waited for; matrix products, arithmetic and copies ran while one was open for 0% of the time, Pallas kernels for 22%

profile of v6, /device:TPU:0, one launch (start us, length us, event | category | flops | bytes accessed | tf_op | source)
XLA Modules:
  0.0 39.7 jit_solution(7318771293826741977)
XLA Ops:
  0.0 3.0 %attend.1 = (bf16[16,768]{1,0:T(8,128)(2,1)S(1)}, bf16[16,896]{1,0:T(8,128)(2,1)S(1)}, bf16[768,2048]{1,0:T(8,128)(2,1)S(1)}) custom-call(s32[16]{0:T(128)} %refs_0_.2, s32[16]{0:T(128)} %refs_1_.4, s32[2,16]{1,0:T(2,128)} %bitcast.18, bf16[16,768]{1,0:T(8,128)(2,1)} %refs_3_.1, bf16[16,768]{1,0:T(8,128)(2,1)} %refs_4_.1, bf16[16,256]{1,0:T(8,128)(2,1)} %refs_5_.1, ...), custom_call_target="tpu_custom_call" | custom-call | flops 200000000 | bytes 6000000 | tf_op jit(solution)/shard_map/attend/pallas_call | solution.py:188
  3.0 3.1 %collective-permute-start = (bf16[16,896]{1,0:T(8,128)(2,1)S(1)}, bf16[16,896]{1,0:T(8,128)(2,1)S(1)}, u32[]{:S(2)}, u32[]{:S(2)}) collective-permute-start(bf16[16,896]{1,0:T(8,128)(2,1)S(1)} %get-tuple-element.13.after.first), channel_id=1, source_target_pairs={{0,4},{4,0},{8,12},{12,8},{1,5},{5,1},{9,13},{13,9},{2,6},{6,2},{1... | collective-permute-start | bytes 86024 | tf_op jit(solution)/shard_map/ppermute | solution.py:420
  6.1 0.0 slice-start.3
  6.1 0.0 slice-start.4
  6.1 2.0 %load.2.refs_0_.gate_part = bf16[768,2048]{1,0:T(8,128)(2,1)S(1)} custom-call(bf16[3072,2048]{1,0:T(8,128)(2,1)} %refs_1_.7, bf16[16,896]{1,0:T(8,128)(2,1)S(1)} %get-tuple-element.13.after.first), custom_call_target="tpu_custom_call" | custom-call | bytes 3145728 | tf_op jit(solution)/shard_map/load/pallas_call | solution.py:216
  8.1 0.0 collective-permute-done.second
  8.2 0.0 slice-start.5
  8.2 2.9 %collective-permute-start.1 = (bf16[32,896]{1,0:T(8,128)(2,1)S(1)}, bf16[32,896]{1,0:T(8,128)(2,1)S(1)}, u32[]{:S(2)}, u32[]{:S(2)}) collective-permute-start(bf16[32,896]{1,0:T(8,128)(2,1)S(1)} %join.2.after.first), channel_id=1, source_target_pairs={{0,8},{4,12},{8,0},{12,4},{1,9},{5,13},{9,1},{13,5},{2,10},{6,14},... | collective-permute-start | bytes 172040 | tf_op jit(solution)/shard_map/ppermute | solution.py:420
  11.0 0.0 slice-start
  11.0 0.0 slice-start.1
  11.0 2.0 %load.3.refs_0_.refs_4_ = bf16[768,2048]{1,0:T(8,128)(2,1)S(1)} custom-call(bf16[3072,2048]{1,0:T(8,128)(2,1)} %refs_1_.7, bf16[32,896]{1,0:T(8,128)(2,1)S(1)} %join.2.after.first), custom_call_target="tpu_custom_call" | custom-call | bytes 3145728 | tf_op jit(solution)/shard_map/load/pallas_call | solution.py:216
  13.1 0.0 slice-start.2
  13.1 0.0 copy-start
  13.1 0.2 collective-permute-done.1.second
  13.3 0.0 slice-done.3
  13.3 0.0 slice-done.4
  13.3 0.0 slice-done.5
  13.4 1.8 %collective-permute-start.2 = (bf16[64,896]{1,0:T(8,128)(2,1)S(1)}, bf16[64,896]{1,0:T(8,128)(2,1)S(1)}, u32[]{:S(2)}, u32[]{:S(2)}) collective-permute-start(bf16[64,896]{1,0:T(8,128)(2,1)S(1)} %join.3.block.refs_0_), channel_id=1, source_target_pairs={{0,2},{1,3},{2,0},{3,1},{4,6},{5,7},{6,4},{7,5},{8,10},{9,11},{10,... | collective-permute-start | bytes 344072 | tf_op jit(solution)/shard_map/ppermute | solution.py:420
  15.1 0.0 collective-permute-start.3
  15.1 0.0 slice-done
  15.1 0.5 %slice-done.1 = s8[4194304]{0:T(1024)(128)(4,1)S(1)} async-done(((s8[12582912]{0:T(1024)(128)(4,1)}), s8[4194304]{0:T(1024)(128)(4,1)S(1)}, s32[]{:S(2)}) %slice-start.1) | async-done | bytes 4194328
  15.6 1.2 %slice-done.2 = s8[4194304]{0:T(1024)(128)(4,1)S(1)} async-done(((s8[12582912]{0:T(1024)(128)(4,1)}), s8[4194304]{0:T(1024)(128)(4,1)S(1)}, s32[]{:S(2)}) %slice-start.2) | async-done | bytes 4194328
  16.8 0.0 copy-done
  16.8 1.9 %partial.2 = (f32[2,64,2048]{2,1,0:T(8,128)S(1)}, bf16[768,2048]{1,0:T(8,128)(2,1)S(1)}) custom-call(bf16[64,896]{1,0:T(8,128)(2,1)S(1)} %join.3.block.refs_0_, bf16[768,2048]{1,0:T(8,128)(2,1)S(1)} %get-tuple-element.14.gate_part, bf16[3072,2048]{1,0:T(8,128)(2,1)S(1)} %bitcast.13, bf16[3072,2048]{1,0:T(8,128)(2,1)} %refs_1_.7, ...), custom_call_target="tpu_custom_call" | custom-call | flops 402653184 | bytes 3145728 | tf_op jit(solution)/shard_map/partial/pallas_call | solution.py:260
  18.7 0.0 collective-permute-done.2.array
  18.7 0.1 collective-permute-start.4
  18.8 1.3 %partial.3.sums = f32[2,64,2048]{2,1,0:T(8,128)S(1)} custom-call(bf16[64,896]{1,0:T(8,128)(2,1)S(1)} %tie.1.block.refs_1_, bf16[768,2048]{1,0:T(8,128)(2,1)S(1)} %load.2.refs_0_.gate_part, bf16[3072,2048]{1,0:T(8,128)(2,1)S(1)} %bitcast.13, f32[2,64,2048]{2,1,0:T(8,128)S(1)} %get-tuple-element.15.after.refs_0_, bf16[3072,2048]{1,0:T(8,128)(2,1)} %refs_1_.7), custom_call_target="tpu_custom_call" | custom-call | flops 402653184 | bytes 3145728 | tf_op jit(solution)/shard_map/partial/pallas_call | solution.py:260
  20.2 0.0 collective-permute-done.3.refs_2_
  20.2 0.0 collective-permute-done.4.refs_3_
  20.2 3.1 %experts.1 = (bf16[2,64,768]{2,1,0:T(8,128)(2,1)S(1)}, bf16[64,2048]{1,0:T(8,128)(2,1)S(1)}) custom-call(f32[2,64,2048]{2,1,0:T(8,128)S(1)} %partial.3.sums, bf16[64,896]{1,0:T(8,128)(2,1)S(1)} %join.3.block.refs_0_, bf16[64,896]{1,0:T(8,128)(2,1)S(1)} %tie.1.block.refs_1_, bf16[64,896]{1,0:T(8,128)(2,1)S(1)} %collective-permute-done.3.refs_2_, ...), custom_call_target="tpu_custom_call" | custom-call | flops 1207959552 | tf_op jit(solution)/shard_map/experts/pallas_call | solution.py:345
  23.3 0.5 %collective-permute-start.5 = (bf16[2,64,768]{2,1,0:T(8,128)(2,1)S(1)}, bf16[2,64,768]{2,1,0:T(8,128)(2,1)S(1)}, u32[]{:S(2)}, u32[]{:S(2)}) collective-permute-start(bf16[2,64,768]{2,1,0:T(8,128)(2,1)S(1)} %get-tuple-element.18.after), channel_id=1, source_target_pairs={{0,1},{1,0},{2,3},{3,2},{4,5},{5,4},{6,7},{7,6},{8,9},{9,8},{10,11... | collective-permute-start | bytes 589832 | tf_op jit(solution)/shard_map/ppermute | solution.py:420
  23.8 0.7 %down.2 = f32[1,64,768]{2,1,0:T(8,128)S(1)} custom-call(bf16[64,2048]{1,0:T(8,128)(2,1)S(1)} %get-tuple-element.17.active, bf16[2048,3072]{1,0:T(8,128)(2,1)S(1)} %bitcast.11, bf16[2,64,768]{2,1,0:T(8,128)(2,1)S(1)} %get-tuple-element.18.after), custom_call_target="tpu_custom_call" | custom-call | flops 201326592 | tf_op jit(solution)/shard_map/down/pallas_call | solution.py:369
  24.5 0.4 collective-permute-done.5
  24.9 1.6 %collective-permute-start.6 = (bf16[1,64,768]{2,1,0:T(8,128)(2,1)S(1)}, bf16[1,64,768]{2,1,0:T(8,128)(2,1)S(1)}, u32[]{:S(2)}, u32[]{:S(2)}) collective-permute-start(bf16[1,64,768]{2,1,0:T(8,128)(2,1)S(1)} %add_convert_fusion.after), channel_id=1, source_target_pairs={{0,2},{1,3},{2,0},{3,1},{4,6},{5,7},{6,4},{7,5},{8,10},{9,11},{10,... | collective-permute-start | bytes 294920 | tf_op jit(solution)/shard_map/ppermute | solution.py:420
  26.5 0.7 %down.3 = f32[1,64,768]{2,1,0:T(8,128)S(1)} custom-call(bf16[64,2048]{1,0:T(8,128)(2,1)S(1)} %get-tuple-element.17.active, bf16[2048,3072]{1,0:T(8,128)(2,1)S(1)} %bitcast.11, bf16[1,64,768]{2,1,0:T(8,128)(2,1)S(1)} %add_convert_fusion.after), custom_call_target="tpu_custom_call" | custom-call | flops 201326592 | tf_op jit(solution)/shard_map/down/pallas_call | solution.py:369
  27.2 2.9 %collective-permute-done.6 = bf16[1,64,768]{2,1,0:T(8,128)(2,1)S(1)} collective-permute-done((bf16[1,64,768]{2,1,0:T(8,128)(2,1)S(1)}, bf16[1,64,768]{2,1,0:T(8,128)(2,1)S(1)}, u32[]{:S(2)}, u32[]{:S(2)}) %collective-permute-start.6) | collective-permute-done | bytes 98336 | tf_op jit(solution)/shard_map/ppermute | solution.py:420
  30.1 1.7 %collective-permute-start.7 = (bf16[2,16,768]{2,1,0:T(8,128)(2,1)S(1)}, bf16[2,16,768]{2,1,0:T(8,128)(2,1)S(1)}, u32[]{:S(2)}, u32[]{:S(2)}) collective-permute-start(bf16[2,16,768]{2,1,0:T(8,128)(2,1)S(1)} %slice.25), channel_id=1, source_target_pairs={{0,4},{4,0},{8,12},{12,8},{1,5},{5,1},{9,13},{13,9},{2,6},{6,2},{1... | collective-permute-start | bytes 147464 | tf_op jit(solution)/shard_map/ppermute | solution.py:420
  31.9 2.4 %collective-permute-done.7 = bf16[2,16,768]{2,1,0:T(8,128)(2,1)S(1)} collective-permute-done((bf16[2,16,768]{2,1,0:T(8,128)(2,1)S(1)}, bf16[2,16,768]{2,1,0:T(8,128)(2,1)S(1)}, u32[]{:S(2)}, u32[]{:S(2)}) %collective-permute-start.7) | collective-permute-done | bytes 49184 | tf_op jit(solution)/shard_map/ppermute | solution.py:420
  34.3 2.3 %collective-permute-start.8 = (bf16[1,16,768]{2,1,0:T(8,128)(2,1)S(1)}, bf16[1,16,768]{2,1,0:T(8,128)(2,1)S(1)}, u32[]{:S(2)}, u32[]{:S(2)}) collective-permute-start(bf16[1,16,768]{2,1,0:T(8,128)(2,1)S(1)} %slice.43), channel_id=1, source_target_pairs={{0,8},{4,12},{8,0},{12,4},{1,9},{5,13},{9,1},{13,5},{2,10},{6,14},... | collective-permute-start | bytes 73736 | tf_op jit(solution)/shard_map/ppermute | solution.py:420
  36.7 2.5 %collective-permute-done.8 = bf16[1,16,768]{2,1,0:T(8,128)(2,1)S(1)} collective-permute-done((bf16[1,16,768]{2,1,0:T(8,128)(2,1)S(1)}, bf16[1,16,768]{2,1,0:T(8,128)(2,1)S(1)}, u32[]{:S(2)}, u32[]{:S(2)}) %collective-permute-start.8) | collective-permute-done | bytes 24608 | tf_op jit(solution)/shard_map/ppermute | solution.py:420
  39.1 0.6 %fusion.2 = bf16[16,768]{1,0:T(8,128)(2,1)} fusion(f32[2,16,768]{2,1,0:T(8,128)S(1)} %convert_add_fusion.1, bf16[1,16,768]{2,1,0:T(8,128)(2,1)S(1)} %collective-permute-done.8, bf16[16,768]{1,0:T(8,128)(2,1)S(1)} %get-tuple-element.12), kind=kLoop, calls=%fused_computation.7 | loop fusion | flops 61440 | bytes 122880 | tf_op jit(solution)/shard_map/convert_element_type | solution.py:522
  (11 shorter events, 0.1 us)
Async XLA Ops:
  3.0 5.2 %collective-permute-start = (bf16[16,896]{1,0:T(8,128)(2,1)S(1)}, bf16[16,896]{1,0:T(8,128)(2,1)S(1)}, u32[]{:S(2)}, u32[]{:S(2)}) collective-permute-start(bf16[16,896]{1,0:T(8,128)(2,1)S(1)} %get-tuple-element.13.after.first), channel_id=1, source_target_pairs={{0,4},{4,0},{8,12},{12,8},{1,5},{5,1},{9,13},{13,9},{2,6},{6,2},{1... | collective-permute-start | bytes 86024 | tf_op jit(solution)/shard_map/ppermute | solution.py:420
  6.1 7.2 %slice-start.3 = ((s8[12582912]{0:T(1024)(128)(4,1)}), s8[4194304]{0:T(1024)(128)(4,1)S(1)}, s32[]{:S(2)}) async-start(s8[12582912]{0:T(1024)(128)(4,1)} %bitcast.12), calls=%async_computation.3 | async-start | bytes 8388608
  6.1 7.2 %slice-start.4 = ((s8[12582912]{0:T(1024)(128)(4,1)}), s8[4194304]{0:T(1024)(128)(4,1)S(1)}, s32[]{:S(2)}) async-start(s8[12582912]{0:T(1024)(128)(4,1)} %bitcast.12), calls=%async_computation.4 | async-start | bytes 8388608
  8.2 5.2 %slice-start.5 = ((s8[12582912]{0:T(1024)(128)(4,1)}), s8[4194304]{0:T(1024)(128)(4,1)S(1)}, s32[]{:S(2)}) async-start(s8[12582912]{0:T(1024)(128)(4,1)} %bitcast.12), calls=%async_computation.5 | async-start | bytes 8388608
  8.2 5.1 %collective-permute-start.1 = (bf16[32,896]{1,0:T(8,128)(2,1)S(1)}, bf16[32,896]{1,0:T(8,128)(2,1)S(1)}, u32[]{:S(2)}, u32[]{:S(2)}) collective-permute-start(bf16[32,896]{1,0:T(8,128)(2,1)S(1)} %join.2.after.first), channel_id=1, source_target_pairs={{0,8},{4,12},{8,0},{12,4},{1,9},{5,13},{9,1},{13,5},{2,10},{6,14},... | collective-permute-start | bytes 172040 | tf_op jit(solution)/shard_map/ppermute | solution.py:420
  11.0 4.1 %slice-start = ((s8[12582912]{0:T(1024)(128)(4,1)}), s8[4194304]{0:T(1024)(128)(4,1)S(1)}, s32[]{:S(2)}) async-start(s8[12582912]{0:T(1024)(128)(4,1)} %bitcast.10), calls=%async_computation | async-start | bytes 8388608
  11.0 4.5 %slice-start.1 = ((s8[12582912]{0:T(1024)(128)(4,1)}), s8[4194304]{0:T(1024)(128)(4,1)S(1)}, s32[]{:S(2)}) async-start(s8[12582912]{0:T(1024)(128)(4,1)} %bitcast.10), calls=%async_computation.1 | async-start | bytes 8388608
  13.1 3.7 %slice-start.2 = ((s8[12582912]{0:T(1024)(128)(4,1)}), s8[4194304]{0:T(1024)(128)(4,1)S(1)}, s32[]{:S(2)}) async-start(s8[12582912]{0:T(1024)(128)(4,1)} %bitcast.10), calls=%async_computation.2 | async-start | bytes 8388608
  13.1 3.7 %copy-start = (bf16[128,2048]{1,0:T(8,128)(2,1)S(1)}, bf16[128,2048]{1,0:T(8,128)(2,1)}, u32[]{:S(2)}) copy-start(bf16[128,2048]{1,0:T(8,128)(2,1)} %refs_8_.3) | copy-start | bytes 1572868
  13.4 5.4 %collective-permute-start.2 = (bf16[64,896]{1,0:T(8,128)(2,1)S(1)}, bf16[64,896]{1,0:T(8,128)(2,1)S(1)}, u32[]{:S(2)}, u32[]{:S(2)}) collective-permute-start(bf16[64,896]{1,0:T(8,128)(2,1)S(1)} %join.3.block.refs_0_), channel_id=1, source_target_pairs={{0,2},{1,3},{2,0},{3,1},{4,6},{5,7},{6,4},{7,5},{8,10},{9,11},{10,... | collective-permute-start | bytes 344072 | tf_op jit(solution)/shard_map/ppermute | solution.py:420
  15.1 5.0 %collective-permute-start.3 = (bf16[64,896]{1,0:T(8,128)(2,1)S(1)}, bf16[64,896]{1,0:T(8,128)(2,1)S(1)}, u32[]{:S(2)}, u32[]{:S(2)}) collective-permute-start(bf16[64,896]{1,0:T(8,128)(2,1)S(1)} %join.3.block.refs_0_), channel_id=1, source_target_pairs={{0,1},{1,0},{2,3},{3,2},{4,5},{5,4},{6,7},{7,6},{8,9},{9,8},{10,11... | collective-permute-start | bytes 344072 | tf_op jit(solution)/shard_map/ppermute | solution.py:420
  18.7 1.4 %collective-permute-start.4 = (bf16[64,896]{1,0:T(8,128)(2,1)S(1)}, bf16[64,896]{1,0:T(8,128)(2,1)S(1)}, u32[]{:S(2)}, u32[]{:S(2)}) collective-permute-start(bf16[64,896]{1,0:T(8,128)(2,1)S(1)} %tie.1.block.refs_1_), channel_id=1, source_target_pairs={{0,1},{1,0},{2,3},{3,2},{4,5},{5,4},{6,7},{7,6},{8,9},{9,8},{10,11... | collective-permute-start | bytes 344072 | tf_op jit(solution)/shard_map/ppermute | solution.py:420
  23.3 1.6 %collective-permute-start.5 = (bf16[2,64,768]{2,1,0:T(8,128)(2,1)S(1)}, bf16[2,64,768]{2,1,0:T(8,128)(2,1)S(1)}, u32[]{:S(2)}, u32[]{:S(2)}) collective-permute-start(bf16[2,64,768]{2,1,0:T(8,128)(2,1)S(1)} %get-tuple-element.18.after), channel_id=1, source_target_pairs={{0,1},{1,0},{2,3},{3,2},{4,5},{5,4},{6,7},{7,6},{8,9},{9,8},{10,11... | collective-permute-start | bytes 589832 | tf_op jit(solution)/shard_map/ppermute | solution.py:420
  24.9 5.1 %collective-permute-start.6 = (bf16[1,64,768]{2,1,0:T(8,128)(2,1)S(1)}, bf16[1,64,768]{2,1,0:T(8,128)(2,1)S(1)}, u32[]{:S(2)}, u32[]{:S(2)}) collective-permute-start(bf16[1,64,768]{2,1,0:T(8,128)(2,1)S(1)} %add_convert_fusion.after), channel_id=1, source_target_pairs={{0,2},{1,3},{2,0},{3,1},{4,6},{5,7},{6,4},{7,5},{8,10},{9,11},{10,... | collective-permute-start | bytes 294920 | tf_op jit(solution)/shard_map/ppermute | solution.py:420
  30.1 4.2 %collective-permute-start.7 = (bf16[2,16,768]{2,1,0:T(8,128)(2,1)S(1)}, bf16[2,16,768]{2,1,0:T(8,128)(2,1)S(1)}, u32[]{:S(2)}, u32[]{:S(2)}) collective-permute-start(bf16[2,16,768]{2,1,0:T(8,128)(2,1)S(1)} %slice.25), channel_id=1, source_target_pairs={{0,4},{4,0},{8,12},{12,8},{1,5},{5,1},{9,13},{13,9},{2,6},{6,2},{1... | collective-permute-start | bytes 147464 | tf_op jit(solution)/shard_map/ppermute | solution.py:420
  34.3 4.8 %collective-permute-start.8 = (bf16[1,16,768]{2,1,0:T(8,128)(2,1)S(1)}, bf16[1,16,768]{2,1,0:T(8,128)(2,1)S(1)}, u32[]{:S(2)}, u32[]{:S(2)}) collective-permute-start(bf16[1,16,768]{2,1,0:T(8,128)(2,1)S(1)} %slice.43), channel_id=1, source_target_pairs={{0,8},{4,12},{8,0},{12,4},{1,9},{5,13},{9,1},{13,5},{2,10},{6,14},... | collective-permute-start | bytes 73736 | tf_op jit(solution)/shard_map/ppermute | solution.py:420

commit v7 on v6

--- a/solution.py
+++ b/solution.py
@@ -41,27 +41,16 @@
     return pl.ds(pl.multiple_of((lax.axis_index("tp") ^ distance) * size, size), size)
 
 
-def fetch(gate_weight, distance, part, arrived):
-    copy = pltpu.make_async_copy(
-        gate_weight.at[at_distance(distance, part.shape[0]), :], part, arrived
-    )
-    copy.start()
-    return copy
-
-
 def attend_kernel(*refs):
     count = 12
-    sources, gate_weight, outs, part = refs[:count], refs[count], refs[count + 1 : count + 3], refs[count + 3]
-    buffers, arrived, part_arrived = refs[count + 4 : -2], refs[-2], refs[-1]
+    sources, outs, buffers, arrived = refs[:count], refs[count : count + 2], refs[count + 2 : -1], refs[-1]
     copies = [
         pltpu.make_async_copy(source, buffer, arrived.at[i])
         for i, (source, buffer) in enumerate(zip(sources, buffers, strict=True))
     ]
     for i in (7, 4, 0, 5, 8, 6, 3, 9, 1, 2, 10, 11):
         copies[i].start()
-    fetched = fetch(gate_weight, 0, part, part_arrived)
     attend_body(*buffers, *outs, wait=lambda *which: [copies[i].wait() for i in which])
-    fetched.wait()
 
 
 def attend_body(
@@ -183,89 +172,82 @@
     payload_out[:, features:] = tail.astype(BF16)
 
 
-def attend(args, gate_weight):
+def attend(args):
     rows, features = args[3].shape
     return pl.pallas_call(
         attend_kernel,
         out_shape=(
             jax.ShapeDtypeStruct((rows, features), BF16),
             jax.ShapeDtypeStruct((rows, features + LANES), BF16),
-            jax.ShapeDtypeStruct((features, gate_weight.shape[1]), BF16),
-        ),
-        in_specs=[HBM] * (len(args) + 1),
-        out_specs=(VMEM,) * 3,
+        ),
+        in_specs=[HBM] * len(args),
+        out_specs=(VMEM,) * 2,
         scratch_shapes=[
             (pltpu.SMEM if i < 3 else pltpu.VMEM)(arg.shape, arg.dtype)
             for i, arg in enumerate(args)
         ]
-        + [pltpu.SemaphoreType.DMA((len(args),)), pltpu.SemaphoreType.DMA],
+        + [pltpu.SemaphoreType.DMA((len(args),))],
         compiler_params=pltpu.CompilerParams(vmem_limit_bytes=6 * 2**20),
         cost_estimate=pl.CostEstimate(
-            flops=200_000_000, bytes_accessed=6_000_000, transcendentals=20_000
+            flops=200_000_000, bytes_accessed=3_000_000, transcendentals=20_000
         ),
         name="attend",
-    )(*in_hbm(*args, gate_weight))
-
-
-def load_kernel(distance, gate_weight, after, part, arrived):
-    fetch(gate_weight, distance, part, arrived).wait()
-
-
-def load(gate_weight, distance, features, after):
-    hidden = gate_weight.shape[1]
-    return pl.pallas_call(
-        functools.partial(load_kernel, distance),
-        out_shape=jax.ShapeDtypeStruct((features, hidden), BF16),
-        in_specs=[HBM] * 2,
-        out_specs=VMEM,
-        scratch_shapes=[pltpu.SemaphoreType.DMA],
-        compiler_params=pltpu.CompilerParams(vmem_limit_bytes=2**20),
-        cost_estimate=pl.CostEstimate(
-            flops=0, bytes_accessed=2 * features * hidden, transcendentals=0
-        ),
-        name="load",
-    )(*in_hbm(gate_weight), after)
+    )(*in_hbm(*args))
+
+
+def fetch(down_weight, distances, parts, arrived):
+    copies = [
+        pltpu.make_async_copy(
+            down_weight.at[:, at_distance(distance, part.shape[1])], part, arrived.at[i]
+        )
+        for i, (distance, part) in enumerate(zip(distances, parts, strict=True))
+    ]
+    for copy in copies:
+        copy.start()
+    return copies
 
 
 def halves(hidden):
     return hidden // 2 if hidden % (2 * LANES) == 0 else hidden
 
 
-def partial_kernel(distance, fetched, first, soon, block, gate_part, up_weight, *refs):
-    features, hidden = gate_part.shape
+def partial_kernel(distance, fetched, first, soon, block, gate_weight, up_weight, *refs):
+    hidden = gate_weight.shape[1]
+    features = block.shape[1] - LANES
     sums, refs = (None, refs) if first else (refs[0], refs[1:])
-    gate_weight, totals = refs[0], refs[1 + soon]
-    copy = None if fetched is None else fetch(gate_weight, fetched, refs[2 + soon], refs[-1])
+    down_weight, totals = refs[0], refs[1 + soon]
+    copies = fetch(down_weight, fetched, refs[2 + soon : -1], refs[-1])
     tile = halves(hidden)
     depth = at_distance(distance, features)
 
     def products(n, carry):
         lanes = pl.ds(pl.multiple_of(n * tile, tile), tile)
-        for i, part in enumerate((gate_part[:, lanes], up_weight[depth, lanes])):
-            product = jnp.dot(block[:, :features], part, preferred_element_type=F32)
+        for i, weight in enumerate((gate_weight, up_weight)):
+            product = jnp.dot(
+                block[:, :features], weight[depth, lanes], preferred_element_type=F32
+            )
             totals[i, :, lanes] = product if first else sums[i, :, lanes] + product
         return carry
 
     lax.fori_loop(0, hidden // tile, products, 0)
-    if copy is not None:
+    for copy in copies:
         copy.wait()
 
 
-def partial(block, distance, part, sums, gate_weight, up_weight, fetched, soon):
+def partial(block, distance, sums, gate_weight, up_weight, down_weight, fetched, soon):
     rows, width = block.shape
     features = width - LANES
     hidden = gate_weight.shape[1]
     first = sums is None
-    more = int(fetched is not None)
     return pl.pallas_call(
         functools.partial(partial_kernel, distance, fetched, first, len(soon)),
         out_shape=(
             jax.ShapeDtypeStruct((2, rows, hidden), F32),
-            *[jax.ShapeDtypeStruct((features, hidden), BF16)] * more,
+            *[jax.ShapeDtypeStruct((hidden, features), BF16)] * len(fetched),
         ),
         in_specs=[VMEM] * (3 if first else 4) + [HBM] * (1 + len(soon)),
-        out_specs=(VMEM,) * (1 + more),
-        scratch_shapes=[pltpu.SemaphoreType.DMA],
+        out_specs=(VMEM,) * (1 + len(fetched)),
+        scratch_shapes=[pltpu.SemaphoreType.DMA((max(1, len(fetched)),))],
         compiler_params=pltpu.CompilerParams(vmem_limit_bytes=3 * 2**20),
         cost_estimate=pl.CostEstimate(
             flops=4 * rows * features * hidden,
@@ -273,112 +255,136 @@
             transcendentals=0,
         ),
         name="partial",
-    )(block, part, up_weight, *(() if first else (sums,)), *in_hbm(gate_weight), *soon)
-
-
-def expert_kernel(replicas, targets, order, known, sums, *refs):
+    )(block, gate_weight, up_weight, *(() if first else (sums,)), *in_hbm(down_weight), *soon)
+
+
+def expert_kernel(replicas, late, following, order, known, early, sums, *refs):
     tensor_devices = len(order)
-    blocks, parts = refs[:tensor_devices], refs[tensor_devices : 2 * tensor_devices - known]
-    up_weight, down_weight, adapter_up, out, active = refs[2 * tensor_devices - known :]
+    blocks, refs = refs[:tensor_devices], refs[tensor_devices:]
+    gate_weight, up_weight, adapter_up, refs = *refs[:3], refs[3:]
+    early_parts, refs = refs[:early], refs[early:]
+    down_weight, out, active, refs = *refs[:3], refs[3:]
+    next_parts, late_parts, arrived = refs[: len(following)], refs[len(following) : -1], refs[-1]
     rows, width = blocks[0].shape
     features = width - LANES
     hidden = active.shape[1]
-    expert = lax.axis_index("ep") // replicas
-    tail = jnp.zeros((rows, LANES), F32)
-    for block in blocks:
-        tail = tail + block[:, features:].astype(F32)
-    place = lambda k: tail[:, k : k + 1]
-    here = blocks[0][:, features:].astype(F32)
-    inverse_rms = lax.rsqrt(
-        (place(SQ_HI) + place(SQ_LO)) / (features * tensor_devices) + 1e-05
-    )
-    diff = (place(DIFF_HI) + place(DIFF_LO)) * inverse_rms
-    expert_float = expert.astype(F32)
-    is_first = here[:, FIRST : FIRST + 1] == expert_float
-    is_second = here[:, SECOND : SECOND + 1] == expert_float
-    weight = jnp.where(
-        is_first, jax.nn.sigmoid(diff), jnp.where(is_second, jax.nn.sigmoid(-diff), 0.0)
-    )
-    lowrank = (tail * inverse_rms).astype(BF16)
-    spread_shape = (LANES, TENANT_COUNT * ADAPTER_RANK)
-    source = lax.broadcasted_iota(jnp.int32, spread_shape, 0)
-    target = lax.broadcasted_iota(jnp.int32, spread_shape, 1)
-    spread = jnp.where(
-        source == expert * ADAPTER_RANK + lax.rem(target, jnp.int32(ADAPTER_RANK)), 1.0, 0.0
-    ).astype(BF16)
-    lane = lax.broadcasted_iota(jnp.int32, (rows, TENANT_COUNT * ADAPTER_RANK), 1)
-    own_tenant = (lane // ADAPTER_RANK).astype(F32) == here[:, TENANT : TENANT + 1]
-    adapter_rows = jnp.where(
-        own_tenant, jnp.dot(lowrank, spread, preferred_element_type=F32), 0.0
-    ).astype(BF16)
+    copies = fetch(down_weight, late + following, (*late_parts, *next_parts), arrived)
     tile = halves(hidden)
-    for start in range(0, hidden, tile):
-        lanes = slice(start, start + tile)
-        gate, up = sums[0, :, lanes], sums[1, :, lanes]
-        for block, part, distance in zip(blocks[known:], parts, order[known:], strict=True):
-            scaled = block[:, :features]
-            gate = gate + jnp.dot(scaled, part[:, lanes], preferred_element_type=F32)
-            up = up + jnp.dot(
-                scaled,
-                up_weight[at_distance(distance, features), lanes],
-                preferred_element_type=F32,
+
+    @pl.when(lax.axis_index("tp") >= 0)
+    def _():
+        expert = lax.axis_index("ep") // replicas
+        tail = jnp.zeros((rows, LANES), F32)
+        for block in blocks:
+            tail = tail + block[:, features:].astype(F32)
+        place = lambda k: tail[:, k : k + 1]
+        here = blocks[0][:, features:].astype(F32)
+        inverse_rms = lax.rsqrt(
+            (place(SQ_HI) + place(SQ_LO)) / (features * tensor_devices) + 1e-05
+        )
+        diff = (place(DIFF_HI) + place(DIFF_LO)) * inverse_rms
+        expert_float = expert.astype(F32)
+        is_first = here[:, FIRST : FIRST + 1] == expert_float
+        is_second = here[:, SECOND : SECOND + 1] == expert_float
+        weight = jnp.where(
+            is_first, jax.nn.sigmoid(diff), jnp.where(is_second, jax.nn.sigmoid(-diff), 0.0)
+        )
+        lowrank = (tail * inverse_rms).astype(BF16)
+        spread_shape = (LANES, TENANT_COUNT * ADAPTER_RANK)
+        source = lax.broadcasted_iota(jnp.int32, spread_shape, 0)
+        target = lax.broadcasted_iota(jnp.int32, spread_shape, 1)
+        spread = jnp.where(
+            source == expert * ADAPTER_RANK + lax.rem(target, jnp.int32(ADAPTER_RANK)), 1.0, 0.0
+        ).astype(BF16)
+        lane = lax.broadcasted_iota(jnp.int32, (rows, TENANT_COUNT * ADAPTER_RANK), 1)
+        own_tenant = (lane // ADAPTER_RANK).astype(F32) == here[:, TENANT : TENANT + 1]
+        adapter_rows = jnp.where(
+            own_tenant, jnp.dot(lowrank, spread, preferred_element_type=F32), 0.0
+        ).astype(BF16)
+        for start in range(0, hidden, tile):
+            lanes = slice(start, start + tile)
+            gate, up = sums[0, :, lanes], sums[1, :, lanes]
+            for block, distance in zip(blocks[known:], order[known:], strict=True):
+                scaled = block[:, :features]
+                depth = at_distance(distance, features)
+                gate = gate + jnp.dot(
+                    scaled, gate_weight[depth, lanes], preferred_element_type=F32
+                )
+                up = up + jnp.dot(scaled, up_weight[depth, lanes], preferred_element_type=F32)
+            gate = gate * inverse_rms
+            up = up * inverse_rms + jnp.dot(
+                adapter_rows, adapter_up[:, lanes], preferred_element_type=F32
             )
-        gate = gate * inverse_rms
-        up = up * inverse_rms + jnp.dot(
-            adapter_rows, adapter_up[:, lanes], preferred_element_type=F32
-        )
-        active[:, lanes] = (gate * jax.nn.sigmoid(gate) * up * weight).astype(BF16)
-    down_products(targets, active, down_weight, out)
-
-
-def down_products(targets, active, down_weight, out):
-    for i, distance in enumerate(targets):
-        lanes = at_distance(distance, out.shape[2])
-        out[i] = jnp.dot(
-            active[...], down_weight[:, lanes], preferred_element_type=F32
-        ).astype(out.dtype)
-
-
-def experts(replicas, targets, order, sums, known, blocks, parts, up_weight, down_weight, adapter_up):
+            active[:, lanes] = (gate * jax.nn.sigmoid(gate) * up * weight).astype(BF16)
+        for i, part in enumerate((*early_parts, *late_parts)):
+            if i >= early:
+                copies[i - early].wait()
+            out[i] = jnp.dot(active[...], part[...], preferred_element_type=F32).astype(out.dtype)
+
+    for copy in copies[len(late) :]:
+        copy.wait()
+
+
+def experts(
+    replicas, late, following, order, sums, known, blocks, gate_weight, up_weight, adapter_up, parts, down_weight
+):
     rows, width = blocks[0].shape
     features, hidden = width - LANES, sums.shape[2]
-    return pl.pallas_call(
-        functools.partial(expert_kernel, replicas, targets, order, known),
+    count = len(parts) + len(late)
+    columns = (hidden, features)
+    return pl.pallas_call(
+        functools.partial(expert_kernel, replicas, late, following, order, known, len(parts)),
         out_shape=(
-            jax.ShapeDtypeStruct((len(targets), rows, features), BF16),
+            jax.ShapeDtypeStruct((count, rows, features), BF16),
             jax.ShapeDtypeStruct((rows, hidden), BF16),
-        ),
-        in_specs=[VMEM] * (4 + len(blocks) + len(parts)),
-        out_specs=(VMEM, VMEM),
-        compiler_params=pltpu.CompilerParams(vmem_limit_bytes=4 * 2**20),
+            *[jax.ShapeDtypeStruct(columns, BF16)] * len(following),
+        ),
+        in_specs=[VMEM] * (4 + len(blocks) + len(parts)) + [HBM],
+        out_specs=(VMEM,) * (2 + len(following)),
+        scratch_shapes=[pltpu.VMEM(columns, BF16)] * len(late)
+        + [pltpu.SemaphoreType.DMA((len(late) + len(following),))],
+        compiler_params=pltpu.CompilerParams(vmem_limit_bytes=5 * 2**20),
         cost_estimate=pl.CostEstimate(
-            flops=2 * rows * hidden * features * (2 * len(parts) + len(targets)),
-            bytes_accessed=0,
+            flops=2 * rows * hidden * features * (2 * (len(blocks) - known) + count),
+            bytes_accessed=2 * hidden * features * (len(late) + len(following)),
             transcendentals=0,
         ),
         name="experts",
-    )(sums, *blocks, *parts, up_weight, down_weight, adapter_up)
-
-
-def down_kernel(targets, active, down_weight, after, out):
-    down_products(targets, active, down_weight, out)
-
-
-def down(targets, active, down_weight, features, after):
+    )(sums, *blocks, gate_weight, up_weight, adapter_up, *parts, *in_hbm(down_weight))
+
+
+def down_kernel(active, after, *refs):
+    *parts, out = refs
+    for i, part in enumerate(parts):
+        out[i] = jnp.dot(active[...], part[...], preferred_element_type=F32)
+
+
+def down_fetching_kernel(targets, active, after, down_weight, out, *refs):
+    parts, arrived = refs[:-1], refs[-1]
+    for i, copy in enumerate(fetch(down_weight, targets, parts, arrived)):
+        copy.wait()
+        out[i] = jnp.dot(active[...], parts[i][...], preferred_element_type=F32)
+
+
+def down(targets, active, parts, down_weight, features, after):
     rows, hidden = active.shape
-    return pl.pallas_call(
-        functools.partial(down_kernel, targets),
-        out_shape=jax.ShapeDtypeStruct((len(targets), rows, features), F32),
-        in_specs=[VMEM, VMEM, HBM],
+    count = len(targets)
+    columns = pltpu.VMEM((hidden, features), BF16)
+    scratch = () if parts else (*[columns] * count, pltpu.SemaphoreType.DMA((count,)))
+    return pl.pallas_call(
+        down_kernel if parts else functools.partial(down_fetching_kernel, targets),
+        out_shape=jax.ShapeDtypeStruct((count, rows, features), F32),
+        in_specs=[VMEM, HBM] + ([VMEM] * count if parts else [HBM]),
         out_specs=VMEM,
-        compiler_params=pltpu.CompilerParams(vmem_limit_bytes=4 * 2**20),
+        scratch_shapes=scratch,
+        compiler_params=pltpu.CompilerParams(vmem_limit_bytes=5 * 2**20),
         cost_estimate=pl.CostEstimate(
-            flops=2 * rows * hidden * features * len(targets),
-            bytes_accessed=0,
+            flops=2 * rows * hidden * features * count,
+            bytes_accessed=2 * hidden * features * count,
             transcendentals=0,
         ),
         name="down",
-    )(active, down_weight, after)
+    )(active, after, *(parts if parts else in_hbm(down_weight)))
 
 
 def join_kernel(first, second, *refs):
@@ -397,6 +403,21 @@
         compiler_params=pltpu.CompilerParams(vmem_limit_bytes=1 * 2**20),
         name="join",
     )(first, second, *after)
+
+
+def mark_kernel(after, weight, out):
+    out[...] = jnp.zeros_like(out)
+
+
+def mark(after, weight):
+    return pl.pallas_call(
+        mark_kernel,
+        out_shape=jax.ShapeDtypeStruct((8, LANES), F32),
+        in_specs=[HBM, HBM],
+        out_specs=VMEM,
+        compiler_params=pltpu.CompilerParams(vmem_limit_bytes=2**20),
+        name="mark",
+    )(after, *in_hbm(weight))
 
 
 def tie_kernel(array, after, out):
@@ -445,7 +466,7 @@
     rows, features = residual.shape
     expert_devices = lax.axis_size("ep")
     tensor_devices = lax.axis_size("tp")
-    state, held, *parts = attend(
+    state, held = attend(
         (
             lengths,
             tenants,
@@ -460,53 +481,53 @@
             router.T,
             adapter_down_map,
         ),
-        expert_gate_weight,
     )
-    order = [0]
-    for distance in reversed(bits(tensor_devices)):
-        order += [at ^ distance for at in order]
     for distance in bits(expert_devices):
         other = swap(held, "ep", distance)
-        if len(parts) < tensor_devices:
-            parts.append(load(expert_gate_weight, order[len(parts)], features, held))
         last = 2 * distance == expert_devices
-        held = join(held, other, parts[-1], *((expert_up_weight,) if last else ()))
-    blocks, known, sums = [held], 0, None
-    for distance in reversed(bits(tensor_devices)):
+        beside = mark(held, expert_down_weight)
+        held = join(held, other, beside, *((expert_up_weight,) if last else ()))
+    steps = bits(tensor_devices)
+    groups = [tuple(k for k in range(tensor_devices) if k & -k == step) for step in steps] + [(0,)]
+    early, late = groups[0][-1:], groups[0][:-1]
+    blocks, order, known, sums, parts = [held], [0], 0, None, []
+    for distance in reversed(steps):
         others = [swap(block, "tp", distance) for block in blocks]
         for block in blocks[known:]:
-            fetched = order[len(parts)] if len(parts) < tensor_devices else None
             sums, *more = partial(
                 block,
                 order[known],
-                parts[known],
                 sums,
                 expert_gate_weight,
                 expert_up_weight,
-                fetched,
-                (adapter_up_map, expert_down_weight) if not known else (),
+                expert_down_weight,
+                () if known else early,
+                () if known else (expert_gate_weight, adapter_up_map),
             )
             parts += more
             known += 1
         blocks = blocks + [tie(block, sums) if distance > 1 else block for block in others]
-    steps = bits(tensor_devices)
-    groups = [tuple(k for k in range(tensor_devices) if k & -k == step) for step in steps] + [(0,)]
-    sent, active = experts(
+        order = order + [at ^ distance for at in order]
+    sent, active, *parts = experts(
         expert_devices // EXPERT_COUNT,
-        groups[0],
+        late,
+        groups[1],
         tuple(order),
         sums,
         known,
         blocks,
-        parts[known:],
+        expert_gate_weight,
         expert_up_weight,
+        adapter_up_map,
+        parts,
         expert_down_weight,
-        adapter_up_map,
     )
     received = {k: [] for k in range(tensor_devices)}
+    groups[0] = early + late
     for step, group, following in zip(steps, groups[:-1], groups[1:], strict=True):
         arriving = swap(sent, "tp", step)
-        made = down(following, active, expert_down_weight, features, sent)
+        made = down(following, active, parts, expert_down_weight, features, sent)
+        parts = []
         for i, k in enumerate(group):
             received[k ^ step].append(arriving[i])
         kept = [

time: 39.9 us -> 39.5 us (0.990)
  Pallas kernels: 14.8 us -> 12.7 us
  waiting for transfers between devices: 8.35 us -> 10.3 us
  local copies, waits for them, and re-layouts: 1.72 us -> 0.05 us
  starting transfers between devices: 13.9 us -> 15.4 us
    pallas_call x5, Pallas kernels: 8.57 us -> 6.57 us  [the longest x1 3.36 us: experts(): pl.pallas_call(functools.partial(expert_kernel, replicas, late, following...]
    ppermute x9, waiting for transfers between devices: 8.35 us -> 10.3 us  [swap(): return lax.ppermute(x, axis, [(i, i ^ distance) for i in range(count)])]
    unnamed x14, local copies, waits for them, and re-layouts: 1.71 us -> 0.04 us
    ppermute x9, starting transfers between devices: 13.9 us -> 15.4 us  [swap(): return lax.ppermute(x, axis, [(i, i ^ distance) for i in range(count)])]
  transfers between devices with their start and end apart: 9 -> 9, of which waited for: 5 -> 7; matrix products, arithmetic and copies ran while one was open for 0% -> 0% of each run, Pallas kernels for 22% -> 16%
where the time goes in v7:
time: 39.5 us; the launch traced here: 39.3 us
  starting transfers between devices  15.4 us (39%)
  Pallas kernels  12.7 us (32%)
  waiting for transfers between devices  10.3 us (26%)
  other arithmetic  0.71 us (2%)
    ppermute x9, starting transfers between devices, swap(): return lax.ppermute(x, axis, [(i, i ^ distance) for i in range(count)])  15.4 us
    ppermute x9, waiting for transfers between devices, swap(): return lax.ppermute(x, axis, [(i, i ^ distance) for i in range(count)])  10.3 us
    pallas_call x1, Pallas kernels, experts(): pl.pallas_call(functools.partial(expert_kernel, replicas, late, following...  3.36 us
    pallas_call x2, Pallas kernels, partial(): pl.pallas_call(functools.partial(partial_kernel, distance, fetched, first...  3.25 us
    pallas_call x2, Pallas kernels, down(): pl.pallas_call(down_kernel if parts else functools.partial(down_fetching_...  3.21 us
    pallas_call x1, Pallas kernels, attend(): pl.pallas_call(attend_kernel, out_shape=(jax.ShapeDtypeStruct((rows, feat...  2.87 us
  transfers between devices with their start and end apart: 9, of which 7 were waited for; matrix products, arithmetic and copies ran while one was open for 0% of the time, Pallas kernels for 16%

profile of v7, /device:TPU:0, one launch (start us, length us, event | category | flops | bytes accessed | tf_op | source)
XLA Modules:
  0.0 39.3 jit_solution(9710577294362366273)
XLA Ops:
  0.0 0.0 slice-start.3
  0.0 2.9 %attend.1 = (bf16[16,768]{1,0:T(8,128)(2,1)S(1)}, bf16[16,896]{1,0:T(8,128)(2,1)S(1)}) custom-call(s32[16]{0:T(128)} %refs_0_.2, s32[16]{0:T(128)} %refs_1_.4, s32[2,16]{1,0:T(2,128)} %bitcast.18, bf16[16,768]{1,0:T(8,128)(2,1)} %refs_3_.1, bf16[16,768]{1,0:T(8,128)(2,1)} %refs_4_.2, bf16[16,256]{1,0:T(8,128)(2,1)} %refs_5_.2, bf16[16,256]{1,0:T(8,128)(2,1)} %refs_6_.2, ...), custom_call_target="tpu_custom_call" | custom-call | flops 200000000 | bytes 3000000 | tf_op jit(solution)/shard_map/attend/pallas_call | solution.py:177
  2.9 0.0 slice-start
  2.9 0.0 slice-start.1
  2.9 0.0 slice-start.4
  2.9 3.1 %collective-permute-start = (bf16[16,896]{1,0:T(8,128)(2,1)S(1)}, bf16[16,896]{1,0:T(8,128)(2,1)S(1)}, u32[]{:S(2)}, u32[]{:S(2)}) collective-permute-start(bf16[16,896]{1,0:T(8,128)(2,1)S(1)} %get-tuple-element.13.after.first), channel_id=1, source_target_pairs={{0,4},{4,0},{8,12},{12,8},{1,5},{5,1},{9,13},{13,9},{2,6},{6,2},{1... | collective-permute-start | bytes 86024 | tf_op jit(solution)/shard_map/ppermute | solution.py:441
  6.0 1.8 %collective-permute-done.second = bf16[16,896]{1,0:T(8,128)(2,1)S(1)} collective-permute-done((bf16[16,896]{1,0:T(8,128)(2,1)S(1)}, bf16[16,896]{1,0:T(8,128)(2,1)S(1)}, u32[]{:S(2)}, u32[]{:S(2)}) %collective-permute-start) | collective-permute-done | bytes 28704 | tf_op jit(solution)/shard_map/ppermute | solution.py:441
  7.9 0.0 slice-start.2
  7.9 0.0 slice-start.5
  7.9 0.0 copy-start
  7.9 3.1 %collective-permute-start.1 = (bf16[32,896]{1,0:T(8,128)(2,1)S(1)}, bf16[32,896]{1,0:T(8,128)(2,1)S(1)}, u32[]{:S(2)}, u32[]{:S(2)}) collective-permute-start(bf16[32,896]{1,0:T(8,128)(2,1)S(1)} %join.2.after.first), channel_id=1, source_target_pairs={{0,8},{4,12},{8,0},{12,4},{1,9},{5,13},{9,1},{13,5},{2,10},{6,14},... | collective-permute-start | bytes 172040 | tf_op jit(solution)/shard_map/ppermute | solution.py:441
  11.0 2.2 %collective-permute-done.1.second = bf16[32,896]{1,0:T(8,128)(2,1)S(1)} collective-permute-done((bf16[32,896]{1,0:T(8,128)(2,1)S(1)}, bf16[32,896]{1,0:T(8,128)(2,1)S(1)}, u32[]{:S(2)}, u32[]{:S(2)}) %collective-permute-start.1) | collective-permute-done | bytes 57376 | tf_op jit(solution)/shard_map/ppermute | solution.py:441
  13.1 0.0 slice-done
  13.2 0.0 slice-done.1
  13.2 0.0 slice-done.2
  13.2 1.9 %collective-permute-start.2 = (bf16[64,896]{1,0:T(8,128)(2,1)S(1)}, bf16[64,896]{1,0:T(8,128)(2,1)S(1)}, u32[]{:S(2)}, u32[]{:S(2)}) collective-permute-start(bf16[64,896]{1,0:T(8,128)(2,1)S(1)} %join.3.block.refs_0_), channel_id=1, source_target_pairs={{0,2},{1,3},{2,0},{3,1},{4,6},{5,7},{6,4},{7,5},{8,10},{9,11},{10,... | collective-permute-start | bytes 344072 | tf_op jit(solution)/shard_map/ppermute | solution.py:441
  15.1 0.0 collective-permute-start.3
  15.1 0.0 slice-done.3
  15.1 0.0 slice-done.4
  15.1 0.0 slice-done.5
  15.1 0.0 copy-done
  15.1 1.9 %partial.2 = (f32[2,64,2048]{2,1,0:T(8,128)S(1)}, bf16[2048,768]{1,0:T(8,128)(2,1)S(1)}) custom-call(bf16[64,896]{1,0:T(8,128)(2,1)S(1)} %join.3.block.refs_0_, bf16[3072,2048]{1,0:T(8,128)(2,1)S(1)} %bitcast.13, bf16[3072,2048]{1,0:T(8,128)(2,1)S(1)} %bitcast.11, bf16[2048,3072]{1,0:T(8,128)(2,1)} %down_weight.1, bf16[3072,2048]{1,0:T(8,128)(2,1)S(1)} %bitcast.13, ...), custom_call_target="tpu_custom_call" | custom-call | flops 402653184 | bytes 3145728 | tf_op jit(solution)/shard_map/partial/pallas_call | solution.py:242
  17.0 1.0 %collective-permute-done.2.array = bf16[64,896]{1,0:T(8,128)(2,1)S(1)} collective-permute-done((bf16[64,896]{1,0:T(8,128)(2,1)S(1)}, bf16[64,896]{1,0:T(8,128)(2,1)S(1)}, u32[]{:S(2)}, u32[]{:S(2)}) %collective-permute-start.2) | collective-permute-done | bytes 114720 | tf_op jit(solution)/shard_map/ppermute | solution.py:441
  18.0 0.0 collective-permute-start.4
  18.0 1.3 %partial.3.sums = f32[2,64,2048]{2,1,0:T(8,128)S(1)} custom-call(bf16[64,896]{1,0:T(8,128)(2,1)S(1)} %tie.1.block.refs_1_, bf16[3072,2048]{1,0:T(8,128)(2,1)S(1)} %bitcast.13, bf16[3072,2048]{1,0:T(8,128)(2,1)S(1)} %bitcast.11, f32[2,64,2048]{2,1,0:T(8,128)S(1)} %get-tuple-element.14.after.refs_0_, bf16[2048,3072]{1,0:T(8,128)(2,1)} %down_weight.1), custom_call_target="tpu_custom_call" | custom-call | flops 402653184 | bytes 3145728 | tf_op jit(solution)/shard_map/partial/pallas_call | solution.py:242
  19.4 0.0 collective-permute-done.3.refs_2_
  19.4 0.0 collective-permute-done.4.refs_3_
  19.4 3.4 %experts.1 = (bf16[2,64,768]{2,1,0:T(8,128)(2,1)S(1)}, bf16[64,2048]{1,0:T(8,128)(2,1)S(1)}, bf16[2048,768]{1,0:T(8,128)(2,1)S(1)}) custom-call(f32[2,64,2048]{2,1,0:T(8,128)S(1)} %partial.3.sums, bf16[64,896]{1,0:T(8,128)(2,1)S(1)} %join.3.block.refs_0_, bf16[64,896]{1,0:T(8,128)(2,1)S(1)} %tie.1.block.refs_1_, ...), custom_call_target="tpu_custom_call" | custom-call | flops 1207959552 | bytes 6291456 | tf_op jit(solution)/shard_map/experts/pallas_call | solution.py:335
  22.8 0.6 %collective-permute-start.5 = (bf16[2,64,768]{2,1,0:T(8,128)(2,1)S(1)}, bf16[2,64,768]{2,1,0:T(8,128)(2,1)S(1)}, u32[]{:S(2)}, u32[]{:S(2)}) collective-permute-start(bf16[2,64,768]{2,1,0:T(8,128)(2,1)S(1)} %get-tuple-element.17.after), channel_id=1, source_target_pairs={{0,1},{1,0},{2,3},{3,2},{4,5},{5,4},{6,7},{7,6},{8,9},{9,8},{10,11... | collective-permute-start | bytes 589832 | tf_op jit(solution)/shard_map/ppermute | solution.py:441
  23.4 0.7 %down.2 = f32[1,64,768]{2,1,0:T(8,128)S(1)} custom-call(bf16[64,2048]{1,0:T(8,128)(2,1)S(1)} %get-tuple-element.16.active, bf16[2,64,768]{2,1,0:T(8,128)(2,1)S(1)} %get-tuple-element.17.after, bf16[2048,768]{1,0:T(8,128)(2,1)S(1)} %get-tuple-element.18.refs_0_), custom_call_target="tpu_custom_call" | custom-call | flops 201326592 | bytes 3145728 | tf_op jit(solution)/shard_map/down/pallas_call | solution.py:374
  24.0 0.4 %collective-permute-done.5 = bf16[2,64,768]{2,1,0:T(8,128)(2,1)S(1)} collective-permute-done((bf16[2,64,768]{2,1,0:T(8,128)(2,1)S(1)}, bf16[2,64,768]{2,1,0:T(8,128)(2,1)S(1)}, u32[]{:S(2)}, u32[]{:S(2)}) %collective-permute-start.5) | collective-permute-done | bytes 196640 | tf_op jit(solution)/shard_map/ppermute | solution.py:441
  24.5 1.9 %collective-permute-start.6 = (bf16[1,64,768]{2,1,0:T(8,128)(2,1)S(1)}, bf16[1,64,768]{2,1,0:T(8,128)(2,1)S(1)}, u32[]{:S(2)}, u32[]{:S(2)}) collective-permute-start(bf16[1,64,768]{2,1,0:T(8,128)(2,1)S(1)} %add_convert_fusion.after), channel_id=1, source_target_pairs={{0,2},{1,3},{2,0},{3,1},{4,6},{5,7},{6,4},{7,5},{8,10},{9,11},{10,... | collective-permute-start | bytes 294920 | tf_op jit(solution)/shard_map/ppermute | solution.py:441
  26.4 2.6 %down.3 = f32[1,64,768]{2,1,0:T(8,128)S(1)} custom-call(bf16[64,2048]{1,0:T(8,128)(2,1)S(1)} %get-tuple-element.16.active, bf16[1,64,768]{2,1,0:T(8,128)(2,1)S(1)} %add_convert_fusion.after, bf16[2048,3072]{1,0:T(8,128)(2,1)} %down_weight.1), custom_call_target="tpu_custom_call" | custom-call | flops 201326592 | bytes 3145728 | tf_op jit(solution)/shard_map/down/pallas_call | solution.py:374
  28.9 0.8 %collective-permute-done.6 = bf16[1,64,768]{2,1,0:T(8,128)(2,1)S(1)} collective-permute-done((bf16[1,64,768]{2,1,0:T(8,128)(2,1)S(1)}, bf16[1,64,768]{2,1,0:T(8,128)(2,1)S(1)}, u32[]{:S(2)}, u32[]{:S(2)}) %collective-permute-start.6) | collective-permute-done | bytes 98336 | tf_op jit(solution)/shard_map/ppermute | solution.py:441
  29.7 1.9 %collective-permute-start.7 = (bf16[2,16,768]{2,1,0:T(8,128)(2,1)S(1)}, bf16[2,16,768]{2,1,0:T(8,128)(2,1)S(1)}, u32[]{:S(2)}, u32[]{:S(2)}) collective-permute-start(bf16[2,16,768]{2,1,0:T(8,128)(2,1)S(1)} %slice.25), channel_id=1, source_target_pairs={{0,4},{4,0},{8,12},{12,8},{1,5},{5,1},{9,13},{13,9},{2,6},{6,2},{1... | collective-permute-start | bytes 147464 | tf_op jit(solution)/shard_map/ppermute | solution.py:441
  31.6 2.3 %collective-permute-done.7 = bf16[2,16,768]{2,1,0:T(8,128)(2,1)S(1)} collective-permute-done((bf16[2,16,768]{2,1,0:T(8,128)(2,1)S(1)}, bf16[2,16,768]{2,1,0:T(8,128)(2,1)S(1)}, u32[]{:S(2)}, u32[]{:S(2)}) %collective-permute-start.7) | collective-permute-done | bytes 49184 | tf_op jit(solution)/shard_map/ppermute | solution.py:441
  33.9 3.0 %collective-permute-start.8 = (bf16[1,16,768]{2,1,0:T(8,128)(2,1)S(1)}, bf16[1,16,768]{2,1,0:T(8,128)(2,1)S(1)}, u32[]{:S(2)}, u32[]{:S(2)}) collective-permute-start(bf16[1,16,768]{2,1,0:T(8,128)(2,1)S(1)} %slice.43), channel_id=1, source_target_pairs={{0,8},{4,12},{8,0},{12,4},{1,9},{5,13},{9,1},{13,5},{2,10},{6,14},... | collective-permute-start | bytes 73736 | tf_op jit(solution)/shard_map/ppermute | solution.py:441
  36.9 1.8 %collective-permute-done.8 = bf16[1,16,768]{2,1,0:T(8,128)(2,1)S(1)} collective-permute-done((bf16[1,16,768]{2,1,0:T(8,128)(2,1)S(1)}, bf16[1,16,768]{2,1,0:T(8,128)(2,1)S(1)}, u32[]{:S(2)}, u32[]{:S(2)}) %collective-permute-start.8) | collective-permute-done | bytes 24608 | tf_op jit(solution)/shard_map/ppermute | solution.py:441
  38.7 0.6 %fusion.2 = bf16[16,768]{1,0:T(8,128)(2,1)} fusion(f32[2,16,768]{2,1,0:T(8,128)S(1)} %convert_add_fusion.1, bf16[1,16,768]{2,1,0:T(8,128)(2,1)S(1)} %collective-permute-done.8, bf16[16,768]{1,0:T(8,128)(2,1)S(1)} %get-tuple-element.12), kind=kLoop, calls=%fused_computation.7 | loop fusion | flops 61440 | bytes 122880 | tf_op jit(solution)/shard_map/convert_element_type | solution.py:543
  (13 shorter events, 0.1 us)
Async XLA Ops:
  0.0 15.1 %slice-start.3 = ((s8[12582912]{0:T(1024)(128)(4,1)}), s8[4194304]{0:T(1024)(128)(4,1)S(1)}, s32[]{:S(2)}) async-start(s8[12582912]{0:T(1024)(128)(4,1)} %bitcast.12), calls=%async_computation.3 | async-start | bytes 8388608
  2.9 10.3 %slice-start = ((s8[12582912]{0:T(1024)(128)(4,1)}), s8[4194304]{0:T(1024)(128)(4,1)S(1)}, s32[]{:S(2)}) async-start(s8[12582912]{0:T(1024)(128)(4,1)} %bitcast.10), calls=%async_computation | async-start | bytes 8388608
  2.9 10.3 %slice-start.1 = ((s8[12582912]{0:T(1024)(128)(4,1)}), s8[4194304]{0:T(1024)(128)(4,1)S(1)}, s32[]{:S(2)}) async-start(s8[12582912]{0:T(1024)(128)(4,1)} %bitcast.10), calls=%async_computation.1 | async-start | bytes 8388608
  2.9 12.2 %slice-start.4 = ((s8[12582912]{0:T(1024)(128)(4,1)}), s8[4194304]{0:T(1024)(128)(4,1)S(1)}, s32[]{:S(2)}) async-start(s8[12582912]{0:T(1024)(128)(4,1)} %bitcast.12), calls=%async_computation.4 | async-start | bytes 8388608
  2.9 4.9 %collective-permute-start = (bf16[16,896]{1,0:T(8,128)(2,1)S(1)}, bf16[16,896]{1,0:T(8,128)(2,1)S(1)}, u32[]{:S(2)}, u32[]{:S(2)}) collective-permute-start(bf16[16,896]{1,0:T(8,128)(2,1)S(1)} %get-tuple-element.13.after.first), channel_id=1, source_target_pairs={{0,4},{4,0},{8,12},{12,8},{1,5},{5,1},{9,13},{13,9},{2,6},{6,2},{1... | collective-permute-start | bytes 86024 | tf_op jit(solution)/shard_map/ppermute | solution.py:441
  7.9 5.3 %slice-start.2 = ((s8[12582912]{0:T(1024)(128)(4,1)}), s8[4194304]{0:T(1024)(128)(4,1)S(1)}, s32[]{:S(2)}) async-start(s8[12582912]{0:T(1024)(128)(4,1)} %bitcast.10), calls=%async_computation.2 | async-start | bytes 8388608
  7.9 7.2 %slice-start.5 = ((s8[12582912]{0:T(1024)(128)(4,1)}), s8[4194304]{0:T(1024)(128)(4,1)S(1)}, s32[]{:S(2)}) async-start(s8[12582912]{0:T(1024)(128)(4,1)} %bitcast.12), calls=%async_computation.5 | async-start | bytes 8388608
  7.9 7.2 %copy-start = (bf16[128,2048]{1,0:T(8,128)(2,1)S(1)}, bf16[128,2048]{1,0:T(8,128)(2,1)}, u32[]{:S(2)}) copy-start(bf16[128,2048]{1,0:T(8,128)(2,1)} %refs_6_.3) | copy-start | bytes 1572868
  7.9 5.3 %collective-permute-start.1 = (bf16[32,896]{1,0:T(8,128)(2,1)S(1)}, bf16[32,896]{1,0:T(8,128)(2,1)S(1)}, u32[]{:S(2)}, u32[]{:S(2)}) collective-permute-start(bf16[32,896]{1,0:T(8,128)(2,1)S(1)} %join.2.after.first), channel_id=1, source_target_pairs={{0,8},{4,12},{8,0},{12,4},{1,9},{5,13},{9,1},{13,5},{2,10},{6,14},... | collective-permute-start | bytes 172040 | tf_op jit(solution)/shard_map/ppermute | solution.py:441
  13.2 4.9 %collective-permute-start.2 = (bf16[64,896]{1,0:T(8,128)(2,1)S(1)}, bf16[64,896]{1,0:T(8,128)(2,1)S(1)}, u32[]{:S(2)}, u32[]{:S(2)}) collective-permute-start(bf16[64,896]{1,0:T(8,128)(2,1)S(1)} %join.3.block.refs_0_), channel_id=1, source_target_pairs={{0,2},{1,3},{2,0},{3,1},{4,6},{5,7},{6,4},{7,5},{8,10},{9,11},{10,... | collective-permute-start | bytes 344072 | tf_op jit(solution)/shard_map/ppermute | solution.py:441
  15.1 4.3 %collective-permute-start.3 = (bf16[64,896]{1,0:T(8,128)(2,1)S(1)}, bf16[64,896]{1,0:T(8,128)(2,1)S(1)}, u32[]{:S(2)}, u32[]{:S(2)}) collective-permute-start(bf16[64,896]{1,0:T(8,128)(2,1)S(1)} %join.3.block.refs_0_), channel_id=1, source_target_pairs={{0,1},{1,0},{2,3},{3,2},{4,5},{5,4},{6,7},{7,6},{8,9},{9,8},{10,11... | collective-permute-start | bytes 344072 | tf_op jit(solution)/shard_map/ppermute | solution.py:441
  18.0 1.4 %collective-permute-start.4 = (bf16[64,896]{1,0:T(8,128)(2,1)S(1)}, bf16[64,896]{1,0:T(8,128)(2,1)S(1)}, u32[]{:S(2)}, u32[]{:S(2)}) collective-permute-start(bf16[64,896]{1,0:T(8,128)(2,1)S(1)} %tie.1.block.refs_1_), channel_id=1, source_target_pairs={{0,1},{1,0},{2,3},{3,2},{4,5},{5,4},{6,7},{7,6},{8,9},{9,8},{10,11... | collective-permute-start | bytes 344072 | tf_op jit(solution)/shard_map/ppermute | solution.py:441
  22.8 1.6 %collective-permute-start.5 = (bf16[2,64,768]{2,1,0:T(8,128)(2,1)S(1)}, bf16[2,64,768]{2,1,0:T(8,128)(2,1)S(1)}, u32[]{:S(2)}, u32[]{:S(2)}) collective-permute-start(bf16[2,64,768]{2,1,0:T(8,128)(2,1)S(1)} %get-tuple-element.17.after), channel_id=1, source_target_pairs={{0,1},{1,0},{2,3},{3,2},{4,5},{5,4},{6,7},{7,6},{8,9},{9,8},{10,11... | collective-permute-start | bytes 589832 | tf_op jit(solution)/shard_map/ppermute | solution.py:441
  24.5 5.2 %collective-permute-start.6 = (bf16[1,64,768]{2,1,0:T(8,128)(2,1)S(1)}, bf16[1,64,768]{2,1,0:T(8,128)(2,1)S(1)}, u32[]{:S(2)}, u32[]{:S(2)}) collective-permute-start(bf16[1,64,768]{2,1,0:T(8,128)(2,1)S(1)} %add_convert_fusion.after), channel_id=1, source_target_pairs={{0,2},{1,3},{2,0},{3,1},{4,6},{5,7},{6,4},{7,5},{8,10},{9,11},{10,... | collective-permute-start | bytes 294920 | tf_op jit(solution)/shard_map/ppermute | solution.py:441
  29.7 4.2 %collective-permute-start.7 = (bf16[2,16,768]{2,1,0:T(8,128)(2,1)S(1)}, bf16[2,16,768]{2,1,0:T(8,128)(2,1)S(1)}, u32[]{:S(2)}, u32[]{:S(2)}) collective-permute-start(bf16[2,16,768]{2,1,0:T(8,128)(2,1)S(1)} %slice.25), channel_id=1, source_target_pairs={{0,4},{4,0},{8,12},{12,8},{1,5},{5,1},{9,13},{13,9},{2,6},{6,2},{1... | collective-permute-start | bytes 147464 | tf_op jit(solution)/shard_map/ppermute | solution.py:441
  33.9 4.8 %collective-permute-start.8 = (bf16[1,16,768]{2,1,0:T(8,128)(2,1)S(1)}, bf16[1,16,768]{2,1,0:T(8,128)(2,1)S(1)}, u32[]{:S(2)}, u32[]{:S(2)}) collective-permute-start(bf16[1,16,768]{2,1,0:T(8,128)(2,1)S(1)} %slice.43), channel_id=1, source_target_pairs={{0,8},{4,12},{8,0},{12,4},{1,9},{5,13},{9,1},{13,5},{2,10},{6,14},... | collective-permute-start | bytes 73736 | tf_op jit(solution)/shard_map/ppermute | solution.py:441

commit v8 on v7

--- a/solution.py
+++ b/solution.py
@@ -13,6 +13,7 @@
 EXPERT_COUNT = 4
 ADAPTER_RANK = 16
 TENANT_COUNT = 8
+CAP = 10
 LANES = 128
 ADAPTER_LANES = EXPERT_COUNT * ADAPTER_RANK
 DIFF_HI, DIFF_LO, SQ_HI, SQ_LO, FIRST, SECOND, TENANT = range(ADAPTER_LANES, ADAPTER_LANES + 7)
@@ -405,6 +406,77 @@
     )(first, second, *after)
 
 
+def pack_kernel(replicas, first, second, *refs):
+    packed, place = refs[-2:]
+    rows, slots = place.shape
+    half = first.shape[0]
+    features = first.shape[1] - LANES
+    every = jnp.concatenate([first[...], second[...]], axis=0)
+    tail = every[:, features:].astype(F32)
+    expert = (lax.axis_index("ep") // replicas).astype(F32)
+    named = jnp.where(
+        (tail[:, FIRST : FIRST + 1] == expert) | (tail[:, SECOND : SECOND + 1] == expert), 1.0, 0.0
+    )
+    row = lax.broadcasted_iota(jnp.int32, (rows, rows), 0)
+    before = jnp.where(lax.broadcasted_iota(jnp.int32, (rows, rows), 1) < row, 1.0, 0.0)
+    named = jnp.broadcast_to(named, (rows, slots))
+    slot = jnp.dot(before.astype(BF16), named.astype(BF16), preferred_element_type=F32)
+    lane = lax.broadcasted_iota(jnp.int32, (rows, slots), 1).astype(F32)
+    at = jnp.where(lane == slot, named, 0.0)
+    place[...] = at.astype(BF16)
+    packed[...] = lax.dot_general(
+        at.astype(BF16), every, (((0,), (0,)), ((), ())), preferred_element_type=F32
+    ).astype(BF16)
+
+
+def pack(first, second, replicas, slots, *after):
+    rows, width = 2 * first.shape[0], first.shape[1]
+    return pl.pallas_call(
+        functools.partial(pack_kernel, replicas),
+        out_shape=(
+            jax.ShapeDtypeStruct((slots, width), BF16),
+            jax.ShapeDtypeStruct((rows, slots), BF16),
+        ),
+        in_specs=[VMEM, VMEM] + [HBM] * len(after),
+        out_specs=(VMEM, VMEM),
+        compiler_params=pltpu.CompilerParams(vmem_limit_bytes=4 * 2**20),
+        name="pack",
+    )(first, second, *after)
+
+
+def unpack_kernel(place, made, *refs):
+    *arrived, kept, sent = refs
+    total = made[0]
+    for block in arrived:
+        total = total + block[0].astype(F32)
+    high = total.astype(BF16)
+    low = (total - high.astype(F32)).astype(BF16)
+    at = place[...]
+    full = jnp.dot(at, high, preferred_element_type=F32) + jnp.dot(
+        at, low, preferred_element_type=F32
+    )
+    rows = kept.shape[1]
+    for j in range(kept.shape[0]):
+        kept[j] = full[2 * j * rows : (2 * j + 1) * rows]
+        sent[j] = full[(2 * j + 1) * rows : (2 * j + 2) * rows].astype(BF16)
+
+
+def unpack(place, made, arrived, rows):
+    features = made.shape[2]
+    pairs = place.shape[0] // (2 * rows)
+    return pl.pallas_call(
+        unpack_kernel,
+        out_shape=(
+            jax.ShapeDtypeStruct((pairs, rows, features), F32),
+            jax.ShapeDtypeStruct((pairs, rows, features), BF16),
+        ),
+        in_specs=[VMEM] * (2 + len(arrived)),
+        out_specs=(VMEM, VMEM),
+        compiler_params=pltpu.CompilerParams(vmem_limit_bytes=4 * 2**20),
+        name="unpack",
+    )(place, made, *arrived)
+
+
 def mark_kernel(after, weight, out):
     out[...] = jnp.zeros_like(out)
 
@@ -482,11 +554,16 @@
             adapter_down_map,
         ),
     )
+    replicas = expert_devices // EXPERT_COUNT
     for distance in bits(expert_devices):
         other = swap(held, "ep", distance)
         last = 2 * distance == expert_devices
         beside = mark(held, expert_down_weight)
-        held = join(held, other, beside, *((expert_up_weight,) if last else ()))
+        if last:
+            slots = expert_devices * CAP
+            held, place = pack(held, other, replicas, slots, beside, expert_up_weight)
+        else:
+            held = join(held, other, beside)
     steps = bits(tensor_devices)
     groups = [tuple(k for k in range(tensor_devices) if k & -k == step) for step in steps] + [(0,)]
     early, late = groups[0][-1:], groups[0][:-1]
@@ -509,7 +586,7 @@
         blocks = blocks + [tie(block, sums) if distance > 1 else block for block in others]
         order = order + [at ^ distance for at in order]
     sent, active, *parts = experts(
-        expert_devices // EXPERT_COUNT,
+        replicas,
         late,
         groups[1],
         tuple(order),
@@ -530,15 +607,16 @@
         parts = []
         for i, k in enumerate(group):
             received[k ^ step].append(arriving[i])
-        kept = [
-            sum((block.astype(F32) for block in received[k]), made[i])
-            for i, k in enumerate(following)
-        ]
         if following != (0,):
+            kept = [
+                sum((block.astype(F32) for block in received[k]), made[i])
+                for i, k in enumerate(following)
+            ]
             sent = jnp.stack([block.astype(BF16) for block in kept])
-    kept = kept[0].reshape(expert_devices, rows, features)
+    kept, sent = unpack(place, made, [block[None] for block in received[0]], rows)
     for distance in bits(expert_devices):
-        kept, sent = kept[0::2], kept[1::2].astype(BF16)
+        if distance > 1:
+            kept, sent = kept[0::2], kept[1::2].astype(BF16)
         kept = kept + swap(sent, "ep", distance).astype(F32)
     return (state.astype(F32) + kept[0]).astype(BF16)
 

time: 39.5 us -> 38.8 us (0.982)
  waiting for transfers between devices: 10.3 us -> 9.12 us
  Pallas kernels: 12.7 us -> 13.3 us
    ppermute x9, waiting for transfers between devices: 10.3 us -> 9.12 us  [swap(): return lax.ppermute(x, axis, [(i, i ^ distance) for i in range(count)])]
    pallas_call x0 -> x2, Pallas kernels: none -> 0.68 us  [the longest x1 0.48 us: pack(): pl.pallas_call(functools.partial(pack_kernel, replicas), out_shape=(jax.S...]
  transfers between devices with their start and end apart: 9 -> 9, of which waited for: 7 -> 6; matrix products, arithmetic and copies ran while one was open for 0% -> 0% of each run, Pallas kernels for 16% -> 17%
where the time goes in v8:
time: 38.8 us; the launch traced here: 38.6 us
  starting transfers between devices  15.3 us (39%)
  Pallas kernels  13.3 us (34%)
  waiting for transfers between devices  9.12 us (24%)
  other arithmetic  0.65 us (2%)
    ppermute x9, starting transfers between devices, swap(): return lax.ppermute(x, axis, [(i, i ^ distance) for i in range(count)])  15.3 us
    ppermute x9, waiting for transfers between devices, swap(): return lax.ppermute(x, axis, [(i, i ^ distance) for i in range(count)])  9.12 us
    pallas_call x1, Pallas kernels, experts(): pl.pallas_call(functools.partial(expert_kernel, replicas, late, following...  3.33 us
    pallas_call x2, Pallas kernels, partial(): pl.pallas_call(functools.partial(partial_kernel, distance, fetched, first...  3.26 us
    pallas_call x2, Pallas kernels, down(): pl.pallas_call(down_kernel if parts else functools.partial(down_fetching_...  3.2 us
    pallas_call x1, Pallas kernels, attend(): pl.pallas_call(attend_kernel, out_shape=(jax.ShapeDtypeStruct((rows, feat...  2.87 us
  transfers between devices with their start and end apart: 9, of which 6 were waited for; matrix products, arithmetic and copies ran while one was open for 0% of the time, Pallas kernels for 17%

profile of v8, /device:TPU:0, one launch (start us, length us, event | category | flops | bytes accessed | tf_op | source)
XLA Modules:
  0.0 38.6 jit_solution(895364088536517911)
XLA Ops:
  0.0 0.0 slice-start.3
  0.0 2.9 %attend.1 = (bf16[16,768]{1,0:T(8,128)(2,1)S(1)}, bf16[16,896]{1,0:T(8,128)(2,1)S(1)}) custom-call(s32[16]{0:T(128)} %refs_0_.2, s32[16]{0:T(128)} %refs_1_.4, s32[2,16]{1,0:T(2,128)} %bitcast.15, bf16[16,768]{1,0:T(8,128)(2,1)} %refs_3_.1, bf16[16,768]{1,0:T(8,128)(2,1)} %refs_4_.2, bf16[16,256]{1,0:T(8,128)(2,1)} %refs_5_.2, bf16[16,256]{1,0:T(8,128)(2,1)} %refs_6_.2, ...), custom_call_target="tpu_custom_call" | custom-call | flops 200000000 | bytes 3000000 | tf_op jit(solution)/shard_map/attend/pallas_call | solution.py:178
  2.9 0.0 slice-start
  2.9 0.0 slice-start.1
  2.9 0.0 slice-start.4
  2.9 3.1 %collective-permute-start = (bf16[16,896]{1,0:T(8,128)(2,1)S(1)}, bf16[16,896]{1,0:T(8,128)(2,1)S(1)}, u32[]{:S(2)}, u32[]{:S(2)}) collective-permute-start(bf16[16,896]{1,0:T(8,128)(2,1)S(1)} %get-tuple-element.17.after.first), channel_id=1, source_target_pairs={{0,4},{4,0},{8,12},{12,8},{1,5},{5,1},{9,13},{13,9},{2,6},{6,2},{1... | collective-permute-start | bytes 86024 | tf_op jit(solution)/shard_map/ppermute | solution.py:513
  6.0 1.8 %collective-permute-done.second = bf16[16,896]{1,0:T(8,128)(2,1)S(1)} collective-permute-done((bf16[16,896]{1,0:T(8,128)(2,1)S(1)}, bf16[16,896]{1,0:T(8,128)(2,1)S(1)}, u32[]{:S(2)}, u32[]{:S(2)}) %collective-permute-start) | collective-permute-done | bytes 28704 | tf_op jit(solution)/shard_map/ppermute | solution.py:513
  7.9 0.0 slice-start.2
  7.9 0.0 slice-start.5
  7.9 0.0 copy-start
  7.9 3.1 %collective-permute-start.1 = (bf16[32,896]{1,0:T(8,128)(2,1)S(1)}, bf16[32,896]{1,0:T(8,128)(2,1)S(1)}, u32[]{:S(2)}, u32[]{:S(2)}) collective-permute-start(bf16[32,896]{1,0:T(8,128)(2,1)S(1)} %join.1.after.first), channel_id=1, source_target_pairs={{0,8},{4,12},{8,0},{12,4},{1,9},{5,13},{9,1},{13,5},{2,10},{6,14},... | collective-permute-start | bytes 172040 | tf_op jit(solution)/shard_map/ppermute | solution.py:513
  11.0 2.2 %collective-permute-done.1.second = bf16[32,896]{1,0:T(8,128)(2,1)S(1)} collective-permute-done((bf16[32,896]{1,0:T(8,128)(2,1)S(1)}, bf16[32,896]{1,0:T(8,128)(2,1)S(1)}, u32[]{:S(2)}, u32[]{:S(2)}) %collective-permute-start.1) | collective-permute-done | bytes 57376 | tf_op jit(solution)/shard_map/ppermute | solution.py:513
  13.1 0.0 slice-done
  13.2 0.0 slice-done.1
  13.2 0.0 slice-done.2
  13.2 0.5 %pack.1 = (bf16[40,896]{1,0:T(8,128)(2,1)S(1)}, bf16[64,40]{1,0:T(8,128)(2,1)S(1)}) custom-call(bf16[32,896]{1,0:T(8,128)(2,1)S(1)} %join.1.after.first, bf16[32,896]{1,0:T(8,128)(2,1)S(1)} %collective-permute-done.1.second, f32[8,128]{1,0:T(8,128)S(1)} %mark.3.refs_0_, bf16[3072,2048]{1,0:T(8,128)(2,1)S(1)} %bitcast.10), custom_call_target="tpu_custom_call" | custom-call | tf_op jit(solution)/shard_map/pack/pallas_call | solution.py:434
  13.6 1.9 %collective-permute-start.2 = (bf16[40,896]{1,0:T(8,128)(2,1)S(1)}, bf16[40,896]{1,0:T(8,128)(2,1)S(1)}, u32[]{:S(2)}, u32[]{:S(2)}) collective-permute-start(bf16[40,896]{1,0:T(8,128)(2,1)S(1)} %get-tuple-element.19.block.refs_0_), channel_id=1, source_target_pairs={{0,2},{1,3},{2,0},{3,1},{4,6},{5,7},{6,4},{7,5},{8,10},{9,11},{10,... | collective-permute-start | bytes 215048 | tf_op jit(solution)/shard_map/ppermute | solution.py:513
  15.5 0.0 collective-permute-start.3
  15.5 0.0 slice-done.3
  15.5 0.0 slice-done.4
  15.5 0.0 slice-done.5
  15.6 0.0 copy-done
  15.6 1.9 %partial.2 = (f32[2,40,2048]{2,1,0:T(8,128)S(1)}, bf16[2048,768]{1,0:T(8,128)(2,1)S(1)}) custom-call(bf16[40,896]{1,0:T(8,128)(2,1)S(1)} %get-tuple-element.19.block.refs_0_, bf16[3072,2048]{1,0:T(8,128)(2,1)S(1)} %bitcast.12, bf16[3072,2048]{1,0:T(8,128)(2,1)S(1)} %bitcast.10, bf16[2048,3072]{1,0:T(8,128)(2,1)} %down_weight.1, ...), custom_call_target="tpu_custom_call" | custom-call | flops 251658240 | bytes 3145728 | tf_op jit(solution)/shard_map/partial/pallas_call | solution.py:243
  17.5 0.6 %collective-permute-done.2.array = bf16[40,896]{1,0:T(8,128)(2,1)S(1)} collective-permute-done((bf16[40,896]{1,0:T(8,128)(2,1)S(1)}, bf16[40,896]{1,0:T(8,128)(2,1)S(1)}, u32[]{:S(2)}, u32[]{:S(2)}) %collective-permute-start.2) | collective-permute-done | bytes 71712 | tf_op jit(solution)/shard_map/ppermute | solution.py:513
  18.0 0.0 collective-permute-start.4
  18.1 1.3 %partial.3.sums = f32[2,40,2048]{2,1,0:T(8,128)S(1)} custom-call(bf16[40,896]{1,0:T(8,128)(2,1)S(1)} %tie.1.block.refs_1_, bf16[3072,2048]{1,0:T(8,128)(2,1)S(1)} %bitcast.12, bf16[3072,2048]{1,0:T(8,128)(2,1)S(1)} %bitcast.10, f32[2,40,2048]{2,1,0:T(8,128)S(1)} %get-tuple-element.20.after.refs_0_, bf16[2048,3072]{1,0:T(8,128)(2,1)} %down_weight.1), custom_call_target="tpu_custom_call" | custom-call | flops 251658240 | bytes 3145728 | tf_op jit(solution)/shard_map/partial/pallas_call | solution.py:243
  19.4 0.0 collective-permute-done.3.refs_2_
  19.4 0.0 collective-permute-done.4.refs_3_
  19.4 3.3 %experts.1 = (bf16[2,40,768]{2,1,0:T(8,128)(2,1)S(1)}, bf16[40,2048]{1,0:T(8,128)(2,1)S(1)}, bf16[2048,768]{1,0:T(8,128)(2,1)S(1)}) custom-call(f32[2,40,2048]{2,1,0:T(8,128)S(1)} %partial.3.sums, bf16[40,896]{1,0:T(8,128)(2,1)S(1)} %get-tuple-element.19.block.refs_0_, bf16[40,896]{1,0:T(8,128)(2,1)S(1)} %tie.1.block.refs_1_, ...), custom_call_target="tpu_custom_call" | custom-call | flops 754974720 | bytes 6291456 | tf_op jit(solution)/shard_map/experts/pallas_call | solution.py:336
  22.8 0.6 %collective-permute-start.5 = (bf16[2,40,768]{2,1,0:T(8,128)(2,1)S(1)}, bf16[2,40,768]{2,1,0:T(8,128)(2,1)S(1)}, u32[]{:S(2)}, u32[]{:S(2)}) collective-permute-start(bf16[2,40,768]{2,1,0:T(8,128)(2,1)S(1)} %get-tuple-element.23.after), channel_id=1, source_target_pairs={{0,1},{1,0},{2,3},{3,2},{4,5},{5,4},{6,7},{7,6},{8,9},{9,8},{10,11... | collective-permute-start | bytes 368648 | tf_op jit(solution)/shard_map/ppermute | solution.py:513
  23.3 0.6 %down.2 = f32[1,40,768]{2,1,0:T(8,128)S(1)} custom-call(bf16[40,2048]{1,0:T(8,128)(2,1)S(1)} %get-tuple-element.22.active, bf16[2,40,768]{2,1,0:T(8,128)(2,1)S(1)} %get-tuple-element.23.after, bf16[2048,768]{1,0:T(8,128)(2,1)S(1)} %get-tuple-element.24.refs_0_), custom_call_target="tpu_custom_call" | custom-call | flops 125829120 | bytes 3145728 | tf_op jit(solution)/shard_map/down/pallas_call | solution.py:375
  24.0 0.3 collective-permute-done.5
  24.3 1.9 %collective-permute-start.6 = (bf16[1,40,768]{2,1,0:T(8,128)(2,1)S(1)}, bf16[1,40,768]{2,1,0:T(8,128)(2,1)S(1)}, u32[]{:S(2)}, u32[]{:S(2)}) collective-permute-start(bf16[1,40,768]{2,1,0:T(8,128)(2,1)S(1)} %add_convert_fusion.after), channel_id=1, source_target_pairs={{0,2},{1,3},{2,0},{3,1},{4,6},{5,7},{6,4},{7,5},{8,10},{9,11},{10,... | collective-permute-start | bytes 184328 | tf_op jit(solution)/shard_map/ppermute | solution.py:513
  26.2 2.6 %down.3.made = f32[1,40,768]{2,1,0:T(8,128)S(1)} custom-call(bf16[40,2048]{1,0:T(8,128)(2,1)S(1)} %get-tuple-element.22.active, bf16[1,40,768]{2,1,0:T(8,128)(2,1)S(1)} %add_convert_fusion.after, bf16[2048,3072]{1,0:T(8,128)(2,1)} %down_weight.1), custom_call_target="tpu_custom_call" | custom-call | flops 125829120 | bytes 3145728 | tf_op jit(solution)/shard_map/down/pallas_call | solution.py:375
  28.8 0.0 collective-permute-done.6.refs_1_
  28.8 0.2 unpack.1
  29.0 1.8 %collective-permute-start.7 = (bf16[2,16,768]{2,1,0:T(8,128)(2,1)S(1)}, bf16[2,16,768]{2,1,0:T(8,128)(2,1)S(1)}, u32[]{:S(2)}, u32[]{:S(2)}) collective-permute-start(bf16[2,16,768]{2,1,0:T(8,128)(2,1)S(1)} %get-tuple-element.26), channel_id=1, source_target_pairs={{0,4},{4,0},{8,12},{12,8},{1,5},{5,1},{9,13},{13,9},{2,6},{6,2},{1... | collective-permute-start | bytes 147464 | tf_op jit(solution)/shard_map/ppermute | solution.py:513
  30.8 2.3 %collective-permute-done.7 = bf16[2,16,768]{2,1,0:T(8,128)(2,1)S(1)} collective-permute-done((bf16[2,16,768]{2,1,0:T(8,128)(2,1)S(1)}, bf16[2,16,768]{2,1,0:T(8,128)(2,1)S(1)}, u32[]{:S(2)}, u32[]{:S(2)}) %collective-permute-start.7) | collective-permute-done | bytes 49184 | tf_op jit(solution)/shard_map/ppermute | solution.py:513
  33.2 2.9 %collective-permute-start.8 = (bf16[1,16,768]{2,1,0:T(8,128)(2,1)S(1)}, bf16[1,16,768]{2,1,0:T(8,128)(2,1)S(1)}, u32[]{:S(2)}, u32[]{:S(2)}) collective-permute-start(bf16[1,16,768]{2,1,0:T(8,128)(2,1)S(1)} %slice.32), channel_id=1, source_target_pairs={{0,8},{4,12},{8,0},{12,4},{1,9},{5,13},{9,1},{13,5},{2,10},{6,14},... | collective-permute-start | bytes 73736 | tf_op jit(solution)/shard_map/ppermute | solution.py:513
  36.1 1.9 %collective-permute-done.8 = bf16[1,16,768]{2,1,0:T(8,128)(2,1)S(1)} collective-permute-done((bf16[1,16,768]{2,1,0:T(8,128)(2,1)S(1)}, bf16[1,16,768]{2,1,0:T(8,128)(2,1)S(1)}, u32[]{:S(2)}, u32[]{:S(2)}) %collective-permute-start.8) | collective-permute-done | bytes 24608 | tf_op jit(solution)/shard_map/ppermute | solution.py:513
  38.0 0.6 %fusion.2 = bf16[16,768]{1,0:T(8,128)(2,1)} fusion(f32[2,16,768]{2,1,0:T(8,128)S(1)} %convert_add_fusion, bf16[1,16,768]{2,1,0:T(8,128)(2,1)S(1)} %collective-permute-done.8, bf16[16,768]{1,0:T(8,128)(2,1)S(1)} %get-tuple-element.16), kind=kLoop, calls=%fused_computation.6 | loop fusion | flops 61440 | bytes 122880 | tf_op jit(solution)/shard_map/convert_element_type | solution.py:621
  (10 shorter events, 0.0 us)
Async XLA Ops:
  0.0 15.5 %slice-start.3 = ((s8[12582912]{0:T(1024)(128)(4,1)}), s8[4194304]{0:T(1024)(128)(4,1)S(1)}, s32[]{:S(2)}) async-start(s8[12582912]{0:T(1024)(128)(4,1)} %bitcast.11), calls=%async_computation.3 | async-start | bytes 8388608
  2.9 10.3 %slice-start = ((s8[12582912]{0:T(1024)(128)(4,1)}), s8[4194304]{0:T(1024)(128)(4,1)S(1)}, s32[]{:S(2)}) async-start(s8[12582912]{0:T(1024)(128)(4,1)} %bitcast.9), calls=%async_computation | async-start | bytes 8388608
  2.9 10.3 %slice-start.1 = ((s8[12582912]{0:T(1024)(128)(4,1)}), s8[4194304]{0:T(1024)(128)(4,1)S(1)}, s32[]{:S(2)}) async-start(s8[12582912]{0:T(1024)(128)(4,1)} %bitcast.9), calls=%async_computation.1 | async-start | bytes 8388608
  2.9 12.6 %slice-start.4 = ((s8[12582912]{0:T(1024)(128)(4,1)}), s8[4194304]{0:T(1024)(128)(4,1)S(1)}, s32[]{:S(2)}) async-start(s8[12582912]{0:T(1024)(128)(4,1)} %bitcast.11), calls=%async_computation.4 | async-start | bytes 8388608
  2.9 4.9 %collective-permute-start = (bf16[16,896]{1,0:T(8,128)(2,1)S(1)}, bf16[16,896]{1,0:T(8,128)(2,1)S(1)}, u32[]{:S(2)}, u32[]{:S(2)}) collective-permute-start(bf16[16,896]{1,0:T(8,128)(2,1)S(1)} %get-tuple-element.17.after.first), channel_id=1, source_target_pairs={{0,4},{4,0},{8,12},{12,8},{1,5},{5,1},{9,13},{13,9},{2,6},{6,2},{1... | collective-permute-start | bytes 86024 | tf_op jit(solution)/shard_map/ppermute | solution.py:513
  7.9 5.3 %slice-start.2 = ((s8[12582912]{0:T(1024)(128)(4,1)}), s8[4194304]{0:T(1024)(128)(4,1)S(1)}, s32[]{:S(2)}) async-start(s8[12582912]{0:T(1024)(128)(4,1)} %bitcast.9), calls=%async_computation.2 | async-start | bytes 8388608
  7.9 7.7 %slice-start.5 = ((s8[12582912]{0:T(1024)(128)(4,1)}), s8[4194304]{0:T(1024)(128)(4,1)S(1)}, s32[]{:S(2)}) async-start(s8[12582912]{0:T(1024)(128)(4,1)} %bitcast.11), calls=%async_computation.5 | async-start | bytes 8388608
  7.9 7.7 %copy-start = (bf16[128,2048]{1,0:T(8,128)(2,1)S(1)}, bf16[128,2048]{1,0:T(8,128)(2,1)}, u32[]{:S(2)}) copy-start(bf16[128,2048]{1,0:T(8,128)(2,1)} %refs_6_.3) | copy-start | bytes 1572868
  7.9 5.3 %collective-permute-start.1 = (bf16[32,896]{1,0:T(8,128)(2,1)S(1)}, bf16[32,896]{1,0:T(8,128)(2,1)S(1)}, u32[]{:S(2)}, u32[]{:S(2)}) collective-permute-start(bf16[32,896]{1,0:T(8,128)(2,1)S(1)} %join.1.after.first), channel_id=1, source_target_pairs={{0,8},{4,12},{8,0},{12,4},{1,9},{5,13},{9,1},{13,5},{2,10},{6,14},... | collective-permute-start | bytes 172040 | tf_op jit(solution)/shard_map/ppermute | solution.py:513
  13.6 4.4 %collective-permute-start.2 = (bf16[40,896]{1,0:T(8,128)(2,1)S(1)}, bf16[40,896]{1,0:T(8,128)(2,1)S(1)}, u32[]{:S(2)}, u32[]{:S(2)}) collective-permute-start(bf16[40,896]{1,0:T(8,128)(2,1)S(1)} %get-tuple-element.19.block.refs_0_), channel_id=1, source_target_pairs={{0,2},{1,3},{2,0},{3,1},{4,6},{5,7},{6,4},{7,5},{8,10},{9,11},{10,... | collective-permute-start | bytes 215048 | tf_op jit(solution)/shard_map/ppermute | solution.py:513
  15.5 3.9 %collective-permute-start.3 = (bf16[40,896]{1,0:T(8,128)(2,1)S(1)}, bf16[40,896]{1,0:T(8,128)(2,1)S(1)}, u32[]{:S(2)}, u32[]{:S(2)}) collective-permute-start(bf16[40,896]{1,0:T(8,128)(2,1)S(1)} %get-tuple-element.19.block.refs_0_), channel_id=1, source_target_pairs={{0,1},{1,0},{2,3},{3,2},{4,5},{5,4},{6,7},{7,6},{8,9},{9,8},{10,11... | collective-permute-start | bytes 215048 | tf_op jit(solution)/shard_map/ppermute | solution.py:513
  18.0 1.4 %collective-permute-start.4 = (bf16[40,896]{1,0:T(8,128)(2,1)S(1)}, bf16[40,896]{1,0:T(8,128)(2,1)S(1)}, u32[]{:S(2)}, u32[]{:S(2)}) collective-permute-start(bf16[40,896]{1,0:T(8,128)(2,1)S(1)} %tie.1.block.refs_1_), channel_id=1, source_target_pairs={{0,1},{1,0},{2,3},{3,2},{4,5},{5,4},{6,7},{7,6},{8,9},{9,8},{10,11... | collective-permute-start | bytes 215048 | tf_op jit(solution)/shard_map/ppermute | solution.py:513
  22.8 1.5 %collective-permute-start.5 = (bf16[2,40,768]{2,1,0:T(8,128)(2,1)S(1)}, bf16[2,40,768]{2,1,0:T(8,128)(2,1)S(1)}, u32[]{:S(2)}, u32[]{:S(2)}) collective-permute-start(bf16[2,40,768]{2,1,0:T(8,128)(2,1)S(1)} %get-tuple-element.23.after), channel_id=1, source_target_pairs={{0,1},{1,0},{2,3},{3,2},{4,5},{5,4},{6,7},{7,6},{8,9},{9,8},{10,11... | collective-permute-start | bytes 368648 | tf_op jit(solution)/shard_map/ppermute | solution.py:513
  24.3 4.5 %collective-permute-start.6 = (bf16[1,40,768]{2,1,0:T(8,128)(2,1)S(1)}, bf16[1,40,768]{2,1,0:T(8,128)(2,1)S(1)}, u32[]{:S(2)}, u32[]{:S(2)}) collective-permute-start(bf16[1,40,768]{2,1,0:T(8,128)(2,1)S(1)} %add_convert_fusion.after), channel_id=1, source_target_pairs={{0,2},{1,3},{2,0},{3,1},{4,6},{5,7},{6,4},{7,5},{8,10},{9,11},{10,... | collective-permute-start | bytes 184328 | tf_op jit(solution)/shard_map/ppermute | solution.py:513
  29.0 4.2 %collective-permute-start.7 = (bf16[2,16,768]{2,1,0:T(8,128)(2,1)S(1)}, bf16[2,16,768]{2,1,0:T(8,128)(2,1)S(1)}, u32[]{:S(2)}, u32[]{:S(2)}) collective-permute-start(bf16[2,16,768]{2,1,0:T(8,128)(2,1)S(1)} %get-tuple-element.26), channel_id=1, source_target_pairs={{0,4},{4,0},{8,12},{12,8},{1,5},{5,1},{9,13},{13,9},{2,6},{6,2},{1... | collective-permute-start | bytes 147464 | tf_op jit(solution)/shard_map/ppermute | solution.py:513
  33.2 4.8 %collective-permute-start.8 = (bf16[1,16,768]{2,1,0:T(8,128)(2,1)S(1)}, bf16[1,16,768]{2,1,0:T(8,128)(2,1)S(1)}, u32[]{:S(2)}, u32[]{:S(2)}) collective-permute-start(bf16[1,16,768]{2,1,0:T(8,128)(2,1)S(1)} %slice.32), channel_id=1, source_target_pairs={{0,8},{4,12},{8,0},{12,4},{1,9},{5,13},{9,1},{13,5},{2,10},{6,14},... | collective-permute-start | bytes 73736 | tf_op jit(solution)/shard_map/ppermute | solution.py:513

commit v9 on v8

--- a/solution.py
+++ b/solution.py
@@ -477,19 +477,20 @@
     )(place, made, *arrived)
 
 
-def mark_kernel(after, weight, out):
+def mark_kernel(after, *refs):
+    out = refs[-1]
     out[...] = jnp.zeros_like(out)
 
 
-def mark(after, weight):
+def mark(after, *weights):
     return pl.pallas_call(
         mark_kernel,
         out_shape=jax.ShapeDtypeStruct((8, LANES), F32),
-        in_specs=[HBM, HBM],
+        in_specs=[HBM] * (1 + len(weights)),
         out_specs=VMEM,
         compiler_params=pltpu.CompilerParams(vmem_limit_bytes=2**20),
         name="mark",
-    )(after, *in_hbm(weight))
+    )(after, *in_hbm(*weights))
 
 
 def tie_kernel(array, after, out):
@@ -558,7 +559,7 @@
     for distance in bits(expert_devices):
         other = swap(held, "ep", distance)
         last = 2 * distance == expert_devices
-        beside = mark(held, expert_down_weight)
+        beside = mark(held, *((expert_down_weight,) if last else (expert_down_weight, expert_gate_weight, expert_up_weight)))
         if last:
             slots = expert_devices * CAP
             held, place = pack(held, other, replicas, slots, beside, expert_up_weight)
@@ -566,7 +567,7 @@
             held = join(held, other, beside)
     steps = bits(tensor_devices)
     groups = [tuple(k for k in range(tensor_devices) if k & -k == step) for step in steps] + [(0,)]
-    early, late = groups[0][-1:], groups[0][:-1]
+    early, late = groups[0][-1:], groups[0][1:-1]
     blocks, order, known, sums, parts = [held], [0], 0, None, []
     for distance in reversed(steps):
         others = [swap(block, "tp", distance) for block in blocks]
@@ -588,7 +589,7 @@
     sent, active, *parts = experts(
         replicas,
         late,
-        groups[1],
+        groups[1] + (1,),
         tuple(order),
         sums,
         known,
@@ -603,7 +604,10 @@
     groups[0] = early + late
     for step, group, following in zip(steps, groups[:-1], groups[1:], strict=True):
         arriving = swap(sent, "tp", step)
-        made = down(following, active, parts, expert_down_weight, features, sent)
+        more = (1,) if parts else ()
+        made = down(following + more, active, parts, expert_down_weight, features, sent)
+        if more:
+            received[0].append(swap(made[-1:].astype(BF16), "tp", 1)[0])
         parts = []
         for i, k in enumerate(group):
             received[k ^ step].append(arriving[i])

time: 38.8 us -> 38.6 us (level)
    pallas_call x2, Pallas kernels: 3.2 us -> 3.74 us  [down(): pl.pallas_call(down_kernel if parts else functools.partial(down_fetching_...]
    pallas_call x1, Pallas kernels: 3.33 us -> 2.89 us  [experts(): pl.pallas_call(functools.partial(expert_kernel, replicas, late, following...]
    ppermute x9 -> x10, waiting for transfers between devices: 9.12 us -> 8.74 us  [swap(): return lax.ppermute(x, axis, [(i, i ^ distance) for i in range(count)])]
    ppermute x9 -> x10, starting transfers between devices: 15.3 us -> 15.5 us  [swap(): return lax.ppermute(x, axis, [(i, i ^ distance) for i in range(count)])]
  transfers between devices with their start and end apart: 9 -> 10, of which waited for: 6 -> 6; matrix products, arithmetic and copies ran while one was open for 0% -> 0% of each run, Pallas kernels for 17% -> 18%
where the time goes in v9:
time: 38.6 us; the launch traced here: 38.4 us
  starting transfers between devices  15.5 us (40%)
  Pallas kernels  13.3 us (34%)
  waiting for transfers between devices  8.74 us (23%)
  other arithmetic  0.65 us (2%)
    ppermute x10, starting transfers between devices, swap(): return lax.ppermute(x, axis, [(i, i ^ distance) for i in range(count)])  15.5 us
    ppermute x10, waiting for transfers between devices, swap(): return lax.ppermute(x, axis, [(i, i ^ distance) for i in range(count)])  8.74 us
    pallas_call x2, Pallas kernels, down(): pl.pallas_call(down_kernel if parts else functools.partial(down_fetching_...  3.74 us
    pallas_call x2, Pallas kernels, partial(): pl.pallas_call(functools.partial(partial_kernel, distance, fetched, first...  3.26 us
    pallas_call x1, Pallas kernels, experts(): pl.pallas_call(functools.partial(expert_kernel, replicas, late, following...  2.89 us
    pallas_call x1, Pallas kernels, attend(): pl.pallas_call(attend_kernel, out_shape=(jax.ShapeDtypeStruct((rows, feat...  2.72 us
  transfers between devices with their start and end apart: 10, of which 6 were waited for; matrix products, arithmetic and copies ran while one was open for 0% of the time, Pallas kernels for 18%

profile of v9, /device:TPU:0, one launch (start us, length us, event | category | flops | bytes accessed | tf_op | source)
XLA Modules:
  0.0 38.4 jit_solution(12088879082000297631)
XLA Ops:
  0.0 2.7 %attend.1 = (bf16[16,768]{1,0:T(8,128)(2,1)S(1)}, bf16[16,896]{1,0:T(8,128)(2,1)S(1)}) custom-call(s32[16]{0:T(128)} %refs_0_.4, s32[16]{0:T(128)} %refs_1_.5, s32[2,16]{1,0:T(2,128)} %bitcast.15, bf16[16,768]{1,0:T(8,128)(2,1)} %refs_3_.1, bf16[16,768]{1,0:T(8,128)(2,1)} %refs_4_.2, bf16[16,256]{1,0:T(8,128)(2,1)} %refs_5_.2, bf16[16,256]{1,0:T(8,128)(2,1)} %refs_6_.2, ...), custom_call_target="tpu_custom_call" | custom-call | flops 200000000 | bytes 3000000 | tf_op jit(solution)/shard_map/attend/pallas_call | solution.py:178
  2.7 0.0 slice-start.3
  2.7 0.0 slice-start.4
  2.7 0.0 slice-start.5
  2.8 3.1 %collective-permute-start = (bf16[16,896]{1,0:T(8,128)(2,1)S(1)}, bf16[16,896]{1,0:T(8,128)(2,1)S(1)}, u32[]{:S(2)}, u32[]{:S(2)}) collective-permute-start(bf16[16,896]{1,0:T(8,128)(2,1)S(1)} %get-tuple-element.18.after.first), channel_id=1, source_target_pairs={{0,4},{4,0},{8,12},{12,8},{1,5},{5,1},{9,13},{13,9},{2,6},{6,2},{1... | collective-permute-start | bytes 86024 | tf_op jit(solution)/shard_map/ppermute | solution.py:514
  5.9 1.8 %collective-permute-done.second = bf16[16,896]{1,0:T(8,128)(2,1)S(1)} collective-permute-done((bf16[16,896]{1,0:T(8,128)(2,1)S(1)}, bf16[16,896]{1,0:T(8,128)(2,1)S(1)}, u32[]{:S(2)}, u32[]{:S(2)}) %collective-permute-start) | collective-permute-done | bytes 28704 | tf_op jit(solution)/shard_map/ppermute | solution.py:514
  7.7 0.0 slice-start
  7.7 0.0 slice-start.1
  7.7 0.0 copy-start
  7.7 3.1 %collective-permute-start.1 = (bf16[32,896]{1,0:T(8,128)(2,1)S(1)}, bf16[32,896]{1,0:T(8,128)(2,1)S(1)}, u32[]{:S(2)}, u32[]{:S(2)}) collective-permute-start(bf16[32,896]{1,0:T(8,128)(2,1)S(1)} %join.1.after.first), channel_id=1, source_target_pairs={{0,8},{4,12},{8,0},{12,4},{1,9},{5,13},{9,1},{13,5},{2,10},{6,14},... | collective-permute-start | bytes 172040 | tf_op jit(solution)/shard_map/ppermute | solution.py:514
  10.8 0.0 slice-start.2
  10.8 2.2 %collective-permute-done.1.second = bf16[32,896]{1,0:T(8,128)(2,1)S(1)} collective-permute-done((bf16[32,896]{1,0:T(8,128)(2,1)S(1)}, bf16[32,896]{1,0:T(8,128)(2,1)S(1)}, u32[]{:S(2)}, u32[]{:S(2)}) %collective-permute-start.1) | collective-permute-done | bytes 57376 | tf_op jit(solution)/shard_map/ppermute | solution.py:514
  13.0 0.0 slice-done.3
  13.0 0.0 slice-done.4
  13.0 0.0 slice-done.5
  13.0 0.5 %pack.1 = (bf16[40,896]{1,0:T(8,128)(2,1)S(1)}, bf16[64,40]{1,0:T(8,128)(2,1)S(1)}) custom-call(bf16[32,896]{1,0:T(8,128)(2,1)S(1)} %join.1.after.first, bf16[32,896]{1,0:T(8,128)(2,1)S(1)} %collective-permute-done.1.second, f32[8,128]{1,0:T(8,128)S(1)} %mark.3.refs_0_, bf16[3072,2048]{1,0:T(8,128)(2,1)S(1)} %bitcast.12), custom_call_target="tpu_custom_call" | custom-call | tf_op jit(solution)/shard_map/pack/pallas_call | solution.py:434
  13.5 1.9 %collective-permute-start.2 = (bf16[40,896]{1,0:T(8,128)(2,1)S(1)}, bf16[40,896]{1,0:T(8,128)(2,1)S(1)}, u32[]{:S(2)}, u32[]{:S(2)}) collective-permute-start(bf16[40,896]{1,0:T(8,128)(2,1)S(1)} %get-tuple-element.20.block.refs_0_), channel_id=1, source_target_pairs={{0,2},{1,3},{2,0},{3,1},{4,6},{5,7},{6,4},{7,5},{8,10},{9,11},{10,... | collective-permute-start | bytes 215048 | tf_op jit(solution)/shard_map/ppermute | solution.py:514
  15.4 0.0 collective-permute-start.3
  15.4 0.0 slice-done
  15.4 0.0 slice-done.1
  15.4 0.0 copy-done
  15.4 0.0 slice-done.2
  15.4 1.9 %partial.2 = (f32[2,40,2048]{2,1,0:T(8,128)S(1)}, bf16[2048,768]{1,0:T(8,128)(2,1)S(1)}) custom-call(bf16[40,896]{1,0:T(8,128)(2,1)S(1)} %get-tuple-element.20.block.refs_0_, bf16[3072,2048]{1,0:T(8,128)(2,1)S(1)} %bitcast.10, bf16[3072,2048]{1,0:T(8,128)(2,1)S(1)} %bitcast.12, bf16[2048,3072]{1,0:T(8,128)(2,1)} %down_weight.1, ...), custom_call_target="tpu_custom_call" | custom-call | flops 251658240 | bytes 3145728 | tf_op jit(solution)/shard_map/partial/pallas_call | solution.py:243
  17.3 0.5 %collective-permute-done.2.array = bf16[40,896]{1,0:T(8,128)(2,1)S(1)} collective-permute-done((bf16[40,896]{1,0:T(8,128)(2,1)S(1)}, bf16[40,896]{1,0:T(8,128)(2,1)S(1)}, u32[]{:S(2)}, u32[]{:S(2)}) %collective-permute-start.2) | collective-permute-done | bytes 71712 | tf_op jit(solution)/shard_map/ppermute | solution.py:514
  17.9 0.0 collective-permute-start.4
  17.9 1.3 %partial.3.sums = f32[2,40,2048]{2,1,0:T(8,128)S(1)} custom-call(bf16[40,896]{1,0:T(8,128)(2,1)S(1)} %tie.1.block.refs_1_, bf16[3072,2048]{1,0:T(8,128)(2,1)S(1)} %bitcast.10, bf16[3072,2048]{1,0:T(8,128)(2,1)S(1)} %bitcast.12, f32[2,40,2048]{2,1,0:T(8,128)S(1)} %get-tuple-element.21.after.refs_0_, bf16[2048,3072]{1,0:T(8,128)(2,1)} %down_weight.1), custom_call_target="tpu_custom_call" | custom-call | flops 251658240 | bytes 3145728 | tf_op jit(solution)/shard_map/partial/pallas_call | solution.py:243
  19.3 0.0 collective-permute-done.3.refs_2_
  19.3 0.0 collective-permute-done.4.refs_3_
  19.3 2.9 %experts.1 = (bf16[1,40,768]{2,1,0:T(8,128)(2,1)S(1)}, bf16[40,2048]{1,0:T(8,128)(2,1)S(1)}, bf16[2048,768]{1,0:T(8,128)(2,1)S(1)}, bf16[2048,768]{1,0:T(8,128)(2,1)S(1)}) custom-call(f32[2,40,2048]{2,1,0:T(8,128)S(1)} %partial.3.sums, bf16[40,896]{1,0:T(8,128)(2,1)S(1)} %get-tuple-element.20.block.refs_0_, bf16[40,896]{1,0:T(8,128)(2,1)S(1)} %tie.1.block.refs_1_, ...), custom_call_target="tpu_custom_call" | custom-call | flops 629145600 | bytes 6291456 | tf_op jit(solution)/shard_map/experts/pallas_call | solution.py:336
  22.2 0.5 %collective-permute-start.5 = (bf16[1,40,768]{2,1,0:T(8,128)(2,1)S(1)}, bf16[1,40,768]{2,1,0:T(8,128)(2,1)S(1)}, u32[]{:S(2)}, u32[]{:S(2)}) collective-permute-start(bf16[1,40,768]{2,1,0:T(8,128)(2,1)S(1)} %get-tuple-element.24.after), channel_id=1, source_target_pairs={{0,1},{1,0},{2,3},{3,2},{4,5},{5,4},{6,7},{7,6},{8,9},{9,8},{10,11... | collective-permute-start | bytes 184328 | tf_op jit(solution)/shard_map/ppermute | solution.py:514
  22.7 1.2 %down.2 = f32[2,40,768]{2,1,0:T(8,128)S(1)} custom-call(bf16[40,2048]{1,0:T(8,128)(2,1)S(1)} %get-tuple-element.23.active, bf16[1,40,768]{2,1,0:T(8,128)(2,1)S(1)} %get-tuple-element.24.after, bf16[2048,768]{1,0:T(8,128)(2,1)S(1)} %get-tuple-element.25.refs_0_, bf16[2048,768]{1,0:T(8,128)(2,1)S(1)} %get-tuple-element.26.refs_1_), custom_call_target="tpu_custom_call" | custom-call | flops 251658240 | bytes 6291456 | tf_op jit(solution)/shard_map/down/pallas_call | solution.py:375
  23.9 0.1 collective-permute-start.6
  24.0 0.0 collective-permute-done.5
  24.1 1.9 %collective-permute-start.7 = (bf16[1,40,768]{2,1,0:T(8,128)(2,1)S(1)}, bf16[1,40,768]{2,1,0:T(8,128)(2,1)S(1)}, u32[]{:S(2)}, u32[]{:S(2)}) collective-permute-start(bf16[1,40,768]{2,1,0:T(8,128)(2,1)S(1)} %fusion.after), channel_id=1, source_target_pairs={{0,2},{1,3},{2,0},{3,1},{4,6},{5,7},{6,4},{7,5},{8,10},{9,11},{10,... | collective-permute-start | bytes 184328 | tf_op jit(solution)/shard_map/ppermute | solution.py:514
  25.9 2.6 %down.3.made = f32[1,40,768]{2,1,0:T(8,128)S(1)} custom-call(bf16[40,2048]{1,0:T(8,128)(2,1)S(1)} %get-tuple-element.23.active, bf16[1,40,768]{2,1,0:T(8,128)(2,1)S(1)} %fusion.after, bf16[2048,3072]{1,0:T(8,128)(2,1)} %down_weight.1), custom_call_target="tpu_custom_call" | custom-call | flops 125829120 | bytes 3145728 | tf_op jit(solution)/shard_map/down/pallas_call | solution.py:375
  28.5 0.0 collective-permute-done.6.refs_0_
  28.5 0.1 collective-permute-done.7.refs_1_
  28.6 0.2 unpack.1
  28.8 1.9 %collective-permute-start.8 = (bf16[2,16,768]{2,1,0:T(8,128)(2,1)S(1)}, bf16[2,16,768]{2,1,0:T(8,128)(2,1)S(1)}, u32[]{:S(2)}, u32[]{:S(2)}) collective-permute-start(bf16[2,16,768]{2,1,0:T(8,128)(2,1)S(1)} %get-tuple-element.28), channel_id=1, source_target_pairs={{0,4},{4,0},{8,12},{12,8},{1,5},{5,1},{9,13},{13,9},{2,6},{6,2},{1... | collective-permute-start | bytes 147464 | tf_op jit(solution)/shard_map/ppermute | solution.py:514
  30.7 2.3 %collective-permute-done.8 = bf16[2,16,768]{2,1,0:T(8,128)(2,1)S(1)} collective-permute-done((bf16[2,16,768]{2,1,0:T(8,128)(2,1)S(1)}, bf16[2,16,768]{2,1,0:T(8,128)(2,1)S(1)}, u32[]{:S(2)}, u32[]{:S(2)}) %collective-permute-start.8) | collective-permute-done | bytes 49184 | tf_op jit(solution)/shard_map/ppermute | solution.py:514
  33.0 3.0 %collective-permute-start.9 = (bf16[1,16,768]{2,1,0:T(8,128)(2,1)S(1)}, bf16[1,16,768]{2,1,0:T(8,128)(2,1)S(1)}, u32[]{:S(2)}, u32[]{:S(2)}) collective-permute-start(bf16[1,16,768]{2,1,0:T(8,128)(2,1)S(1)} %slice.37), channel_id=1, source_target_pairs={{0,8},{4,12},{8,0},{12,4},{1,9},{5,13},{9,1},{13,5},{2,10},{6,14},... | collective-permute-start | bytes 73736 | tf_op jit(solution)/shard_map/ppermute | solution.py:514
  36.0 1.8 %collective-permute-done.9 = bf16[1,16,768]{2,1,0:T(8,128)(2,1)S(1)} collective-permute-done((bf16[1,16,768]{2,1,0:T(8,128)(2,1)S(1)}, bf16[1,16,768]{2,1,0:T(8,128)(2,1)S(1)}, u32[]{:S(2)}, u32[]{:S(2)}) %collective-permute-start.9) | collective-permute-done | bytes 24608 | tf_op jit(solution)/shard_map/ppermute | solution.py:514
  37.8 0.6 %fusion.3 = bf16[16,768]{1,0:T(8,128)(2,1)} fusion(f32[2,16,768]{2,1,0:T(8,128)S(1)} %convert_add_fusion, bf16[1,16,768]{2,1,0:T(8,128)(2,1)S(1)} %collective-permute-done.9, bf16[16,768]{1,0:T(8,128)(2,1)S(1)} %get-tuple-element.17), kind=kLoop, calls=%fused_computation.8 | loop fusion | flops 61440 | bytes 122880 | tf_op jit(solution)/shard_map/convert_element_type | solution.py:625
  (10 shorter events, 0.1 us)
Async XLA Ops:
  2.7 10.3 %slice-start.3 = ((s8[12582912]{0:T(1024)(128)(4,1)}), s8[4194304]{0:T(1024)(128)(4,1)S(1)}, s32[]{:S(2)}) async-start(s8[12582912]{0:T(1024)(128)(4,1)} %bitcast.11), calls=%async_computation.3 | async-start | bytes 8388608
  2.7 10.3 %slice-start.4 = ((s8[12582912]{0:T(1024)(128)(4,1)}), s8[4194304]{0:T(1024)(128)(4,1)S(1)}, s32[]{:S(2)}) async-start(s8[12582912]{0:T(1024)(128)(4,1)} %bitcast.11), calls=%async_computation.4 | async-start | bytes 8388608
  2.7 10.2 %slice-start.5 = ((s8[12582912]{0:T(1024)(128)(4,1)}), s8[4194304]{0:T(1024)(128)(4,1)S(1)}, s32[]{:S(2)}) async-start(s8[12582912]{0:T(1024)(128)(4,1)} %bitcast.11), calls=%async_computation.5 | async-start | bytes 8388608
  2.8 4.9 %collective-permute-start = (bf16[16,896]{1,0:T(8,128)(2,1)S(1)}, bf16[16,896]{1,0:T(8,128)(2,1)S(1)}, u32[]{:S(2)}, u32[]{:S(2)}) collective-permute-start(bf16[16,896]{1,0:T(8,128)(2,1)S(1)} %get-tuple-element.18.after.first), channel_id=1, source_target_pairs={{0,4},{4,0},{8,12},{12,8},{1,5},{5,1},{9,13},{13,9},{2,6},{6,2},{1... | collective-permute-start | bytes 86024 | tf_op jit(solution)/shard_map/ppermute | solution.py:514
  7.7 7.7 %slice-start = ((s8[12582912]{0:T(1024)(128)(4,1)}), s8[4194304]{0:T(1024)(128)(4,1)S(1)}, s32[]{:S(2)}) async-start(s8[12582912]{0:T(1024)(128)(4,1)} %bitcast.9), calls=%async_computation | async-start | bytes 8388608
  7.7 7.7 %slice-start.1 = ((s8[12582912]{0:T(1024)(128)(4,1)}), s8[4194304]{0:T(1024)(128)(4,1)S(1)}, s32[]{:S(2)}) async-start(s8[12582912]{0:T(1024)(128)(4,1)} %bitcast.9), calls=%async_computation.1 | async-start | bytes 8388608
  7.7 7.7 %copy-start = (bf16[128,2048]{1,0:T(8,128)(2,1)S(1)}, bf16[128,2048]{1,0:T(8,128)(2,1)}, u32[]{:S(2)}) copy-start(bf16[128,2048]{1,0:T(8,128)(2,1)} %refs_6_.3) | copy-start | bytes 1572868
  7.7 5.3 %collective-permute-start.1 = (bf16[32,896]{1,0:T(8,128)(2,1)S(1)}, bf16[32,896]{1,0:T(8,128)(2,1)S(1)}, u32[]{:S(2)}, u32[]{:S(2)}) collective-permute-start(bf16[32,896]{1,0:T(8,128)(2,1)S(1)} %join.1.after.first), channel_id=1, source_target_pairs={{0,8},{4,12},{8,0},{12,4},{1,9},{5,13},{9,1},{13,5},{2,10},{6,14},... | collective-permute-start | bytes 172040 | tf_op jit(solution)/shard_map/ppermute | solution.py:514
  10.8 4.6 %slice-start.2 = ((s8[12582912]{0:T(1024)(128)(4,1)}), s8[4194304]{0:T(1024)(128)(4,1)S(1)}, s32[]{:S(2)}) async-start(s8[12582912]{0:T(1024)(128)(4,1)} %bitcast.9), calls=%async_computation.2 | async-start | bytes 8388608
  13.5 4.4 %collective-permute-start.2 = (bf16[40,896]{1,0:T(8,128)(2,1)S(1)}, bf16[40,896]{1,0:T(8,128)(2,1)S(1)}, u32[]{:S(2)}, u32[]{:S(2)}) collective-permute-start(bf16[40,896]{1,0:T(8,128)(2,1)S(1)} %get-tuple-element.20.block.refs_0_), channel_id=1, source_target_pairs={{0,2},{1,3},{2,0},{3,1},{4,6},{5,7},{6,4},{7,5},{8,10},{9,11},{10,... | collective-permute-start | bytes 215048 | tf_op jit(solution)/shard_map/ppermute | solution.py:514
  15.4 3.9 %collective-permute-start.3 = (bf16[40,896]{1,0:T(8,128)(2,1)S(1)}, bf16[40,896]{1,0:T(8,128)(2,1)S(1)}, u32[]{:S(2)}, u32[]{:S(2)}) collective-permute-start(bf16[40,896]{1,0:T(8,128)(2,1)S(1)} %get-tuple-element.20.block.refs_0_), channel_id=1, source_target_pairs={{0,1},{1,0},{2,3},{3,2},{4,5},{5,4},{6,7},{7,6},{8,9},{9,8},{10,11... | collective-permute-start | bytes 215048 | tf_op jit(solution)/shard_map/ppermute | solution.py:514
  17.9 1.4 %collective-permute-start.4 = (bf16[40,896]{1,0:T(8,128)(2,1)S(1)}, bf16[40,896]{1,0:T(8,128)(2,1)S(1)}, u32[]{:S(2)}, u32[]{:S(2)}) collective-permute-start(bf16[40,896]{1,0:T(8,128)(2,1)S(1)} %tie.1.block.refs_1_), channel_id=1, source_target_pairs={{0,1},{1,0},{2,3},{3,2},{4,5},{5,4},{6,7},{7,6},{8,9},{9,8},{10,11... | collective-permute-start | bytes 215048 | tf_op jit(solution)/shard_map/ppermute | solution.py:514
  22.2 1.9 %collective-permute-start.5 = (bf16[1,40,768]{2,1,0:T(8,128)(2,1)S(1)}, bf16[1,40,768]{2,1,0:T(8,128)(2,1)S(1)}, u32[]{:S(2)}, u32[]{:S(2)}) collective-permute-start(bf16[1,40,768]{2,1,0:T(8,128)(2,1)S(1)} %get-tuple-element.24.after), channel_id=1, source_target_pairs={{0,1},{1,0},{2,3},{3,2},{4,5},{5,4},{6,7},{7,6},{8,9},{9,8},{10,11... | collective-permute-start | bytes 184328 | tf_op jit(solution)/shard_map/ppermute | solution.py:514
  23.9 4.6 %collective-permute-start.6 = (bf16[1,40,768]{2,1,0:T(8,128)(2,1)S(1)}, bf16[1,40,768]{2,1,0:T(8,128)(2,1)S(1)}, u32[]{:S(2)}, u32[]{:S(2)}) collective-permute-start(bf16[1,40,768]{2,1,0:T(8,128)(2,1)S(1)} %slice.36), channel_id=1, source_target_pairs={{0,1},{1,0},{2,3},{3,2},{4,5},{5,4},{6,7},{7,6},{8,9},{9,8},{10,11... | collective-permute-start | bytes 184328 | tf_op jit(solution)/shard_map/ppermute | solution.py:514
  24.1 4.5 %collective-permute-start.7 = (bf16[1,40,768]{2,1,0:T(8,128)(2,1)S(1)}, bf16[1,40,768]{2,1,0:T(8,128)(2,1)S(1)}, u32[]{:S(2)}, u32[]{:S(2)}) collective-permute-start(bf16[1,40,768]{2,1,0:T(8,128)(2,1)S(1)} %fusion.after), channel_id=1, source_target_pairs={{0,2},{1,3},{2,0},{3,1},{4,6},{5,7},{6,4},{7,5},{8,10},{9,11},{10,... | collective-permute-start | bytes 184328 | tf_op jit(solution)/shard_map/ppermute | solution.py:514
  28.8 4.2 %collective-permute-start.8 = (bf16[2,16,768]{2,1,0:T(8,128)(2,1)S(1)}, bf16[2,16,768]{2,1,0:T(8,128)(2,1)S(1)}, u32[]{:S(2)}, u32[]{:S(2)}) collective-permute-start(bf16[2,16,768]{2,1,0:T(8,128)(2,1)S(1)} %get-tuple-element.28), channel_id=1, source_target_pairs={{0,4},{4,0},{8,12},{12,8},{1,5},{5,1},{9,13},{13,9},{2,6},{6,2},{1... | collective-permute-start | bytes 147464 | tf_op jit(solution)/shard_map/ppermute | solution.py:514
  33.0 4.8 %collective-permute-start.9 = (bf16[1,16,768]{2,1,0:T(8,128)(2,1)S(1)}, bf16[1,16,768]{2,1,0:T(8,128)(2,1)S(1)}, u32[]{:S(2)}, u32[]{:S(2)}) collective-permute-start(bf16[1,16,768]{2,1,0:T(8,128)(2,1)S(1)} %slice.37), channel_id=1, source_target_pairs={{0,8},{4,12},{8,0},{12,4},{1,9},{5,13},{9,1},{13,5},{2,10},{6,14},... | collective-permute-start | bytes 73736 | tf_op jit(solution)/shard_map/ppermute | solution.py:514

commit v10 on v9

--- a/solution.py
+++ b/solution.py
@@ -601,13 +601,18 @@
         expert_down_weight,
     )
     received = {k: [] for k in range(tensor_devices)}
-    groups[0] = early + late
+    groups[0], one = early + late, None
     for step, group, following in zip(steps, groups[:-1], groups[1:], strict=True):
+        if one is not None:
+            sent, one = lax.optimization_barrier((sent, one))
         arriving = swap(sent, "tp", step)
+        if one is not None:
+            received[0].append(swap(one, "tp", 1)[0])
+        one = None
         more = (1,) if parts else ()
         made = down(following + more, active, parts, expert_down_weight, features, sent)
         if more:
-            received[0].append(swap(made[-1:].astype(BF16), "tp", 1)[0])
+            one = made[-1:].astype(BF16)
         parts = []
         for i, k in enumerate(group):
             received[k ^ step].append(arriving[i])

time: 38.6 us -> 38.6 us (level)
  transfers between devices with their start and end apart: 10 -> 10, of which waited for: 6 -> 5; matrix products, arithmetic and copies ran while one was open for 0% -> 0% of each run, Pallas kernels for 18% -> 18%
where the time goes in v10:
time: 38.6 us; the launch traced here: 38.4 us
  starting transfers between devices  15.5 us (40%)
  Pallas kernels  13.3 us (34%)
  waiting for transfers between devices  8.65 us (22%)
  other arithmetic  0.65 us (2%)
    ppermute x10, starting transfers between devices, swap(): return lax.ppermute(x, axis, [(i, i ^ distance) for i in range(count)])  15.5 us
    ppermute x10, waiting for transfers between devices, swap(): return lax.ppermute(x, axis, [(i, i ^ distance) for i in range(count)])  8.65 us
    pallas_call x2, Pallas kernels, down(): pl.pallas_call(down_kernel if parts else functools.partial(down_fetching_...  3.74 us
    pallas_call x2, Pallas kernels, partial(): pl.pallas_call(functools.partial(partial_kernel, distance, fetched, first...  3.26 us
    pallas_call x1, Pallas kernels, experts(): pl.pallas_call(functools.partial(expert_kernel, replicas, late, following...  2.89 us
    pallas_call x1, Pallas kernels, attend(): pl.pallas_call(attend_kernel, out_shape=(jax.ShapeDtypeStruct((rows, feat...  2.72 us
  transfers between devices with their start and end apart: 10, of which 5 were waited for; matrix products, arithmetic and copies ran while one was open for 0% of the time, Pallas kernels for 18%

profile of v10, /device:TPU:0, one launch (start us, length us, event | category | flops | bytes accessed | tf_op | source)
XLA Modules:
  0.0 38.4 jit_solution(17117341699027388975)
XLA Ops:
  0.0 2.7 %attend.1 = (bf16[16,768]{1,0:T(8,128)(2,1)S(1)}, bf16[16,896]{1,0:T(8,128)(2,1)S(1)}) custom-call(s32[16]{0:T(128)} %refs_0_.4, s32[16]{0:T(128)} %refs_1_.5, s32[2,16]{1,0:T(2,128)} %bitcast.15, bf16[16,768]{1,0:T(8,128)(2,1)} %refs_3_.1, bf16[16,768]{1,0:T(8,128)(2,1)} %refs_4_.2, bf16[16,256]{1,0:T(8,128)(2,1)} %refs_5_.2, bf16[16,256]{1,0:T(8,128)(2,1)} %refs_6_.2, ...), custom_call_target="tpu_custom_call" | custom-call | flops 200000000 | bytes 3000000 | tf_op jit(solution)/shard_map/attend/pallas_call | solution.py:178
  2.7 0.0 slice-start.3
  2.7 0.0 slice-start.4
  2.7 0.0 slice-start.5
  2.8 3.1 %collective-permute-start = (bf16[16,896]{1,0:T(8,128)(2,1)S(1)}, bf16[16,896]{1,0:T(8,128)(2,1)S(1)}, u32[]{:S(2)}, u32[]{:S(2)}) collective-permute-start(bf16[16,896]{1,0:T(8,128)(2,1)S(1)} %get-tuple-element.20.after.first), channel_id=1, source_target_pairs={{0,4},{4,0},{8,12},{12,8},{1,5},{5,1},{9,13},{13,9},{2,6},{6,2},{1... | collective-permute-start | bytes 86024 | tf_op jit(solution)/shard_map/ppermute | solution.py:514
  5.9 1.8 %collective-permute-done.second = bf16[16,896]{1,0:T(8,128)(2,1)S(1)} collective-permute-done((bf16[16,896]{1,0:T(8,128)(2,1)S(1)}, bf16[16,896]{1,0:T(8,128)(2,1)S(1)}, u32[]{:S(2)}, u32[]{:S(2)}) %collective-permute-start) | collective-permute-done | bytes 28704 | tf_op jit(solution)/shard_map/ppermute | solution.py:514
  7.7 0.0 slice-start
  7.7 0.0 slice-start.1
  7.7 0.0 copy-start
  7.7 3.1 %collective-permute-start.1 = (bf16[32,896]{1,0:T(8,128)(2,1)S(1)}, bf16[32,896]{1,0:T(8,128)(2,1)S(1)}, u32[]{:S(2)}, u32[]{:S(2)}) collective-permute-start(bf16[32,896]{1,0:T(8,128)(2,1)S(1)} %join.1.after.first), channel_id=1, source_target_pairs={{0,8},{4,12},{8,0},{12,4},{1,9},{5,13},{9,1},{13,5},{2,10},{6,14},... | collective-permute-start | bytes 172040 | tf_op jit(solution)/shard_map/ppermute | solution.py:514
  10.8 0.0 slice-start.2
  10.8 2.2 %collective-permute-done.1.second = bf16[32,896]{1,0:T(8,128)(2,1)S(1)} collective-permute-done((bf16[32,896]{1,0:T(8,128)(2,1)S(1)}, bf16[32,896]{1,0:T(8,128)(2,1)S(1)}, u32[]{:S(2)}, u32[]{:S(2)}) %collective-permute-start.1) | collective-permute-done | bytes 57376 | tf_op jit(solution)/shard_map/ppermute | solution.py:514
  13.0 0.0 slice-done.3
  13.0 0.0 slice-done.4
  13.0 0.0 slice-done.5
  13.0 0.5 %pack.1 = (bf16[40,896]{1,0:T(8,128)(2,1)S(1)}, bf16[64,40]{1,0:T(8,128)(2,1)S(1)}) custom-call(bf16[32,896]{1,0:T(8,128)(2,1)S(1)} %join.1.after.first, bf16[32,896]{1,0:T(8,128)(2,1)S(1)} %collective-permute-done.1.second, f32[8,128]{1,0:T(8,128)S(1)} %mark.3.refs_0_, bf16[3072,2048]{1,0:T(8,128)(2,1)S(1)} %bitcast.12), custom_call_target="tpu_custom_call" | custom-call | tf_op jit(solution)/shard_map/pack/pallas_call | solution.py:434
  13.5 1.9 %collective-permute-start.2 = (bf16[40,896]{1,0:T(8,128)(2,1)S(1)}, bf16[40,896]{1,0:T(8,128)(2,1)S(1)}, u32[]{:S(2)}, u32[]{:S(2)}) collective-permute-start(bf16[40,896]{1,0:T(8,128)(2,1)S(1)} %get-tuple-element.22.block.refs_0_), channel_id=1, source_target_pairs={{0,2},{1,3},{2,0},{3,1},{4,6},{5,7},{6,4},{7,5},{8,10},{9,11},{10,... | collective-permute-start | bytes 215048 | tf_op jit(solution)/shard_map/ppermute | solution.py:514
  15.4 0.0 collective-permute-start.3
  15.4 0.0 slice-done
  15.4 0.0 slice-done.1
  15.4 0.0 copy-done
  15.4 0.0 slice-done.2
  15.4 1.9 %partial.2 = (f32[2,40,2048]{2,1,0:T(8,128)S(1)}, bf16[2048,768]{1,0:T(8,128)(2,1)S(1)}) custom-call(bf16[40,896]{1,0:T(8,128)(2,1)S(1)} %get-tuple-element.22.block.refs_0_, bf16[3072,2048]{1,0:T(8,128)(2,1)S(1)} %bitcast.10, bf16[3072,2048]{1,0:T(8,128)(2,1)S(1)} %bitcast.12, bf16[2048,3072]{1,0:T(8,128)(2,1)} %down_weight.1, ...), custom_call_target="tpu_custom_call" | custom-call | flops 251658240 | bytes 3145728 | tf_op jit(solution)/shard_map/partial/pallas_call | solution.py:243
  17.3 0.5 %collective-permute-done.2.array = bf16[40,896]{1,0:T(8,128)(2,1)S(1)} collective-permute-done((bf16[40,896]{1,0:T(8,128)(2,1)S(1)}, bf16[40,896]{1,0:T(8,128)(2,1)S(1)}, u32[]{:S(2)}, u32[]{:S(2)}) %collective-permute-start.2) | collective-permute-done | bytes 71712 | tf_op jit(solution)/shard_map/ppermute | solution.py:514
  17.9 0.0 collective-permute-start.4
  17.9 1.3 %partial.3.sums = f32[2,40,2048]{2,1,0:T(8,128)S(1)} custom-call(bf16[40,896]{1,0:T(8,128)(2,1)S(1)} %tie.1.block.refs_1_, bf16[3072,2048]{1,0:T(8,128)(2,1)S(1)} %bitcast.10, bf16[3072,2048]{1,0:T(8,128)(2,1)S(1)} %bitcast.12, f32[2,40,2048]{2,1,0:T(8,128)S(1)} %get-tuple-element.23.after.refs_0_, bf16[2048,3072]{1,0:T(8,128)(2,1)} %down_weight.1), custom_call_target="tpu_custom_call" | custom-call | flops 251658240 | bytes 3145728 | tf_op jit(solution)/shard_map/partial/pallas_call | solution.py:243
  19.3 0.0 collective-permute-done.3.refs_2_
  19.3 0.0 collective-permute-done.4.refs_3_
  19.3 2.9 %experts.1 = (bf16[1,40,768]{2,1,0:T(8,128)(2,1)S(1)}, bf16[40,2048]{1,0:T(8,128)(2,1)S(1)}, bf16[2048,768]{1,0:T(8,128)(2,1)S(1)}, bf16[2048,768]{1,0:T(8,128)(2,1)S(1)}) custom-call(f32[2,40,2048]{2,1,0:T(8,128)S(1)} %partial.3.sums, bf16[40,896]{1,0:T(8,128)(2,1)S(1)} %get-tuple-element.22.block.refs_0_, bf16[40,896]{1,0:T(8,128)(2,1)S(1)} %tie.1.block.refs_1_, ...), custom_call_target="tpu_custom_call" | custom-call | flops 629145600 | bytes 6291456 | tf_op jit(solution)/shard_map/experts/pallas_call | solution.py:336
  22.2 0.5 %collective-permute-start.5 = (bf16[1,40,768]{2,1,0:T(8,128)(2,1)S(1)}, bf16[1,40,768]{2,1,0:T(8,128)(2,1)S(1)}, u32[]{:S(2)}, u32[]{:S(2)}) collective-permute-start(bf16[1,40,768]{2,1,0:T(8,128)(2,1)S(1)} %get-tuple-element.26.after), channel_id=1, source_target_pairs={{0,1},{1,0},{2,3},{3,2},{4,5},{5,4},{6,7},{7,6},{8,9},{9,8},{10,11... | collective-permute-start | bytes 184328 | tf_op jit(solution)/shard_map/ppermute | solution.py:514
  22.7 1.2 %down.2 = f32[2,40,768]{2,1,0:T(8,128)S(1)} custom-call(bf16[40,2048]{1,0:T(8,128)(2,1)S(1)} %get-tuple-element.25.active, bf16[1,40,768]{2,1,0:T(8,128)(2,1)S(1)} %get-tuple-element.26.after, bf16[2048,768]{1,0:T(8,128)(2,1)S(1)} %get-tuple-element.27.refs_0_, bf16[2048,768]{1,0:T(8,128)(2,1)S(1)} %get-tuple-element.28.refs_1_), custom_call_target="tpu_custom_call" | custom-call | flops 251658240 | bytes 6291456 | tf_op jit(solution)/shard_map/down/pallas_call | solution.py:375
  23.9 0.0 collective-permute-done.5
  24.0 0.1 collective-permute-start.6
  24.1 1.9 %collective-permute-start.7 = (bf16[1,40,768]{2,1,0:T(8,128)(2,1)S(1)}, bf16[1,40,768]{2,1,0:T(8,128)(2,1)S(1)}, u32[]{:S(2)}, u32[]{:S(2)}) collective-permute-start(bf16[1,40,768]{2,1,0:T(8,128)(2,1)S(1)} %fusion.after), channel_id=1, source_target_pairs={{0,2},{1,3},{2,0},{3,1},{4,6},{5,7},{6,4},{7,5},{8,10},{9,11},{10,... | collective-permute-start | bytes 184328 | tf_op jit(solution)/shard_map/ppermute | solution.py:514
  25.9 2.6 %down.3.made = f32[1,40,768]{2,1,0:T(8,128)S(1)} custom-call(bf16[40,2048]{1,0:T(8,128)(2,1)S(1)} %get-tuple-element.25.active, bf16[1,40,768]{2,1,0:T(8,128)(2,1)S(1)} %fusion.after, bf16[2048,3072]{1,0:T(8,128)(2,1)} %down_weight.1), custom_call_target="tpu_custom_call" | custom-call | flops 125829120 | bytes 3145728 | tf_op jit(solution)/shard_map/down/pallas_call | solution.py:375
  28.5 0.0 collective-permute-done.6.refs_0_
  28.5 0.0 collective-permute-done.7.refs_1_
  28.5 0.2 unpack.1
  28.8 1.9 %collective-permute-start.8 = (bf16[2,16,768]{2,1,0:T(8,128)(2,1)S(1)}, bf16[2,16,768]{2,1,0:T(8,128)(2,1)S(1)}, u32[]{:S(2)}, u32[]{:S(2)}) collective-permute-start(bf16[2,16,768]{2,1,0:T(8,128)(2,1)S(1)} %get-tuple-element.32), channel_id=1, source_target_pairs={{0,4},{4,0},{8,12},{12,8},{1,5},{5,1},{9,13},{13,9},{2,6},{6,2},{1... | collective-permute-start | bytes 147464 | tf_op jit(solution)/shard_map/ppermute | solution.py:514
  30.7 2.3 %collective-permute-done.8 = bf16[2,16,768]{2,1,0:T(8,128)(2,1)S(1)} collective-permute-done((bf16[2,16,768]{2,1,0:T(8,128)(2,1)S(1)}, bf16[2,16,768]{2,1,0:T(8,128)(2,1)S(1)}, u32[]{:S(2)}, u32[]{:S(2)}) %collective-permute-start.8) | collective-permute-done | bytes 49184 | tf_op jit(solution)/shard_map/ppermute | solution.py:514
  32.9 3.0 %collective-permute-start.9 = (bf16[1,16,768]{2,1,0:T(8,128)(2,1)S(1)}, bf16[1,16,768]{2,1,0:T(8,128)(2,1)S(1)}, u32[]{:S(2)}, u32[]{:S(2)}) collective-permute-start(bf16[1,16,768]{2,1,0:T(8,128)(2,1)S(1)} %slice.37), channel_id=1, source_target_pairs={{0,8},{4,12},{8,0},{12,4},{1,9},{5,13},{9,1},{13,5},{2,10},{6,14},... | collective-permute-start | bytes 73736 | tf_op jit(solution)/shard_map/ppermute | solution.py:514
  35.9 1.8 %collective-permute-done.9 = bf16[1,16,768]{2,1,0:T(8,128)(2,1)S(1)} collective-permute-done((bf16[1,16,768]{2,1,0:T(8,128)(2,1)S(1)}, bf16[1,16,768]{2,1,0:T(8,128)(2,1)S(1)}, u32[]{:S(2)}, u32[]{:S(2)}) %collective-permute-start.9) | collective-permute-done | bytes 24608 | tf_op jit(solution)/shard_map/ppermute | solution.py:514
  37.7 0.6 %fusion.3 = bf16[16,768]{1,0:T(8,128)(2,1)} fusion(f32[2,16,768]{2,1,0:T(8,128)S(1)} %convert_add_fusion, bf16[1,16,768]{2,1,0:T(8,128)(2,1)S(1)} %collective-permute-done.9, bf16[16,768]{1,0:T(8,128)(2,1)S(1)} %get-tuple-element.19), kind=kLoop, calls=%fused_computation.8 | loop fusion | flops 61440 | bytes 122880 | tf_op jit(solution)/shard_map/convert_element_type | solution.py:630
  (10 shorter events, 0.1 us)
Async XLA Ops:
  2.7 10.3 %slice-start.3 = ((s8[12582912]{0:T(1024)(128)(4,1)}), s8[4194304]{0:T(1024)(128)(4,1)S(1)}, s32[]{:S(2)}) async-start(s8[12582912]{0:T(1024)(128)(4,1)} %bitcast.11), calls=%async_computation.3 | async-start | bytes 8388608
  2.7 10.3 %slice-start.4 = ((s8[12582912]{0:T(1024)(128)(4,1)}), s8[4194304]{0:T(1024)(128)(4,1)S(1)}, s32[]{:S(2)}) async-start(s8[12582912]{0:T(1024)(128)(4,1)} %bitcast.11), calls=%async_computation.4 | async-start | bytes 8388608
  2.7 10.2 %slice-start.5 = ((s8[12582912]{0:T(1024)(128)(4,1)}), s8[4194304]{0:T(1024)(128)(4,1)S(1)}, s32[]{:S(2)}) async-start(s8[12582912]{0:T(1024)(128)(4,1)} %bitcast.11), calls=%async_computation.5 | async-start | bytes 8388608
  2.8 4.9 %collective-permute-start = (bf16[16,896]{1,0:T(8,128)(2,1)S(1)}, bf16[16,896]{1,0:T(8,128)(2,1)S(1)}, u32[]{:S(2)}, u32[]{:S(2)}) collective-permute-start(bf16[16,896]{1,0:T(8,128)(2,1)S(1)} %get-tuple-element.20.after.first), channel_id=1, source_target_pairs={{0,4},{4,0},{8,12},{12,8},{1,5},{5,1},{9,13},{13,9},{2,6},{6,2},{1... | collective-permute-start | bytes 86024 | tf_op jit(solution)/shard_map/ppermute | solution.py:514
  7.7 7.7 %slice-start = ((s8[12582912]{0:T(1024)(128)(4,1)}), s8[4194304]{0:T(1024)(128)(4,1)S(1)}, s32[]{:S(2)}) async-start(s8[12582912]{0:T(1024)(128)(4,1)} %bitcast.9), calls=%async_computation | async-start | bytes 8388608
  7.7 7.7 %slice-start.1 = ((s8[12582912]{0:T(1024)(128)(4,1)}), s8[4194304]{0:T(1024)(128)(4,1)S(1)}, s32[]{:S(2)}) async-start(s8[12582912]{0:T(1024)(128)(4,1)} %bitcast.9), calls=%async_computation.1 | async-start | bytes 8388608
  7.7 7.7 %copy-start = (bf16[128,2048]{1,0:T(8,128)(2,1)S(1)}, bf16[128,2048]{1,0:T(8,128)(2,1)}, u32[]{:S(2)}) copy-start(bf16[128,2048]{1,0:T(8,128)(2,1)} %refs_6_.3) | copy-start | bytes 1572868
  7.7 5.3 %collective-permute-start.1 = (bf16[32,896]{1,0:T(8,128)(2,1)S(1)}, bf16[32,896]{1,0:T(8,128)(2,1)S(1)}, u32[]{:S(2)}, u32[]{:S(2)}) collective-permute-start(bf16[32,896]{1,0:T(8,128)(2,1)S(1)} %join.1.after.first), channel_id=1, source_target_pairs={{0,8},{4,12},{8,0},{12,4},{1,9},{5,13},{9,1},{13,5},{2,10},{6,14},... | collective-permute-start | bytes 172040 | tf_op jit(solution)/shard_map/ppermute | solution.py:514
  10.8 4.6 %slice-start.2 = ((s8[12582912]{0:T(1024)(128)(4,1)}), s8[4194304]{0:T(1024)(128)(4,1)S(1)}, s32[]{:S(2)}) async-start(s8[12582912]{0:T(1024)(128)(4,1)} %bitcast.9), calls=%async_computation.2 | async-start | bytes 8388608
  13.5 4.4 %collective-permute-start.2 = (bf16[40,896]{1,0:T(8,128)(2,1)S(1)}, bf16[40,896]{1,0:T(8,128)(2,1)S(1)}, u32[]{:S(2)}, u32[]{:S(2)}) collective-permute-start(bf16[40,896]{1,0:T(8,128)(2,1)S(1)} %get-tuple-element.22.block.refs_0_), channel_id=1, source_target_pairs={{0,2},{1,3},{2,0},{3,1},{4,6},{5,7},{6,4},{7,5},{8,10},{9,11},{10,... | collective-permute-start | bytes 215048 | tf_op jit(solution)/shard_map/ppermute | solution.py:514
  15.4 3.9 %collective-permute-start.3 = (bf16[40,896]{1,0:T(8,128)(2,1)S(1)}, bf16[40,896]{1,0:T(8,128)(2,1)S(1)}, u32[]{:S(2)}, u32[]{:S(2)}) collective-permute-start(bf16[40,896]{1,0:T(8,128)(2,1)S(1)} %get-tuple-element.22.block.refs_0_), channel_id=1, source_target_pairs={{0,1},{1,0},{2,3},{3,2},{4,5},{5,4},{6,7},{7,6},{8,9},{9,8},{10,11... | collective-permute-start | bytes 215048 | tf_op jit(solution)/shard_map/ppermute | solution.py:514
  17.9 1.4 %collective-permute-start.4 = (bf16[40,896]{1,0:T(8,128)(2,1)S(1)}, bf16[40,896]{1,0:T(8,128)(2,1)S(1)}, u32[]{:S(2)}, u32[]{:S(2)}) collective-permute-start(bf16[40,896]{1,0:T(8,128)(2,1)S(1)} %tie.1.block.refs_1_), channel_id=1, source_target_pairs={{0,1},{1,0},{2,3},{3,2},{4,5},{5,4},{6,7},{7,6},{8,9},{9,8},{10,11... | collective-permute-start | bytes 215048 | tf_op jit(solution)/shard_map/ppermute | solution.py:514
  22.2 1.8 %collective-permute-start.5 = (bf16[1,40,768]{2,1,0:T(8,128)(2,1)S(1)}, bf16[1,40,768]{2,1,0:T(8,128)(2,1)S(1)}, u32[]{:S(2)}, u32[]{:S(2)}) collective-permute-start(bf16[1,40,768]{2,1,0:T(8,128)(2,1)S(1)} %get-tuple-element.26.after), channel_id=1, source_target_pairs={{0,1},{1,0},{2,3},{3,2},{4,5},{5,4},{6,7},{7,6},{8,9},{9,8},{10,11... | collective-permute-start | bytes 184328 | tf_op jit(solution)/shard_map/ppermute | solution.py:514
  24.0 4.5 %collective-permute-start.6 = (bf16[1,40,768]{2,1,0:T(8,128)(2,1)S(1)}, bf16[1,40,768]{2,1,0:T(8,128)(2,1)S(1)}, u32[]{:S(2)}, u32[]{:S(2)}) collective-permute-start(bf16[1,40,768]{2,1,0:T(8,128)(2,1)S(1)} %slice.36), channel_id=1, source_target_pairs={{0,1},{1,0},{2,3},{3,2},{4,5},{5,4},{6,7},{7,6},{8,9},{9,8},{10,11... | collective-permute-start | bytes 184328 | tf_op jit(solution)/shard_map/ppermute | solution.py:514
  24.1 4.5 %collective-permute-start.7 = (bf16[1,40,768]{2,1,0:T(8,128)(2,1)S(1)}, bf16[1,40,768]{2,1,0:T(8,128)(2,1)S(1)}, u32[]{:S(2)}, u32[]{:S(2)}) collective-permute-start(bf16[1,40,768]{2,1,0:T(8,128)(2,1)S(1)} %fusion.after), channel_id=1, source_target_pairs={{0,2},{1,3},{2,0},{3,1},{4,6},{5,7},{6,4},{7,5},{8,10},{9,11},{10,... | collective-permute-start | bytes 184328 | tf_op jit(solution)/shard_map/ppermute | solution.py:514
  28.8 4.2 %collective-permute-start.8 = (bf16[2,16,768]{2,1,0:T(8,128)(2,1)S(1)}, bf16[2,16,768]{2,1,0:T(8,128)(2,1)S(1)}, u32[]{:S(2)}, u32[]{:S(2)}) collective-permute-start(bf16[2,16,768]{2,1,0:T(8,128)(2,1)S(1)} %get-tuple-element.32), channel_id=1, source_target_pairs={{0,4},{4,0},{8,12},{12,8},{1,5},{5,1},{9,13},{13,9},{2,6},{6,2},{1... | collective-permute-start | bytes 147464 | tf_op jit(solution)/shard_map/ppermute | solution.py:514
  32.9 4.8 %collective-permute-start.9 = (bf16[1,16,768]{2,1,0:T(8,128)(2,1)S(1)}, bf16[1,16,768]{2,1,0:T(8,128)(2,1)S(1)}, u32[]{:S(2)}, u32[]{:S(2)}) collective-permute-start(bf16[1,16,768]{2,1,0:T(8,128)(2,1)S(1)} %slice.37), channel_id=1, source_target_pairs={{0,8},{4,12},{8,0},{12,4},{1,9},{5,13},{9,1},{13,5},{2,10},{6,14},... | collective-permute-start | bytes 73736 | tf_op jit(solution)/shard_map/ppermute | solution.py:514

commit v11 on v9

--- a/solution.py
+++ b/solution.py
@@ -360,24 +360,44 @@
         out[i] = jnp.dot(active[...], part[...], preferred_element_type=F32)
 
 
-def down_fetching_kernel(targets, active, after, down_weight, out, *refs):
-    parts, arrived = refs[:-1], refs[-1]
-    for i, copy in enumerate(fetch(down_weight, targets, parts, arrived)):
+def down_fetching_kernel(targets, active, after, down_weight, out, parts, arrived):
+    hidden = active.shape[1]
+    tile = halves(hidden)
+    pieces = [(i, start) for i in range(len(targets)) for start in range(0, hidden, tile)]
+    copies = []
+    for n, (i, start) in enumerate(pieces):
+        lanes = at_distance(targets[i], out.shape[2])
+        copies.append(
+            pltpu.make_async_copy(
+                down_weight.at[pl.ds(start, tile), lanes],
+                parts.at[i, pl.ds(start, tile), :],
+                arrived.at[n],
+            )
+        )
+        copies[-1].start()
+    for (i, start), copy in zip(pieces, copies, strict=True):
         copy.wait()
-        out[i] = jnp.dot(active[...], parts[i][...], preferred_element_type=F32)
+        product = jnp.dot(
+            active[:, start : start + tile],
+            parts[i, start : start + tile, :],
+            preferred_element_type=F32,
+        )
+        out[i] = out[i] + product if start else product
 
 
 def down(targets, active, parts, down_weight, features, after):
     rows, hidden = active.shape
     count = len(targets)
-    columns = pltpu.VMEM((hidden, features), BF16)
-    scratch = () if parts else (*[columns] * count, pltpu.SemaphoreType.DMA((count,)))
+    scratch = (
+        pltpu.VMEM((count, hidden, features), BF16),
+        pltpu.SemaphoreType.DMA((count * (hidden // halves(hidden)),)),
+    )
     return pl.pallas_call(
         down_kernel if parts else functools.partial(down_fetching_kernel, targets),
         out_shape=jax.ShapeDtypeStruct((count, rows, features), F32),
         in_specs=[VMEM, HBM] + ([VMEM] * count if parts else [HBM]),
         out_specs=VMEM,
-        scratch_shapes=scratch,
+        scratch_shapes=() if parts else scratch,
         compiler_params=pltpu.CompilerParams(vmem_limit_bytes=5 * 2**20),
         cost_estimate=pl.CostEstimate(
             flops=2 * rows * hidden * features * count,

time: 38.6 us -> 38.6 us (level)
  no operation moved by 1% of the time
where the time goes in v11:
time: 38.6 us; the launch traced here: 38.4 us
  starting transfers between devices  15.5 us (40%)
  Pallas kernels  13.1 us (34%)
  waiting for transfers between devices  8.95 us (23%)
  other arithmetic  0.65 us (2%)
    ppermute x10, starting transfers between devices, swap(): return lax.ppermute(x, axis, [(i, i ^ distance) for i in range(count)])  15.5 us
    ppermute x10, waiting for transfers between devices, swap(): return lax.ppermute(x, axis, [(i, i ^ distance) for i in range(count)])  8.95 us
    pallas_call x2, Pallas kernels, down(): pl.pallas_call(down_kernel if parts else functools.partial(down_fetching_...  3.53 us
    pallas_call x2, Pallas kernels, partial(): pl.pallas_call(functools.partial(partial_kernel, distance, fetched, first...  3.26 us
    pallas_call x1, Pallas kernels, experts(): pl.pallas_call(functools.partial(expert_kernel, replicas, late, following...  2.89 us
    pallas_call x1, Pallas kernels, attend(): pl.pallas_call(attend_kernel, out_shape=(jax.ShapeDtypeStruct((rows, feat...  2.72 us
  transfers between devices with their start and end apart: 10, of which 6 were waited for; matrix products, arithmetic and copies ran while one was open for 0% of the time, Pallas kernels for 18%

profile of v11, /device:TPU:0, one launch (start us, length us, event | category | flops | bytes accessed | tf_op | source)
XLA Modules:
  0.0 38.4 jit_solution(2987713128544675128)
XLA Ops:
  0.0 2.7 %attend.1 = (bf16[16,768]{1,0:T(8,128)(2,1)S(1)}, bf16[16,896]{1,0:T(8,128)(2,1)S(1)}) custom-call(s32[16]{0:T(128)} %refs_0_.4, s32[16]{0:T(128)} %refs_1_.5, s32[2,16]{1,0:T(2,128)} %bitcast.15, bf16[16,768]{1,0:T(8,128)(2,1)} %refs_3_.1, bf16[16,768]{1,0:T(8,128)(2,1)} %refs_4_.2, bf16[16,256]{1,0:T(8,128)(2,1)} %refs_5_.2, bf16[16,256]{1,0:T(8,128)(2,1)} %refs_6_.2, ...), custom_call_target="tpu_custom_call" | custom-call | flops 200000000 | bytes 3000000 | tf_op jit(solution)/shard_map/attend/pallas_call | solution.py:178
  2.7 0.0 slice-start.3
  2.7 0.0 slice-start.4
  2.7 0.0 slice-start.5
  2.8 3.1 %collective-permute-start = (bf16[16,896]{1,0:T(8,128)(2,1)S(1)}, bf16[16,896]{1,0:T(8,128)(2,1)S(1)}, u32[]{:S(2)}, u32[]{:S(2)}) collective-permute-start(bf16[16,896]{1,0:T(8,128)(2,1)S(1)} %get-tuple-element.18.after.first), channel_id=1, source_target_pairs={{0,4},{4,0},{8,12},{12,8},{1,5},{5,1},{9,13},{13,9},{2,6},{6,2},{1... | collective-permute-start | bytes 86024 | tf_op jit(solution)/shard_map/ppermute | solution.py:534
  5.9 1.8 %collective-permute-done.second = bf16[16,896]{1,0:T(8,128)(2,1)S(1)} collective-permute-done((bf16[16,896]{1,0:T(8,128)(2,1)S(1)}, bf16[16,896]{1,0:T(8,128)(2,1)S(1)}, u32[]{:S(2)}, u32[]{:S(2)}) %collective-permute-start) | collective-permute-done | bytes 28704 | tf_op jit(solution)/shard_map/ppermute | solution.py:534
  7.7 0.0 slice-start
  7.7 0.0 slice-start.1
  7.7 0.0 copy-start
  7.7 3.1 %collective-permute-start.1 = (bf16[32,896]{1,0:T(8,128)(2,1)S(1)}, bf16[32,896]{1,0:T(8,128)(2,1)S(1)}, u32[]{:S(2)}, u32[]{:S(2)}) collective-permute-start(bf16[32,896]{1,0:T(8,128)(2,1)S(1)} %join.1.after.first), channel_id=1, source_target_pairs={{0,8},{4,12},{8,0},{12,4},{1,9},{5,13},{9,1},{13,5},{2,10},{6,14},... | collective-permute-start | bytes 172040 | tf_op jit(solution)/shard_map/ppermute | solution.py:534
  10.8 0.0 slice-start.2
  10.8 2.2 %collective-permute-done.1.second = bf16[32,896]{1,0:T(8,128)(2,1)S(1)} collective-permute-done((bf16[32,896]{1,0:T(8,128)(2,1)S(1)}, bf16[32,896]{1,0:T(8,128)(2,1)S(1)}, u32[]{:S(2)}, u32[]{:S(2)}) %collective-permute-start.1) | collective-permute-done | bytes 57376 | tf_op jit(solution)/shard_map/ppermute | solution.py:534
  13.0 0.0 slice-done.3
  13.0 0.0 slice-done.4
  13.0 0.0 slice-done.5
  13.0 0.5 %pack.1 = (bf16[40,896]{1,0:T(8,128)(2,1)S(1)}, bf16[64,40]{1,0:T(8,128)(2,1)S(1)}) custom-call(bf16[32,896]{1,0:T(8,128)(2,1)S(1)} %join.1.after.first, bf16[32,896]{1,0:T(8,128)(2,1)S(1)} %collective-permute-done.1.second, f32[8,128]{1,0:T(8,128)S(1)} %mark.3.refs_0_, bf16[3072,2048]{1,0:T(8,128)(2,1)S(1)} %bitcast.12), custom_call_target="tpu_custom_call" | custom-call | tf_op jit(solution)/shard_map/pack/pallas_call | solution.py:454
  13.5 1.9 %collective-permute-start.2 = (bf16[40,896]{1,0:T(8,128)(2,1)S(1)}, bf16[40,896]{1,0:T(8,128)(2,1)S(1)}, u32[]{:S(2)}, u32[]{:S(2)}) collective-permute-start(bf16[40,896]{1,0:T(8,128)(2,1)S(1)} %get-tuple-element.20.block.refs_0_), channel_id=1, source_target_pairs={{0,2},{1,3},{2,0},{3,1},{4,6},{5,7},{6,4},{7,5},{8,10},{9,11},{10,... | collective-permute-start | bytes 215048 | tf_op jit(solution)/shard_map/ppermute | solution.py:534
  15.4 0.0 collective-permute-start.3
  15.4 0.0 slice-done
  15.4 0.0 slice-done.1
  15.4 0.0 copy-done
  15.4 0.0 slice-done.2
  15.4 1.9 %partial.2 = (f32[2,40,2048]{2,1,0:T(8,128)S(1)}, bf16[2048,768]{1,0:T(8,128)(2,1)S(1)}) custom-call(bf16[40,896]{1,0:T(8,128)(2,1)S(1)} %get-tuple-element.20.block.refs_0_, bf16[3072,2048]{1,0:T(8,128)(2,1)S(1)} %bitcast.10, bf16[3072,2048]{1,0:T(8,128)(2,1)S(1)} %bitcast.12, bf16[2048,3072]{1,0:T(8,128)(2,1)} %down_weight.1, ...), custom_call_target="tpu_custom_call" | custom-call | flops 251658240 | bytes 3145728 | tf_op jit(solution)/shard_map/partial/pallas_call | solution.py:243
  17.3 0.5 %collective-permute-done.2.array = bf16[40,896]{1,0:T(8,128)(2,1)S(1)} collective-permute-done((bf16[40,896]{1,0:T(8,128)(2,1)S(1)}, bf16[40,896]{1,0:T(8,128)(2,1)S(1)}, u32[]{:S(2)}, u32[]{:S(2)}) %collective-permute-start.2) | collective-permute-done | bytes 71712 | tf_op jit(solution)/shard_map/ppermute | solution.py:534
  17.9 0.0 collective-permute-start.4
  17.9 1.3 %partial.3.sums = f32[2,40,2048]{2,1,0:T(8,128)S(1)} custom-call(bf16[40,896]{1,0:T(8,128)(2,1)S(1)} %tie.1.block.refs_1_, bf16[3072,2048]{1,0:T(8,128)(2,1)S(1)} %bitcast.10, bf16[3072,2048]{1,0:T(8,128)(2,1)S(1)} %bitcast.12, f32[2,40,2048]{2,1,0:T(8,128)S(1)} %get-tuple-element.21.after.refs_0_, bf16[2048,3072]{1,0:T(8,128)(2,1)} %down_weight.1), custom_call_target="tpu_custom_call" | custom-call | flops 251658240 | bytes 3145728 | tf_op jit(solution)/shard_map/partial/pallas_call | solution.py:243
  19.3 0.0 collective-permute-done.3.refs_2_
  19.3 0.0 collective-permute-done.4.refs_3_
  19.3 2.9 %experts.1 = (bf16[1,40,768]{2,1,0:T(8,128)(2,1)S(1)}, bf16[40,2048]{1,0:T(8,128)(2,1)S(1)}, bf16[2048,768]{1,0:T(8,128)(2,1)S(1)}, bf16[2048,768]{1,0:T(8,128)(2,1)S(1)}) custom-call(f32[2,40,2048]{2,1,0:T(8,128)S(1)} %partial.3.sums, bf16[40,896]{1,0:T(8,128)(2,1)S(1)} %get-tuple-element.20.block.refs_0_, bf16[40,896]{1,0:T(8,128)(2,1)S(1)} %tie.1.block.refs_1_, ...), custom_call_target="tpu_custom_call" | custom-call | flops 629145600 | bytes 6291456 | tf_op jit(solution)/shard_map/experts/pallas_call | solution.py:336
  22.2 0.5 %collective-permute-start.5 = (bf16[1,40,768]{2,1,0:T(8,128)(2,1)S(1)}, bf16[1,40,768]{2,1,0:T(8,128)(2,1)S(1)}, u32[]{:S(2)}, u32[]{:S(2)}) collective-permute-start(bf16[1,40,768]{2,1,0:T(8,128)(2,1)S(1)} %get-tuple-element.24.after), channel_id=1, source_target_pairs={{0,1},{1,0},{2,3},{3,2},{4,5},{5,4},{6,7},{7,6},{8,9},{9,8},{10,11... | collective-permute-start | bytes 184328 | tf_op jit(solution)/shard_map/ppermute | solution.py:534
  22.7 1.2 %down.2 = f32[2,40,768]{2,1,0:T(8,128)S(1)} custom-call(bf16[40,2048]{1,0:T(8,128)(2,1)S(1)} %get-tuple-element.23.active, bf16[1,40,768]{2,1,0:T(8,128)(2,1)S(1)} %get-tuple-element.24.after, bf16[2048,768]{1,0:T(8,128)(2,1)S(1)} %get-tuple-element.25.refs_0_, bf16[2048,768]{1,0:T(8,128)(2,1)S(1)} %get-tuple-element.26.refs_1_), custom_call_target="tpu_custom_call" | custom-call | flops 251658240 | bytes 6291456 | tf_op jit(solution)/shard_map/down/pallas_call | solution.py:395
  23.9 0.1 collective-permute-start.6
  24.0 0.0 collective-permute-done.5
  24.1 1.9 %collective-permute-start.7 = (bf16[1,40,768]{2,1,0:T(8,128)(2,1)S(1)}, bf16[1,40,768]{2,1,0:T(8,128)(2,1)S(1)}, u32[]{:S(2)}, u32[]{:S(2)}) collective-permute-start(bf16[1,40,768]{2,1,0:T(8,128)(2,1)S(1)} %fusion.after), channel_id=1, source_target_pairs={{0,2},{1,3},{2,0},{3,1},{4,6},{5,7},{6,4},{7,5},{8,10},{9,11},{10,... | collective-permute-start | bytes 184328 | tf_op jit(solution)/shard_map/ppermute | solution.py:534
  25.9 2.3 %down.3.made = f32[1,40,768]{2,1,0:T(8,128)S(1)} custom-call(bf16[40,2048]{1,0:T(8,128)(2,1)S(1)} %get-tuple-element.23.active, bf16[1,40,768]{2,1,0:T(8,128)(2,1)S(1)} %fusion.after, bf16[2048,3072]{1,0:T(8,128)(2,1)} %down_weight.1), custom_call_target="tpu_custom_call" | custom-call | flops 125829120 | bytes 3145728 | tf_op jit(solution)/shard_map/down/pallas_call | solution.py:395
  28.3 0.0 collective-permute-done.6.refs_0_
  28.3 0.3 collective-permute-done.7.refs_1_
  28.6 0.2 unpack.1
  28.8 1.9 %collective-permute-start.8 = (bf16[2,16,768]{2,1,0:T(8,128)(2,1)S(1)}, bf16[2,16,768]{2,1,0:T(8,128)(2,1)S(1)}, u32[]{:S(2)}, u32[]{:S(2)}) collective-permute-start(bf16[2,16,768]{2,1,0:T(8,128)(2,1)S(1)} %get-tuple-element.28), channel_id=1, source_target_pairs={{0,4},{4,0},{8,12},{12,8},{1,5},{5,1},{9,13},{13,9},{2,6},{6,2},{1... | collective-permute-start | bytes 147464 | tf_op jit(solution)/shard_map/ppermute | solution.py:534
  30.7 2.3 %collective-permute-done.8 = bf16[2,16,768]{2,1,0:T(8,128)(2,1)S(1)} collective-permute-done((bf16[2,16,768]{2,1,0:T(8,128)(2,1)S(1)}, bf16[2,16,768]{2,1,0:T(8,128)(2,1)S(1)}, u32[]{:S(2)}, u32[]{:S(2)}) %collective-permute-start.8) | collective-permute-done | bytes 49184 | tf_op jit(solution)/shard_map/ppermute | solution.py:534
  33.0 3.0 %collective-permute-start.9 = (bf16[1,16,768]{2,1,0:T(8,128)(2,1)S(1)}, bf16[1,16,768]{2,1,0:T(8,128)(2,1)S(1)}, u32[]{:S(2)}, u32[]{:S(2)}) collective-permute-start(bf16[1,16,768]{2,1,0:T(8,128)(2,1)S(1)} %slice.37), channel_id=1, source_target_pairs={{0,8},{4,12},{8,0},{12,4},{1,9},{5,13},{9,1},{13,5},{2,10},{6,14},... | collective-permute-start | bytes 73736 | tf_op jit(solution)/shard_map/ppermute | solution.py:534
  36.0 1.8 %collective-permute-done.9 = bf16[1,16,768]{2,1,0:T(8,128)(2,1)S(1)} collective-permute-done((bf16[1,16,768]{2,1,0:T(8,128)(2,1)S(1)}, bf16[1,16,768]{2,1,0:T(8,128)(2,1)S(1)}, u32[]{:S(2)}, u32[]{:S(2)}) %collective-permute-start.9) | collective-permute-done | bytes 24608 | tf_op jit(solution)/shard_map/ppermute | solution.py:534
  37.8 0.6 %fusion.3 = bf16[16,768]{1,0:T(8,128)(2,1)} fusion(f32[2,16,768]{2,1,0:T(8,128)S(1)} %convert_add_fusion, bf16[1,16,768]{2,1,0:T(8,128)(2,1)S(1)} %collective-permute-done.9, bf16[16,768]{1,0:T(8,128)(2,1)S(1)} %get-tuple-element.17), kind=kLoop, calls=%fused_computation.8 | loop fusion | flops 61440 | bytes 122880 | tf_op jit(solution)/shard_map/convert_element_type | solution.py:645
  (10 shorter events, 0.1 us)
Async XLA Ops:
  2.7 10.3 %slice-start.3 = ((s8[12582912]{0:T(1024)(128)(4,1)}), s8[4194304]{0:T(1024)(128)(4,1)S(1)}, s32[]{:S(2)}) async-start(s8[12582912]{0:T(1024)(128)(4,1)} %bitcast.11), calls=%async_computation.3 | async-start | bytes 8388608
  2.7 10.3 %slice-start.4 = ((s8[12582912]{0:T(1024)(128)(4,1)}), s8[4194304]{0:T(1024)(128)(4,1)S(1)}, s32[]{:S(2)}) async-start(s8[12582912]{0:T(1024)(128)(4,1)} %bitcast.11), calls=%async_computation.4 | async-start | bytes 8388608
  2.7 10.2 %slice-start.5 = ((s8[12582912]{0:T(1024)(128)(4,1)}), s8[4194304]{0:T(1024)(128)(4,1)S(1)}, s32[]{:S(2)}) async-start(s8[12582912]{0:T(1024)(128)(4,1)} %bitcast.11), calls=%async_computation.5 | async-start | bytes 8388608
  2.8 4.9 %collective-permute-start = (bf16[16,896]{1,0:T(8,128)(2,1)S(1)}, bf16[16,896]{1,0:T(8,128)(2,1)S(1)}, u32[]{:S(2)}, u32[]{:S(2)}) collective-permute-start(bf16[16,896]{1,0:T(8,128)(2,1)S(1)} %get-tuple-element.18.after.first), channel_id=1, source_target_pairs={{0,4},{4,0},{8,12},{12,8},{1,5},{5,1},{9,13},{13,9},{2,6},{6,2},{1... | collective-permute-start | bytes 86024 | tf_op jit(solution)/shard_map/ppermute | solution.py:534
  7.7 7.7 %slice-start = ((s8[12582912]{0:T(1024)(128)(4,1)}), s8[4194304]{0:T(1024)(128)(4,1)S(1)}, s32[]{:S(2)}) async-start(s8[12582912]{0:T(1024)(128)(4,1)} %bitcast.9), calls=%async_computation | async-start | bytes 8388608
  7.7 7.7 %slice-start.1 = ((s8[12582912]{0:T(1024)(128)(4,1)}), s8[4194304]{0:T(1024)(128)(4,1)S(1)}, s32[]{:S(2)}) async-start(s8[12582912]{0:T(1024)(128)(4,1)} %bitcast.9), calls=%async_computation.1 | async-start | bytes 8388608
  7.7 7.7 %copy-start = (bf16[128,2048]{1,0:T(8,128)(2,1)S(1)}, bf16[128,2048]{1,0:T(8,128)(2,1)}, u32[]{:S(2)}) copy-start(bf16[128,2048]{1,0:T(8,128)(2,1)} %refs_6_.3) | copy-start | bytes 1572868
  7.7 5.3 %collective-permute-start.1 = (bf16[32,896]{1,0:T(8,128)(2,1)S(1)}, bf16[32,896]{1,0:T(8,128)(2,1)S(1)}, u32[]{:S(2)}, u32[]{:S(2)}) collective-permute-start(bf16[32,896]{1,0:T(8,128)(2,1)S(1)} %join.1.after.first), channel_id=1, source_target_pairs={{0,8},{4,12},{8,0},{12,4},{1,9},{5,13},{9,1},{13,5},{2,10},{6,14},... | collective-permute-start | bytes 172040 | tf_op jit(solution)/shard_map/ppermute | solution.py:534
  10.8 4.6 %slice-start.2 = ((s8[12582912]{0:T(1024)(128)(4,1)}), s8[4194304]{0:T(1024)(128)(4,1)S(1)}, s32[]{:S(2)}) async-start(s8[12582912]{0:T(1024)(128)(4,1)} %bitcast.9), calls=%async_computation.2 | async-start | bytes 8388608
  13.5 4.4 %collective-permute-start.2 = (bf16[40,896]{1,0:T(8,128)(2,1)S(1)}, bf16[40,896]{1,0:T(8,128)(2,1)S(1)}, u32[]{:S(2)}, u32[]{:S(2)}) collective-permute-start(bf16[40,896]{1,0:T(8,128)(2,1)S(1)} %get-tuple-element.20.block.refs_0_), channel_id=1, source_target_pairs={{0,2},{1,3},{2,0},{3,1},{4,6},{5,7},{6,4},{7,5},{8,10},{9,11},{10,... | collective-permute-start | bytes 215048 | tf_op jit(solution)/shard_map/ppermute | solution.py:534
  15.4 3.9 %collective-permute-start.3 = (bf16[40,896]{1,0:T(8,128)(2,1)S(1)}, bf16[40,896]{1,0:T(8,128)(2,1)S(1)}, u32[]{:S(2)}, u32[]{:S(2)}) collective-permute-start(bf16[40,896]{1,0:T(8,128)(2,1)S(1)} %get-tuple-element.20.block.refs_0_), channel_id=1, source_target_pairs={{0,1},{1,0},{2,3},{3,2},{4,5},{5,4},{6,7},{7,6},{8,9},{9,8},{10,11... | collective-permute-start | bytes 215048 | tf_op jit(solution)/shard_map/ppermute | solution.py:534
  17.9 1.4 %collective-permute-start.4 = (bf16[40,896]{1,0:T(8,128)(2,1)S(1)}, bf16[40,896]{1,0:T(8,128)(2,1)S(1)}, u32[]{:S(2)}, u32[]{:S(2)}) collective-permute-start(bf16[40,896]{1,0:T(8,128)(2,1)S(1)} %tie.1.block.refs_1_), channel_id=1, source_target_pairs={{0,1},{1,0},{2,3},{3,2},{4,5},{5,4},{6,7},{7,6},{8,9},{9,8},{10,11... | collective-permute-start | bytes 215048 | tf_op jit(solution)/shard_map/ppermute | solution.py:534
  22.2 1.9 %collective-permute-start.5 = (bf16[1,40,768]{2,1,0:T(8,128)(2,1)S(1)}, bf16[1,40,768]{2,1,0:T(8,128)(2,1)S(1)}, u32[]{:S(2)}, u32[]{:S(2)}) collective-permute-start(bf16[1,40,768]{2,1,0:T(8,128)(2,1)S(1)} %get-tuple-element.24.after), channel_id=1, source_target_pairs={{0,1},{1,0},{2,3},{3,2},{4,5},{5,4},{6,7},{7,6},{8,9},{9,8},{10,11... | collective-permute-start | bytes 184328 | tf_op jit(solution)/shard_map/ppermute | solution.py:534
  23.9 4.4 %collective-permute-start.6 = (bf16[1,40,768]{2,1,0:T(8,128)(2,1)S(1)}, bf16[1,40,768]{2,1,0:T(8,128)(2,1)S(1)}, u32[]{:S(2)}, u32[]{:S(2)}) collective-permute-start(bf16[1,40,768]{2,1,0:T(8,128)(2,1)S(1)} %slice.36), channel_id=1, source_target_pairs={{0,1},{1,0},{2,3},{3,2},{4,5},{5,4},{6,7},{7,6},{8,9},{9,8},{10,11... | collective-permute-start | bytes 184328 | tf_op jit(solution)/shard_map/ppermute | solution.py:534
  24.1 4.5 %collective-permute-start.7 = (bf16[1,40,768]{2,1,0:T(8,128)(2,1)S(1)}, bf16[1,40,768]{2,1,0:T(8,128)(2,1)S(1)}, u32[]{:S(2)}, u32[]{:S(2)}) collective-permute-start(bf16[1,40,768]{2,1,0:T(8,128)(2,1)S(1)} %fusion.after), channel_id=1, source_target_pairs={{0,2},{1,3},{2,0},{3,1},{4,6},{5,7},{6,4},{7,5},{8,10},{9,11},{10,... | collective-permute-start | bytes 184328 | tf_op jit(solution)/shard_map/ppermute | solution.py:534
  28.8 4.2 %collective-permute-start.8 = (bf16[2,16,768]{2,1,0:T(8,128)(2,1)S(1)}, bf16[2,16,768]{2,1,0:T(8,128)(2,1)S(1)}, u32[]{:S(2)}, u32[]{:S(2)}) collective-permute-start(bf16[2,16,768]{2,1,0:T(8,128)(2,1)S(1)} %get-tuple-element.28), channel_id=1, source_target_pairs={{0,4},{4,0},{8,12},{12,8},{1,5},{5,1},{9,13},{13,9},{2,6},{6,2},{1... | collective-permute-start | bytes 147464 | tf_op jit(solution)/shard_map/ppermute | solution.py:534
  33.0 4.8 %collective-permute-start.9 = (bf16[1,16,768]{2,1,0:T(8,128)(2,1)S(1)}, bf16[1,16,768]{2,1,0:T(8,128)(2,1)S(1)}, u32[]{:S(2)}, u32[]{:S(2)}) collective-permute-start(bf16[1,16,768]{2,1,0:T(8,128)(2,1)S(1)} %slice.37), channel_id=1, source_target_pairs={{0,8},{4,12},{8,0},{12,4},{1,9},{5,13},{9,1},{13,5},{2,10},{6,14},... | collective-permute-start | bytes 73736 | tf_op jit(solution)/shard_map/ppermute | solution.py:534
